TPU v7x, 128 devices: a whole 4x4x4 slice. The times are simulated.
128 devices in a mesh: ep: 32 (over x, y, core), tp: 4 (over z).
Axes of the slice: x: 4, y: 4, z: 4, core: 2. Of those that a mesh axis runs over, the one named last changes fastest.
Arguments:
- tokens: bfloat16 [6144, 2048], P('ep'), may hold values from -27 to 27
- expert_ids: int32 [6144, 6], P('ep'), may hold values from 0 to 63, as said below
- route_slots: int32 [6144, 6], P('ep'), may hold values from 0 to 35, as said below
- doc_ids: int32 [32, 192], P('ep'), may hold values from 0 to 11, never falling along the last dimension, each value on 1 to 144 neighbouring positions
- prenorm: bfloat16 [2048], P('ep'), may hold values from 0.5 to 1.5
- query_w: bfloat16 [2048, 3072], P('ep', 'tp'), may hold values from -0.125 to 0.125
- latent_w: bfloat16 [2048, 576], P('ep'), may hold values from -0.125 to 0.125
- latnorm: bfloat16 [512], P('ep'), may hold values from 0.5 to 1.5
- keyval_w: bfloat16 [512, 4096], P('ep', 'tp'), may hold values from -0.25 to 0.25
- output_w: bfloat16 [2048, 2048], P('tp', 'ep'), may hold values from -0.75 to 0.75
- midnorm: bfloat16 [2048], P('ep'), may hold values from 0.5 to 1.5
- router_w: bfloat16 [2048, 64], P('ep'), may hold values from -0.0625 to 0.0625
- shgate_w: bfloat16 [2048, 2816], P('ep', 'tp'), may hold values from -0.125 to 0.125
- shup_w: bfloat16 [2048, 2816], P('ep', 'tp'), may hold values from -0.125 to 0.125
- shdown_w: bfloat16 [2816, 2048], P('tp', 'ep'), may hold values from -0.109375 to 0.109375
- exgate_w: bfloat16 [64, 2048, 1408], P('ep', None, 'tp'), may hold values from -0.125 to 0.125
- exup_w: bfloat16 [64, 2048, 1408], P('ep', None, 'tp'), may hold values from -0.125 to 0.125
- exdown_w: bfloat16 [64, 1408, 2048], P('ep', 'tp'), may hold values from -0.15625 to 0.15625
- cotangent: bfloat16 [6144, 2048], P('ep'), may hold values from -6 to 6
Outputs:
- layer_out: bfloat16 [6144, 2048], P('ep')
- tokens_grad: bfloat16 [6144, 2048], P('ep')
- prenorm_grad: float32 [2048], P('ep')
- query_grad: float32 [2048, 3072], P('ep', 'tp')
- latent_grad: float32 [2048, 576], P('ep')
- latnorm_grad: float32 [512], P('ep')
- keyval_grad: float32 [512, 4096], P('ep', 'tp')
- output_grad: float32 [2048, 2048], P('tp', 'ep')
- midnorm_grad: float32 [2048], P('ep')
- router_grad: float32 [2048, 64], P('ep')
- shgate_grad: float32 [2048, 2816], P('ep', 'tp')
- shup_grad: float32 [2048, 2816], P('ep', 'tp')
- shdown_grad: float32 [2816, 2048], P('tp', 'ep')
- exgate_grad: float32 [64, 2048, 1408], P('ep', None, 'tp')
- exup_grad: float32 [64, 2048, 1408], P('ep', None, 'tp')
- exdown_grad: float32 [64, 1408, 2048], P('ep', 'tp')
Inputs may be any that keep to these rules, and one draw needn't show every extreme that they name: `expert_ids`: the 6 experts of a token differ. Among the tokens of one aligned block of 192, at most 36 routes name one expert, and in every draw one expert is named by exactly 36 routes of every such block. `route_slots`: among the tokens of one aligned block of 192, the routes that name one expert have different slots.
All inputs are finite; a program needn't handle non-finite values.
Results may differ from a plain program's by a relative error of at most 0.03.
Values may be sent and summed in bfloat16 or wider, within the bound.
No kernel may reach another device: no remote copies, remote signals or barrier semaphores. Data moves between devices by JAX's collectives and lax.ppermute only.
A program may use at most 256 MiB of HBM per device.

v0:
```python
import math

import jax
import jax.numpy as jnp
from jax import lax
from jax.sharding import PartitionSpec as P

D = 2048
DN = 128
DR = 64
DV = 128
KVR = 512
TOPK = 6
EXP_DEV = 2


epsilon = 1e-06
route_scale = 2.446
rope_base = 50000.0
masked_fill = -1000000000.0


def side_by_side(arrays, axis, dim, along):
    widths = [math.prod(a.shape[along:]) for a in arrays]
    both = jnp.concatenate(
        [a.reshape(*a.shape[:along], w) for a, w in zip(arrays, widths)], axis=along
    )
    filled = lax.all_gather(both, axis, axis=dim, tiled=True)
    tiles = jnp.split(filled, [sum(widths[:k]) for k in range(1, len(widths))], axis=along)
    return tuple(
        (b.reshape(*filled.shape[:along], *a.shape[along:]) for a, b in zip(arrays, tiles))
    )


def from_everyone(value, axis):
    size = lax.axis_size(axis)
    return lax.all_to_all(
        jnp.broadcast_to(value[None], (size, *value.shape)), axis, 0, 0, tiled=True
    )


def over_copies(value, axis):
    return from_everyone(value, axis).astype(jnp.float32).sum(axis=0)


def packed_total(arrays, axis):
    ends = [0]
    for a in arrays:
        ends.append(ends[-1] + a.size)
    so_far = lax.psum(jnp.concatenate([a.ravel() for a in arrays]), axis)
    return tuple((so_far[b:e].reshape(a.shape) for a, b, e in zip(arrays, ends, ends[1:])))


def side_by_side_2(arrays, axis, dim, along):
    widths = [math.prod(a.shape[along:]) for a in arrays]
    both = jnp.concatenate(
        [a.reshape(*a.shape[:along], w) for a, w in zip(arrays, widths)], axis=along
    )
    filled = lax.psum_scatter(both, axis, scatter_dimension=dim, tiled=True)
    tiles = jnp.split(filled, [sum(widths[:k]) for k in range(1, len(widths))], axis=along)
    return tuple(
        (b.reshape(*filled.shape[:along], *a.shape[along:]) for a, b in zip(arrays, tiles))
    )


def matmul(left_mat, right_mat):
    return jnp.dot(left_mat, right_mat, preferred_element_type=jnp.float32)


def silu(values):
    return values / (1.0 + jnp.exp(-values))


def rms_scale(values):
    return lax.rsqrt(jnp.mean(values * values, -1, keepdims=True) + epsilon)


def rms_back(values, scale_vals, gain_vec, upstream):
    weighted = upstream * gain_vec
    inner_mean = jnp.mean(weighted * values, -1, keepdims=True)
    grad_in = scale_vals * weighted - values * scale_vals * scale_vals * scale_vals * inner_mean
    grad_gain = jnp.sum(upstream * values * scale_vals, 0)
    return (grad_in, grad_gain)


def rope_tables(row_count):
    half_dim = DR // 2
    freq_vec = rope_base ** (-(jnp.arange(half_dim, dtype=jnp.float32) * (2.0 / DR)))
    angle_tab = jnp.arange(row_count, dtype=jnp.float32)[:, None] * freq_vec[None, :]
    return (jnp.cos(angle_tab), jnp.sin(angle_tab))


def rotate(values, cos_tab, sine_tab):
    half_dim = values.shape[-1] // 2
    first_half = values[..., :half_dim]
    second_half = values[..., half_dim:]
    return jnp.concatenate(
        [
            first_half * cos_tab - second_half * sine_tab,
            second_half * cos_tab + first_half * sine_tab,
        ],
        -1,
    )


def per_device(
    tokens,
    expert_ids,
    route_slots,
    doc_ids,
    prenorm,
    query_w,
    latent_w,
    latnorm,
    keyval_w,
    output_w,
    midnorm,
    router_w,
    shgate_w,
    shup_w,
    shdown_w,
    exgate_w,
    exup_w,
    exdown_w,
    cotangent,
):
    lane_count = lax.axis_size("tp")
    owner_count = lax.axis_size("ep")
    lane_index = lax.axis_index("tp")
    experts = owner_count * EXP_DEV
    tok_count = tokens.shape[0]
    capacity = 2 * tok_count * TOPK // experts
    lane_slots = capacity // lane_count
    head_count = query_w.shape[1] // (DN + DR)
    score_scale = (DN + DR) ** (-0.5)

    def fetch_dense():
        return (
            *side_by_side((prenorm, query_w, latent_w), "ep", 0, 1),
            *side_by_side((latnorm, keyval_w), "ep", 0, 1),
            lax.all_gather(output_w, "ep", axis=1, tiled=True),
            *side_by_side((midnorm, router_w, shgate_w, shup_w), "ep", 0, 1),
            lax.all_gather(shdown_w, "ep", axis=1, tiled=True),
        )

    gathered = fetch_dense()
    (
        pre_gain,
        query_full,
        latent_full,
        lat_gain,
        keyval_full,
        output_full,
        mid_gain,
        router_full,
        shgate_full,
        shup_full,
        shdown_full,
    ) = gathered
    resid_in = tokens.astype(jnp.float32)
    pre_scale = rms_scale(resid_in)
    pre_weight = pre_gain.astype(jnp.float32)
    normed = (resid_in * pre_scale * pre_weight).astype(jnp.bfloat16)
    query_raw = matmul(normed, query_full).reshape(tok_count, head_count, DN + DR)
    latent_all = matmul(normed, latent_full)
    latent = latent_all[:, :KVR]
    lat_scale = rms_scale(latent)
    lat_weight = lat_gain.astype(jnp.float32)
    latent_n = (latent * lat_scale * lat_weight).astype(jnp.bfloat16)
    keyval = (
        matmul(latent_n, keyval_full).astype(jnp.bfloat16).reshape(tok_count, head_count, DN + DV)
    )
    cos_tab, sine_tab = rope_tables(tok_count)
    q_all = jnp.concatenate(
        [
            query_raw[..., :DN],
            rotate(query_raw[..., DN:], cos_tab[:, None, :], sine_tab[:, None, :]),
        ],
        -1,
    ).astype(jnp.bfloat16)
    key_rot = rotate(latent_all[:, KVR:], cos_tab, sine_tab).astype(jnp.bfloat16)
    key_all = jnp.concatenate(
        [keyval[..., :DN], jnp.broadcast_to(key_rot[:, None, :], (tok_count, head_count, DR))], -1
    )
    values = keyval[..., DN:]
    position = jnp.arange(tok_count)
    doc_row = doc_ids[0]
    allowed = ((doc_row[:, None] == doc_row[None, :]) & (position[:, None] >= position[None, :]))[
        None
    ]

    def masked_scores():
        raw_scores = (
            jnp.einsum("thd,shd->hts", q_all, key_all, preferred_element_type=jnp.float32)
            * score_scale
        )
        return jnp.where(allowed, raw_scores, masked_fill)

    masked = masked_scores()
    row_max = jnp.max(masked, -1, keepdims=True)
    exp_scores = jnp.exp(masked - row_max)
    softmax_sum = jnp.sum(exp_scores, -1, keepdims=True)
    log_total = row_max + jnp.log(softmax_sum)
    attn_probs = (exp_scores / softmax_sum).astype(jnp.bfloat16)
    attended = jnp.einsum("hts,shd->thd", attn_probs, values, preferred_element_type=jnp.float32)
    attended = attended.reshape(tok_count, head_count * DV).astype(jnp.bfloat16)
    attn_out = over_copies(matmul(attended, output_full).astype(jnp.bfloat16), "tp").astype(
        jnp.float32
    )
    mid_resid = resid_in + attn_out
    mid_scale = rms_scale(mid_resid)
    mid_weight = mid_gain.astype(jnp.float32)
    normed2 = (mid_resid * mid_scale * mid_weight).astype(jnp.bfloat16)
    logits = matmul(normed2, router_full)
    chosen = jnp.take_along_axis(logits, expert_ids, 1)
    sel_vals = 1.0 / (1.0 + jnp.exp(-chosen))
    sel_total = jnp.sum(sel_vals, -1, keepdims=True)
    gate_vals = route_scale * sel_vals / sel_total
    sh_gate = matmul(normed2, shgate_full)
    sh_up = matmul(normed2, shup_full)
    sh_hidden = (silu(sh_gate) * sh_up).astype(jnp.bfloat16)
    sh_part = matmul(sh_hidden, shdown_full)
    flat_ids = expert_ids.reshape(-1)
    flat_slots = route_slots.reshape(-1)
    route_id = jnp.arange(tok_count * TOPK, dtype=jnp.int32)
    inverse = (
        jnp.full((experts * capacity,), -1, jnp.int32)
        .at[flat_ids * capacity + flat_slots]
        .set(route_id)
        .reshape(experts, capacity)
    )
    gate_flat = gate_vals.reshape(-1)

    def send_rows(make_rows):
        lane_table = lax.dynamic_slice_in_dim(inverse, lane_index * lane_slots, lane_slots, 1)
        outgoing = make_rows(lane_table).reshape(owner_count, EXP_DEV, lane_slots, D)
        partial_rows = lax.all_to_all(outgoing, "ep", split_axis=0, concat_axis=0, tiled=True)
        arrived_rows = lax.all_gather(partial_rows, "tp", axis=2, tiled=True)
        return arrived_rows

    def give_back(partial_sum):
        summed = lax.psum_scatter(
            partial_sum.astype(jnp.bfloat16), "tp", scatter_dimension=2, tiled=True
        )
        back_rows = lax.all_to_all(summed, "ep", split_axis=0, concat_axis=0, tiled=True)
        return back_rows.reshape(experts * lane_slots, D)

    def forward_rows(index_table):
        filled = index_table >= 0
        picked = normed2[jnp.where(filled, index_table, 0) // TOPK]
        return jnp.where(filled[..., None], picked, jnp.zeros((), jnp.bfloat16))

    arrived = send_rows(forward_rows)
    ex_gate = jnp.einsum("secd,edf->secf", arrived, exgate_w, preferred_element_type=jnp.float32)
    ex_up = jnp.einsum("secd,edf->secf", arrived, exup_w, preferred_element_type=jnp.float32)
    ex_hidden = (silu(ex_gate) * ex_up).astype(jnp.bfloat16)
    returned = give_back(
        jnp.einsum("secf,efd->secd", ex_hidden, exdown_w, preferred_element_type=jnp.float32)
    )
    lane_slot = flat_slots - lane_index * lane_slots
    in_lane = (lane_slot >= 0) & (lane_slot < lane_slots)
    back_index = flat_ids * lane_slots + jnp.where(in_lane, lane_slot, 0)
    fetched = (
        jnp.where(in_lane[:, None], returned[back_index], jnp.zeros((), jnp.bfloat16))
        .astype(jnp.float32)
        .reshape(tok_count, TOPK, D)
    )
    routed = jnp.sum(fetched * gate_vals[:, :, None], 1)
    mixed_out = over_copies((routed + sh_part).astype(jnp.bfloat16), "tp").astype(jnp.float32)
    layer_out = (mid_resid + mixed_out).astype(jnp.bfloat16)
    back_weights = fetch_dense()
    (
        pre_gain,
        query_full,
        latent_full,
        lat_gain,
        keyval_full,
        output_full,
        mid_gain,
        router_full,
        shgate_full,
        shup_full,
        shdown_full,
    ) = back_weights
    upstream = cotangent.astype(jnp.float32)
    dgate_part = jnp.sum(fetched * upstream[:, None, :], -1)

    def grad_rows(index_table):
        filled = index_table >= 0
        safe_index = jnp.where(filled, index_table, 0)
        picked = upstream[safe_index // TOPK] * gate_flat[safe_index][..., None]
        return jnp.where(filled[..., None], picked, 0.0).astype(jnp.bfloat16)

    grad_arrived = send_rows(grad_rows)
    ex_dhidden = jnp.einsum(
        "secd,efd->secf", grad_arrived, exdown_w, preferred_element_type=jnp.float32
    )
    ex_sig = 1.0 / (1.0 + jnp.exp(-ex_gate))
    ex_dgate = (ex_dhidden * ex_up * ex_sig * (1.0 + ex_gate * (1.0 - ex_sig))).astype(jnp.bfloat16)
    ex_dup = (ex_dhidden * ex_gate * ex_sig).astype(jnp.bfloat16)
    exdown_grad = jnp.einsum(
        "secf,secd->efd", ex_hidden, grad_arrived, preferred_element_type=jnp.float32
    )
    exgate_grad = jnp.einsum(
        "secd,secf->edf", arrived, ex_dgate, preferred_element_type=jnp.float32
    )
    exup_grad = jnp.einsum("secd,secf->edf", arrived, ex_dup, preferred_element_type=jnp.float32)
    row_grads = jnp.einsum(
        "secf,edf->secd", ex_dgate, exgate_w, preferred_element_type=jnp.float32
    ) + jnp.einsum("secf,edf->secd", ex_dup, exup_w, preferred_element_type=jnp.float32)
    returned_grad = give_back(row_grads)
    routed_grad = jnp.sum(
        jnp.where(in_lane[:, None], returned_grad[back_index], jnp.zeros((), jnp.bfloat16))
        .astype(jnp.float32)
        .reshape(tok_count, TOPK, D),
        1,
    )
    sh_dhidden = jnp.einsum("td,fd->tf", cotangent, shdown_full, preferred_element_type=jnp.float32)
    sh_sig = 1.0 / (1.0 + jnp.exp(-sh_gate))
    sh_dgate = (sh_dhidden * sh_up * sh_sig * (1.0 + sh_gate * (1.0 - sh_sig))).astype(jnp.bfloat16)
    sh_dup = (sh_dhidden * sh_gate * sh_sig).astype(jnp.bfloat16)
    shdown_grad = jnp.einsum("tf,td->fd", sh_hidden, cotangent, preferred_element_type=jnp.float32)
    shgate_grad = jnp.einsum("td,tf->df", normed2, sh_dgate, preferred_element_type=jnp.float32)
    shup_grad = jnp.einsum("td,tf->df", normed2, sh_dup, preferred_element_type=jnp.float32)
    sh_dnormed = jnp.einsum(
        "tf,df->td", sh_dgate, shgate_full, preferred_element_type=jnp.float32
    ) + jnp.einsum("tf,df->td", sh_dup, shup_full, preferred_element_type=jnp.float32)
    dnormed2, dgate_all = (
        over_copies((routed_grad + sh_dnormed).astype(jnp.bfloat16), "tp").astype(jnp.float32),
        over_copies(dgate_part.astype(jnp.bfloat16), "tp").astype(jnp.float32),
    )
    weighted = jnp.sum(dgate_all * gate_vals, -1, keepdims=True) / route_scale
    dsel_vals = route_scale / sel_total * (dgate_all - weighted)
    dchosen = dsel_vals * sel_vals * (1.0 - sel_vals)
    onehot = (expert_ids[:, :, None] == jnp.arange(experts, dtype=jnp.int32)[None, None, :]).astype(
        jnp.float32
    )
    dlogits = jnp.sum(onehot * dchosen[:, :, None], 1).astype(jnp.bfloat16)
    router_grad = jnp.einsum("td,te->de", normed2, dlogits, preferred_element_type=jnp.float32)
    dnormed2 = dnormed2 + jnp.einsum(
        "te,de->td", dlogits, router_full, preferred_element_type=jnp.float32
    )
    dmid_norm, midnorm_grad = rms_back(mid_resid, mid_scale, mid_weight, dnormed2)
    dmid = upstream + dmid_norm
    dmid16 = dmid.astype(jnp.bfloat16)
    output_grad = jnp.einsum("tj,td->jd", attended, dmid16, preferred_element_type=jnp.float32)
    dattended = (
        jnp.einsum("td,jd->tj", dmid16, output_full, preferred_element_type=jnp.float32)
        .astype(jnp.bfloat16)
        .reshape(tok_count, head_count, DV)
    )
    probs_again = jnp.exp(masked_scores() - log_total)
    dprobs = jnp.einsum("thd,shd->hts", dattended, values, preferred_element_type=jnp.float32)
    dscores = (probs_again * (dprobs - jnp.sum(probs_again * dprobs, -1, keepdims=True))).astype(
        jnp.bfloat16
    )
    dq_all = (
        jnp.einsum("hts,shd->thd", dscores, key_all, preferred_element_type=jnp.float32)
        * score_scale
    )
    dkey_all = (
        jnp.einsum("hts,thd->shd", dscores, q_all, preferred_element_type=jnp.float32) * score_scale
    )
    dvalues = jnp.einsum(
        "hts,thd->shd",
        probs_again.astype(jnp.bfloat16),
        dattended,
        preferred_element_type=jnp.float32,
    )
    dquery = jnp.concatenate(
        [dq_all[..., :DN], rotate(dq_all[..., DN:], cos_tab[:, None, :], -sine_tab[:, None, :])], -1
    )
    dquery = dquery.reshape(tok_count, head_count * (DN + DR)).astype(jnp.bfloat16)
    query_grad = jnp.einsum("td,tj->dj", normed, dquery, preferred_element_type=jnp.float32)
    dkeyval = (
        jnp.concatenate([dkey_all[..., :DN], dvalues], -1)
        .reshape(tok_count, head_count * (DN + DV))
        .astype(jnp.bfloat16)
    )
    keyval_grad = jnp.einsum("tr,tj->rj", latent_n, dkeyval, preferred_element_type=jnp.float32)
    dlatent_part = jnp.einsum("tj,rj->tr", dkeyval, keyval_full, preferred_element_type=jnp.float32)
    dkey_part = jnp.sum(dkey_all[..., DN:], 1)
    dnormed_part = jnp.einsum("tj,dj->td", dquery, query_full, preferred_element_type=jnp.float32)
    dlatent_n, dkey_rot, dnormed_query = tuple(
        (
            part.astype(jnp.float32)
            for part in packed_total(
                (
                    dlatent_part.astype(jnp.bfloat16),
                    dkey_part.astype(jnp.bfloat16),
                    dnormed_part.astype(jnp.bfloat16),
                ),
                "tp",
            )
        )
    )
    dlatent, latnorm_grad = rms_back(latent, lat_scale, lat_weight, dlatent_n)
    dlatent_all = jnp.concatenate([dlatent, rotate(dkey_rot, cos_tab, -sine_tab)], -1).astype(
        jnp.bfloat16
    )
    latent_grad = jnp.einsum("td,tj->dj", normed, dlatent_all, preferred_element_type=jnp.float32)
    dnormed = dnormed_query + jnp.einsum(
        "tj,dj->td", dlatent_all, latent_full, preferred_element_type=jnp.float32
    )
    dtokens, prenorm_grad = rms_back(resid_in, pre_scale, pre_weight, dnormed)
    tokens_grad = (dmid + dtokens).astype(jnp.bfloat16)
    summed_grads = (
        *tuple(
            (
                part.astype(jnp.float32)
                for part in side_by_side_2(
                    (
                        prenorm_grad.astype(jnp.bfloat16),
                        query_grad.astype(jnp.bfloat16),
                        latent_grad.astype(jnp.bfloat16),
                    ),
                    "ep",
                    0,
                    1,
                )
            )
        ),
        *tuple(
            (
                part.astype(jnp.float32)
                for part in side_by_side_2(
                    (latnorm_grad.astype(jnp.bfloat16), keyval_grad.astype(jnp.bfloat16)),
                    "ep",
                    0,
                    1,
                )
            )
        ),
        lax.psum_scatter(
            output_grad.astype(jnp.bfloat16), "ep", scatter_dimension=1, tiled=True
        ).astype(jnp.float32),
        *tuple(
            (
                part.astype(jnp.float32)
                for part in side_by_side_2(
                    (
                        midnorm_grad.astype(jnp.bfloat16),
                        router_grad.astype(jnp.bfloat16),
                        shgate_grad.astype(jnp.bfloat16),
                        shup_grad.astype(jnp.bfloat16),
                    ),
                    "ep",
                    0,
                    1,
                )
            )
        ),
        lax.psum_scatter(
            shdown_grad.astype(jnp.bfloat16), "ep", scatter_dimension=1, tiled=True
        ).astype(jnp.float32),
    )
    return (
        layer_out,
        tokens_grad,
        summed_grads[0],
        summed_grads[1],
        summed_grads[2],
        summed_grads[3],
        summed_grads[4],
        summed_grads[5],
        summed_grads[6],
        summed_grads[7],
        summed_grads[8],
        summed_grads[9],
        summed_grads[10],
        exgate_grad,
        exup_grad,
        exdown_grad,
    )


def solution(mesh):
    in_specs = (
        P("ep", None),
        P("ep", None),
        P("ep", None),
        P("ep", None),
        P("ep"),
        P("ep", "tp"),
        P("ep", None),
        P("ep"),
        P("ep", "tp"),
        P("tp", "ep"),
        P("ep"),
        P("ep", None),
        P("ep", "tp"),
        P("ep", "tp"),
        P("tp", "ep"),
        P("ep", None, "tp"),
        P("ep", None, "tp"),
        P("ep", "tp", None),
        P("ep", None),
    )
    out_specs = (
        P("ep", None),
        P("ep", None),
        P("ep"),
        P("ep", "tp"),
        P("ep", None),
        P("ep"),
        P("ep", "tp"),
        P("tp", "ep"),
        P("ep"),
        P("ep", None),
        P("ep", "tp"),
        P("ep", "tp"),
        P("tp", "ep"),
        P("ep", None, "tp"),
        P("ep", None, "tp"),
        P("ep", "tp", None),
    )
    return jax.shard_map(
        per_device, mesh=mesh, in_specs=in_specs, out_specs=out_specs, check_vma=False
    )
```

profile of v0, /device:TPU:0, one launch (start us, length us, event | category | flops | bytes accessed | tf_op | source)
XLA Modules:
  0.0 1583.1 jit_solution(18348010463106623697)
XLA Ops:
  17.9 38.3 %all-gather.10.cloned.1.call-done = bf16[512,1025]{1,0:T(8,128)(2,1)} async-done(((bf16[16,1025]{1,0:T(8,128)(2,1)}), bf16[512,1025]{1,0:T(8,128)(2,1)}) %all-gather.10.cloned.1.call-update) | async-done | bytes 1049616 | tf_op jit(solution)/shard_map/all_gather | solution.py:28
  57.3 49.3 %all-gather.8.cloned.1.call-done = bf16[2048,1345]{1,0:T(8,128)(2,1)} async-done(((bf16[64,1345]{1,0:T(8,128)(2,1)}), bf16[2048,1345]{1,0:T(8,128)(2,1)}) %all-gather.8.cloned.1.call-update) | async-done | bytes 5509136 | tf_op jit(solution)/shard_map/all_gather | solution.py:28
  130.9 20.9 %all-gather.12.cloned.1.call-done = bf16[512,2048]{0,1:T(8,128)(2,1)} async-done(((bf16[512,64]{0,1:T(8,128)(2,1)}), bf16[512,2048]{0,1:T(8,128)(2,1)}) %all-gather.12.cloned.1.call-update) | async-done | bytes 2097168 | tf_op jit(solution)/shard_map/all_gather | solution.py:141
  161.5 6.9 scatter_custom_fusion
  169.0 33.8 %all-gather.14.cloned.1.call-done = bf16[2048,1473]{1,0:T(8,128)(2,1)} async-done(((bf16[64,1473]{1,0:T(8,128)(2,1)}), bf16[2048,1473]{1,0:T(8,128)(2,1)}) %all-gather.14.cloned.1.call-update) | async-done | bytes 6033424 | tf_op jit(solution)/shard_map/all_gather | solution.py:28
  209.4 8.1 gather_fusion
  229.4 36.0 %all_to_all.40 = bf16[32,2,9,2048]{3,1,2,0:T(2,128)(2,1)S(1)} all-to-all(bf16[32,2,9,2048]{3,1,2,0:T(2,128)(2,1)S(1)} %copy.281), channel_id=1, replica_groups=mesh['ep'=32,'tp'=4] {'ep'}, dimensions={0} | all-to-all | bytes 4718592 | tf_op jit(solution)/shard_map/all_to_all | solution.py:237
  268.1 89.9 %all-gather.16.cloned.1.call-done = bf16[32,2,36,2048]{3,0,1,2:T(8,128)(2,1)} async-done(((bf16[32,2,9,2048]{3,0,1,2:T(8,128)(2,1)}), bf16[32,2,36,2048]{3,0,1,2:T(8,128)(2,1)}) %all-gather.16.cloned.1.call-update) | async-done | bytes 9437200 | tf_op jit(solution)/shard_map/all_gather | solution.py:238
  358.0 8.6 fusion.7
  366.7 7.1 fusion.19
  375.0 8.4 convert_bitcast_fusion
  383.4 12.7 copy.286
  396.1 90.3 %reduce-scatter.12.cloned.1.call-done = bf16[32,2,9,2048]{3,0,1,2:T(8,128)(2,1)} async-done(((bf16[32,2,36,2048]{3,0,1,2:T(8,128)(2,1)}), bf16[32,2,9,2048]{3,0,1,2:T(8,128)(2,1)}) %reduce-scatter.12.cloned.1.call-update) | async-done | bytes 2359312 | tf_op jit(solution)/shard_map/reduce_scatter | solution.py:242
  492.0 7.5 all-to-all-start.2
  501.9 8.1 gather_fusion.2
  516.3 7.3 mul.674
  523.6 11.6 mul.675
  538.5 9.3 gather_fusion.5
  557.9 12.6 gather_fusion.1
  570.5 6.4 multiply_reduce_fusion.1
  591.0 6.6 fusion.10
  600.0 38.7 %all_to_all.41 = bf16[32,2,9,2048]{3,1,2,0:T(2,128)(2,1)S(1)} all-to-all(bf16[32,2,9,2048]{3,1,2,0:T(2,128)(2,1)S(1)} %copy.297), channel_id=1, replica_groups=mesh['ep'=32,'tp'=4] {'ep'}, dimensions={0} | all-to-all | bytes 4718592 | tf_op jit(solution)/shard_map/all_to_all | solution.py:237
  641.2 88.1 %all-gather.20.cloned.1.call-done = bf16[32,2,36,2048]{3,0,1,2:T(8,128)(2,1)} async-done(((bf16[32,2,9,2048]{3,0,1,2:T(8,128)(2,1)}), bf16[32,2,36,2048]{3,0,1,2:T(8,128)(2,1)}) %all-gather.20.cloned.1.call-update) | async-done | bytes 9437200 | tf_op jit(solution)/shard_map/all_gather | solution.py:238
  729.2 10.0 fusion.18
  739.3 9.9 fusion.26
  749.2 12.4 fusion
  761.6 12.9 copy.302
  775.3 89.6 %reduce-scatter.14.cloned.1.call-done = bf16[32,2,9,2048]{3,0,1,2:T(8,128)(2,1)} async-done(((bf16[32,2,36,2048]{3,0,1,2:T(8,128)(2,1)}), bf16[32,2,9,2048]{3,0,1,2:T(8,128)(2,1)}) %reduce-scatter.14.cloned.1.call-update) | async-done | bytes 2359312 | tf_op jit(solution)/shard_map/reduce_scatter | solution.py:242
  870.3 7.6 all-to-all-start.5
  878.0 48.2 %all-gather.18.cloned.1.call-done = bf16[704,2048]{0,1:T(8,128)(2,1)} async-done(((bf16[704,64]{0,1:T(8,128)(2,1)}), bf16[704,2048]{0,1:T(8,128)(2,1)}) %all-gather.18.cloned.1.call-update) | async-done | bytes 2883600 | tf_op jit(solution)/shard_map/all_gather | solution.py:143
  937.3 8.5 gather.30
  955.4 12.6 gather_fusion.4
  968.1 8.5 gather.36
  976.6 14.2 convert_reduce_fusion
  1005.0 34.4 %all-to-all-done.6 = bf16[4,192,2048]{2,1,0:T(8,128)(2,1)} async-done(((bf16[4,192,2048]{2,1,0:T(8,128)(2,1)}), bf16[4,192,2048]{2,1,0:T(8,128)(2,1)}, u32[]{:S(2)}, u32[]{:S(2)}) %all-to-all-start.6) | async-done | bytes 3145760 | tf_op jit(solution)/shard_map/all_to_all | solution.py:37
  1053.4 31.4 %all-to-all-done.3 = bf16[4,192,2048]{2,1,0:T(8,128)(2,1)} async-done(((bf16[4,192,2048]{2,1,0:T(8,128)(2,1)}), bf16[4,192,2048]{2,1,0:T(8,128)(2,1)}, u32[]{:S(2)}, u32[]{:S(2)}) %all-to-all-start.3) | async-done | bytes 3145760 | tf_op jit(solution)/shard_map/all_to_all | solution.py:37
  1109.2 38.0 %all-reduce.2.cloned.1.call-done = bf16[503808]{0:T(1024)(128)(2,1)} async-done(((bf16[503808]{0:T(1024)(128)(2,1)}), bf16[503808]{0:T(1024)(128)(2,1)}) %all-reduce.2.cloned.1.call-update) | async-done | bytes 1007632 | tf_op jit(solution)/shard_map/psum | solution.py:50
  1162.1 31.7 %concatenate.63 = bf16[2048,1473]{0,1:T(8,128)(2,1)} concatenate(bf16[2048,1]{0,1:T(2,128)(2,1)S(1)} %convert_element_type.386, bf16[2048,64]{0,1:T(8,128)(2,1)S(1)} %convolution_convert_fusion.7, bf16[2048,704]{0,1:T(8,128)(2,1)} %convolution_convert_fusion.3, bf16[2048,704]{0,1:T(8,128)(2,1)} %convolution_convert_fusion.2), dimensions={1} | concatenate | bytes 12066816 | tf_op jit(solution)/shard_map/concatenate | solution.py:56
  1193.7 8.7 copy.339
  1216.5 29.1 %concatenate.61 = bf16[2048,1345]{0,1:T(8,128)(2,1)} concatenate(bf16[2048,1]{0,1:T(2,128)(2,1)S(1)} %convert_element_type.370, bf16[2048,768]{0,1:T(8,128)(2,1)} %convolution_convert_fusion.1, bf16[2048,576]{0,1:T(8,128)(2,1)} %convolution_convert_fusion.4), dimensions={1} | concatenate | bytes 11018240 | tf_op jit(solution)/shard_map/concatenate | solution.py:56
  1245.6 8.6 copy.337
  1256.0 10.4 convolution_bitcast_fusion.1
  1266.4 10.4 convolution_bitcast_fusion
  1276.7 10.4 fusion.11
  1288.6 22.7 %reduce-scatter.16.cloned.1.call-done = bf16[16,1025]{1,0:T(8,128)(2,1)} async-done(((bf16[512,1025]{1,0:T(8,128)(2,1)}), bf16[16,1025]{1,0:T(8,128)(2,1)}) %reduce-scatter.16.cloned.1.call-update) | async-done | bytes 32816 | tf_op jit(solution)/shard_map/reduce_scatter | solution.py:59
  1314.1 78.9 %reduce-scatter.18.cloned.1.call-done = bf16[512,64]{0,1:T(8,128)(2,1)} async-done(((bf16[512,2048]{0,1:T(8,128)(2,1)}), bf16[512,64]{0,1:T(8,128)(2,1)}) %reduce-scatter.18.cloned.1.call-update) | async-done | bytes 65552 | tf_op jit(solution)/shard_map/reduce_scatter | solution.py:434
  1394.5 87.7 %reduce-scatter.24.cloned.1.call-done = bf16[64,1473]{1,0:T(8,128)(2,1)} async-done(((bf16[2048,1473]{1,0:T(8,128)(2,1)}), bf16[64,1473]{1,0:T(8,128)(2,1)}) %reduce-scatter.24.cloned.1.call-update) | async-done | bytes 188560
  1488.2 82.7 %reduce-scatter.22.cloned.1.call-done = bf16[64,1345]{1,0:T(8,128)(2,1)} async-done(((bf16[2048,1345]{1,0:T(8,128)(2,1)}), bf16[64,1345]{1,0:T(8,128)(2,1)}) %reduce-scatter.22.cloned.1.call-update) | async-done | bytes 172176
  (384 shorter events, 241.2 us)
Async XLA Ops:
  7.2 367.8 %copy-start = (bf16[2,352,2048]{2,1,0:T(8,128)(2,1)S(1)}, bf16[2,352,2048]{2,1,0:T(8,128)(2,1)}, u32[]{:S(2)}) copy-start(bf16[2,352,2048]{2,1,0:T(8,128)(2,1)} %param.36) | copy-start | bytes 8650756
  7.2 49.0 %all-gather.10.cloned.1.call-start = ((), (), s32[]{:S(2)}) async-start(), calls=%async_computation.16 | async-start | bytes 1216512 | tf_op jit(solution)/shard_map/all_gather | solution.py:28
  9.6 97.0 %all-gather.8.cloned.1.call-start = ((), (), s32[]{:S(2)}) async-start(), calls=%async_computation.15 | async-start | bytes 5947392 | tf_op jit(solution)/shard_map/all_gather | solution.py:28
  12.2 139.5 %all-gather.12.cloned.1.call-start = ((), (), s32[]{:S(2)}) async-start(), calls=%async_computation.17 | async-start | bytes 2162688 | tf_op jit(solution)/shard_map/all_gather | solution.py:141
  13.0 189.8 %all-gather.14.cloned.1.call-start = ((), (), s32[]{:S(2)}) async-start(), calls=%async_computation.18 | async-start | bytes 6488064 | tf_op jit(solution)/shard_map/all_gather | solution.py:28
  15.6 110.6 %copy-start.74 = (f32[32]{0:T(128)}, f32[32]{0:T(128)S(1)}, u32[]{:S(2)}) copy-start(f32[32]{0:T(128)S(1)} %negate_power_fusion) | copy-start | bytes 388
  17.0 100.9 %copy-start.63 = (f32[192]{0:T(256)}, f32[192]{0:T(256)S(1)}, u32[]{:S(2)}) copy-start(f32[192]{0:T(256)S(1)} %add_rsqrt_fusion.2) | copy-start | bytes 2308
  57.3 54.2 %copy-start.61 = (f32[512]{0:T(512)}, f32[512]{0:T(512)S(1)}, u32[]{:S(2)}) copy-start(f32[512]{0:T(512)S(1)} %convert_reduce_fusion.6) | copy-start | bytes 6148
  107.9 10.1 copy-start.55
  111.3 14.9 copy-start.16
  129.4 24.8 %copy-start.65 = (f32[4,192]{1,0:T(4,128)}, f32[4,192]{1,0:T(4,128)S(1)}, u32[]{:S(2)}) copy-start(f32[4,192]{1,0:T(4,128)S(1)} %get-tuple-element.158) | copy-start | bytes 9220
  130.8 25.4 %copy-start.50 = (bf16[4,24,8,128]{3,2,1,0:T(8,128)(2,1)}, bf16[4,24,8,128]{3,2,1,0:T(8,128)(2,1)S(1)}, u32[]{:S(2)}) copy-start(bf16[4,24,8,128]{3,2,1,0:T(8,128)(2,1)S(1)} %fusion.83) | copy-start | bytes 589828
  156.3 47.7 %all-to-all-start = ((bf16[4,192,2048]{2,1,0:T(8,128)(2,1)}), bf16[4,192,2048]{2,1,0:T(8,128)(2,1)}, u32[]{:S(2)}, u32[]{:S(2)}) async-start(bf16[4,192,2048]{2,1,0:T(8,128)(2,1)} %broadcast_in_dim.90), calls=%async_computation | async-start | bytes 6291456 | tf_op jit(solution)/shard_map/all_to_all | solution.py:37
  161.1 196.9 %all-gather.16.cloned.1.call-start = ((), (), s32[]{:S(2)}) async-start(), calls=%async_computation.19 | async-start | bytes 11796480 | tf_op jit(solution)/shard_map/all_gather | solution.py:238
  207.1 10.3 copy-start.71
  267.9 218.6 %reduce-scatter.12.cloned.1.call-start = ((), (), s32[]{:S(2)}) async-start(), calls=%async_computation.20 | async-start | bytes 11796480 | tf_op jit(solution)/shard_map/reduce_scatter | solution.py:242
  492.0 56.1 %all-to-all-start.2 = ((bf16[32,2,9,2048]{3,1,2,0:T(2,128)(2,1)}), bf16[32,2,9,2048]{3,1,2,0:T(2,128)(2,1)}, u32[]{:S(2)}, u32[]{:S(2)}) async-start(bf16[32,2,9,2048]{3,1,2,0:T(2,128)(2,1)} %copy.287), calls=%async_computation.3 | async-start | bytes 4718592 | tf_op jit(solution)/shard_map/all_to_all | solution.py:245
  577.8 8.6 all-to-all-start.7
  581.0 148.2 %all-gather.20.cloned.1.call-start = ((), (), s32[]{:S(2)}) async-start(), calls=%async_computation.22 | async-start | bytes 11796480 | tf_op jit(solution)/shard_map/all_gather | solution.py:238
  641.1 223.7 %reduce-scatter.14.cloned.1.call-start = ((), (), s32[]{:S(2)}) async-start(), calls=%async_computation.23 | async-start | bytes 11796480 | tf_op jit(solution)/shard_map/reduce_scatter | solution.py:242
  729.2 10.0 copy-start.22
  739.2 10.0 copy-start.20
  739.2 9.9 copy-start.25
  739.3 9.9 copy-start.24
  774.5 151.7 %all-gather.18.cloned.1.call-start = ((), (), s32[]{:S(2)}) async-start(), calls=%async_computation.21 | async-start | bytes 3244032 | tf_op jit(solution)/shard_map/all_gather | solution.py:143
  870.3 55.8 %copy-start.8 = (bf16[192,2048]{1,0:T(8,128)(2,1)S(1)}, bf16[192,2048]{1,0:T(8,128)(2,1)}, u32[]{:S(2)}) copy-start(bf16[192,2048]{1,0:T(8,128)(2,1)} %param.37) | copy-start | bytes 2359300
  870.3 75.4 %all-to-all-start.5 = ((bf16[32,2,9,2048]{3,1,2,0:T(2,128)(2,1)}), bf16[32,2,9,2048]{3,1,2,0:T(2,128)(2,1)}, u32[]{:S(2)}, u32[]{:S(2)}) async-start(bf16[32,2,9,2048]{3,1,2,0:T(2,128)(2,1)} %copy.303), calls=%async_computation.7 | async-start | bytes 4718592 | tf_op jit(solution)/shard_map/all_to_all | solution.py:245
  878.0 50.9 %copy-start.2 = (bf16[192,2048]{1,0:T(8,128)(2,1)S(1)}, bf16[192,2048]{1,0:T(8,128)(2,1)}, u32[]{:S(2)}) copy-start(bf16[192,2048]{1,0:T(8,128)(2,1)} %multiply_convert_fusion) | copy-start | bytes 2359300
  935.9 9.8 copy-start.30
  935.9 54.9 %copy-start.32 = (bf16[192,704]{1,0:T(8,128)(2,1)}, bf16[192,704]{1,0:T(8,128)(2,1)S(1)}, u32[]{:S(2)}) copy-start(bf16[192,704]{1,0:T(8,128)(2,1)S(1)} %get-tuple-element.134) | copy-start | bytes 811012
  996.3 43.1 %all-to-all-start.6 = ((bf16[4,192,2048]{2,1,0:T(8,128)(2,1)}), bf16[4,192,2048]{2,1,0:T(8,128)(2,1)}, u32[]{:S(2)}, u32[]{:S(2)}) async-start(bf16[4,192,2048]{2,1,0:T(8,128)(2,1)} %broadcast_in_dim.165), calls=%async_computation.8 | async-start | bytes 6291456 | tf_op jit(solution)/shard_map/all_to_all | solution.py:37
  1042.6 42.3 %all-to-all-start.3 = ((bf16[4,192,2048]{2,1,0:T(8,128)(2,1)}), bf16[4,192,2048]{2,1,0:T(8,128)(2,1)}, u32[]{:S(2)}, u32[]{:S(2)}) async-start(bf16[4,192,2048]{2,1,0:T(8,128)(2,1)} %broadcast_in_dim.99), calls=%async_computation.4 | async-start | bytes 6291456 | tf_op jit(solution)/shard_map/all_to_all | solution.py:37
  1047.4 99.9 %all-reduce.2.cloned.1.call-start = ((), (), s32[]{:S(2)}) async-start(), calls=%async_computation.24 | async-start | bytes 2015232 | tf_op jit(solution)/shard_map/psum | solution.py:50
  1103.8 150.5 %reduce-scatter.20.cloned.1.call-start = ((), (), s32[]{:S(2)}) async-start(), calls=%async_computation.27 | async-start | bytes 3244032 | tf_op jit(solution)/shard_map/reduce_scatter | solution.py:453
  1106.6 204.7 %reduce-scatter.16.cloned.1.call-start = ((), (), s32[]{:S(2)}) async-start(), calls=%async_computation.25 | async-start | bytes 1216512 | tf_op jit(solution)/shard_map/reduce_scatter | solution.py:59
  1109.2 44.0 %copy-start.6 = (f32[192,2048]{1,0:T(8,128)S(1)}, f32[192,2048]{1,0:T(8,128)}, u32[]{:S(2)}) copy-start(f32[192,2048]{1,0:T(8,128)} %copy-done.5) | copy-start | bytes 4718596
  1109.2 44.1 %copy-start.51 = (bf16[4,24,8,128]{3,2,1,0:T(8,128)(2,1)S(1)}, bf16[4,24,8,128]{3,2,1,0:T(8,128)(2,1)}, u32[]{:S(2)}) copy-start(bf16[4,24,8,128]{3,2,1,0:T(8,128)(2,1)} %copy-done.50) | copy-start | bytes 589828
  1153.2 239.8 %reduce-scatter.18.cloned.1.call-start = ((), (), s32[]{:S(2)}) async-start(), calls=%async_computation.26 | async-start | bytes 2162688 | tf_op jit(solution)/shard_map/reduce_scatter | solution.py:434
  1155.5 326.7 %reduce-scatter.24.cloned.1.call-start = ((), (), s32[]{:S(2)}) async-start(), calls=%async_computation.29 | async-start | bytes 6488064
  1193.7 8.7 copy-start.56
  1193.7 8.7 copy-start.64
  1205.2 365.6 %reduce-scatter.22.cloned.1.call-start = ((), (), s32[]{:S(2)}) async-start(), calls=%async_computation.28 | async-start | bytes 5947392
  1256.0 10.4 copy-start.26
  1266.4 10.4 copy-start.78
  1276.7 10.4 copy-start.7
  1276.7 10.4 copy-start.12
  1276.7 10.4 copy-start.27
  1287.2 288.9 %copy-start.1 = (bf16[2,352,2048]{2,1,0:T(8,128)(2,1)S(1)}, bf16[2,352,2048]{2,1,0:T(8,128)(2,1)}, u32[]{:S(2)}) copy-start(bf16[2,352,2048]{2,1,0:T(8,128)(2,1)} %param.36) | copy-start | bytes 8650756
  (55 other events, 173.6 us)
Sparse Core Ops, SparseCore 0:
  10.9 45.2 all-gather.9
  59.1 47.4 all-gather.7
  108.9 42.8 all-gather.11
  154.5 48.2 all-gather.13
  268.0 89.9 all-gather.15
  396.2 90.1 reduce-scatter.11
  641.2 87.9 all-gather.19
  774.6 90.1 reduce-scatter.13
  867.1 59.0 all-gather.17
  1103.9 43.2 all-reduce.1
  1151.9 80.8 reduce-scatter.19
  1236.2 75.0 reduce-scatter.15
  1314.9 78.0 reduce-scatter.17
  1396.6 85.5 reduce-scatter.23
  1486.3 84.5 reduce-scatter.21
where the time goes:
time: 1600 us; the launch traced here: 1580 us
  waiting for transfers between devices  931 us (58%)
  local copies, waits for them, and re-layouts  301 us (19%)
  matrix products  153 us (10%)
  blocking collectives  74.7 us (5%)
  other arithmetic  73.5 us (5%)
  starting transfers between devices  33.8 us (2%)
    reduce_scatter x2, waiting for transfers between devices, give_back(): lax.psum_scatter(partial_sum.astype(jnp.bfloat16), 'tp', scatter_dimensio...  180 us
    all_gather x2, waiting for transfers between devices, send_rows(): arrived_rows = lax.all_gather(partial_rows, 'tp', axis=2, tiled=True)  178 us
    unnamed x17, waiting for transfers between devices  172 us
    all_gather x3, waiting for transfers between devices, side_by_side(): filled = lax.all_gather(both, axis, axis=dim, tiled=True)  121 us
    reduce_scatter x1, waiting for transfers between devices, per_device(): lax.psum_scatter(output_grad.astype(jnp.bfloat16), 'ep', scatter_dimensio...  78.9 us
    all_to_all x2, blocking collectives, send_rows(): lax.all_to_all(outgoing, 'ep', split_axis=0, concat_axis=0, tiled=True)  74.7 us
    all_to_all x4, waiting for transfers between devices, from_everyone(): lax.all_to_all(jnp.broadcast_to(value[None], (size, *value.shape)), axis,...  71.1 us
    concatenate x2, local copies, waits for them, and re-layouts, side_by_side_2(): jnp.concatenate([a.reshape(*a.shape[:along], w) for a, w in zip(arrays, w...  60.7 us
  transfers between devices with their start and end apart: 21, of which 17 were waited for; matrix products, arithmetic and copies ran while one was open for 18% of the time, Pallas kernels for 0%

commit v1 on v0

v1 whole, which is shorter than its diff:
```python
import jax
import jax.numpy as jnp
from jax import lax
from jax.sharding import PartitionSpec as P

D = 2048
DN = 128
DR = 64
DV = 128
KVR = 512
TOPK = 6
EXP_DEV = 2
MAIN = 32

epsilon = 1e-06
route_scale = 2.446
rope_base = 50000.0
masked_fill = -1000000000.0

bf16 = jnp.bfloat16
f32 = jnp.float32


def matmul(left_mat, right_mat):
    return jnp.dot(left_mat, right_mat, preferred_element_type=f32)


def matmul_nt(left_mat, right_mat):
    return lax.dot_general(
        left_mat, right_mat, (((1,), (1,)), ((), ())), preferred_element_type=f32
    )


def matmul_tn(left_mat, right_mat):
    return lax.dot_general(
        left_mat, right_mat, (((0,), (0,)), ((), ())), preferred_element_type=f32
    )


def rms_scale(values):
    return lax.rsqrt(jnp.mean(values * values, -1, keepdims=True) + epsilon)


def rms_back(values, scale_vals, gain_vec, upstream):
    weighted = upstream * gain_vec
    inner_mean = jnp.mean(weighted * values, -1, keepdims=True)
    grad_in = scale_vals * weighted - values * scale_vals * scale_vals * scale_vals * inner_mean
    grad_gain = jnp.sum(upstream * values * scale_vals, 0)
    return (grad_in, grad_gain)


def rope_tables(row_count):
    half_dim = DR // 2
    freq_vec = rope_base ** (-(jnp.arange(half_dim, dtype=f32) * (2.0 / DR)))
    angle_tab = jnp.arange(row_count, dtype=f32)[:, None] * freq_vec[None, :]
    return (jnp.cos(angle_tab), jnp.sin(angle_tab))


def rotate(values, cos_tab, sine_tab):
    half_dim = values.shape[-1] // 2
    first_half = values[..., :half_dim]
    second_half = values[..., half_dim:]
    return jnp.concatenate(
        [
            first_half * cos_tab - second_half * sine_tab,
            second_half * cos_tab + first_half * sine_tab,
        ],
        -1,
    )


def shift(value, step):
    lanes = lax.axis_size("tp")
    return lax.ppermute(value, "tp", [(i, (i + step) % lanes) for i in range(lanes)])


def quarter_of(value, step):
    lanes = lax.axis_size("tp")
    width = value.shape[1] // lanes
    lane = lax.rem(lax.axis_index("tp") + step, lanes)
    return lax.dynamic_slice_in_dim(value, lane * width, width, 1)


def sum_to_quarter(partial):
    low = partial.astype(bf16)
    total = quarter_of(low, 0).astype(f32)
    for step in (1, 3, 2):
        total = total + shift(quarter_of(low, step), step).astype(f32)
    return total


def gather_quarters(piece):
    return lax.all_gather(piece, "tp", axis=1, tiled=True)


def sum_small(partial):
    total = partial.astype(f32)
    for step in (1, 3, 2):
        total = total + shift(partial, step).astype(f32)
    return total


def exchange(value):
    return lax.all_to_all(value, "ep", 0, 0, tiled=True)


def to_experts(value):
    blocks = value.shape[0]
    rest = value.shape[2:]
    return jnp.concatenate(
        [
            value[:, :MAIN].reshape(blocks * MAIN, *rest),
            value[:, MAIN:-MAIN].reshape(-1, *rest),
            value[:, -MAIN:].reshape(blocks * MAIN, *rest),
        ],
        0,
    )


def from_experts(value, blocks):
    rest = value.shape[1:]
    edge = blocks * MAIN
    return jnp.concatenate(
        [
            value[:edge].reshape(blocks, MAIN, *rest),
            value[edge:-edge].reshape(blocks, -1, *rest),
            value[-edge:].reshape(blocks, MAIN, *rest),
        ],
        1,
    )


def lanes_gather(piece):
    half = piece.shape[0] // 2
    width = piece.shape[1]
    lane = lax.axis_index("tp")
    lanes = lax.axis_size("tp")
    from_prev = shift(piece, 1)
    from_next = shift(piece, 3)
    far_top = shift(from_prev[:half], 1)
    far_bottom = shift(from_next[half:], 3)
    full = jnp.zeros((piece.shape[0], width * lanes), piece.dtype)
    for part, row, step in (
        (piece, 0, 0),
        (from_next, 0, 1),
        (from_prev, 0, 3),
        (far_top, 0, 2),
        (far_bottom, half, 2),
    ):
        place = lax.rem(lane + step, lanes) * width
        full = lax.dynamic_update_slice(full, part, (row, place))
    return full


def lanes_sum(parts):
    own, after, far, before = parts
    half = own.shape[0] // 2
    top = shift(far[:half], 1)
    bottom = shift(far[half:], 3)

    def plus(one, two):
        return (one.astype(f32) + two.astype(f32)).astype(bf16)

    from_prev = shift(jnp.concatenate([plus(after[:half], top), after[half:]], 0), 1)
    from_next = shift(jnp.concatenate([before[:half], plus(before[half:], bottom)], 0), 3)
    return (own.astype(f32) + from_prev.astype(f32) + from_next.astype(f32)).astype(bf16)


def per_device(
    tokens,
    expert_ids,
    route_slots,
    doc_ids,
    prenorm,
    query_w,
    latent_w,
    latnorm,
    keyval_w,
    output_w,
    midnorm,
    router_w,
    shgate_w,
    shup_w,
    shdown_w,
    exgate_w,
    exup_w,
    exdown_w,
    cotangent,
):
    owner_count = lax.axis_size("ep")
    experts = owner_count * EXP_DEV
    tok_count = tokens.shape[0]
    capacity = 2 * tok_count * TOPK // experts
    spill = capacity - MAIN
    width = EXP_DEV * capacity
    slot_rows = owner_count * width
    head_count = query_w.shape[1] // (DN + DR)
    score_scale = (DN + DR) ** (-0.5)
    shard = query_w.shape[0]
    q_cols = query_w.shape[1]
    lat_cols = latent_w.shape[1]
    kv_cols = keyval_w.shape[0] * keyval_w.shape[1] // shard
    out_cols = output_w.shape[0]
    sh_cols = shgate_w.shape[1]

    gains = jnp.stack(
        [prenorm, jnp.pad(latnorm, (0, shard - latnorm.shape[0])), midnorm], 1
    )
    gains = jnp.pad(gains, ((0, 0), (0, 128 - gains.shape[1])))
    first_pack = jnp.concatenate(
        [query_w, latent_w, router_w, keyval_w.reshape(shard, kv_cols), output_w.T, gains], 1
    )
    first_full = lax.all_gather(first_pack, "ep", axis=0, tiled=True)
    edges = [0]
    for cols in (q_cols, lat_cols, experts, kv_cols, out_cols, 128):
        edges.append(edges[-1] + cols)
    query_full = first_full[:, edges[0] : edges[1]]
    latent_full = first_full[:, edges[1] : edges[2]]
    router_full = first_full[:, edges[2] : edges[3]]
    keyval_full = first_full[:, edges[3] : edges[4]].reshape(KVR, keyval_w.shape[1])
    output_t = first_full[:, edges[4] : edges[5]]
    pre_gain = first_full[:, edges[5]]
    lat_gain = first_full[:, edges[5] + 1].reshape(owner_count, shard)[:, : latnorm.shape[0]]
    lat_gain = lat_gain.reshape(KVR)
    mid_gain = first_full[:, edges[5] + 2]

    local = expert_ids % EXP_DEV
    inside = jnp.where(
        route_slots < MAIN,
        local * (MAIN + EXP_DEV * spill) + route_slots,
        MAIN + local * spill + (route_slots - MAIN),
    )
    place = (expert_ids // EXP_DEV) * width + inside
    row_iota = lax.broadcasted_iota(jnp.int32, (slot_rows, tok_count), 0)
    matches = [row_iota == place[:, k][None, :] for k in range(TOPK)]
    pick = matches[0]
    for k in range(1, TOPK):
        pick = pick | matches[k]
    pick = pick.astype(bf16)
    token_iota = lax.broadcasted_iota(jnp.int32, (slot_rows, tok_count), 1)
    table = jnp.sum(jnp.where(pick > 0, token_iota + 1, 0), 1).astype(jnp.int32) - 1
    table = exchange(table.reshape(owner_count, width))

    upstream_all, first_full_ = lax.optimization_barrier((cotangent, first_full))
    dy_all = lax.all_gather(upstream_all, "ep", axis=0, tiled=True)
    dy_all = dy_all.reshape(owner_count, tok_count, D)
    second_pack = jnp.concatenate([shgate_w, shup_w, shdown_w.T], 1)
    second_pack, dy_all = lax.optimization_barrier((second_pack, dy_all))
    second_full = lax.all_gather(second_pack, "ep", axis=0, tiled=True)
    gateup_full = second_full[:, : 2 * sh_cols]
    shdown_t = second_full[:, 2 * sh_cols :]

    resid_in = tokens.astype(f32)
    pre_scale = rms_scale(resid_in)
    pre_weight = pre_gain.astype(f32)
    normed = (resid_in * pre_scale * pre_weight).astype(bf16)
    query_raw = matmul(normed, query_full).reshape(tok_count, head_count, DN + DR)
    latent_all = matmul(normed, latent_full)
    latent = latent_all[:, :KVR]
    lat_scale = rms_scale(latent)
    lat_weight = lat_gain.astype(f32)
    latent_n = (latent * lat_scale * lat_weight).astype(bf16)
    keyval = matmul(latent_n, keyval_full).astype(bf16).reshape(tok_count, head_count, DN + DV)
    cos_tab, sine_tab = rope_tables(tok_count)
    q_all = jnp.concatenate(
        [
            query_raw[..., :DN],
            rotate(query_raw[..., DN:], cos_tab[:, None, :], sine_tab[:, None, :]),
        ],
        -1,
    ).astype(bf16)
    key_rot = rotate(latent_all[:, KVR:], cos_tab, sine_tab).astype(bf16)
    key_all = jnp.concatenate(
        [keyval[..., :DN], jnp.broadcast_to(key_rot[:, None, :], (tok_count, head_count, DR))], -1
    )
    values = keyval[..., DN:]
    position = jnp.arange(tok_count)
    doc_row = doc_ids[0]
    allowed = ((doc_row[:, None] == doc_row[None, :]) & (position[:, None] >= position[None, :]))[
        None
    ]
    raw_scores = (
        jnp.einsum("thd,shd->hts", q_all, key_all, preferred_element_type=f32) * score_scale
    )
    masked = jnp.where(allowed, raw_scores, masked_fill)
    row_max = jnp.max(masked, -1, keepdims=True)
    exp_scores = jnp.exp(masked - row_max)
    softmax_sum = jnp.sum(exp_scores, -1, keepdims=True)
    probs = exp_scores / softmax_sum
    probs16 = probs.astype(bf16)
    attended = jnp.einsum("hts,shd->thd", probs16, values, preferred_element_type=f32)
    attended = attended.reshape(tok_count, head_count * DV).astype(bf16)
    attn_sum = gather_quarters(sum_to_quarter(matmul_nt(attended, output_t)).astype(bf16))
    mid_resid = resid_in + attn_sum.astype(f32)
    mid_scale = rms_scale(mid_resid)
    mid_weight = mid_gain.astype(f32)
    normed2 = (mid_resid * mid_scale * mid_weight).astype(bf16)

    sent = matmul(pick, quarter_of(normed2, 0)).astype(bf16)
    arrived = to_experts(exchange(sent.reshape(owner_count, width, -1)))
    rows = lanes_gather(arrived)

    logits = matmul(normed2, router_full)
    onehot = (
        expert_ids[:, :, None] == jnp.arange(experts, dtype=jnp.int32)[None, None, :]
    ).astype(f32)
    chosen = jnp.sum(onehot * logits[:, None, :], -1)
    sel_vals = 1.0 / (1.0 + jnp.exp(-chosen))
    sel_total = jnp.sum(sel_vals, -1, keepdims=True)
    gate_vals = route_scale * sel_vals / sel_total
    gate_rows = jnp.zeros((slot_rows, tok_count), f32)
    for k in range(TOPK):
        gate_rows = gate_rows + jnp.where(matches[k], gate_vals[:, k][None, :], 0.0)
    gate_rows = jnp.sum(gate_rows, 1).reshape(owner_count, width)
    gate_rows = to_experts(exchange(gate_rows))[:, None]

    upstream = cotangent.astype(f32)
    sh_both = matmul(normed2, gateup_full)
    sh_gate = sh_both[:, :sh_cols]
    sh_up = sh_both[:, sh_cols:]
    sh_sig = 1.0 / (1.0 + jnp.exp(-sh_gate))
    sh_hidden = (sh_gate * sh_sig * sh_up).astype(bf16)
    shared_q = sum_to_quarter(matmul_nt(sh_hidden, shdown_t))
    sh_dhidden = matmul(cotangent, shdown_t)
    sh_dgate = (sh_dhidden * sh_up * sh_sig * (1.0 + sh_gate * (1.0 - sh_sig))).astype(bf16)
    sh_dup = (sh_dhidden * sh_gate * sh_sig).astype(bf16)
    sh_dboth = jnp.concatenate([sh_dgate, sh_dup], 1)
    sh_dnormed_q = sum_to_quarter(matmul_nt(sh_dboth, gateup_full))
    second_grad = jnp.concatenate(
        [matmul_tn(normed2, sh_dboth).astype(bf16), matmul_tn(cotangent, sh_hidden).astype(bf16)],
        1,
    )
    second_sum = lax.psum_scatter(second_grad, "ep", scatter_dimension=0, tiled=True)

    pick_in = (
        table[:, :, None] == lax.broadcasted_iota(jnp.int32, (owner_count, width, tok_count), 2)
    ).astype(bf16)
    dy_rows = jnp.einsum("ist,itd->isd", pick_in, dy_all, preferred_element_type=f32)
    dy_rows = to_experts(dy_rows.astype(bf16))
    edge = owner_count * MAIN
    extra = slot_rows - 2 * edge
    span = edge + extra
    extra_iota = lax.broadcasted_iota(jnp.int32, (span, 1), 0)
    owned = (
        (extra_iota < edge) | ((extra_iota - edge) % (EXP_DEV * spill) < spill),
        (extra_iota >= extra) | (extra_iota % (EXP_DEV * spill) >= spill),
    )

    def join(first, second):
        return jnp.concatenate([first[:edge], first[edge:] + second[:extra], second[extra:]], 0)

    outs, drows, dgates = [], [], []
    exgate_grad, exup_grad, exdown_grad = [], [], []
    for e in range(EXP_DEV):
        at = slice(0, span) if e == 0 else slice(edge, slot_rows)
        e_rows, e_dy, e_gate = rows[at], dy_rows[at], gate_rows[at]
        ex_gate = matmul(e_rows, exgate_w[e])
        ex_up = matmul(e_rows, exup_w[e])
        ex_sig = 1.0 / (1.0 + jnp.exp(-ex_gate))
        ex_hidden = jnp.where(owned[e], ex_gate * ex_sig * ex_up, 0.0).astype(bf16)
        outs.append(matmul(ex_hidden, exdown_w[e]) * e_gate)
        ex_dh = matmul_nt(e_dy, exdown_w[e])
        dgates.append(jnp.sum(ex_hidden.astype(f32) * ex_dh, 1))
        ex_dh = jnp.where(owned[e], ex_dh * e_gate, 0.0)
        ex_dgate = (ex_dh * ex_up * ex_sig * (1.0 + ex_gate * (1.0 - ex_sig))).astype(bf16)
        ex_dup = (ex_dh * ex_gate * ex_sig).astype(bf16)
        drows.append(matmul_nt(ex_dgate, exgate_w[e]) + matmul_nt(ex_dup, exup_w[e]))
        exgate_grad.append(matmul_tn(e_rows, ex_dgate))
        exup_grad.append(matmul_tn(e_rows, ex_dup))
        exdown_grad.append(
            matmul_tn((ex_hidden.astype(f32) * e_gate).astype(bf16), e_dy)
        )
    out_rows = join(*outs).astype(bf16)
    drow_rows = join(*drows).astype(bf16)
    dgate_rows = exchange(from_experts(join(*dgates), owner_count)).reshape(-1)

    def give_back(value):
        summed = lanes_sum([quarter_of(value, step) for step in range(4)])
        back = exchange(from_experts(summed, owner_count)).reshape(slot_rows, -1)
        return matmul_tn(pick, back)

    routed_grad_q = give_back(drow_rows)
    routed_q = give_back(out_rows)
    layer_q = (quarter_of(mid_resid, 0) + routed_q + shared_q).astype(bf16)
    layer_out = gather_quarters(layer_q)

    dgate_part = jnp.stack(
        [jnp.sum(jnp.where(matches[k], dgate_rows[:, None], 0.0), 0) for k in range(TOPK)], 1
    )
    dgate_all = sum_small(dgate_part)
    weighted = jnp.sum(dgate_all * gate_vals, -1, keepdims=True) / route_scale
    dsel_vals = route_scale / sel_total * (dgate_all - weighted)
    dchosen = dsel_vals * sel_vals * (1.0 - sel_vals)
    dlogits = jnp.sum(onehot * dchosen[:, :, None], 1).astype(bf16)
    router_grad = matmul_tn(normed2, dlogits)
    dnormed2 = gather_quarters((routed_grad_q + sh_dnormed_q).astype(bf16)).astype(f32)
    dnormed2 = dnormed2 + matmul_nt(dlogits, router_full)
    dmid_norm, midnorm_grad = rms_back(mid_resid, mid_scale, mid_weight, dnormed2)
    dmid = upstream + dmid_norm
    dmid16 = dmid.astype(bf16)
    output_grad_t = matmul_tn(dmid16, attended)
    dattended = matmul(dmid16, output_t).astype(bf16).reshape(tok_count, head_count, DV)
    dprobs = jnp.einsum("thd,shd->hts", dattended, values, preferred_element_type=f32)
    dscores = (probs * (dprobs - jnp.sum(probs * dprobs, -1, keepdims=True))).astype(bf16)
    dq_all = (
        jnp.einsum("hts,shd->thd", dscores, key_all, preferred_element_type=f32) * score_scale
    )
    dkey_all = jnp.einsum("hts,thd->shd", dscores, q_all, preferred_element_type=f32) * score_scale
    dvalues = jnp.einsum("hts,thd->shd", probs16, dattended, preferred_element_type=f32)
    dquery = jnp.concatenate(
        [dq_all[..., :DN], rotate(dq_all[..., DN:], cos_tab[:, None, :], -sine_tab[:, None, :])], -1
    )
    dquery = dquery.reshape(tok_count, head_count * (DN + DR)).astype(bf16)
    dkeyval = (
        jnp.concatenate([dkey_all[..., :DN], dvalues], -1)
        .reshape(tok_count, head_count * (DN + DV))
        .astype(bf16)
    )
    keyval_grad = matmul_tn(latent_n, dkeyval)
    dlatent_part = matmul_nt(dkeyval, keyval_full)
    dkey_part = jnp.sum(dkey_all[..., DN:], 1)
    dlat_sum = sum_small(jnp.concatenate([dlatent_part, dkey_part], 1).astype(bf16))
    dnormed_q = sum_to_quarter(matmul_nt(dquery, query_full))
    dlatent, latnorm_grad = rms_back(latent, lat_scale, lat_weight, dlat_sum[:, :KVR])
    dlatent_all = jnp.concatenate(
        [dlatent, rotate(dlat_sum[:, KVR:], cos_tab, -sine_tab)], -1
    ).astype(bf16)
    dnormed = gather_quarters(dnormed_q.astype(bf16)).astype(f32) + matmul_nt(
        dlatent_all, latent_full
    )
    dtokens, prenorm_grad = rms_back(resid_in, pre_scale, pre_weight, dnormed)
    tokens_grad = (dmid + dtokens).astype(bf16)
    gain_grads = jnp.stack(
        [
            prenorm_grad,
            jnp.pad(
                latnorm_grad.reshape(owner_count, -1),
                ((0, 0), (0, shard - latnorm.shape[0])),
            ).reshape(-1),
            midnorm_grad,
        ],
        1,
    )
    gain_grads = jnp.pad(gain_grads, ((0, 0), (0, 128 - gain_grads.shape[1])))
    first_grad = jnp.concatenate(
        [
            matmul_tn(normed, dquery).astype(bf16),
            matmul_tn(normed, dlatent_all).astype(bf16),
            router_grad.astype(bf16),
            keyval_grad.astype(bf16).reshape(D, kv_cols),
            output_grad_t.astype(bf16),
            gain_grads.astype(bf16),
        ],
        1,
    )
    first_sum = lax.psum_scatter(first_grad, "ep", scatter_dimension=0, tiled=True).astype(f32)
    second_sum = second_sum.astype(f32)
    return (
        layer_out,
        tokens_grad,
        first_sum[:, edges[5]],
        first_sum[:, edges[0] : edges[1]],
        first_sum[:, edges[1] : edges[2]],
        first_sum[: latnorm.shape[0], edges[5] + 1],
        first_sum[:, edges[3] : edges[4]].reshape(keyval_w.shape),
        first_sum[:, edges[4] : edges[5]].T,
        first_sum[:, edges[5] + 2],
        first_sum[:, edges[2] : edges[3]],
        second_sum[:, :sh_cols],
        second_sum[:, sh_cols : 2 * sh_cols],
        second_sum[:, 2 * sh_cols :].T,
        jnp.stack(exgate_grad),
        jnp.stack(exup_grad),
        jnp.stack(exdown_grad),
    )


def solution(mesh):
    in_specs = (
        P("ep", None),
        P("ep", None),
        P("ep", None),
        P("ep", None),
        P("ep"),
        P("ep", "tp"),
        P("ep", None),
        P("ep"),
        P("ep", "tp"),
        P("tp", "ep"),
        P("ep"),
        P("ep", None),
        P("ep", "tp"),
        P("ep", "tp"),
        P("tp", "ep"),
        P("ep", None, "tp"),
        P("ep", None, "tp"),
        P("ep", "tp", None),
        P("ep", None),
    )
    out_specs = (
        P("ep", None),
        P("ep", None),
        P("ep"),
        P("ep", "tp"),
        P("ep", None),
        P("ep"),
        P("ep", "tp"),
        P("tp", "ep"),
        P("ep"),
        P("ep", None),
        P("ep", "tp"),
        P("ep", "tp"),
        P("tp", "ep"),
        P("ep", None, "tp"),
        P("ep", None, "tp"),
        P("ep", "tp", None),
    )
    return jax.shard_map(
        per_device, mesh=mesh, in_specs=in_specs, out_specs=out_specs, check_vma=False
    )
```

time: 1600 us -> 828 us (0.52)
  waiting for transfers between devices: 931 us -> 278 us
  local copies, waits for them, and re-layouts: 301 us -> 105 us
  blocking collectives: 74.7 us -> 118 us
  starting transfers between devices: 33.8 us -> 73.2 us
    all_gather x7 -> x3, waiting for transfers between devices: 369 us -> 57.9 us  [the longest x1 57.9 us: per_device(): first_full = lax.all_gather(first_pack, 'ep', axis=0, tiled=True)]
    reduce_scatter x5 -> x0, waiting for transfers between devices: 282 us -> none  [the longest x2 180 us: give_back(): lax.psum_scatter(partial_sum.astype(jnp.bfloat16), 'tp', scatter_dimensio...]
    ppermute x0 -> x30, waiting for transfers between devices: none -> 175 us  [shift(): lax.ppermute(value, 'tp', [(i, (i + step) % lanes) for i in range(lanes)])]
    unnamed x17 -> x7, waiting for transfers between devices: 172 us -> 0.09 us
    gather x14 -> x0, local copies, waits for them, and re-layouts: 83 us -> none  [the longest x2 21.1 us: per_device(): returned_grad[back_index]]
    concatenate x4, local copies, waits for them, and re-layouts: 64.3 us -> 2.6 us  [the longest x1 1.74 us: per_device(): jnp.concatenate([query_w, latent_w, router_w, keyval_w.reshape(shard, kv_...]
    all_gather x0 -> x4, blocking collectives: none -> 56.4 us  [gather_quarters(): return lax.all_gather(piece, 'tp', axis=1, tiled=True)]
    ppermute x0 -> x30, starting transfers between devices: none -> 47.1 us  [shift(): lax.ppermute(value, 'tp', [(i, (i + step) % lanes) for i in range(lanes)])]
  transfers between devices with their start and end apart: 21 -> 40, of which waited for: 17 -> 21; matrix products, arithmetic and copies ran while one was open for 18% -> 38% of each run, Pallas kernels for 0% -> 0%
where the time goes in v1:
time: 828 us; the launch traced here: 817 us
  waiting for transfers between devices  278 us (34%)
  matrix products  160 us (19%)
  blocking collectives  118 us (14%)
  local copies, waits for them, and re-layouts  105 us (13%)
  starting transfers between devices  73.2 us (9%)
  other arithmetic  67.1 us (8%)
  between operations  16.3 us (2%)
    ppermute x30, waiting for transfers between devices, shift(): lax.ppermute(value, 'tp', [(i, (i + step) % lanes) for i in range(lanes)])  175 us
    all_to_all x1, blocking collectives, exchange(): return lax.all_to_all(value, 'ep', 0, 0, tiled=True)  61.3 us
    all_gather x1, waiting for transfers between devices, per_device(): first_full = lax.all_gather(first_pack, 'ep', axis=0, tiled=True)  57.9 us
    all_gather x4, blocking collectives, gather_quarters(): return lax.all_gather(piece, 'tp', axis=1, tiled=True)  56.4 us
    dot_general x14, matrix products, matmul(): return jnp.dot(left_mat, right_mat, preferred_element_type=f32)  52.1 us
    ppermute x30, starting transfers between devices, shift(): lax.ppermute(value, 'tp', [(i, (i + step) % lanes) for i in range(lanes)])  47.1 us
    unnamed x239, local copies, waits for them, and re-layouts  46.5 us
    dot_general x15, matrix products, matmul_tn(): lax.dot_general(left_mat, right_mat, (((0,), (0,)), ((), ())), preferred_...  46.4 us
  transfers between devices with their start and end apart: 40, of which 21 were waited for; matrix products, arithmetic and copies ran while one was open for 38% of the time, Pallas kernels for 0%

profile of v1, /device:TPU:0, one launch (start us, length us, event | category | flops | bytes accessed | tf_op | source)
XLA Modules:
  0.0 817.0 jit_solution(7824648080610096319)
XLA Ops:
  11.4 57.9 %all-gather.4.cloned.1.call-done = bf16[2048,2304]{1,0:T(8,128)(2,1)} async-done(((bf16[64,2304]{1,0:T(8,128)(2,1)}), bf16[2048,2304]{1,0:T(8,128)(2,1)}) %all-gather.4.cloned.1.call-update) | async-done | bytes 9437200 | tf_op jit(solution)/shard_map/all_gather | solution.py:213
  103.3 14.0 %all_gather.22 = bf16[192,2048]{1,0:T(8,128)(2,1)S(1)} all-gather(bf16[192,512]{1,0:T(8,128)(2,1)S(1)} %add_convert_fusion.10), channel_id=1, replica_groups=mesh['ep'=32,'tp'=4] {'tp'}, dimensions={1}, use_global_device_ids=true | all-gather | bytes 983040 | tf_op jit(solution)/shard_map/all_gather | solution.py:93
  120.0 61.3 %all_to_all.42 = bf16[32,72,512]{2,1,0:T(8,128)(2,1)S(1)} all-to-all(bf16[32,72,512]{2,1,0:T(8,128)(2,1)S(1)} %bitcast.182), channel_id=1, replica_groups=mesh['ep'=32,'tp'=4] {'ep'}, dimensions={0} | all-to-all | bytes 4718592 | tf_op jit(solution)/shard_map/all_to_all | solution.py:104
  181.6 4.8 broadcast_in_dim.177
  194.8 4.7 all-to-all-start.3
  202.2 42.3 %collective-permute-done.4 = bf16[2304,512]{1,0:T(8,128)(2,1)} collective-permute-done((bf16[2304,512]{1,0:T(8,128)(2,1)}, bf16[2304,512]{1,0:T(8,128)(2,1)}, u32[]{:S(2)}, u32[]{:S(2)}) %collective-permute-start.4) | collective-permute-done | bytes 2359328 | tf_op jit(solution)/shard_map/ppermute | solution.py:74
  257.3 17.8 %collective-permute-done.5 = bf16[1152,512]{1,0:T(8,128)(2,1)S(1)} collective-permute-done((bf16[1152,512]{1,0:T(8,128)(2,1)S(1)}, bf16[1152,512]{1,0:T(8,128)(2,1)S(1)}, u32[]{:S(2)}, u32[]{:S(2)}) %collective-permute-start.5) | collective-permute-done | bytes 1179680 | tf_op jit(solution)/shard_map/ppermute | solution.py:74
  277.4 5.8 fusion.22
  283.2 5.8 fusion.14
  289.0 6.4 fusion.24
  295.4 6.0 fusion.16
  301.4 13.8 %convolution_convert_fusion.1 = bf16[32,72,2048]{2,1,0:T(8,128)(2,1)} fusion(bf16[32,192,2048]{2,1,0:T(8,128)(2,1)} %bitcast.167, s32[32,72]{1,0:T(8,128)S(1)} %bitcast.185), kind=kOutput, calls=%fused_computation.16 | convolution fusion | flops 1817100288 | bytes 34612224 | tf_op jit(solution)/shard_map/ist,itd->isd/dot_general | solution.py:338
  316.5 6.5 fusion.212
  325.8 3.8 fusion.72
  329.7 8.1 fusion.74
  338.6 3.8 all-to-all-start.5
  342.5 7.3 all-to-all-done.5
  355.1 3.8 all-to-all-start.1
  359.4 6.8 all-to-all-done.1
  366.7 3.6 multiply_convert_fusion.2
  385.1 4.8 convolution_add_fusion
  394.8 3.8 pad_maximum_fusion.1
  402.6 25.9 %collective-permute-done.14 = bf16[1152,512]{1,0:T(8,128)(2,1)S(1)} collective-permute-done((bf16[1152,512]{1,0:T(8,128)(2,1)S(1)}, bf16[1152,512]{1,0:T(8,128)(2,1)S(1)}, u32[]{:S(2)}, u32[]{:S(2)}) %collective-permute-start.14) | collective-permute-done | bytes 1179680 | tf_op jit(solution)/shard_map/ppermute | solution.py:74
  435.9 4.0 fusion.3
  445.7 4.0 pad_maximum_fusion.2
  449.7 11.7 %copy.155 = bf16[2048,2112]{1,0:T(8,128)(2,1)} copy(bf16[2048,2112]{0,1:T(8,128)(2,1)} %pad_maximum_fusion.2) | data formatting | bytes 17301504
  461.4 23.6 %collective-permute-done.15 = bf16[2304,512]{1,0:T(8,128)(2,1)} collective-permute-done((bf16[2304,512]{1,0:T(8,128)(2,1)}, bf16[2304,512]{1,0:T(8,128)(2,1)}, u32[]{:S(2)}, u32[]{:S(2)}) %collective-permute-start.15) | collective-permute-done | bytes 2359328 | tf_op jit(solution)/shard_map/ppermute | solution.py:74
  486.0 4.4 add_convert_fusion
  492.2 4.8 all-to-all-start.4
  506.1 5.1 fusion.57
  515.1 25.3 %all-to-all-done.4 = bf16[32,72,512]{2,1,0:T(8,128)(2,1)} async-done(((bf16[32,72,512]{2,1,0:T(8,128)(2,1)}), bf16[32,72,512]{2,1,0:T(8,128)(2,1)}, u32[]{:S(2)}, u32[]{:S(2)}) %all-to-all-start.4) | async-done | bytes 2359328 | tf_op jit(solution)/shard_map/all_to_all | solution.py:104
  544.3 14.6 %all_gather.26 = bf16[192,2048]{1,0:T(8,128)(2,1)S(1)} all-gather(bf16[192,512]{1,0:T(8,128)(2,1)S(1)} %add_convert_fusion.8), channel_id=1, replica_groups=mesh['ep'=32,'tp'=4] {'tp'}, dimensions={1}, use_global_device_ids=true | all-gather | bytes 983040 | tf_op jit(solution)/shard_map/all_gather | solution.py:93
  597.8 5.3 collective-permute-done.25
  603.2 14.1 %all_gather.27 = bf16[192,2048]{1,0:T(8,128)(2,1)S(1)} all-gather(bf16[192,512]{1,0:T(8,128)(2,1)S(1)} %add_convert_fusion.6), channel_id=1, replica_groups=mesh['ep'=32,'tp'=4] {'tp'}, dimensions={1}, use_global_device_ids=true | all-gather | bytes 983040 | tf_op jit(solution)/shard_map/all_gather | solution.py:93
  629.6 12.8 %copy.153 = bf16[2048,2304]{1,0:T(8,128)(2,1)} copy(bf16[2048,2304]{0,1:T(8,128)(2,1)} %fusion.142) | data formatting | bytes 18874368
  642.4 4.6 convolution_multiply_fusion.1
  649.7 4.8 convolution_multiply_fusion
  659.5 3.7 pad_maximum_fusion
  667.2 21.4 %collective-permute-done.7 = bf16[1152,512]{1,0:T(8,128)(2,1)S(1)} collective-permute-done((bf16[1152,512]{1,0:T(8,128)(2,1)S(1)}, bf16[1152,512]{1,0:T(8,128)(2,1)S(1)}, u32[]{:S(2)}, u32[]{:S(2)}) %collective-permute-start.7) | collective-permute-done | bytes 1179680 | tf_op jit(solution)/shard_map/ppermute | solution.py:74
  702.0 6.5 fusion.31
  708.4 6.2 fusion.37
  714.6 20.6 %collective-permute-done.8 = bf16[2304,512]{1,0:T(8,128)(2,1)S(1)} collective-permute-done((bf16[2304,512]{1,0:T(8,128)(2,1)S(1)}, bf16[2304,512]{1,0:T(8,128)(2,1)S(1)}, u32[]{:S(2)}, u32[]{:S(2)}) %collective-permute-start.8) | collective-permute-done | bytes 2359328 | tf_op jit(solution)/shard_map/ppermute | solution.py:74
  738.8 8.3 %all-to-all-start.2 = ((bf16[32,72,512]{2,1,0:T(8,128)(2,1)}), bf16[32,72,512]{2,1,0:T(8,128)(2,1)}, u32[]{:S(2)}, u32[]{:S(2)}) async-start(bf16[32,72,512]{2,1,0:T(8,128)(2,1)} %pad_maximum_fusion.19), calls=%async_computation.2 | async-start | bytes 4718592 | tf_op jit(solution)/shard_map/all_to_all | solution.py:104
  747.2 6.0 pad_maximum_fusion.4
  753.2 4.7 fusion.34
  757.9 4.6 fusion.40
  773.6 5.4 all-to-all-done.2
  783.5 13.7 %all_gather.25 = bf16[192,2048]{1,0:T(8,128)(2,1)S(1)} all-gather(bf16[192,512]{1,0:T(8,128)(2,1)S(1)} %add_convert_fusion.9), channel_id=1, replica_groups=mesh['ep'=32,'tp'=4] {'tp'}, dimensions={1}, use_global_device_ids=true | all-gather | bytes 983040 | tf_op jit(solution)/shard_map/all_gather | solution.py:93
  (489 shorter events, 241.8 us)
Async XLA Ops:
  7.2 62.4 %copy-start.91 = (s32[1,192]{1,0:T(1,128)S(1)}, s32[1,192]{1,0:T(1,128)}, u32[]{:S(2)}) copy-start(s32[1,192]{1,0:T(1,128)} %param.22) | copy-start | bytes 2308
  7.2 62.1 %all-gather.4.cloned.1.call-start = ((), (), s32[]{:S(2)}) async-start(), calls=%async_computation.8 | async-start | bytes 9732096 | tf_op jit(solution)/shard_map/all_gather | solution.py:213
  11.4 277.6 %all-gather.6.cloned.1.call-start = ((), (), s32[]{:S(2)}) async-start(), calls=%async_computation.9 | async-start | bytes 25952256 | tf_op jit(solution)/shard_map/all_gather | solution.py:245
  89.5 8.4 %collective-permute-start = (bf16[192,512]{1,0:T(8,128)(2,1)S(1)}, bf16[192,512]{1,0:T(8,128)(2,1)S(1)}, u32[]{:S(2)}, u32[]{:S(2)}) collective-permute-start(bf16[192,512]{1,0:T(8,128)(2,1)S(1)} %get-tuple-element.153), channel_id=1, source_target_pairs={{0,1},{1,2},{2,3},{3,0},{4,5},{5,6},{6,7},{7,4},{8,9},{9,10},{10,1... | collective-permute-start | bytes 589832 | tf_op jit(solution)/shard_map/ppermute | solution.py:74
  91.1 10.3 %collective-permute-start.1 = (bf16[192,512]{1,0:T(8,128)(2,1)S(1)}, bf16[192,512]{1,0:T(8,128)(2,1)S(1)}, u32[]{:S(2)}, u32[]{:S(2)}) collective-permute-start(bf16[192,512]{1,0:T(8,128)(2,1)S(1)} %get-tuple-element.155), channel_id=1, source_target_pairs={{0,3},{1,0},{2,1},{3,2},{4,7},{5,4},{6,5},{7,6},{8,11},{9,8},{10,9... | collective-permute-start | bytes 589832 | tf_op jit(solution)/shard_map/ppermute | solution.py:74
  92.8 10.4 %collective-permute-start.2 = (bf16[192,512]{1,0:T(8,128)(2,1)S(1)}, bf16[192,512]{1,0:T(8,128)(2,1)S(1)}, u32[]{:S(2)}, u32[]{:S(2)}) collective-permute-start(bf16[192,512]{1,0:T(8,128)(2,1)S(1)} %get-tuple-element.154), channel_id=1, source_target_pairs={{0,2},{1,3},{2,0},{3,1},{4,6},{5,7},{6,4},{7,5},{8,10},{9,11},{10,... | collective-permute-start | bytes 589832 | tf_op jit(solution)/shard_map/ppermute | solution.py:74
  94.7 446.3 %copy-start.94 = (s32[192,1]{0,1:T(1,128)}, s32[192,1]{0,1:T(1,128)S(1)}, u32[]{:S(2)}) copy-start(s32[192,1]{0,1:T(1,128)S(1)} %get-tuple-element.174) | copy-start | bytes 2308
  94.7 446.3 %copy-start.96 = (s32[192,1]{0,1:T(1,128)}, s32[192,1]{0,1:T(1,128)S(1)}, u32[]{:S(2)}) copy-start(s32[192,1]{0,1:T(1,128)S(1)} %get-tuple-element.175) | copy-start | bytes 2308
  94.7 446.3 %copy-start.98 = (s32[192,1]{0,1:T(1,128)}, s32[192,1]{0,1:T(1,128)S(1)}, u32[]{:S(2)}) copy-start(s32[192,1]{0,1:T(1,128)S(1)} %get-tuple-element.176) | copy-start | bytes 2308
  94.7 446.3 %copy-start.100 = (s32[192,1]{0,1:T(1,128)}, s32[192,1]{0,1:T(1,128)S(1)}, u32[]{:S(2)}) copy-start(s32[192,1]{0,1:T(1,128)S(1)} %get-tuple-element.177) | copy-start | bytes 2308
  94.7 446.3 %copy-start.102 = (s32[192,1]{0,1:T(1,128)}, s32[192,1]{0,1:T(1,128)S(1)}, u32[]{:S(2)}) copy-start(s32[192,1]{0,1:T(1,128)S(1)} %get-tuple-element.178) | copy-start | bytes 2308
  94.7 446.3 %copy-start.104 = (s32[192,1]{0,1:T(1,128)}, s32[192,1]{0,1:T(1,128)S(1)}, u32[]{:S(2)}) copy-start(s32[192,1]{0,1:T(1,128)S(1)} %get-tuple-element.179) | copy-start | bytes 2308
  118.2 82.2 %copy-start.6 = (bf16[192,2048]{1,0:T(8,128)(2,1)}, bf16[192,2048]{1,0:T(8,128)(2,1)S(1)}, u32[]{:S(2)}) copy-start(bf16[192,2048]{1,0:T(8,128)(2,1)S(1)} %multiply_convert_fusion.4) | copy-start | bytes 2359300
  189.0 55.5 %collective-permute-start.4 = (bf16[2304,512]{1,0:T(8,128)(2,1)}, bf16[2304,512]{1,0:T(8,128)(2,1)}, u32[]{:S(2)}, u32[]{:S(2)}) collective-permute-start(bf16[2304,512]{1,0:T(8,128)(2,1)} %get-tuple-element.129), channel_id=1, source_target_pairs={{0,1},{1,2},{2,3},{3,0},{4,5},{5,6},{6,7},{7,4},{8,9},{9,10},{10,1... | collective-permute-start | bytes 7077896 | tf_op jit(solution)/shard_map/ppermute | solution.py:74
  189.6 56.4 %collective-permute-start.3 = (bf16[2304,512]{1,0:T(8,128)(2,1)}, bf16[2304,512]{1,0:T(8,128)(2,1)}, u32[]{:S(2)}, u32[]{:S(2)}) collective-permute-start(bf16[2304,512]{1,0:T(8,128)(2,1)} %get-tuple-element.129), channel_id=1, source_target_pairs={{0,3},{1,0},{2,1},{3,2},{4,7},{5,4},{6,5},{7,6},{8,11},{9,8},{10,9... | collective-permute-start | bytes 7077896 | tf_op jit(solution)/shard_map/ppermute | solution.py:74
  194.8 106.6 %all-to-all-start.3 = ((s32[32,1,72]{2,1,0:T(1,128)}), s32[32,1,72]{2,1,0:T(1,128)S(1)}, u32[]{:S(2)}, u32[]{:S(2)}) async-start(s32[32,1,72]{2,1,0:T(1,128)} %sub.85), calls=%async_computation.3 | async-start | bytes 32768 | tf_op jit(solution)/shard_map/all_to_all | solution.py:104
  199.5 236.4 %all-gather.8.cloned.1.call-start = ((), (), s32[]{:S(2)}) async-start(), calls=%async_computation.10 | async-start | bytes 9191424 | tf_op jit(solution)/shard_map/all_gather | solution.py:249
  245.8 29.3 %collective-permute-start.5 = (bf16[1152,512]{1,0:T(8,128)(2,1)S(1)}, bf16[1152,512]{1,0:T(8,128)(2,1)S(1)}, u32[]{:S(2)}, u32[]{:S(2)}) collective-permute-start(bf16[1152,512]{1,0:T(8,128)(2,1)S(1)} %slice.495), channel_id=1, source_target_pairs={{0,1},{1,2},{2,3},{3,0},{4,5},{5,6},{6,7},{7,4},{8,9},{9,10},{10,1... | collective-permute-start | bytes 3538952 | tf_op jit(solution)/shard_map/ppermute | solution.py:74
  247.4 28.9 %collective-permute-start.6 = (bf16[1152,512]{1,0:T(8,128)(2,1)S(1)}, bf16[1152,512]{1,0:T(8,128)(2,1)S(1)}, u32[]{:S(2)}, u32[]{:S(2)}) collective-permute-start(bf16[1152,512]{1,0:T(8,128)(2,1)S(1)} %slice.496), channel_id=1, source_target_pairs={{0,3},{1,0},{2,1},{3,2},{4,7},{5,4},{6,5},{7,6},{8,11},{9,8},{10,9... | collective-permute-start | bytes 3538952 | tf_op jit(solution)/shard_map/ppermute | solution.py:74
  338.6 11.1 %all-to-all-start.5 = ((f32[32,1,72]{2,1,0:T(1,128)}), f32[32,1,72]{2,1,0:T(1,128)S(1)}, u32[]{:S(2)}, u32[]{:S(2)}) async-start(f32[32,1,72]{2,1,0:T(1,128)} %bitcast.44), calls=%async_computation.5 | async-start | bytes 32768 | tf_op jit(solution)/shard_map/all_to_all | solution.py:104
  355.1 11.1 %all-to-all-start.1 = ((f32[32,1,72]{2,1,0:T(1,128)}), f32[32,1,72]{2,1,0:T(1,128)S(1)}, u32[]{:S(2)}, u32[]{:S(2)}) async-start(f32[32,1,72]{2,1,0:T(1,128)} %all_to_all.28), calls=%async_computation.1 | async-start | bytes 32768 | tf_op jit(solution)/shard_map/all_to_all | solution.py:104
  359.0 439.9 %reduce-scatter.9.cloned.1.call-start = ((), (), s32[]{:S(2)}) async-start(), calls=%async_computation.12 | async-start | bytes 9191424
  399.2 29.4 %collective-permute-start.14 = (bf16[1152,512]{1,0:T(8,128)(2,1)S(1)}, bf16[1152,512]{1,0:T(8,128)(2,1)S(1)}, u32[]{:S(2)}, u32[]{:S(2)}) collective-permute-start(bf16[1152,512]{1,0:T(8,128)(2,1)S(1)} %get-tuple-element.109), channel_id=1, source_target_pairs={{0,1},{1,2},{2,3},{3,0},{4,5},{5,6},{6,7},{7,4},{8,9},{9,10},{10,1... | collective-permute-start | bytes 3538952 | tf_op jit(solution)/shard_map/ppermute | solution.py:74
  399.3 29.3 %collective-permute-start.16 = (bf16[1152,512]{1,0:T(8,128)(2,1)S(1)}, bf16[1152,512]{1,0:T(8,128)(2,1)S(1)}, u32[]{:S(2)}, u32[]{:S(2)}) collective-permute-start(bf16[1152,512]{1,0:T(8,128)(2,1)S(1)} %get-tuple-element.111), channel_id=1, source_target_pairs={{0,3},{1,0},{2,1},{3,2},{4,7},{5,4},{6,5},{7,6},{8,11},{9,8},{10,9... | collective-permute-start | bytes 3538952 | tf_op jit(solution)/shard_map/ppermute | solution.py:74
  431.1 54.0 %collective-permute-start.15 = (bf16[2304,512]{1,0:T(8,128)(2,1)}, bf16[2304,512]{1,0:T(8,128)(2,1)}, u32[]{:S(2)}, u32[]{:S(2)}) collective-permute-start(bf16[2304,512]{1,0:T(8,128)(2,1)} %pad_maximum_fusion.20), channel_id=1, source_target_pairs={{0,1},{1,2},{2,3},{3,0},{4,5},{5,6},{6,7},{7,4},{8,9},{9,10},{10,1... | collective-permute-start | bytes 7077896 | tf_op jit(solution)/shard_map/ppermute | solution.py:74
  433.8 52.2 %collective-permute-start.17 = (bf16[2304,512]{1,0:T(8,128)(2,1)}, bf16[2304,512]{1,0:T(8,128)(2,1)}, u32[]{:S(2)}, u32[]{:S(2)}) collective-permute-start(bf16[2304,512]{1,0:T(8,128)(2,1)} %pad_maximum_fusion.21), channel_id=1, source_target_pairs={{0,3},{1,0},{2,1},{3,2},{4,7},{5,4},{6,5},{7,6},{8,11},{9,8},{10,9... | collective-permute-start | bytes 7077896 | tf_op jit(solution)/shard_map/ppermute | solution.py:74
  492.2 48.2 %all-to-all-start.4 = ((bf16[32,72,512]{2,1,0:T(8,128)(2,1)}), bf16[32,72,512]{2,1,0:T(8,128)(2,1)}, u32[]{:S(2)}, u32[]{:S(2)}) async-start(bf16[32,72,512]{2,1,0:T(8,128)(2,1)} %pad_maximum_fusion.22), calls=%async_computation.4 | async-start | bytes 4718592 | tf_op jit(solution)/shard_map/all_to_all | solution.py:104
  497.0 305.8 %reduce-scatter.7.cloned.1.call-start = ((), (), s32[]{:S(2)}) async-start(), calls=%async_computation.11 | async-start | bytes 9732096
  497.1 5.5 collective-permute-start.21
  498.7 3.8 collective-permute-start.22
  500.8 5.2 collective-permute-start.23
  511.2 29.2 %collective-permute-start.18 = (bf16[192,512]{1,0:T(8,128)(2,1)S(1)}, bf16[192,512]{1,0:T(8,128)(2,1)S(1)}, u32[]{:S(2)}, u32[]{:S(2)}) collective-permute-start(bf16[192,512]{1,0:T(8,128)(2,1)S(1)} %get-tuple-element.147), channel_id=1, source_target_pairs={{0,1},{1,2},{2,3},{3,0},{4,5},{5,6},{6,7},{7,4},{8,9},{9,10},{10,1... | collective-permute-start | bytes 589832 | tf_op jit(solution)/shard_map/ppermute | solution.py:74
  511.3 29.1 %collective-permute-start.19 = (bf16[192,512]{1,0:T(8,128)(2,1)S(1)}, bf16[192,512]{1,0:T(8,128)(2,1)S(1)}, u32[]{:S(2)}, u32[]{:S(2)}) collective-permute-start(bf16[192,512]{1,0:T(8,128)(2,1)S(1)} %get-tuple-element.149), channel_id=1, source_target_pairs={{0,3},{1,0},{2,1},{3,2},{4,7},{5,4},{6,5},{7,6},{8,11},{9,8},{10,9... | collective-permute-start | bytes 589832 | tf_op jit(solution)/shard_map/ppermute | solution.py:74
  514.5 25.9 %collective-permute-start.20 = (bf16[192,512]{1,0:T(8,128)(2,1)S(1)}, bf16[192,512]{1,0:T(8,128)(2,1)S(1)}, u32[]{:S(2)}, u32[]{:S(2)}) collective-permute-start(bf16[192,512]{1,0:T(8,128)(2,1)S(1)} %get-tuple-element.148), channel_id=1, source_target_pairs={{0,2},{1,3},{2,0},{3,1},{4,6},{5,7},{6,4},{7,5},{8,10},{9,11},{10,... | collective-permute-start | bytes 589832 | tf_op jit(solution)/shard_map/ppermute | solution.py:74
  569.9 47.5 %collective-permute-start.27 = (bf16[192,576]{1,0:T(8,128)(2,1)}, bf16[192,576]{1,0:T(8,128)(2,1)}, u32[]{:S(2)}, u32[]{:S(2)}) collective-permute-start(bf16[192,576]{1,0:T(8,128)(2,1)} %pad_maximum_fusion.31), channel_id=1, source_target_pairs={{0,1},{1,2},{2,3},{3,0},{4,5},{5,6},{6,7},{7,4},{8,9},{9,10},{10,1... | collective-permute-start | bytes 663560 | tf_op jit(solution)/shard_map/ppermute | solution.py:74
  572.1 45.2 %collective-permute-start.28 = (bf16[192,576]{1,0:T(8,128)(2,1)}, bf16[192,576]{1,0:T(8,128)(2,1)}, u32[]{:S(2)}, u32[]{:S(2)}) collective-permute-start(bf16[192,576]{1,0:T(8,128)(2,1)} %pad_maximum_fusion.31), channel_id=1, source_target_pairs={{0,3},{1,0},{2,1},{3,2},{4,7},{5,4},{6,5},{7,6},{8,11},{9,8},{10,9... | collective-permute-start | bytes 663560 | tf_op jit(solution)/shard_map/ppermute | solution.py:74
  588.1 9.3 %collective-permute-start.24 = (bf16[192,512]{1,0:T(8,128)(2,1)S(1)}, bf16[192,512]{1,0:T(8,128)(2,1)S(1)}, u32[]{:S(2)}, u32[]{:S(2)}) collective-permute-start(bf16[192,512]{1,0:T(8,128)(2,1)S(1)} %get-tuple-element.144), channel_id=1, source_target_pairs={{0,1},{1,2},{2,3},{3,0},{4,5},{5,6},{6,7},{7,4},{8,9},{9,10},{10,1... | collective-permute-start | bytes 589832 | tf_op jit(solution)/shard_map/ppermute | solution.py:74
  588.9 14.2 %collective-permute-start.25 = (bf16[192,512]{1,0:T(8,128)(2,1)S(1)}, bf16[192,512]{1,0:T(8,128)(2,1)S(1)}, u32[]{:S(2)}, u32[]{:S(2)}) collective-permute-start(bf16[192,512]{1,0:T(8,128)(2,1)S(1)} %get-tuple-element.146), channel_id=1, source_target_pairs={{0,3},{1,0},{2,1},{3,2},{4,7},{5,4},{6,5},{7,6},{8,11},{9,8},{10,9... | collective-permute-start | bytes 589832 | tf_op jit(solution)/shard_map/ppermute | solution.py:74
  591.4 11.8 %collective-permute-start.26 = (bf16[192,512]{1,0:T(8,128)(2,1)S(1)}, bf16[192,512]{1,0:T(8,128)(2,1)S(1)}, u32[]{:S(2)}, u32[]{:S(2)}) collective-permute-start(bf16[192,512]{1,0:T(8,128)(2,1)S(1)} %get-tuple-element.145), channel_id=1, source_target_pairs={{0,2},{1,3},{2,0},{3,1},{4,6},{5,7},{6,4},{7,5},{8,10},{9,11},{10,... | collective-permute-start | bytes 589832 | tf_op jit(solution)/shard_map/ppermute | solution.py:74
  597.3 20.0 %collective-permute-start.29 = (bf16[192,576]{1,0:T(8,128)(2,1)}, bf16[192,576]{1,0:T(8,128)(2,1)S(1)}, u32[]{:S(2)}, u32[]{:S(2)}) collective-permute-start(bf16[192,576]{1,0:T(8,128)(2,1)} %pad_maximum_fusion.31), channel_id=1, source_target_pairs={{0,2},{1,3},{2,0},{3,1},{4,6},{5,7},{6,4},{7,5},{8,10},{9,11},{10,... | collective-permute-start | bytes 663560 | tf_op jit(solution)/shard_map/ppermute | solution.py:74
  663.9 24.8 %collective-permute-start.7 = (bf16[1152,512]{1,0:T(8,128)(2,1)S(1)}, bf16[1152,512]{1,0:T(8,128)(2,1)S(1)}, u32[]{:S(2)}, u32[]{:S(2)}) collective-permute-start(bf16[1152,512]{1,0:T(8,128)(2,1)S(1)} %get-tuple-element.115), channel_id=1, source_target_pairs={{0,1},{1,2},{2,3},{3,0},{4,5},{5,6},{6,7},{7,4},{8,9},{9,10},{10,1... | collective-permute-start | bytes 3538952 | tf_op jit(solution)/shard_map/ppermute | solution.py:74
  665.9 24.0 %collective-permute-start.9 = (bf16[1152,512]{1,0:T(8,128)(2,1)S(1)}, bf16[1152,512]{1,0:T(8,128)(2,1)S(1)}, u32[]{:S(2)}, u32[]{:S(2)}) collective-permute-start(bf16[1152,512]{1,0:T(8,128)(2,1)S(1)} %get-tuple-element.117), channel_id=1, source_target_pairs={{0,3},{1,0},{2,1},{3,2},{4,7},{5,4},{6,5},{7,6},{8,11},{9,8},{10,9... | collective-permute-start | bytes 3538952 | tf_op jit(solution)/shard_map/ppermute | solution.py:74
  691.1 44.1 %collective-permute-start.8 = (bf16[2304,512]{1,0:T(8,128)(2,1)S(1)}, bf16[2304,512]{1,0:T(8,128)(2,1)S(1)}, u32[]{:S(2)}, u32[]{:S(2)}) collective-permute-start(bf16[2304,512]{1,0:T(8,128)(2,1)S(1)} %pad_maximum_fusion.17), channel_id=1, source_target_pairs={{0,1},{1,2},{2,3},{3,0},{4,5},{5,6},{6,7},{7,4},{8,9},{9,10},{10,1... | collective-permute-start | bytes 7077896 | tf_op jit(solution)/shard_map/ppermute | solution.py:74
  692.1 43.5 %collective-permute-start.10 = (bf16[2304,512]{1,0:T(8,128)(2,1)S(1)}, bf16[2304,512]{1,0:T(8,128)(2,1)S(1)}, u32[]{:S(2)}, u32[]{:S(2)}) collective-permute-start(bf16[2304,512]{1,0:T(8,128)(2,1)S(1)} %pad_maximum_fusion.18), channel_id=1, source_target_pairs={{0,3},{1,0},{2,1},{3,2},{4,7},{5,4},{6,5},{7,6},{8,11},{9,8},{10,9... | collective-permute-start | bytes 7077896 | tf_op jit(solution)/shard_map/ppermute | solution.py:74
  738.8 40.1 %all-to-all-start.2 = ((bf16[32,72,512]{2,1,0:T(8,128)(2,1)}), bf16[32,72,512]{2,1,0:T(8,128)(2,1)}, u32[]{:S(2)}, u32[]{:S(2)}) async-start(bf16[32,72,512]{2,1,0:T(8,128)(2,1)} %pad_maximum_fusion.19), calls=%async_computation.2 | async-start | bytes 4718592 | tf_op jit(solution)/shard_map/all_to_all | solution.py:104
  765.6 13.3 %collective-permute-start.11 = (bf16[192,512]{1,0:T(8,128)(2,1)S(1)}, bf16[192,512]{1,0:T(8,128)(2,1)S(1)}, u32[]{:S(2)}, u32[]{:S(2)}) collective-permute-start(bf16[192,512]{1,0:T(8,128)(2,1)S(1)} %get-tuple-element.150), channel_id=1, source_target_pairs={{0,1},{1,2},{2,3},{3,0},{4,5},{5,6},{6,7},{7,4},{8,9},{9,10},{10,1... | collective-permute-start | bytes 589832 | tf_op jit(solution)/shard_map/ppermute | solution.py:74
  767.4 11.6 %collective-permute-start.12 = (bf16[192,512]{1,0:T(8,128)(2,1)S(1)}, bf16[192,512]{1,0:T(8,128)(2,1)S(1)}, u32[]{:S(2)}, u32[]{:S(2)}) collective-permute-start(bf16[192,512]{1,0:T(8,128)(2,1)S(1)} %get-tuple-element.152), channel_id=1, source_target_pairs={{0,3},{1,0},{2,1},{3,2},{4,7},{5,4},{6,5},{7,6},{8,11},{9,8},{10,9... | collective-permute-start | bytes 589832 | tf_op jit(solution)/shard_map/ppermute | solution.py:74
  769.2 10.9 %collective-permute-start.13 = (bf16[192,512]{1,0:T(8,128)(2,1)S(1)}, bf16[192,512]{1,0:T(8,128)(2,1)}, u32[]{:S(2)}, u32[]{:S(2)}) collective-permute-start(bf16[192,512]{1,0:T(8,128)(2,1)S(1)} %get-tuple-element.151), channel_id=1, source_target_pairs={{0,2},{1,3},{2,0},{3,1},{4,6},{5,7},{6,4},{7,5},{8,10},{9,11},{10,... | collective-permute-start | bytes 589832 | tf_op jit(solution)/shard_map/ppermute | solution.py:74
  (104 other events, 977.0 us)
Sparse Core Ops, SparseCore 0:
  11.5 57.7 all-gather.3
  71.5 116.8 all-gather.5
  289.1 52.0 all-gather.7
  461.5 105.9 reduce-scatter.8
  642.5 93.8 reduce-scatter.6

commit v2 on v1

--- a/solution.py
+++ b/solution.py
@@ -1,6 +1,10 @@
+import functools
+
 import jax
 import jax.numpy as jnp
 from jax import lax
+from jax.experimental import pallas as pl
+from jax.experimental.pallas import tpu as pltpu
 from jax.sharding import PartitionSpec as P
 
 D = 2048
@@ -90,7 +94,18 @@
 
 
 def gather_quarters(piece):
-    return lax.all_gather(piece, "tp", axis=1, tiled=True)
+    lanes = lax.axis_size("tp")
+    lane = lax.axis_index("tp")
+    parts = [piece] + [None] * (lanes - 1)
+    for step in (1, 3, 2):
+        parts[step] = shift(piece, lanes - step)
+    full = jnp.concatenate(parts, 1)
+    width = piece.shape[1]
+    parts = []
+    for step in range(lanes):
+        at = lax.rem(lanes - lane + step, lanes) * width
+        parts.append(lax.dynamic_slice_in_dim(full, at, width, 1))
+    return jnp.concatenate(parts, 1)
 
 
 def sum_small(partial):
@@ -130,40 +145,241 @@
     )
 
 
-def lanes_gather(piece):
-    half = piece.shape[0] // 2
-    width = piece.shape[1]
-    lane = lax.axis_index("tp")
-    lanes = lax.axis_size("tp")
-    from_prev = shift(piece, 1)
-    from_next = shift(piece, 3)
-    far_top = shift(from_prev[:half], 1)
-    far_bottom = shift(from_next[half:], 3)
-    full = jnp.zeros((piece.shape[0], width * lanes), piece.dtype)
-    for part, row, step in (
-        (piece, 0, 0),
-        (from_next, 0, 1),
-        (from_prev, 0, 3),
-        (far_top, 0, 2),
-        (far_bottom, half, 2),
-    ):
-        place = lax.rem(lane + step, lanes) * width
-        full = lax.dynamic_update_slice(full, part, (row, place))
-    return full
-
-
-def lanes_sum(parts):
-    own, after, far, before = parts
-    half = own.shape[0] // 2
-    top = shift(far[:half], 1)
-    bottom = shift(far[half:], 3)
-
-    def plus(one, two):
-        return (one.astype(f32) + two.astype(f32)).astype(bf16)
-
-    from_prev = shift(jnp.concatenate([plus(after[:half], top), after[half:]], 0), 1)
-    from_next = shift(jnp.concatenate([before[:half], plus(before[half:], bottom)], 0), 3)
-    return (own.astype(f32) + from_prev.astype(f32) + from_next.astype(f32)).astype(bf16)
+def after(value, *others):
+    return lax.optimization_barrier((value, others))[0]
+
+
+def plus(one, two):
+    return (one.astype(f32) + two.astype(f32)).astype(bf16)
+
+
+def ring_gather_first(one, two):
+    return shift(one, 1), shift(two, 3), shift(two, 1), shift(one, 3)
+
+
+def ring_gather_second(first):
+    return shift(first[0], 1), shift(first[1], 3)
+
+
+def ring_gather_parts(one, two, first, second):
+    one_prev, two_next, two_prev, one_next = first
+    return (one, two, one_next, two_next, second[0], second[1], one_prev, two_prev)
+
+
+def ring_sum_first(far, others):
+    return shift(far[0], 1), shift(far[1], 3), shift(others[4], 3), shift(others[3], 1)
+
+
+def ring_sum_second(first, others):
+    return shift(plus(others[2], first[0]), 1), shift(plus(others[5], first[1]), 3)
+
+
+def add_three(one, two, three):
+    return (one.astype(f32) + two.astype(f32) + three.astype(f32)).astype(bf16)
+
+
+VMEM_BYTES = 44 * 1024 * 1024
+
+
+def first_owner_rows(tiles, tile, spill):
+    row = lax.broadcasted_iota(jnp.int32, (tile, 1), 0) + (pl.program_id(0) - tiles[0]) * tile
+    return lax.rem(row, EXP_DEV * spill) < spill
+
+
+def per_owner(tiles, tile, spill, run):
+    first, mixed = tiles
+    step = pl.program_id(0)
+    mine = first_owner_rows(tiles, tile, spill)
+    is_mixed = (step >= first) & (step < first + mixed)
+
+    @pl.when(is_mixed)
+    def _():
+        run(None, mine)
+
+    @pl.when(jnp.logical_not(is_mixed))
+    def _():
+        run(jnp.where(step < first, 0, 1), None)
+
+
+def hidden_back_kernel(tiles, spill, *refs):
+    pieces, weight, out = refs[:-2], refs[-2], refs[-1]
+    rows = jnp.concatenate([p[...] for p in pieces], 1)
+
+    def run(owner, mine):
+        if owner is None:
+            out[...] = jnp.where(mine, matmul_nt(rows, weight[0]), matmul_nt(rows, weight[1]))
+        else:
+            out[...] = matmul_nt(rows, weight[owner])
+
+    per_owner(tiles, rows.shape[0], spill, run)
+
+
+def hidden_kernel(tiles, spill, *refs):
+    pieces, (weight, dh_ref, gate_ref, hid, dboth, dgate, acc) = refs[:8], refs[8:]
+    rows = jnp.concatenate([p[...] for p in pieces], 1)
+
+    def run(owner, mine):
+        if owner is None:
+            acc[...] = jnp.where(mine, matmul(rows, weight[0]), matmul(rows, weight[1]))
+        else:
+            acc[...] = matmul(rows, weight[owner])
+
+    per_owner(tiles, rows.shape[0], spill, run)
+    wide = hid.shape[1]
+    up = acc[:, wide:]
+    pre = acc[:, :wide]
+    sig = 1.0 / (1.0 + jnp.exp(-pre))
+    act = pre * sig
+    hidden = (act * up).astype(bf16).astype(f32)
+    gate = gate_ref[...]
+    dh = dh_ref[...]
+    dgate[...] = jnp.sum(hidden * dh, 1, keepdims=True)
+    hid[...] = (hidden * gate).astype(bf16)
+    dh = dh * gate
+    dboth[:, :wide] = (dh * up * (sig * (1.0 + pre * (1.0 - sig)))).astype(bf16)
+    dboth[:, wide:] = (dh * act).astype(bf16)
+
+
+def rows_kernel(tiles, spill, transposed, spots, *refs):
+    value, weight, outs = refs[0], refs[1], refs[2:]
+
+    def run(owner, mine):
+        rows = value[...]
+        halves = ((rows, owner),)
+        if owner is None:
+            none = jnp.zeros_like(rows)
+            halves = ((jnp.where(mine, rows, none), 0), (jnp.where(mine, none, rows), 1))
+        for out, spot in zip(outs, spots):
+            cols = slice(spot, spot + out.shape[1])
+            total = None
+            for part, who in halves:
+                if transposed:
+                    term = matmul_nt(part, weight[who, cols, :])
+                else:
+                    term = matmul(part, weight[who, :, cols])
+                total = term if total is None else total + term
+            out[...] = total.astype(bf16)
+
+    per_owner(tiles, value.shape[0], spill, run)
+
+
+def tile_spec(tile, width):
+    return pl.BlockSpec((tile, width), lambda i: (i, 0))
+
+
+def whole_spec(shape):
+    return pl.BlockSpec(shape, lambda i: (0,) * len(shape))
+
+
+def row_call(body, tile, total, ins, in_specs, outs, flops, scratch=()):
+    out_shape = [jax.ShapeDtypeStruct((total, w), t) for w, t in outs]
+    moved = sum(a.size * a.dtype.itemsize for a in (*ins, *out_shape))
+    return pl.pallas_call(
+        body,
+        grid=(total // tile,),
+        in_specs=in_specs,
+        out_specs=[tile_spec(tile, w) for w, _ in outs],
+        out_shape=out_shape,
+        scratch_shapes=list(scratch),
+        cost_estimate=pl.CostEstimate(flops=flops, bytes_accessed=moved, transcendentals=0),
+        compiler_params=pltpu.CompilerParams(
+            dimension_semantics=("arbitrary",), vmem_limit_bytes=VMEM_BYTES
+        ),
+    )(*ins)
+
+
+def first_grad_kernel(
+    kv_rows,
+    normed,
+    normed2,
+    dmid,
+    dquery,
+    dlat,
+    dlogits,
+    attended,
+    latent_n,
+    dkeyval,
+    gains,
+    out,
+    kv_grad,
+):
+    step = pl.program_id(0)
+
+    @pl.when(step == 0)
+    def _():
+        kv_grad[...] = matmul_tn(latent_n[...], dkeyval[...]).astype(bf16)
+
+    rows, kv_cols = out.shape[0], 256
+    at_lat = dquery.shape[1]
+    at_kv = at_lat + dlat.shape[1]
+    at_out = at_kv + kv_cols
+    at_gain = at_out + attended.shape[1]
+    mine = normed[...]
+    out[:, :at_lat] = matmul_tn(mine, dquery[...]).astype(bf16)
+    out[:, at_lat:at_kv] = (
+        matmul_tn(mine, dlat[...]) + matmul_tn(normed2[...], dlogits[...])
+    ).astype(bf16)
+    out[:, at_out:at_gain] = matmul_tn(dmid[...], attended[...]).astype(bf16)
+    out[:, at_gain:] = gains[...]
+    splits = kv_grad.shape[1] // kv_cols
+    count = rows // kv_rows
+    for j in range(count):
+        if count % splits == 0:
+            group = step * (count // splits) + j // splits
+            lanes = slice(j % splits * kv_cols, (j % splits + 1) * kv_cols)
+        else:
+            group = (step * count + j) // splits
+            lanes = pl.ds((step * count + j) % splits * kv_cols, kv_cols)
+        from_rows = pl.ds(pl.multiple_of(group * kv_rows, kv_rows), kv_rows)
+        out[j * kv_rows : (j + 1) * kv_rows, at_kv:at_out] = kv_grad[from_rows, lanes]
+
+
+def first_grads(kv_rows, normed, normed2, dmid, dquery, dlat, dlogits, attended, latent_n, dkeyval, gains):
+    block = 256
+    cols = pl.BlockSpec((normed.shape[0], block), lambda i: (0, i))
+    width = dquery.shape[1] + dlat.shape[1] + 256 + attended.shape[1] + gains.shape[1]
+    whole = (dquery, dlat, dlogits, attended, latent_n, dkeyval)
+    return pl.pallas_call(
+        functools.partial(first_grad_kernel, kv_rows),
+        grid=(D // block,),
+        in_specs=[cols, cols, cols]
+        + [whole_spec(a.shape) for a in whole]
+        + [tile_spec(block, gains.shape[1])],
+        out_specs=tile_spec(block, width),
+        out_shape=jax.ShapeDtypeStruct((D, width), bf16),
+        scratch_shapes=[pltpu.VMEM((KVR, dkeyval.shape[1]), bf16)],
+        cost_estimate=pl.CostEstimate(
+            flops=2 * D * width * normed.shape[0], bytes_accessed=3 * D * width, transcendentals=0
+        ),
+        compiler_params=pltpu.CompilerParams(
+            dimension_semantics=("arbitrary",), vmem_limit_bytes=VMEM_BYTES
+        ),
+    )(normed, normed2, dmid, *whole, gains)
+
+
+def second_grad_kernel(normed2, cotangent, dboth, hidden, out):
+    split = dboth.shape[1]
+    out[:, :split] = matmul_tn(normed2[...], dboth[...]).astype(bf16)
+    out[:, split:] = matmul_tn(cotangent[...], hidden[...]).astype(bf16)
+
+
+def second_grads(normed2, cotangent, dboth, hidden):
+    block = 256
+    cols = pl.BlockSpec((normed2.shape[0], block), lambda i: (0, i))
+    width = dboth.shape[1] + hidden.shape[1]
+    return pl.pallas_call(
+        second_grad_kernel,
+        grid=(D // block,),
+        in_specs=[cols, cols, whole_spec(dboth.shape), whole_spec(hidden.shape)],
+        out_specs=tile_spec(block, width),
+        out_shape=jax.ShapeDtypeStruct((D, width), bf16),
+        cost_estimate=pl.CostEstimate(
+            flops=2 * D * width * normed2.shape[0], bytes_accessed=3 * D * width, transcendentals=0
+        ),
+        compiler_params=pltpu.CompilerParams(
+            dimension_semantics=("arbitrary",), vmem_limit_bytes=VMEM_BYTES
+        ),
+    )(normed2, cotangent, dboth, hidden)
 
 
 def per_device(
@@ -199,7 +415,8 @@
     shard = query_w.shape[0]
     q_cols = query_w.shape[1]
     lat_cols = latent_w.shape[1]
-    kv_cols = keyval_w.shape[0] * keyval_w.shape[1] // shard
+    kv_rows = keyval_w.shape[0]
+    kv_cols = kv_rows * keyval_w.shape[1] // shard
     out_cols = output_w.shape[0]
     sh_cols = shgate_w.shape[1]
 
@@ -208,22 +425,17 @@
     )
     gains = jnp.pad(gains, ((0, 0), (0, 128 - gains.shape[1])))
     first_pack = jnp.concatenate(
-        [query_w, latent_w, router_w, keyval_w.reshape(shard, kv_cols), output_w.T, gains], 1
+        [
+            query_w,
+            latent_w,
+            router_w,
+            keyval_w.reshape(kv_rows, -1, kv_cols).transpose(1, 0, 2).reshape(shard, kv_cols),
+            output_w.T,
+            gains,
+        ],
+        1,
     )
     first_full = lax.all_gather(first_pack, "ep", axis=0, tiled=True)
-    edges = [0]
-    for cols in (q_cols, lat_cols, experts, kv_cols, out_cols, 128):
-        edges.append(edges[-1] + cols)
-    query_full = first_full[:, edges[0] : edges[1]]
-    latent_full = first_full[:, edges[1] : edges[2]]
-    router_full = first_full[:, edges[2] : edges[3]]
-    keyval_full = first_full[:, edges[3] : edges[4]].reshape(KVR, keyval_w.shape[1])
-    output_t = first_full[:, edges[4] : edges[5]]
-    pre_gain = first_full[:, edges[5]]
-    lat_gain = first_full[:, edges[5] + 1].reshape(owner_count, shard)[:, : latnorm.shape[0]]
-    lat_gain = lat_gain.reshape(KVR)
-    mid_gain = first_full[:, edges[5] + 2]
-
     local = expert_ids % EXP_DEV
     inside = jnp.where(
         route_slots < MAIN,
@@ -237,18 +449,65 @@
     for k in range(1, TOPK):
         pick = pick | matches[k]
     pick = pick.astype(bf16)
-    token_iota = lax.broadcasted_iota(jnp.int32, (slot_rows, tok_count), 1)
-    table = jnp.sum(jnp.where(pick > 0, token_iota + 1, 0), 1).astype(jnp.int32) - 1
-    table = exchange(table.reshape(owner_count, width))
-
-    upstream_all, first_full_ = lax.optimization_barrier((cotangent, first_full))
-    dy_all = lax.all_gather(upstream_all, "ep", axis=0, tiled=True)
-    dy_all = dy_all.reshape(owner_count, tok_count, D)
+
+    half = D // 8
+    dy_sent = matmul(pick, quarter_of(cotangent, 0)).astype(bf16)
+    dy_sent = to_experts(exchange(dy_sent.reshape(owner_count, width, -1)))
+    lanes = lax.axis_size("tp")
+    lane = lax.axis_index("tp")
+    quarter = D // lanes
+    hid_cols = exgate_w.shape[2]
+    hid_wide = -(-hid_cols // 128) * 128
+
+    def from_lane(value, axis):
+        parts = []
+        for step in range(lanes):
+            at = lax.rem(lane + step, lanes) * quarter
+            parts.append(lax.dynamic_slice_in_dim(value, at, quarter, axis))
+        return jnp.concatenate(parts, axis)
+
+    def to_lane(value, axis):
+        parts = []
+        for step in range(lanes):
+            at = lax.rem(lanes - lane + step, lanes) * quarter
+            parts.append(lax.dynamic_slice_in_dim(value, at, quarter, axis))
+        return jnp.concatenate(parts, axis)
+
+    fill = hid_wide - hid_cols
+    gateup_w = jnp.concatenate(
+        [
+            jnp.pad(from_lane(exgate_w, 1), ((0, 0), (0, 0), (0, fill))),
+            jnp.pad(from_lane(exup_w, 1), ((0, 0), (0, 0), (0, fill))),
+        ],
+        2,
+    )
+    down_plain = jnp.pad(exdown_w, ((0, 0), (0, fill), (0, 0)))
+    down_w = jnp.pad(from_lane(exdown_w, 2), ((0, 0), (0, fill), (0, 0)))
+    edge = owner_count * MAIN
+    extra = slot_rows - 2 * edge
+    span = edge + extra
+    tile = 256 if edge % 256 == 0 else 128
+    tiles = (edge // tile, extra // tile)
+    big = 2 * (slot_rows + extra) * D * hid_wide
+    first_full, dy_sent, gateup_w, down_w, down_plain = lax.optimization_barrier(
+        (first_full, dy_sent, gateup_w, down_w, down_plain)
+    )
     second_pack = jnp.concatenate([shgate_w, shup_w, shdown_w.T], 1)
-    second_pack, dy_all = lax.optimization_barrier((second_pack, dy_all))
-    second_full = lax.all_gather(second_pack, "ep", axis=0, tiled=True)
-    gateup_full = second_full[:, : 2 * sh_cols]
-    shdown_t = second_full[:, 2 * sh_cols :]
+    second_full = lax.all_gather(after(second_pack, first_full), "ep", axis=0, tiled=True)
+    edges = [0]
+    for cols in (q_cols, lat_cols, experts, kv_cols, out_cols, 128):
+        edges.append(edges[-1] + cols)
+    query_full = first_full[:, edges[0] : edges[1]]
+    latent_full = first_full[:, edges[1] : edges[2]]
+    router_full = first_full[:, edges[2] : edges[3]]
+    keyval_full = first_full[:, edges[3] : edges[4]].reshape(owner_count, -1, kv_rows, kv_cols)
+    keyval_full = keyval_full.transpose(0, 2, 1, 3).reshape(KVR, keyval_w.shape[1])
+    output_t = first_full[:, edges[4] : edges[5]]
+    pre_gain = first_full[:, edges[5]]
+    lat_gain = first_full[:, edges[5] + 1].reshape(owner_count, shard)[:, : latnorm.shape[0]]
+    lat_gain = lat_gain.reshape(KVR)
+    mid_gain = first_full[:, edges[5] + 2]
+
 
     resid_in = tokens.astype(f32)
     pre_scale = rms_scale(resid_in)
@@ -290,15 +549,57 @@
     probs16 = probs.astype(bf16)
     attended = jnp.einsum("hts,shd->thd", probs16, values, preferred_element_type=f32)
     attended = attended.reshape(tok_count, head_count * DV).astype(bf16)
+    dy_all = lax.all_gather(after(dy_sent, attended), "tp", axis=0, tiled=True)
     attn_sum = gather_quarters(sum_to_quarter(matmul_nt(attended, output_t)).astype(bf16))
     mid_resid = resid_in + attn_sum.astype(f32)
     mid_scale = rms_scale(mid_resid)
     mid_weight = mid_gain.astype(f32)
     normed2 = (mid_resid * mid_scale * mid_weight).astype(bf16)
 
-    sent = matmul(pick, quarter_of(normed2, 0)).astype(bf16)
-    arrived = to_experts(exchange(sent.reshape(owner_count, width, -1)))
-    rows = lanes_gather(arrived)
+    sent = matmul(pick, quarter_of(normed2, 0)).astype(bf16).reshape(owner_count, width, -1)
+    one = exchange(sent[:, :, :half])
+    two = exchange(after(sent[:, :, half:], one))
+    own = (to_experts(one), to_experts(two))
+    first = ring_gather_first(*own)
+    dy_all = after(dy_all, two)
+    (ex_dh,) = row_call(
+        functools.partial(hidden_back_kernel, tiles, spill),
+        tile,
+        slot_rows,
+        (*[dy_all] * lanes, down_plain),
+        [
+            pl.BlockSpec((tile, quarter), lambda i, q=q: (q * (slot_rows // tile) + i, 0))
+            for q in range(lanes)
+        ]
+        + [whole_spec(down_plain.shape)],
+        [(hid_wide, f32)],
+        big,
+    )
+
+    upstream = cotangent.astype(f32)
+    sh_in, sh_dy = after((normed2, cotangent), two)
+    gateup_full = second_full[:, : 2 * sh_cols]
+    shdown_t = second_full[:, 2 * sh_cols :]
+    sh_both = matmul(sh_in, gateup_full)
+    sh_gate = sh_both[:, :sh_cols]
+    sh_up = sh_both[:, sh_cols:]
+    sh_sig = 1.0 / (1.0 + jnp.exp(-sh_gate))
+    sh_hidden = (sh_gate * sh_sig * sh_up).astype(bf16)
+    shared_part = matmul_nt(sh_hidden, shdown_t).astype(bf16)
+    sh_dhidden = matmul(sh_dy, shdown_t)
+    sh_dgate = (sh_dhidden * sh_up * sh_sig * (1.0 + sh_gate * (1.0 - sh_sig))).astype(bf16)
+    sh_dup = (sh_dhidden * sh_gate * sh_sig).astype(bf16)
+    sh_dboth = jnp.concatenate([sh_dgate, sh_dup], 1)
+    sh_dnormed_part = matmul_nt(sh_dboth, gateup_full).astype(bf16)
+    second_grad = second_grads(normed2, cotangent, sh_dboth, sh_hidden)
+    second_sum = lax.psum_scatter(second_grad, "ep", scatter_dimension=0, tiled=True)
+
+    first, shared_part, sh_dnormed_part, second_grad = lax.optimization_barrier(
+        (first, shared_part, sh_dnormed_part, second_grad)
+    )
+    shared_q = sum_to_quarter(shared_part)
+    sh_dnormed_q = sum_to_quarter(sh_dnormed_part)
+    rows = ring_gather_parts(*own, first, ring_gather_second(first))
 
     logits = matmul(normed2, router_full)
     onehot = (
@@ -312,77 +613,80 @@
     for k in range(TOPK):
         gate_rows = gate_rows + jnp.where(matches[k], gate_vals[:, k][None, :], 0.0)
     gate_rows = jnp.sum(gate_rows, 1).reshape(owner_count, width)
-    gate_rows = to_experts(exchange(gate_rows))[:, None]
-
-    upstream = cotangent.astype(f32)
-    sh_both = matmul(normed2, gateup_full)
-    sh_gate = sh_both[:, :sh_cols]
-    sh_up = sh_both[:, sh_cols:]
-    sh_sig = 1.0 / (1.0 + jnp.exp(-sh_gate))
-    sh_hidden = (sh_gate * sh_sig * sh_up).astype(bf16)
-    shared_q = sum_to_quarter(matmul_nt(sh_hidden, shdown_t))
-    sh_dhidden = matmul(cotangent, shdown_t)
-    sh_dgate = (sh_dhidden * sh_up * sh_sig * (1.0 + sh_gate * (1.0 - sh_sig))).astype(bf16)
-    sh_dup = (sh_dhidden * sh_gate * sh_sig).astype(bf16)
-    sh_dboth = jnp.concatenate([sh_dgate, sh_dup], 1)
-    sh_dnormed_q = sum_to_quarter(matmul_nt(sh_dboth, gateup_full))
-    second_grad = jnp.concatenate(
-        [matmul_tn(normed2, sh_dboth).astype(bf16), matmul_tn(cotangent, sh_hidden).astype(bf16)],
-        1,
-    )
-    second_sum = lax.psum_scatter(second_grad, "ep", scatter_dimension=0, tiled=True)
-
-    pick_in = (
-        table[:, :, None] == lax.broadcasted_iota(jnp.int32, (owner_count, width, tok_count), 2)
-    ).astype(bf16)
-    dy_rows = jnp.einsum("ist,itd->isd", pick_in, dy_all, preferred_element_type=f32)
-    dy_rows = to_experts(dy_rows.astype(bf16))
-    edge = owner_count * MAIN
-    extra = slot_rows - 2 * edge
-    span = edge + extra
+    gate_rows = to_experts(exchange(after(gate_rows, two)))[:, None]
+
+    ex_hidden, ex_dboth, dgate_rows = row_call(
+        functools.partial(hidden_kernel, tiles, spill),
+        tile,
+        slot_rows,
+        (*rows, gateup_w, ex_dh, gate_rows),
+        [tile_spec(tile, half)] * 8
+        + [whole_spec(gateup_w.shape), tile_spec(tile, hid_wide), tile_spec(tile, 1)],
+        [(hid_wide, bf16), (2 * hid_wide, bf16), (1, f32)],
+        2 * big,
+        [pltpu.VMEM((tile, 2 * hid_wide), f32)],
+    )
+
+    def row_parts(value, weight, transposed, spots):
+        return row_call(
+            functools.partial(rows_kernel, tiles, spill, transposed, spots),
+            tile,
+            slot_rows,
+            (value, weight),
+            [tile_spec(tile, value.shape[1]), whole_spec(weight.shape)],
+            [(half, bf16)] * len(spots),
+            2 * (slot_rows + extra) * value.shape[1] * half * len(spots),
+        )
+
+    far_spots = [2 * quarter, 2 * quarter + half]
+    other_spots = [0, half, quarter, quarter + half, 3 * quarter, 3 * quarter + half]
+
     extra_iota = lax.broadcasted_iota(jnp.int32, (span, 1), 0)
     owned = (
         (extra_iota < edge) | ((extra_iota - edge) % (EXP_DEV * spill) < spill),
         (extra_iota >= extra) | (extra_iota % (EXP_DEV * spill) >= spill),
     )
 
-    def join(first, second):
-        return jnp.concatenate([first[:edge], first[edge:] + second[:extra], second[extra:]], 0)
-
-    outs, drows, dgates = [], [], []
-    exgate_grad, exup_grad, exdown_grad = [], [], []
-    for e in range(EXP_DEV):
-        at = slice(0, span) if e == 0 else slice(edge, slot_rows)
-        e_rows, e_dy, e_gate = rows[at], dy_rows[at], gate_rows[at]
-        ex_gate = matmul(e_rows, exgate_w[e])
-        ex_up = matmul(e_rows, exup_w[e])
-        ex_sig = 1.0 / (1.0 + jnp.exp(-ex_gate))
-        ex_hidden = jnp.where(owned[e], ex_gate * ex_sig * ex_up, 0.0).astype(bf16)
-        outs.append(matmul(ex_hidden, exdown_w[e]) * e_gate)
-        ex_dh = matmul_nt(e_dy, exdown_w[e])
-        dgates.append(jnp.sum(ex_hidden.astype(f32) * ex_dh, 1))
-        ex_dh = jnp.where(owned[e], ex_dh * e_gate, 0.0)
-        ex_dgate = (ex_dh * ex_up * ex_sig * (1.0 + ex_gate * (1.0 - ex_sig))).astype(bf16)
-        ex_dup = (ex_dh * ex_gate * ex_sig).astype(bf16)
-        drows.append(matmul_nt(ex_dgate, exgate_w[e]) + matmul_nt(ex_dup, exup_w[e]))
-        exgate_grad.append(matmul_tn(e_rows, ex_dgate))
-        exup_grad.append(matmul_tn(e_rows, ex_dup))
-        exdown_grad.append(
-            matmul_tn((ex_hidden.astype(f32) * e_gate).astype(bf16), e_dy)
-        )
-    out_rows = join(*outs).astype(bf16)
-    drow_rows = join(*drows).astype(bf16)
-    dgate_rows = exchange(from_experts(join(*dgates), owner_count)).reshape(-1)
-
-    def give_back(value):
-        summed = lanes_sum([quarter_of(value, step) for step in range(4)])
-        back = exchange(from_experts(summed, owner_count)).reshape(slot_rows, -1)
-        return matmul_tn(pick, back)
-
-    routed_grad_q = give_back(drow_rows)
-    routed_q = give_back(out_rows)
-    layer_q = (quarter_of(mid_resid, 0) + routed_q + shared_q).astype(bf16)
-    layer_out = gather_quarters(layer_q)
+    def expert_rows(value, e):
+        return value[:span] if e == 0 else value[edge:]
+
+    def grads_of(e, left, right, cols):
+        kept = jnp.where(owned[e], expert_rows(right, e)[:, cols], jnp.zeros((), bf16))
+        return matmul_tn(expert_rows(left, e), kept)
+
+    def grads_of_down(late):
+        wide_dy = after(dy_all, late).reshape(lanes, slot_rows, quarter)
+        wide_dy = jnp.concatenate([wide_dy[q] for q in range(lanes)], 1)
+        hidden = after(ex_hidden[:, :hid_cols], late)
+        parts = []
+        for e in range(EXP_DEV):
+            kept = jnp.where(owned[e], expert_rows(hidden, e), jnp.zeros((), bf16))
+            parts.append(matmul_tn(kept, expert_rows(wide_dy, e)))
+        return jnp.stack(parts)
+
+    def bring_back(one, two):
+        back_one = exchange(from_experts(one, owner_count)).reshape(slot_rows, -1)
+        back_two = exchange(from_experts(two, owner_count)).reshape(slot_rows, -1)
+        return jnp.concatenate([matmul_tn(pick, back_one), matmul_tn(pick, back_two)], 1)
+
+    drow_far = row_parts(ex_dboth, gateup_w, True, far_spots)
+    drow = row_parts(ex_dboth, gateup_w, True, other_spots)
+    top = shift(drow_far[0], 1)
+    bottom = shift(drow_far[1], 3)
+    from_next_one = shift(drow[4], 3)
+    dgate_rows = after(dgate_rows[:, 0], drow_far)
+    dgate_rows = exchange(from_experts(dgate_rows, owner_count)).reshape(-1)
+    top, dgate_rows = lax.optimization_barrier((top, dgate_rows))
+    next_one = plus(drow[2], top)
+    from_prev_one = shift(next_one, 1)
+    from_prev_two = shift(after(drow[3], from_prev_one), 1)
+    from_next_two = shift(plus(drow[5], bottom), 3)
+    drow_one = add_three(drow[0], from_prev_one, from_next_one)
+    drow_two = add_three(drow[1], from_prev_two, from_next_two)
+    routed_grad_q = bring_back(drow_one, drow_two)
+    out_parts = row_parts(ex_hidden, down_w, False, far_spots + other_spots)
+    out_far, out_own = after(tuple(out_parts[:2]), drow_two), out_parts[2:]
+    out_first = ring_sum_first(out_far, out_own)
 
     dgate_part = jnp.stack(
         [jnp.sum(jnp.where(matches[k], dgate_rows[:, None], 0.0), 0) for k in range(TOPK)], 1
@@ -392,13 +696,12 @@
     dsel_vals = route_scale / sel_total * (dgate_all - weighted)
     dchosen = dsel_vals * sel_vals * (1.0 - sel_vals)
     dlogits = jnp.sum(onehot * dchosen[:, :, None], 1).astype(bf16)
-    router_grad = matmul_tn(normed2, dlogits)
     dnormed2 = gather_quarters((routed_grad_q + sh_dnormed_q).astype(bf16)).astype(f32)
     dnormed2 = dnormed2 + matmul_nt(dlogits, router_full)
     dmid_norm, midnorm_grad = rms_back(mid_resid, mid_scale, mid_weight, dnormed2)
     dmid = upstream + dmid_norm
-    dmid16 = dmid.astype(bf16)
-    output_grad_t = matmul_tn(dmid16, attended)
+    dmid16, out_first = lax.optimization_barrier((dmid.astype(bf16), out_first))
+    out_second = ring_sum_second(out_first, out_own)
     dattended = matmul(dmid16, output_t).astype(bf16).reshape(tok_count, head_count, DV)
     dprobs = jnp.einsum("thd,shd->hts", dattended, values, preferred_element_type=f32)
     dscores = (probs * (dprobs - jnp.sum(probs * dprobs, -1, keepdims=True))).astype(bf16)
@@ -416,11 +719,11 @@
         .reshape(tok_count, head_count * (DN + DV))
         .astype(bf16)
     )
-    keyval_grad = matmul_tn(latent_n, dkeyval)
     dlatent_part = matmul_nt(dkeyval, keyval_full)
     dkey_part = jnp.sum(dkey_all[..., DN:], 1)
     dlat_sum = sum_small(jnp.concatenate([dlatent_part, dkey_part], 1).astype(bf16))
     dnormed_q = sum_to_quarter(matmul_nt(dquery, query_full))
+    dlat_sum, second_sum, out_second = lax.optimization_barrier((dlat_sum, second_sum, out_second))
     dlatent, latnorm_grad = rms_back(latent, lat_scale, lat_weight, dlat_sum[:, :KVR])
     dlatent_all = jnp.concatenate(
         [dlatent, rotate(dlat_sum[:, KVR:], cos_tab, -sine_tab)], -1
@@ -430,9 +733,9 @@
     )
     dtokens, prenorm_grad = rms_back(resid_in, pre_scale, pre_weight, dnormed)
     tokens_grad = (dmid + dtokens).astype(bf16)
+    prenorm_sum = jnp.sum(exchange(prenorm_grad.reshape(owner_count, shard)), 0)
     gain_grads = jnp.stack(
         [
-            prenorm_grad,
             jnp.pad(
                 latnorm_grad.reshape(owner_count, -1),
                 ((0, 0), (0, shard - latnorm.shape[0])),
@@ -442,36 +745,60 @@
         1,
     )
     gain_grads = jnp.pad(gain_grads, ((0, 0), (0, 128 - gain_grads.shape[1])))
-    first_grad = jnp.concatenate(
+    first_grad = first_grads(
+        kv_rows,
+        normed,
+        normed2,
+        dmid16,
+        dquery,
+        jnp.pad(dlatent_all, ((0, 0), (0, experts))),
+        jnp.pad(dlogits, ((0, 0), (lat_cols, 0))),
+        attended,
+        latent_n,
+        dkeyval,
+        gain_grads.astype(bf16),
+    )
+    down_grad = grads_of_down(first_grad)
+    all_rows = jnp.concatenate(after(rows, first_grad), 1)
+    late_dboth = after(ex_dboth, first_grad)
+    exgate_grad = jnp.stack(
+        [grads_of(e, all_rows, late_dboth, slice(0, hid_cols)) for e in range(EXP_DEV)]
+    )
+    exup_grad = jnp.stack(
         [
-            matmul_tn(normed, dquery).astype(bf16),
-            matmul_tn(normed, dlatent_all).astype(bf16),
-            router_grad.astype(bf16),
-            keyval_grad.astype(bf16).reshape(D, kv_cols),
-            output_grad_t.astype(bf16),
-            gain_grads.astype(bf16),
-        ],
-        1,
-    )
+            grads_of(e, all_rows, late_dboth, slice(hid_wide, hid_wide + hid_cols))
+            for e in range(EXP_DEV)
+        ]
+    )
+    exgate_grad = to_lane(exgate_grad, 1)
+    exup_grad = to_lane(exup_grad, 1)
+    out_one = add_three(out_own[0], *after((out_second[0], out_first[2]), first_grad, dnormed))
+    out_two = add_three(out_own[1], *after((out_first[3], out_second[1]), first_grad, dnormed))
+    routed_q = bring_back(out_one, out_two)
+    layer_q = (quarter_of(mid_resid, 0) + routed_q + shared_q).astype(bf16)
+    layer_out = gather_quarters(layer_q)
     first_sum = lax.psum_scatter(first_grad, "ep", scatter_dimension=0, tiled=True).astype(f32)
     second_sum = second_sum.astype(f32)
     return (
         layer_out,
         tokens_grad,
-        first_sum[:, edges[5]],
+        prenorm_sum,
         first_sum[:, edges[0] : edges[1]],
         first_sum[:, edges[1] : edges[2]],
-        first_sum[: latnorm.shape[0], edges[5] + 1],
-        first_sum[:, edges[3] : edges[4]].reshape(keyval_w.shape),
+        first_sum[: latnorm.shape[0], edges[5]],
+        first_sum[:, edges[3] : edges[4]]
+        .reshape(-1, kv_rows, kv_cols)
+        .transpose(1, 0, 2)
+        .reshape(keyval_w.shape),
         first_sum[:, edges[4] : edges[5]].T,
-        first_sum[:, edges[5] + 2],
+        first_sum[:, edges[5] + 1],
         first_sum[:, edges[2] : edges[3]],
         second_sum[:, :sh_cols],
         second_sum[:, sh_cols : 2 * sh_cols],
         second_sum[:, 2 * sh_cols :].T,
-        jnp.stack(exgate_grad),
-        jnp.stack(exup_grad),
-        jnp.stack(exdown_grad),
+        exgate_grad,
+        exup_grad,
+        down_grad,
     )
 
 

time: 828 us -> 797 us (0.963)
  blocking collectives: 118 us -> 14.3 us
  matrix products: 160 us -> 81.2 us
  Pallas kernels: 0 us -> 78.6 us
  starting transfers between devices: 73.2 us -> 122 us
  waiting for transfers between devices: 278 us -> 289 us
  other arithmetic: 67.1 us -> 76.4 us
    pallas_call x0 -> x7, Pallas kernels: none -> 78.6 us  [the longest x5 63.8 us: row_call(): pl.pallas_call(body, grid=(total // tile,), in_specs=in_specs, out_specs=...]
    all_gather x4 -> x0, blocking collectives: 56.4 us -> none  [gather_quarters(): return lax.all_gather(piece, 'tp', axis=1, tiled=True)]
    all_to_all x1, blocking collectives: 61.3 us -> 14.3 us  [exchange(): return lax.all_to_all(value, 'ep', 0, 0, tiled=True)]
    all_gather x1, waiting for transfers between devices: 57.9 us -> 25.2 us  [per_device(): first_full = lax.all_gather(first_pack, 'ep', axis=0, tiled=True)]
    ppermute x30 -> x48, waiting for transfers between devices: 175 us -> 204 us  [shift(): lax.ppermute(value, 'tp', [(i, (i + step) % lanes) for i in range(lanes)])]
    all_to_all x5 -> x9, starting transfers between devices: 25.5 us -> 52.9 us  [exchange(): return lax.all_to_all(value, 'ep', 0, 0, tiled=True)]
    dot_general x14 -> x9, matrix products: 52.1 us -> 25 us  [matmul(): return jnp.dot(left_mat, right_mat, preferred_element_type=f32)]
    ppermute x30 -> x48, starting transfers between devices: 47.1 us -> 69.2 us  [shift(): lax.ppermute(value, 'tp', [(i, (i + step) % lanes) for i in range(lanes)])]
  transfers between devices with their start and end apart: 40 -> 62, of which waited for: 21 -> 29; matrix products, arithmetic and copies ran while one was open for 38% -> 29% of each run, Pallas kernels for 0% -> 6%
where the time goes in v2:
time: 797 us; the launch traced here: 787 us
  waiting for transfers between devices  289 us (36%)
  starting transfers between devices  122 us (15%)
  local copies, waits for them, and re-layouts  109 us (14%)
  matrix products  81.2 us (10%)
  Pallas kernels  78.6 us (10%)
  other arithmetic  76.4 us (10%)
  between operations  16.7 us (2%)
  blocking collectives  14.3 us (2%)
    ppermute x48, waiting for transfers between devices, shift(): lax.ppermute(value, 'tp', [(i, (i + step) % lanes) for i in range(lanes)])  204 us
    ppermute x48, starting transfers between devices, shift(): lax.ppermute(value, 'tp', [(i, (i + step) % lanes) for i in range(lanes)])  69.2 us
    pallas_call x5, Pallas kernels, row_call(): pl.pallas_call(body, grid=(total // tile,), in_specs=in_specs, out_specs=...  63.8 us
    all_to_all x9, waiting for transfers between devices, exchange(): return lax.all_to_all(value, 'ep', 0, 0, tiled=True)  60.1 us
    unnamed x303, local copies, waits for them, and re-layouts  54.9 us
    all_to_all x9, starting transfers between devices, exchange(): return lax.all_to_all(value, 'ep', 0, 0, tiled=True)  52.9 us
    dot_general x10, matrix products, matmul_tn(): lax.dot_general(left_mat, right_mat, (((0,), (0,)), ((), ())), preferred_...  26.8 us
    all_gather x1, waiting for transfers between devices, per_device(): first_full = lax.all_gather(first_pack, 'ep', axis=0, tiled=True)  25.2 us
  transfers between devices with their start and end apart: 62, of which 29 were waited for; matrix products, arithmetic and copies ran while one was open for 29% of the time, Pallas kernels for 6%

profile of v2, /device:TPU:0, one launch (start us, length us, event | category | flops | bytes accessed | tf_op | source)
XLA Modules:
  0.0 787.4 jit_solution(14330028728506171131)
XLA Ops:
  12.1 4.1 convolution_convert_fusion.1
  16.2 7.8 all-to-all-start
  24.1 4.6 constant_dynamic-slice_fusion.35
  64.4 25.2 %all-gather.4.cloned.1.call-done = bf16[2048,2304]{1,0:T(8,128)(2,1)} async-done(((bf16[64,2304]{1,0:T(8,128)(2,1)}), bf16[2048,2304]{1,0:T(8,128)(2,1)}) %all-gather.4.cloned.1.call-update) | async-done | bytes 9437200 | tf_op jit(solution)/shard_map/all_gather | solution.py:438
  100.6 3.6 fusion.62
  138.3 5.4 collective-permute-done.2
  151.3 5.4 collective-permute-done.4
  162.7 5.1 all-to-all-start.1
  169.9 16.3 %all-to-all-done.1 = bf16[32,72,256]{2,1,0:T(8,128)(2,1)} async-done(((bf16[32,72,256]{2,1,0:T(8,128)(2,1)}), bf16[32,72,256]{2,1,0:T(8,128)(2,1)}, u32[]{:S(2)}, u32[]{:S(2)}) %all-to-all-start.1) | async-done | bytes 1179680 | tf_op jit(solution)/shard_map/all_to_all | solution.py:119
  186.2 4.7 all-to-all-start.2
  196.6 12.6 %all-to-all-done.2 = bf16[32,72,256]{2,1,0:T(8,128)(2,1)} async-done(((bf16[32,72,256]{2,1,0:T(8,128)(2,1)}), bf16[32,72,256]{2,1,0:T(8,128)(2,1)}, u32[]{:S(2)}, u32[]{:S(2)}) %all-to-all-start.2) | async-done | bytes 1179680 | tf_op jit(solution)/shard_map/all_to_all | solution.py:119
  215.7 4.4 fusion.19
  223.2 6.9 shard_map.306
  230.9 4.1 fusion.67
  235.0 5.6 fusion.70
  240.6 8.1 %collective-permute-done.9.refs_2_ = bf16[2304,256]{1,0:T(8,128)(2,1)} collective-permute-done((bf16[2304,256]{1,0:T(8,128)(2,1)}, bf16[2304,256]{1,0:T(8,128)(2,1)}, u32[]{:S(2)}, u32[]{:S(2)}) %collective-permute-start.9) | collective-permute-done | bytes 1179680 | tf_op jit(solution)/shard_map/ppermute | solution.py:78
  252.2 37.6 %collective-permute-done.8.refs_7_ = bf16[2304,256]{1,0:T(8,128)(2,1)} collective-permute-done((bf16[2304,256]{1,0:T(8,128)(2,1)}, bf16[2304,256]{1,0:T(8,128)(2,1)}, u32[]{:S(2)}, u32[]{:S(2)}) %collective-permute-start.8) | collective-permute-done | bytes 1179680 | tf_op jit(solution)/shard_map/ppermute | solution.py:78
  294.0 14.3 %all_to_all.65 = f32[32,1,72]{2,1,0:T(1,128)S(1)} all-to-all(f32[32,1,72]{2,1,0:T(1,128)S(1)} %bitcast.170), channel_id=1, replica_groups=mesh['ep'=32,'tp'=4] {'ep'}, dimensions={0} | all-to-all | bytes 18432 | tf_op jit(solution)/shard_map/all_to_all | solution.py:119
  310.1 10.7 %shard_map.307.refs_9_ = f32[2304,384]{1,0:T(8,128)S(1)} custom-call(bf16[9216,512]{1,0:T(8,128)(2,1)} %all-gather.8.cloned.1.call-done.refs_0_.refs_1_.refs_2_.refs_3_, bf16[9216,512]{1,0:T(8,128)(2,1)} %all-gather.8.cloned.1.call-done.refs_0_.refs_1_.refs_2_.refs_3_, bf16[9216,512]{1,0:T(8,128)(2,1)} %all-gather.8.cloned.1.call-done.refs_0_.refs_1_.refs_2_.refs_3_, ...), custom_call_target="tpu_custom_call" | custom-call | flops 4026531840 | bytes 44433408 | tf_op jit(solution)/shard_map/pallas_call | solution.py:277
  322.6 19.3 %shard_map.308 = (bf16[2304,384]{1,0:T(8,128)(2,1)}, bf16[2304,768]{1,0:T(8,128)(2,1)}, f32[2304,1]{1,0:T(8,128)S(1)}) custom-call(bf16[2304,256]{1,0:T(8,128)(2,1)} %pad_maximum_fusion.6.refs_0_, bf16[2304,256]{1,0:T(8,128)(2,1)} %pad_maximum_fusion.7.refs_1_, bf16[2304,256]{1,0:T(8,128)(2,1)} %collective-permute-done.9.refs_2_, ...), custom_call_target="tpu_custom_call" | custom-call | flops 8053063680 | bytes 24594432 | tf_op jit(solution)/shard_map/pallas_call | solution.py:277
  344.3 8.7 %shard_map.311 = (bf16[2304,256]{1,0:T(8,128)(2,1)}, bf16[2304,256]{1,0:T(8,128)(2,1)}) custom-call(bf16[2304,768]{1,0:T(8,128)(2,1)S(1)} %copy-done.6, bf16[2,2048,768]{2,1,0:T(8,128)(2,1)} %pad_maximum_fusion.1.refs_8_.refs_1_), custom_call_target="tpu_custom_call" | custom-call | flops 2013265920 | bytes 12189696 | tf_op jit(solution)/shard_map/pallas_call | solution.py:277
  357.8 3.8 all-to-all-start.4
  361.6 13.4 %shard_map.310 = (bf16[2304,256]{1,0:T(8,128)(2,1)S(1)}, bf16[2304,256]{1,0:T(8,128)(2,1)S(1)}, bf16[2304,256]{1,0:T(8,128)(2,1)S(1)}, bf16[2304,256]{1,0:T(8,12...) custom-call(bf16[2304,768]{1,0:T(8,128)(2,1)} %get-tuple-element.147.refs_0_, ...), custom_call_target="tpu_custom_call" | custom-call | flops 6039797760 | bytes 16908288 | tf_op jit(solution)/shard_map/pallas_call | solution.py:277
  391.5 16.1 %collective-permute-done.16 = bf16[2304,256]{1,0:T(8,128)(2,1)} collective-permute-done((bf16[2304,256]{1,0:T(8,128)(2,1)}, bf16[2304,256]{1,0:T(8,128)(2,1)}, u32[]{:S(2)}, u32[]{:S(2)}) %collective-permute-start.16) | collective-permute-done | bytes 1179680 | tf_op jit(solution)/shard_map/ppermute | solution.py:78
  410.4 3.7 collective-permute-start.17
  415.5 21.6 %collective-permute-done.14 = bf16[2304,256]{1,0:T(8,128)(2,1)} collective-permute-done((bf16[2304,256]{1,0:T(8,128)(2,1)}, bf16[2304,256]{1,0:T(8,128)(2,1)}, u32[]{:S(2)}, u32[]{:S(2)}) %collective-permute-start.14) | collective-permute-done | bytes 1179680 | tf_op jit(solution)/shard_map/ppermute | solution.py:78
  440.1 7.6 all-to-all-start.5
  447.6 14.1 %collective-permute-done.17 = bf16[2304,256]{1,0:T(8,128)(2,1)} collective-permute-done((bf16[2304,256]{1,0:T(8,128)(2,1)}, bf16[2304,256]{1,0:T(8,128)(2,1)}, u32[]{:S(2)}, u32[]{:S(2)}) %collective-permute-start.17) | collective-permute-done | bytes 1179680 | tf_op jit(solution)/shard_map/ppermute | solution.py:78
  466.0 6.5 all-to-all-start.6
  478.8 11.7 %shard_map.309 = (bf16[2304,256]{1,0:T(8,128)(2,1)}, bf16[2304,256]{1,0:T(8,128)(2,1)}, bf16[2304,256]{1,0:T(8,128)(2,1)S(1)}, bf16[2304,256]{1,0:T(8,128)(2,1)S...) custom-call(bf16[2304,384]{1,0:T(8,128)(2,1)} %get-tuple-element.98., ...), custom_call_target="tpu_custom_call" | custom-call | flops 4026531840 | bytes 14352384 | tf_op jit(solution)/shard_map/pallas_call | solution.py:277
  511.2 21.0 %collective-permute-done.23 = bf16[192,512]{1,0:T(8,128)(2,1)S(1)} collective-permute-done((bf16[192,512]{1,0:T(8,128)(2,1)S(1)}, bf16[192,512]{1,0:T(8,128)(2,1)S(1)}, u32[]{:S(2)}, u32[]{:S(2)}) %collective-permute-start.23) | collective-permute-done | bytes 196640 | tf_op jit(solution)/shard_map/ppermute | solution.py:78
  532.3 3.8 collective-permute-done.22
  539.7 20.1 %collective-permute-done.27 = bf16[2304,256]{1,0:T(8,128)(2,1)S(1)} collective-permute-done((bf16[2304,256]{1,0:T(8,128)(2,1)}, bf16[2304,256]{1,0:T(8,128)(2,1)S(1)}, u32[]{:S(2)}, u32[]{:S(2)}) %collective-permute-start.27) | collective-permute-done | bytes 1179680 | tf_op jit(solution)/shard_map/ppermute | solution.py:78
  560.4 3.7 collective-permute-start.35
  577.4 22.0 %collective-permute-done.32 = bf16[192,576]{1,0:T(8,128)(2,1)S(1)} collective-permute-done((bf16[192,576]{1,0:T(8,128)(2,1)S(1)}, bf16[192,576]{1,0:T(8,128)(2,1)S(1)}, u32[]{:S(2)}, u32[]{:S(2)}) %collective-permute-start.32) | collective-permute-done | bytes 221216 | tf_op jit(solution)/shard_map/ppermute | solution.py:78
  599.3 6.0 collective-permute-done.31
  613.4 4.1 fusion.64
  617.5 7.9 %shard_map.312 = bf16[2048,2304]{1,0:T(8,128)(2,1)} custom-call(bf16[192,2048]{1,0:T(8,128)(2,1)S(1)} %copy-done.11, bf16[192,2048]{1,0:T(8,128)(2,1)S(1)} %copy-done.2, bf16[192,2048]{1,0:T(8,128)(2,1)S(1)} %fusion.194.dmid, bf16[192,768]{1,0:T(8,128)(2,1)S(1)} %convert_element_type.375.dquery, bf16[192,640]{1,0:T(8,128)(2,1)S(1)} %pad.46.dlat, ...), custom_call_target="tpu_custom_call" | custom-call | flops 1811939328 | bytes 14155776 | tf_op jit(solution)/shard_map/pallas_call | solution.py:342
  653.5 5.2 fusion.47
  682.4 5.0 collective-permute-done.41
  688.5 4.9 fusion.95
  697.3 7.5 all-to-all-start.7
  708.1 17.3 %all-to-all-done.7 = bf16[32,72,256]{2,1,0:T(8,128)(2,1)} async-done(((bf16[32,72,256]{2,1,0:T(8,128)(2,1)}), bf16[32,72,256]{2,1,0:T(8,128)(2,1)}, u32[]{:S(2)}, u32[]{:S(2)}) %all-to-all-start.7) | async-done | bytes 1179680 | tf_op jit(solution)/shard_map/all_to_all | solution.py:119
  725.5 6.1 all-to-all-start.8
  732.3 3.9 fusion.91
  738.9 11.1 %all-to-all-done.8 = bf16[32,72,256]{2,1,0:T(8,128)(2,1)} async-done(((bf16[32,72,256]{2,1,0:T(8,128)(2,1)}), bf16[32,72,256]{2,1,0:T(8,128)(2,1)}, u32[]{:S(2)}, u32[]{:S(2)}) %all-to-all-start.8) | async-done | bytes 1179680 | tf_op jit(solution)/shard_map/all_to_all | solution.py:119
  750.0 3.8 all-to-all-start.9
  766.5 4.4 collective-permute-done.46
  (601 shorter events, 299.9 us)
Async XLA Ops:
  7.2 82.4 %all-gather.4.cloned.1.call-start = ((), (), s32[]{:S(2)}) async-start(), calls=%async_computation.12 | async-start | bytes 9732096 | tf_op jit(solution)/shard_map/all_gather | solution.py:438
  16.2 43.8 %all-to-all-start = ((bf16[32,72,512]{2,1,0:T(8,128)(2,1)}), bf16[32,72,512]{2,1,0:T(8,128)(2,1)}, u32[]{:S(2)}, u32[]{:S(2)}) async-start(bf16[32,72,512]{2,1,0:T(8,128)(2,1)} %bitcast.149), calls=%async_computation | async-start | bytes 4718592 | tf_op jit(solution)/shard_map/all_to_all | solution.py:119
  24.0 191.7 %all-gather.6.cloned.1.call-start = ((), (), s32[]{:S(2)}) async-start(), calls=%async_computation.13 | async-start | bytes 9191424 | tf_op jit(solution)/shard_map/all_gather | solution.py:496
  89.6 220.4 %all-gather.8.cloned.1.call-start = ((), (), s32[]{:S(2)}) async-start(), calls=%async_computation.14 | async-start | bytes 11796480 | tf_op jit(solution)/shard_map/all_gather | solution.py:552
  162.7 23.5 %all-to-all-start.1 = ((bf16[32,72,256]{2,1,0:T(8,128)(2,1)}), bf16[32,72,256]{2,1,0:T(8,128)(2,1)}, u32[]{:S(2)}, u32[]{:S(2)}) async-start(bf16[32,72,256]{2,1,0:T(8,128)(2,1)} %get-tuple-element.191), calls=%async_computation.1 | async-start | bytes 2359296 | tf_op jit(solution)/shard_map/all_to_all | solution.py:119
  186.2 23.0 %all-to-all-start.2 = ((bf16[32,72,256]{2,1,0:T(8,128)(2,1)}), bf16[32,72,256]{2,1,0:T(8,128)(2,1)}, u32[]{:S(2)}, u32[]{:S(2)}) async-start(bf16[32,72,256]{2,1,0:T(8,128)(2,1)} %get-tuple-element.84), calls=%async_computation.2 | async-start | bytes 2359296 | tf_op jit(solution)/shard_map/all_to_all | solution.py:119
  190.9 415.8 %reduce-scatter.3.cloned.1.call-start = ((), (), s32[]{:S(2)}) async-start(), calls=%async_computation.15 | async-start | bytes 9191424 | tf_op jit(solution)/shard_map/reduce_scatter | solution.py:595
  194.3 54.4 %collective-permute-start.9 = (bf16[2304,256]{1,0:T(8,128)(2,1)}, bf16[2304,256]{1,0:T(8,128)(2,1)}, u32[]{:S(2)}, u32[]{:S(2)}) collective-permute-start(bf16[2304,256]{1,0:T(8,128)(2,1)} %pad_maximum_fusion.6.refs_0_), channel_id=1, source_target_pairs={{0,3},{1,0},{2,1},{3,2},{4,7},{5,4},{6,5},{7,6},{8,11},{9,8},{10,9... | collective-permute-start | bytes 3538952 | tf_op jit(solution)/shard_map/ppermute | solution.py:78
  196.6 55.6 %collective-permute-start.6 = (bf16[2304,256]{1,0:T(8,128)(2,1)}, bf16[2304,256]{1,0:T(8,128)(2,1)}, u32[]{:S(2)}, u32[]{:S(2)}) collective-permute-start(bf16[2304,256]{1,0:T(8,128)(2,1)} %pad_maximum_fusion.6.refs_0_), channel_id=1, source_target_pairs={{0,1},{1,2},{2,3},{3,0},{4,5},{5,6},{6,7},{7,4},{8,9},{9,10},{10,1... | collective-permute-start | bytes 3538952 | tf_op jit(solution)/shard_map/ppermute | solution.py:78
  212.5 77.4 %collective-permute-start.8 = (bf16[2304,256]{1,0:T(8,128)(2,1)}, bf16[2304,256]{1,0:T(8,128)(2,1)}, u32[]{:S(2)}, u32[]{:S(2)}) collective-permute-start(bf16[2304,256]{1,0:T(8,128)(2,1)} %pad_maximum_fusion.7.refs_1_), channel_id=1, source_target_pairs={{0,1},{1,2},{2,3},{3,0},{4,5},{5,6},{6,7},{7,4},{8,9},{9,10},{10,1... | collective-permute-start | bytes 3538952 | tf_op jit(solution)/shard_map/ppermute | solution.py:78
  213.9 75.9 %collective-permute-start.7 = (bf16[2304,256]{1,0:T(8,128)(2,1)}, bf16[2304,256]{1,0:T(8,128)(2,1)}, u32[]{:S(2)}, u32[]{:S(2)}) collective-permute-start(bf16[2304,256]{1,0:T(8,128)(2,1)} %pad_maximum_fusion.7.refs_1_), channel_id=1, source_target_pairs={{0,3},{1,0},{2,1},{3,2},{4,7},{5,4},{6,5},{7,6},{8,11},{9,8},{10,9... | collective-permute-start | bytes 3538952 | tf_op jit(solution)/shard_map/ppermute | solution.py:78
  289.9 32.8 %collective-permute-start.11 = (bf16[2304,256]{1,0:T(8,128)(2,1)}, bf16[2304,256]{1,0:T(8,128)(2,1)}, u32[]{:S(2)}, u32[]{:S(2)}) collective-permute-start(bf16[2304,256]{1,0:T(8,128)(2,1)} %collective-permute-done.7.refs_3_), channel_id=1, source_target_pairs={{0,3},{1,0},{2,1},{3,2},{4,7},{5,4},{6,5},{7,6},{8,11},{9,8},{10,9... | collective-permute-start | bytes 3538952 | tf_op jit(solution)/shard_map/ppermute | solution.py:78
  291.3 31.3 %collective-permute-start.10 = (bf16[2304,256]{1,0:T(8,128)(2,1)}, bf16[2304,256]{1,0:T(8,128)(2,1)}, u32[]{:S(2)}, u32[]{:S(2)}) collective-permute-start(bf16[2304,256]{1,0:T(8,128)(2,1)} %collective-permute-done.6.refs_6_), channel_id=1, source_target_pairs={{0,1},{1,2},{2,3},{3,0},{4,5},{5,6},{6,7},{7,4},{8,9},{9,10},{10,1... | collective-permute-start | bytes 3538952 | tf_op jit(solution)/shard_map/ppermute | solution.py:78
  353.0 29.6 %collective-permute-start.12 = (bf16[2304,256]{1,0:T(8,128)(2,1)}, bf16[2304,256]{1,0:T(8,128)(2,1)}, u32[]{:S(2)}, u32[]{:S(2)}) collective-permute-start(bf16[2304,256]{1,0:T(8,128)(2,1)} %get-tuple-element.104), channel_id=1, source_target_pairs={{0,1},{1,2},{2,3},{3,0},{4,5},{5,6},{6,7},{7,4},{8,9},{9,10},{10,1... | collective-permute-start | bytes 3538952 | tf_op jit(solution)/shard_map/ppermute | solution.py:78
  357.8 23.6 %all-to-all-start.4 = ((f32[32,1,72]{2,1,0:T(1,128)}), f32[32,1,72]{2,1,0:T(1,128)S(1)}, u32[]{:S(2)}, u32[]{:S(2)}) async-start(f32[32,1,72]{2,1,0:T(1,128)} %bitcast.36), calls=%async_computation.4 | async-start | bytes 32768 | tf_op jit(solution)/shard_map/all_to_all | solution.py:119
  378.1 29.6 %collective-permute-start.16 = (bf16[2304,256]{1,0:T(8,128)(2,1)}, bf16[2304,256]{1,0:T(8,128)(2,1)}, u32[]{:S(2)}, u32[]{:S(2)}) collective-permute-start(bf16[2304,256]{1,0:T(8,128)(2,1)} %get-tuple-element.106), channel_id=1, source_target_pairs={{0,3},{1,0},{2,1},{3,2},{4,7},{5,4},{6,5},{7,6},{8,11},{9,8},{10,9... | collective-permute-start | bytes 3538952 | tf_op jit(solution)/shard_map/ppermute | solution.py:78
  381.0 56.1 %collective-permute-start.14 = (bf16[2304,256]{1,0:T(8,128)(2,1)}, bf16[2304,256]{1,0:T(8,128)(2,1)}, u32[]{:S(2)}, u32[]{:S(2)}) collective-permute-start(bf16[2304,256]{1,0:T(8,128)(2,1)} %get-tuple-element.109), channel_id=1, source_target_pairs={{0,3},{1,0},{2,1},{3,2},{4,7},{5,4},{6,5},{7,6},{8,11},{9,8},{10,9... | collective-permute-start | bytes 3538952 | tf_op jit(solution)/shard_map/ppermute | solution.py:78
  384.9 30.5 %collective-permute-start.13 = (bf16[2304,256]{1,0:T(8,128)(2,1)S(1)}, bf16[2304,256]{1,0:T(8,128)(2,1)S(1)}, u32[]{:S(2)}, u32[]{:S(2)}) collective-permute-start(bf16[2304,256]{1,0:T(8,128)(2,1)S(1)} %add_convert_fusion.7), channel_id=1, source_target_pairs={{0,1},{1,2},{2,3},{3,0},{4,5},{5,6},{6,7},{7,4},{8,9},{9,10},{10,1... | collective-permute-start | bytes 3538952 | tf_op jit(solution)/shard_map/ppermute | solution.py:78
  387.5 116.8 %collective-permute-start.18 = (bf16[192,512]{1,0:T(8,128)(2,1)}, bf16[192,512]{1,0:T(8,128)(2,1)S(1)}, u32[]{:S(2)}, u32[]{:S(2)}) collective-permute-start(bf16[192,512]{1,0:T(8,128)(2,1)} %get-tuple-element.233), channel_id=1, source_target_pairs={{0,1},{1,2},{2,3},{3,0},{4,5},{5,6},{6,7},{7,4},{8,9},{9,10},{10,1... | collective-permute-start | bytes 589832 | tf_op jit(solution)/shard_map/ppermute | solution.py:78
  387.5 116.8 %collective-permute-start.20 = (bf16[192,512]{1,0:T(8,128)(2,1)}, bf16[192,512]{1,0:T(8,128)(2,1)}, u32[]{:S(2)}, u32[]{:S(2)}) collective-permute-start(bf16[192,512]{1,0:T(8,128)(2,1)} %get-tuple-element.234), channel_id=1, source_target_pairs={{0,2},{1,3},{2,0},{3,1},{4,6},{5,7},{6,4},{7,5},{8,10},{9,11},{10,... | collective-permute-start | bytes 589832 | tf_op jit(solution)/shard_map/ppermute | solution.py:78
  410.4 51.4 %collective-permute-start.17 = (bf16[2304,256]{1,0:T(8,128)(2,1)}, bf16[2304,256]{1,0:T(8,128)(2,1)}, u32[]{:S(2)}, u32[]{:S(2)}) collective-permute-start(bf16[2304,256]{1,0:T(8,128)(2,1)} %add_convert_fusion.5), channel_id=1, source_target_pairs={{0,3},{1,0},{2,1},{3,2},{4,7},{5,4},{6,5},{7,6},{8,11},{9,8},{10,9... | collective-permute-start | bytes 3538952 | tf_op jit(solution)/shard_map/ppermute | solution.py:78
  415.4 46.3 %collective-permute-start.15 = (bf16[2304,256]{1,0:T(8,128)(2,1)}, bf16[2304,256]{1,0:T(8,128)(2,1)}, u32[]{:S(2)}, u32[]{:S(2)}) collective-permute-start(bf16[2304,256]{1,0:T(8,128)(2,1)} %get-tuple-element.112), channel_id=1, source_target_pairs={{0,1},{1,2},{2,3},{3,0},{4,5},{5,6},{6,7},{7,4},{8,9},{9,10},{10,1... | collective-permute-start | bytes 3538952 | tf_op jit(solution)/shard_map/ppermute | solution.py:78
  440.1 25.9 %all-to-all-start.5 = ((bf16[32,72,256]{2,1,0:T(8,128)(2,1)}), bf16[32,72,256]{2,1,0:T(8,128)(2,1)}, u32[]{:S(2)}, u32[]{:S(2)}) async-start(bf16[32,72,256]{2,1,0:T(8,128)(2,1)} %pad_maximum_fusion.8), calls=%async_computation.5 | async-start | bytes 2359296 | tf_op jit(solution)/shard_map/all_to_all | solution.py:119
  466.0 35.7 %all-to-all-start.6 = ((bf16[32,72,256]{2,1,0:T(8,128)(2,1)}), bf16[32,72,256]{2,1,0:T(8,128)(2,1)}, u32[]{:S(2)}, u32[]{:S(2)}) async-start(bf16[32,72,256]{2,1,0:T(8,128)(2,1)} %pad_maximum_fusion.9), calls=%async_computation.6 | async-start | bytes 2359296 | tf_op jit(solution)/shard_map/all_to_all | solution.py:119
  472.5 299.8 %reduce-scatter.5.cloned.1.call-start = ((), (), s32[]{:S(2)}) async-start(), calls=%async_computation.16 | async-start | bytes 9732096 | tf_op jit(solution)/shard_map/reduce_scatter | solution.py:780
  474.1 20.4 %collective-permute-start.26 = (f32[192,6]{0,1:T(8,128)S(1)}, f32[192,6]{0,1:T(8,128)S(1)}, u32[]{:S(2)}, u32[]{:S(2)}) collective-permute-start(f32[192,6]{0,1:T(8,128)S(1)} %stack.78), channel_id=1, source_target_pairs={{0,2},{1,3},{2,0},{3,1},{4,6},{5,7},{6,4},{7,5},{8,10},{9,11},{10,... | collective-permute-start | bytes 13832 | tf_op jit(solution)/shard_map/ppermute | solution.py:78
  476.5 20.5 %collective-permute-start.25 = (f32[192,6]{0,1:T(8,128)S(1)}, f32[192,6]{0,1:T(8,128)S(1)}, u32[]{:S(2)}, u32[]{:S(2)}) collective-permute-start(f32[192,6]{0,1:T(8,128)S(1)} %stack.78), channel_id=1, source_target_pairs={{0,3},{1,0},{2,1},{3,2},{4,7},{5,4},{6,5},{7,6},{8,11},{9,8},{10,9... | collective-permute-start | bytes 13832 | tf_op jit(solution)/shard_map/ppermute | solution.py:78
  478.0 19.2 %collective-permute-start.24 = (f32[192,6]{0,1:T(8,128)S(1)}, f32[192,6]{0,1:T(8,128)S(1)}, u32[]{:S(2)}, u32[]{:S(2)}) collective-permute-start(f32[192,6]{0,1:T(8,128)S(1)} %stack.78), channel_id=1, source_target_pairs={{0,1},{1,2},{2,3},{3,0},{4,5},{5,6},{6,7},{7,4},{8,9},{9,10},{10,1... | collective-permute-start | bytes 13832 | tf_op jit(solution)/shard_map/ppermute | solution.py:78
  497.0 42.7 %collective-permute-start.29 = (bf16[2304,256]{1,0:T(8,128)(2,1)}, bf16[2304,256]{1,0:T(8,128)(2,1)}, u32[]{:S(2)}, u32[]{:S(2)}) collective-permute-start(bf16[2304,256]{1,0:T(8,128)(2,1)} %get-tuple-element.120), channel_id=1, source_target_pairs={{0,3},{1,0},{2,1},{3,2},{4,7},{5,4},{6,5},{7,6},{8,11},{9,8},{10,9... | collective-permute-start | bytes 3538952 | tf_op jit(solution)/shard_map/ppermute | solution.py:78
  497.2 42.5 %collective-permute-start.30 = (bf16[2304,256]{1,0:T(8,128)(2,1)}, bf16[2304,256]{1,0:T(8,128)(2,1)}, u32[]{:S(2)}, u32[]{:S(2)}) collective-permute-start(bf16[2304,256]{1,0:T(8,128)(2,1)} %get-tuple-element.121), channel_id=1, source_target_pairs={{0,1},{1,2},{2,3},{3,0},{4,5},{5,6},{6,7},{7,4},{8,9},{9,10},{10,1... | collective-permute-start | bytes 3538952 | tf_op jit(solution)/shard_map/ppermute | solution.py:78
  505.4 26.7 %collective-permute-start.23 = (bf16[192,512]{1,0:T(8,128)(2,1)S(1)}, bf16[192,512]{1,0:T(8,128)(2,1)S(1)}, u32[]{:S(2)}, u32[]{:S(2)}) collective-permute-start(bf16[192,512]{1,0:T(8,128)(2,1)S(1)} %fusion.144), channel_id=1, source_target_pairs={{0,1},{1,2},{2,3},{3,0},{4,5},{5,6},{6,7},{7,4},{8,9},{9,10},{10,1... | collective-permute-start | bytes 589832 | tf_op jit(solution)/shard_map/ppermute | solution.py:78
  505.6 30.6 %collective-permute-start.22 = (bf16[192,512]{1,0:T(8,128)(2,1)S(1)}, bf16[192,512]{1,0:T(8,128)(2,1)S(1)}, u32[]{:S(2)}, u32[]{:S(2)}) collective-permute-start(bf16[192,512]{1,0:T(8,128)(2,1)S(1)} %fusion.144), channel_id=1, source_target_pairs={{0,2},{1,3},{2,0},{3,1},{4,6},{5,7},{6,4},{7,5},{8,10},{9,11},{10,... | collective-permute-start | bytes 589832 | tf_op jit(solution)/shard_map/ppermute | solution.py:78
  509.0 27.1 %collective-permute-start.21 = (bf16[192,512]{1,0:T(8,128)(2,1)S(1)}, bf16[192,512]{1,0:T(8,128)(2,1)S(1)}, u32[]{:S(2)}, u32[]{:S(2)}) collective-permute-start(bf16[192,512]{1,0:T(8,128)(2,1)S(1)} %fusion.144), channel_id=1, source_target_pairs={{0,3},{1,0},{2,1},{3,2},{4,7},{5,4},{6,5},{7,6},{8,11},{9,8},{10,9... | collective-permute-start | bytes 589832 | tf_op jit(solution)/shard_map/ppermute | solution.py:78
  532.1 27.7 %collective-permute-start.27 = (bf16[2304,256]{1,0:T(8,128)(2,1)}, bf16[2304,256]{1,0:T(8,128)(2,1)S(1)}, u32[]{:S(2)}, u32[]{:S(2)}) collective-permute-start(bf16[2304,256]{1,0:T(8,128)(2,1)} %get-tuple-element.118), channel_id=1, source_target_pairs={{0,1},{1,2},{2,3},{3,0},{4,5},{5,6},{6,7},{7,4},{8,9},{9,10},{10,1... | collective-permute-start | bytes 3538952 | tf_op jit(solution)/shard_map/ppermute | solution.py:78
  536.1 23.9 %collective-permute-start.28 = (bf16[2304,256]{1,0:T(8,128)(2,1)}, bf16[2304,256]{1,0:T(8,128)(2,1)S(1)}, u32[]{:S(2)}, u32[]{:S(2)}) collective-permute-start(bf16[2304,256]{1,0:T(8,128)(2,1)} %get-tuple-element.119), channel_id=1, source_target_pairs={{0,3},{1,0},{2,1},{3,2},{4,7},{5,4},{6,5},{7,6},{8,11},{9,8},{10,9... | collective-permute-start | bytes 3538952 | tf_op jit(solution)/shard_map/ppermute | solution.py:78
  560.4 45.2 %collective-permute-start.35 = (bf16[2304,256]{1,0:T(8,128)(2,1)S(1)}, bf16[2304,256]{1,0:T(8,128)(2,1)S(1)}, u32[]{:S(2)}, u32[]{:S(2)}) collective-permute-start(bf16[2304,256]{1,0:T(8,128)(2,1)S(1)} %add_convert_fusion.2), channel_id=1, source_target_pairs={{0,3},{1,0},{2,1},{3,2},{4,7},{5,4},{6,5},{7,6},{8,11},{9,8},{10,9... | collective-permute-start | bytes 3538952 | tf_op jit(solution)/shard_map/ppermute | solution.py:78
  564.4 42.2 %collective-permute-start.34 = (bf16[2304,256]{1,0:T(8,128)(2,1)S(1)}, bf16[2304,256]{1,0:T(8,128)(2,1)}, u32[]{:S(2)}, u32[]{:S(2)}) collective-permute-start(bf16[2304,256]{1,0:T(8,128)(2,1)S(1)} %add_convert_fusion.3), channel_id=1, source_target_pairs={{0,1},{1,2},{2,3},{3,0},{4,5},{5,6},{6,7},{7,4},{8,9},{9,10},{10,1... | collective-permute-start | bytes 3538952 | tf_op jit(solution)/shard_map/ppermute | solution.py:78
  570.9 28.4 %collective-permute-start.32 = (bf16[192,576]{1,0:T(8,128)(2,1)S(1)}, bf16[192,576]{1,0:T(8,128)(2,1)S(1)}, u32[]{:S(2)}, u32[]{:S(2)}) collective-permute-start(bf16[192,576]{1,0:T(8,128)(2,1)S(1)} %pad_maximum_fusion.23), channel_id=1, source_target_pairs={{0,3},{1,0},{2,1},{3,2},{4,7},{5,4},{6,5},{7,6},{8,11},{9,8},{10,9... | collective-permute-start | bytes 663560 | tf_op jit(solution)/shard_map/ppermute | solution.py:78
  574.1 31.2 %collective-permute-start.31 = (bf16[192,576]{1,0:T(8,128)(2,1)S(1)}, bf16[192,576]{1,0:T(8,128)(2,1)S(1)}, u32[]{:S(2)}, u32[]{:S(2)}) collective-permute-start(bf16[192,576]{1,0:T(8,128)(2,1)S(1)} %pad_maximum_fusion.23), channel_id=1, source_target_pairs={{0,1},{1,2},{2,3},{3,0},{4,5},{5,6},{6,7},{7,4},{8,9},{9,10},{10,1... | collective-permute-start | bytes 663560 | tf_op jit(solution)/shard_map/ppermute | solution.py:78
  574.1 31.3 %collective-permute-start.33 = (bf16[192,576]{1,0:T(8,128)(2,1)S(1)}, bf16[192,576]{1,0:T(8,128)(2,1)S(1)}, u32[]{:S(2)}, u32[]{:S(2)}) collective-permute-start(bf16[192,576]{1,0:T(8,128)(2,1)S(1)} %pad_maximum_fusion.23), channel_id=1, source_target_pairs={{0,2},{1,3},{2,0},{3,1},{4,6},{5,7},{6,4},{7,5},{8,10},{9,11},{10,... | collective-permute-start | bytes 663560 | tf_op jit(solution)/shard_map/ppermute | solution.py:78
  599.3 157.1 %collective-permute-start.42 = (bf16[192,512]{1,0:T(8,128)(2,1)}, bf16[192,512]{1,0:T(8,128)(2,1)}, u32[]{:S(2)}, u32[]{:S(2)}) collective-permute-start(bf16[192,512]{1,0:T(8,128)(2,1)} %get-tuple-element.219), channel_id=1, source_target_pairs={{0,1},{1,2},{2,3},{3,0},{4,5},{5,6},{6,7},{7,4},{8,9},{9,10},{10,1... | collective-permute-start | bytes 589832 | tf_op jit(solution)/shard_map/ppermute | solution.py:78
  605.3 151.2 %collective-permute-start.44 = (bf16[192,512]{1,0:T(8,128)(2,1)}, bf16[192,512]{1,0:T(8,128)(2,1)}, u32[]{:S(2)}, u32[]{:S(2)}) collective-permute-start(bf16[192,512]{1,0:T(8,128)(2,1)} %get-tuple-element.220), channel_id=1, source_target_pairs={{0,2},{1,3},{2,0},{3,1},{4,6},{5,7},{6,4},{7,5},{8,10},{9,11},{10,... | collective-permute-start | bytes 589832 | tf_op jit(solution)/shard_map/ppermute | solution.py:78
  627.3 49.7 %collective-permute-start.36 = (bf16[192,512]{1,0:T(8,128)(2,1)S(1)}, bf16[192,512]{1,0:T(8,128)(2,1)S(1)}, u32[]{:S(2)}, u32[]{:S(2)}) collective-permute-start(bf16[192,512]{1,0:T(8,128)(2,1)S(1)} %get-tuple-element.226), channel_id=1, source_target_pairs={{0,1},{1,2},{2,3},{3,0},{4,5},{5,6},{6,7},{7,4},{8,9},{9,10},{10,1... | collective-permute-start | bytes 589832 | tf_op jit(solution)/shard_map/ppermute | solution.py:78
  627.7 49.2 %collective-permute-start.38 = (bf16[192,512]{1,0:T(8,128)(2,1)S(1)}, bf16[192,512]{1,0:T(8,128)(2,1)S(1)}, u32[]{:S(2)}, u32[]{:S(2)}) collective-permute-start(bf16[192,512]{1,0:T(8,128)(2,1)S(1)} %get-tuple-element.227), channel_id=1, source_target_pairs={{0,2},{1,3},{2,0},{3,1},{4,6},{5,7},{6,4},{7,5},{8,10},{9,11},{10,... | collective-permute-start | bytes 589832 | tf_op jit(solution)/shard_map/ppermute | solution.py:78
  630.9 46.0 %collective-permute-start.37 = (bf16[192,512]{1,0:T(8,128)(2,1)S(1)}, bf16[192,512]{1,0:T(8,128)(2,1)}, u32[]{:S(2)}, u32[]{:S(2)}) collective-permute-start(bf16[192,512]{1,0:T(8,128)(2,1)S(1)} %get-tuple-element.228), channel_id=1, source_target_pairs={{0,3},{1,0},{2,1},{3,2},{4,7},{5,4},{6,5},{7,6},{8,11},{9,8},{10,9... | collective-permute-start | bytes 589832 | tf_op jit(solution)/shard_map/ppermute | solution.py:78
  687.3 69.2 %collective-permute-start.43 = (bf16[192,512]{1,0:T(8,128)(2,1)}, bf16[192,512]{1,0:T(8,128)(2,1)}, u32[]{:S(2)}, u32[]{:S(2)}) collective-permute-start(bf16[192,512]{1,0:T(8,128)(2,1)} %get-tuple-element.221), channel_id=1, source_target_pairs={{0,3},{1,0},{2,1},{3,2},{4,7},{5,4},{6,5},{7,6},{8,11},{9,8},{10,9... | collective-permute-start | bytes 589832 | tf_op jit(solution)/shard_map/ppermute | solution.py:78
  697.3 28.1 %all-to-all-start.7 = ((bf16[32,72,256]{2,1,0:T(8,128)(2,1)}), bf16[32,72,256]{2,1,0:T(8,128)(2,1)}, u32[]{:S(2)}, u32[]{:S(2)}) async-start(bf16[32,72,256]{2,1,0:T(8,128)(2,1)} %pad_maximum_fusion.10), calls=%async_computation.8 | async-start | bytes 2359296 | tf_op jit(solution)/shard_map/all_to_all | solution.py:119
  725.5 24.5 %all-to-all-start.8 = ((bf16[32,72,256]{2,1,0:T(8,128)(2,1)}), bf16[32,72,256]{2,1,0:T(8,128)(2,1)}, u32[]{:S(2)}, u32[]{:S(2)}) async-start(bf16[32,72,256]{2,1,0:T(8,128)(2,1)} %pad_maximum_fusion.11), calls=%async_computation.9 | async-start | bytes 2359296 | tf_op jit(solution)/shard_map/all_to_all | solution.py:119
  (156 other events, 1451.5 us)
Sparse Core Ops, SparseCore 0:
  11.4 78.1 all-gather.3
  91.9 53.6 all-gather.5
  147.9 133.6 all-gather.7
  355.3 91.8 reduce-scatter.2
  625.6 104.2 reduce-scatter.4

commit v3 on v2

--- a/solution.py
+++ b/solution.py
@@ -166,14 +166,6 @@
     return (one, two, one_next, two_next, second[0], second[1], one_prev, two_prev)
 
 
-def ring_sum_first(far, others):
-    return shift(far[0], 1), shift(far[1], 3), shift(others[4], 3), shift(others[3], 1)
-
-
-def ring_sum_second(first, others):
-    return shift(plus(others[2], first[0]), 1), shift(plus(others[5], first[1]), 3)
-
-
 def add_three(one, two, three):
     return (one.astype(f32) + two.astype(f32) + three.astype(f32)).astype(bf16)
 
@@ -215,7 +207,8 @@
 
 
 def hidden_kernel(tiles, spill, *refs):
-    pieces, (weight, dh_ref, gate_ref, hid, dboth, dgate, acc) = refs[:8], refs[8:]
+    pieces, (weight, dh_ref, gate_ref, hid, dboth, dgate), refs = refs[:8], refs[8:14], refs[14:]
+    drow, acc = refs[:8], refs[8]
     rows = jnp.concatenate([p[...] for p in pieces], 1)
 
     def run(owner, mine):
@@ -239,25 +232,33 @@
     dboth[:, :wide] = (dh * up * (sig * (1.0 + pre * (1.0 - sig)))).astype(bf16)
     dboth[:, wide:] = (dh * act).astype(bf16)
 
-
-def rows_kernel(tiles, spill, transposed, spots, *refs):
-    value, weight, outs = refs[0], refs[1], refs[2:]
-
+    def back(owner, mine):
+        grad = dboth[...]
+        cols = drow[0].shape[1]
+        none = jnp.zeros_like(grad)
+        for j, out in enumerate(drow):
+            at = slice(j * cols, (j + 1) * cols)
+            if owner is None:
+                total = matmul_nt(jnp.where(mine, grad, none), weight[0, at, :])
+                total = total + matmul_nt(jnp.where(mine, none, grad), weight[1, at, :])
+            else:
+                total = matmul_nt(grad, weight[owner, at, :])
+            out[...] = total.astype(bf16)
+
+    per_owner(tiles, rows.shape[0], spill, back)
+
+
+def out_kernel(tiles, spill, value, weight, *outs):
     def run(owner, mine):
         rows = value[...]
-        halves = ((rows, owner),)
-        if owner is None:
-            none = jnp.zeros_like(rows)
-            halves = ((jnp.where(mine, rows, none), 0), (jnp.where(mine, none, rows), 1))
-        for out, spot in zip(outs, spots):
-            cols = slice(spot, spot + out.shape[1])
-            total = None
-            for part, who in halves:
-                if transposed:
-                    term = matmul_nt(part, weight[who, cols, :])
-                else:
-                    term = matmul(part, weight[who, :, cols])
-                total = term if total is None else total + term
+        none = jnp.zeros_like(rows)
+        for j, out in enumerate(outs):
+            at = slice(j * out.shape[1], (j + 1) * out.shape[1])
+            if owner is None:
+                total = matmul(jnp.where(mine, rows, none), weight[0, :, at])
+                total = total + matmul(jnp.where(mine, none, rows), weight[1, :, at])
+            else:
+                total = matmul(rows, weight[owner, :, at])
             out[...] = total.astype(bf16)
 
     per_owner(tiles, value.shape[0], spill, run)
@@ -492,8 +493,7 @@
     first_full, dy_sent, gateup_w, down_w, down_plain = lax.optimization_barrier(
         (first_full, dy_sent, gateup_w, down_w, down_plain)
     )
-    second_pack = jnp.concatenate([shgate_w, shup_w, shdown_w.T], 1)
-    second_full = lax.all_gather(after(second_pack, first_full), "ep", axis=0, tiled=True)
+    dy_all = lax.all_gather(after(dy_sent, first_full), "tp", axis=0, tiled=True)
     edges = [0]
     for cols in (q_cols, lat_cols, experts, kv_cols, out_cols, 128):
         edges.append(edges[-1] + cols)
@@ -549,7 +549,8 @@
     probs16 = probs.astype(bf16)
     attended = jnp.einsum("hts,shd->thd", probs16, values, preferred_element_type=f32)
     attended = attended.reshape(tok_count, head_count * DV).astype(bf16)
-    dy_all = lax.all_gather(after(dy_sent, attended), "tp", axis=0, tiled=True)
+    second_pack = jnp.concatenate([shgate_w, shup_w, shdown_w.T], 1)
+    second_full = lax.all_gather(after(second_pack, attended), "ep", axis=0, tiled=True)
     attn_sum = gather_quarters(sum_to_quarter(matmul_nt(attended, output_t)).astype(bf16))
     mid_resid = resid_in + attn_sum.astype(f32)
     mid_scale = rms_scale(mid_resid)
@@ -594,9 +595,10 @@
     second_grad = second_grads(normed2, cotangent, sh_dboth, sh_hidden)
     second_sum = lax.psum_scatter(second_grad, "ep", scatter_dimension=0, tiled=True)
 
-    first, shared_part, sh_dnormed_part, second_grad = lax.optimization_barrier(
-        (first, shared_part, sh_dnormed_part, second_grad)
-    )
+    going, shared_part, sh_dnormed_part, second_grad = lax.optimization_barrier(
+        (first[:2], shared_part, sh_dnormed_part, second_grad)
+    )
+    first = (*going, *first[2:])
     shared_q = sum_to_quarter(shared_part)
     sh_dnormed_q = sum_to_quarter(sh_dnormed_part)
     rows = ring_gather_parts(*own, first, ring_gather_second(first))
@@ -615,31 +617,17 @@
     gate_rows = jnp.sum(gate_rows, 1).reshape(owner_count, width)
     gate_rows = to_experts(exchange(after(gate_rows, two)))[:, None]
 
-    ex_hidden, ex_dboth, dgate_rows = row_call(
+    ex_hidden, ex_dboth, dgate_rows, *drow = row_call(
         functools.partial(hidden_kernel, tiles, spill),
         tile,
         slot_rows,
         (*rows, gateup_w, ex_dh, gate_rows),
         [tile_spec(tile, half)] * 8
         + [whole_spec(gateup_w.shape), tile_spec(tile, hid_wide), tile_spec(tile, 1)],
-        [(hid_wide, bf16), (2 * hid_wide, bf16), (1, f32)],
-        2 * big,
+        [(hid_wide, bf16), (2 * hid_wide, bf16), (1, f32)] + [(half, bf16)] * 8,
+        4 * big,
         [pltpu.VMEM((tile, 2 * hid_wide), f32)],
     )
-
-    def row_parts(value, weight, transposed, spots):
-        return row_call(
-            functools.partial(rows_kernel, tiles, spill, transposed, spots),
-            tile,
-            slot_rows,
-            (value, weight),
-            [tile_spec(tile, value.shape[1]), whole_spec(weight.shape)],
-            [(half, bf16)] * len(spots),
-            2 * (slot_rows + extra) * value.shape[1] * half * len(spots),
-        )
-
-    far_spots = [2 * quarter, 2 * quarter + half]
-    other_spots = [0, half, quarter, quarter + half, 3 * quarter, 3 * quarter + half]
 
     extra_iota = lax.broadcasted_iota(jnp.int32, (span, 1), 0)
     owned = (
@@ -669,24 +657,37 @@
         back_two = exchange(from_experts(two, owner_count)).reshape(slot_rows, -1)
         return jnp.concatenate([matmul_tn(pick, back_one), matmul_tn(pick, back_two)], 1)
 
-    drow_far = row_parts(ex_dboth, gateup_w, True, far_spots)
-    drow = row_parts(ex_dboth, gateup_w, True, other_spots)
-    top = shift(drow_far[0], 1)
-    bottom = shift(drow_far[1], 3)
-    from_next_one = shift(drow[4], 3)
-    dgate_rows = after(dgate_rows[:, 0], drow_far)
-    dgate_rows = exchange(from_experts(dgate_rows, owner_count)).reshape(-1)
-    top, dgate_rows = lax.optimization_barrier((top, dgate_rows))
-    next_one = plus(drow[2], top)
-    from_prev_one = shift(next_one, 1)
-    from_prev_two = shift(after(drow[3], from_prev_one), 1)
-    from_next_two = shift(plus(drow[5], bottom), 3)
+    out_parts = row_call(
+        functools.partial(out_kernel, tiles, spill),
+        tile,
+        slot_rows,
+        (ex_hidden, down_w),
+        [tile_spec(tile, hid_wide), whole_spec(down_w.shape)],
+        [(half, bf16)] * 8,
+        big,
+    )
+    top = shift(drow[4], 1)
+    bottom = shift(drow[5], 3)
+    dgate_rows = exchange(from_experts(dgate_rows[:, 0], owner_count)).reshape(-1)
+    top, bottom, dgate_rows, out_parts = lax.optimization_barrier(
+        (top, bottom, dgate_rows, out_parts)
+    )
+    from_prev_one = shift(plus(drow[2], top), 1)
+    from_next_one = shift(after(drow[6], bottom), 3)
+    next_two, prev_two = after(
+        (drow[3], plus(drow[7], bottom)), from_prev_one, from_next_one
+    )
+    from_prev_two = shift(next_two, 1)
+    from_next_two = shift(prev_two, 3)
     drow_one = add_three(drow[0], from_prev_one, from_next_one)
     drow_two = add_three(drow[1], from_prev_two, from_next_two)
     routed_grad_q = bring_back(drow_one, drow_two)
-    out_parts = row_parts(ex_hidden, down_w, False, far_spots + other_spots)
-    out_far, out_own = after(tuple(out_parts[:2]), drow_two), out_parts[2:]
-    out_first = ring_sum_first(out_far, out_own)
+    out_far = after(tuple(out_parts[4:6]), drow_two)
+    out_top = shift(out_far[0], 1)
+    out_bottom = shift(out_far[1], 3)
+    routed_grad_q, out_top, out_bottom = lax.optimization_barrier(
+        (routed_grad_q, out_top, out_bottom)
+    )
 
     dgate_part = jnp.stack(
         [jnp.sum(jnp.where(matches[k], dgate_rows[:, None], 0.0), 0) for k in range(TOPK)], 1
@@ -700,8 +701,12 @@
     dnormed2 = dnormed2 + matmul_nt(dlogits, router_full)
     dmid_norm, midnorm_grad = rms_back(mid_resid, mid_scale, mid_weight, dnormed2)
     dmid = upstream + dmid_norm
-    dmid16, out_first = lax.optimization_barrier((dmid.astype(bf16), out_first))
-    out_second = ring_sum_second(out_first, out_own)
+    dmid16 = dmid.astype(bf16)
+    out_prev_one, out_next_two = after(
+        (plus(out_parts[2], out_top), plus(out_parts[7], out_bottom)), dmid16
+    )
+    out_prev_one = shift(out_prev_one, 1)
+    out_next_two = shift(out_next_two, 3)
     dattended = matmul(dmid16, output_t).astype(bf16).reshape(tok_count, head_count, DV)
     dprobs = jnp.einsum("thd,shd->hts", dattended, values, preferred_element_type=f32)
     dscores = (probs * (dprobs - jnp.sum(probs * dprobs, -1, keepdims=True))).astype(bf16)
@@ -721,9 +726,13 @@
     )
     dlatent_part = matmul_nt(dkeyval, keyval_full)
     dkey_part = jnp.sum(dkey_all[..., DN:], 1)
-    dlat_sum = sum_small(jnp.concatenate([dlatent_part, dkey_part], 1).astype(bf16))
+    dlat_part = jnp.concatenate([dlatent_part, dkey_part], 1).astype(bf16)
+    dlat_part, out_prev_one, out_next_two = lax.optimization_barrier(
+        (dlat_part, out_prev_one, out_next_two)
+    )
+    dlat_sum = sum_small(dlat_part)
     dnormed_q = sum_to_quarter(matmul_nt(dquery, query_full))
-    dlat_sum, second_sum, out_second = lax.optimization_barrier((dlat_sum, second_sum, out_second))
+    dlat_sum, second_sum = lax.optimization_barrier((dlat_sum, second_sum))
     dlatent, latnorm_grad = rms_back(latent, lat_scale, lat_weight, dlat_sum[:, :KVR])
     dlatent_all = jnp.concatenate(
         [dlatent, rotate(dlat_sum[:, KVR:], cos_tab, -sine_tab)], -1
@@ -772,9 +781,13 @@
     )
     exgate_grad = to_lane(exgate_grad, 1)
     exup_grad = to_lane(exup_grad, 1)
-    out_one = add_three(out_own[0], *after((out_second[0], out_first[2]), first_grad, dnormed))
-    out_two = add_three(out_own[1], *after((out_first[3], out_second[1]), first_grad, dnormed))
-    routed_q = bring_back(out_one, out_two)
+    out_late = after((out_parts[6], out_parts[3]), first_grad)
+    out_next_one = shift(out_late[0], 3)
+    out_prev_two = shift(out_late[1], 1)
+    routed_q = bring_back(
+        add_three(out_parts[0], out_prev_one, out_next_one),
+        add_three(out_parts[1], out_prev_two, out_next_two),
+    )
     layer_q = (quarter_of(mid_resid, 0) + routed_q + shared_q).astype(bf16)
     layer_out = gather_quarters(layer_q)
     first_sum = lax.psum_scatter(first_grad, "ep", scatter_dimension=0, tiled=True).astype(f32)

time: 797 us -> 809 us (1.015)
  other arithmetic: 76.4 us -> 94.6 us
  Pallas kernels: 78.6 us -> 66.1 us
    all_gather x2, waiting for transfers between devices: 0.01 us -> 26.2 us  [the longest x1 26.2 us: per_device(): lax.all_gather(after(dy_sent, first_full), 'tp', axis=0, tiled=True)]
    ppermute x48, waiting for transfers between devices: 204 us -> 180 us  [shift(): lax.ppermute(value, 'tp', [(i, (i + step) % lanes) for i in range(lanes)])]
    pallas_call x5 -> x3, Pallas kernels: 63.8 us -> 51.3 us  [row_call(): pl.pallas_call(body, grid=(total // tile,), in_specs=in_specs, out_specs=...]
    unnamed x303 -> x359, local copies, waits for them, and re-layouts: 54.9 us -> 54.8 us
  transfers between devices with their start and end apart: 62 -> 62, of which waited for: 29 -> 29; matrix products, arithmetic and copies ran while one was open for 29% -> 27% of each run, Pallas kernels for 6% -> 5%
where the time goes in v3:
time: 809 us; the launch traced here: 801 us
  waiting for transfers between devices  289 us (36%)
  starting transfers between devices  129 us (16%)
  local copies, waits for them, and re-layouts  115 us (14%)
  other arithmetic  94.6 us (12%)
  matrix products  75.4 us (9%)
  Pallas kernels  66.1 us (8%)
  between operations  16.5 us (2%)
  blocking collectives  14.6 us (2%)
    ppermute x48, waiting for transfers between devices, shift(): lax.ppermute(value, 'tp', [(i, (i + step) % lanes) for i in range(lanes)])  180 us
    ppermute x48, starting transfers between devices, shift(): lax.ppermute(value, 'tp', [(i, (i + step) % lanes) for i in range(lanes)])  72.2 us
    all_to_all x9, waiting for transfers between devices, exchange(): return lax.all_to_all(value, 'ep', 0, 0, tiled=True)  57.2 us
    all_to_all x9, starting transfers between devices, exchange(): return lax.all_to_all(value, 'ep', 0, 0, tiled=True)  56.3 us
    unnamed x359, local copies, waits for them, and re-layouts  54.8 us
    pallas_call x3, Pallas kernels, row_call(): pl.pallas_call(body, grid=(total // tile,), in_specs=in_specs, out_specs=...  51.3 us
    all_gather x1, waiting for transfers between devices, per_device(): lax.all_gather(after(dy_sent, first_full), 'tp', axis=0, tiled=True)  26.2 us
    all_gather x1, waiting for transfers between devices, per_device(): first_full = lax.all_gather(first_pack, 'ep', axis=0, tiled=True)  24.8 us
  transfers between devices with their start and end apart: 62, of which 29 were waited for; matrix products, arithmetic and copies ran while one was open for 27% of the time, Pallas kernels for 5%

profile of v3, /device:TPU:0, one launch (start us, length us, event | category | flops | bytes accessed | tf_op | source)
XLA Modules:
  0.0 800.6 jit_solution(10473289998664604198)
XLA Ops:
  12.1 4.1 convolution_convert_fusion.1
  16.3 7.7 all-to-all-start
  24.3 3.6 constant_dynamic-slice_fusion.31
  64.8 24.8 %all-gather.4.cloned.1.call-done = bf16[2048,2304]{1,0:T(8,128)(2,1)} async-done(((bf16[64,2304]{1,0:T(8,128)(2,1)}), bf16[2048,2304]{1,0:T(8,128)(2,1)}) %all-gather.4.cloned.1.call-update) | async-done | bytes 9437200 | tf_op jit(solution)/shard_map/all_gather | solution.py:439
  93.2 3.6 fusion.74
  96.8 3.5 fusion.62
  137.6 5.4 collective-permute-done.2
  151.6 5.2 collective-permute-done.4
  163.0 5.6 all-to-all-start.1
  170.7 21.9 %all-to-all-done.1 = bf16[32,72,256]{2,1,0:T(8,128)(2,1)} async-done(((bf16[32,72,256]{2,1,0:T(8,128)(2,1)}), bf16[32,72,256]{2,1,0:T(8,128)(2,1)}, u32[]{:S(2)}, u32[]{:S(2)}) %all-to-all-start.1) | async-done | bytes 1179680 | tf_op jit(solution)/shard_map/all_to_all | solution.py:119
  192.7 4.7 all-to-all-start.2
  204.5 11.1 %all-to-all-done.2 = bf16[32,72,256]{2,1,0:T(8,128)(2,1)} async-done(((bf16[32,72,256]{2,1,0:T(8,128)(2,1)}), bf16[32,72,256]{2,1,0:T(8,128)(2,1)}, u32[]{:S(2)}, u32[]{:S(2)}) %all-to-all-start.2) | async-done | bytes 1179680 | tf_op jit(solution)/shard_map/all_to_all | solution.py:119
  222.2 4.4 fusion.19
  230.2 6.8 shard_map.306
  237.8 4.2 fusion.67
  242.0 5.6 fusion.70
  247.7 5.3 collective-permute-done.7.refs_6_
  252.9 50.8 %collective-permute-done.8.refs_3_ = bf16[2304,256]{1,0:T(8,128)(2,1)} collective-permute-done((bf16[2304,256]{1,0:T(8,128)(2,1)}, bf16[2304,256]{1,0:T(8,128)(2,1)}, u32[]{:S(2)}, u32[]{:S(2)}) %collective-permute-start.8) | collective-permute-done | bytes 1179680 | tf_op jit(solution)/shard_map/ppermute | solution.py:78
  303.7 3.7 collective-permute-start.10
  310.2 14.6 %all_to_all.65 = f32[32,1,72]{2,1,0:T(1,128)S(1)} all-to-all(f32[32,1,72]{2,1,0:T(1,128)} %bitcast.175), channel_id=1, replica_groups=mesh['ep'=32,'tp'=4] {'ep'}, dimensions={0} | all-to-all | bytes 18432 | tf_op jit(solution)/shard_map/all_to_all | solution.py:119
  331.3 26.2 %all-gather.8.cloned.1.call-done.refs_0_.refs_1_.refs_2_.refs_3_ = bf16[9216,512]{1,0:T(8,128)(2,1)} async-done(((bf16[2304,512]{1,0:T(8,128)(2,1)}), bf16[9216,512]{1,0:T(8,128)(2,1)}) %all-gather.8.cloned.1.call-update) | async-done | bytes 9437200 | tf_op jit(solution)/shard_map/all_gather | solution.py:496
  357.5 10.7 %shard_map.307.refs_9_ = f32[2304,384]{1,0:T(8,128)S(1)} custom-call(bf16[9216,512]{1,0:T(8,128)(2,1)} %all-gather.8.cloned.1.call-done.refs_0_.refs_1_.refs_2_.refs_3_, bf16[9216,512]{1,0:T(8,128)(2,1)} %all-gather.8.cloned.1.call-done.refs_0_.refs_1_.refs_2_.refs_3_, bf16[9216,512]{1,0:T(8,128)(2,1)} %all-gather.8.cloned.1.call-done.refs_0_.refs_1_.refs_2_.refs_3_, ...), custom_call_target="tpu_custom_call" | custom-call | flops 4026531840 | bytes 44433408 | tf_op jit(solution)/shard_map/pallas_call | solution.py:278
  370.1 29.3 %shard_map.308 = (bf16[2304,384]{1,0:T(8,128)(2,1)}, bf16[2304,768]{1,0:T(8,128)(2,1)}, f32[2304,1]{1,0:T(8,128)S(1)}, bf16[2304,256]{1,0:T(8,128)(2,1)S(1)}, bf...) custom-call(bf16[2304,256]{1,0:T(8,128)(2,1)} %pad_maximum_fusion.6., ...), custom_call_target="tpu_custom_call" | custom-call | flops 16106127360 | bytes 34031616 | tf_op jit(solution)/shard_map/pallas_call | solution.py:278
  409.3 7.4 all-to-all-start.4
  416.7 11.3 %shard_map.309 = (bf16[2304,256]{1,0:T(8,128)(2,1)S(1)}, bf16[2304,256]{1,0:T(8,128)(2,1)S(1)}, bf16[2304,256]{1,0:T(8,128)(2,1)S(1)}, bf16[2304,256]{1,0:T(8,12...) custom-call(bf16[2304,384]{1,0:T(8,128)(2,1)} %get-tuple-element.106, ...), custom_call_target="tpu_custom_call" | custom-call | flops 4026531840 | bytes 14352384 | tf_op jit(solution)/shard_map/pallas_call | solution.py:278
  441.0 4.1 collective-permute-start.22
  450.3 13.3 %collective-permute-done.15 = bf16[2304,256]{1,0:T(8,128)(2,1)} collective-permute-done((bf16[2304,256]{1,0:T(8,128)(2,1)}, bf16[2304,256]{1,0:T(8,128)(2,1)}, u32[]{:S(2)}, u32[]{:S(2)}) %collective-permute-start.15) | collective-permute-done | bytes 1179680 | tf_op jit(solution)/shard_map/ppermute | solution.py:78
  463.6 6.3 collective-permute-done.14
  476.6 7.4 all-to-all-start.5
  484.1 18.1 %collective-permute-done.16 = bf16[2304,256]{1,0:T(8,128)(2,1)} collective-permute-done((bf16[2304,256]{1,0:T(8,128)(2,1)}, bf16[2304,256]{1,0:T(8,128)(2,1)}, u32[]{:S(2)}, u32[]{:S(2)}) %collective-permute-start.16) | collective-permute-done | bytes 1179680 | tf_op jit(solution)/shard_map/ppermute | solution.py:78
  507.9 7.5 all-to-all-start.6
  525.4 8.4 %all-to-all-done.6 = bf16[32,72,256]{2,1,0:T(8,128)(2,1)} async-done(((bf16[32,72,256]{2,1,0:T(8,128)(2,1)}), bf16[32,72,256]{2,1,0:T(8,128)(2,1)}, u32[]{:S(2)}, u32[]{:S(2)}) %all-to-all-start.6) | async-done | bytes 1179680 | tf_op jit(solution)/shard_map/all_to_all | solution.py:119
  536.6 11.2 %collective-permute-done.18 = bf16[2304,256]{1,0:T(8,128)(2,1)} collective-permute-done((bf16[2304,256]{1,0:T(8,128)(2,1)}, bf16[2304,256]{1,0:T(8,128)(2,1)}, u32[]{:S(2)}, u32[]{:S(2)}) %collective-permute-start.18) | collective-permute-done | bytes 1179680 | tf_op jit(solution)/shard_map/ppermute | solution.py:78
  550.4 4.0 collective-permute-start.24
  557.6 5.9 collective-permute-done.25
  574.9 20.2 %collective-permute-done.29 = bf16[2304,256]{1,0:T(8,128)(2,1)S(1)} collective-permute-done((bf16[2304,256]{1,0:T(8,128)(2,1)S(1)}, bf16[2304,256]{1,0:T(8,128)(2,1)S(1)}, u32[]{:S(2)}, u32[]{:S(2)}) %collective-permute-start.29) | collective-permute-done | bytes 1179680 | tf_op jit(solution)/shard_map/ppermute | solution.py:78
  602.0 3.6 collective-permute-done.33
  620.6 4.1 fusion.64
  624.7 7.9 shard_map.310
  694.7 7.5 collective-permute-done.47
  712.5 7.3 all-to-all-start.7
  719.8 12.4 %collective-permute-done.35 = bf16[2304,256]{1,0:T(8,128)(2,1)} collective-permute-done((bf16[2304,256]{1,0:T(8,128)(2,1)S(1)}, bf16[2304,256]{1,0:T(8,128)(2,1)}, u32[]{:S(2)}, u32[]{:S(2)}) %collective-permute-start.35) | collective-permute-done | bytes 1179680 | tf_op jit(solution)/shard_map/ppermute | solution.py:78
  735.6 4.7 all-to-all-done.7
  740.3 4.8 all-to-all-start.8
  745.9 3.9 fusion.91
  752.5 11.0 %all-to-all-done.8 = bf16[32,72,256]{2,1,0:T(8,128)(2,1)} async-done(((bf16[32,72,256]{2,1,0:T(8,128)(2,1)}), bf16[32,72,256]{2,1,0:T(8,128)(2,1)}, u32[]{:S(2)}, u32[]{:S(2)}) %all-to-all-start.8) | async-done | bytes 1179680 | tf_op jit(solution)/shard_map/all_to_all | solution.py:119
  763.5 3.8 all-to-all-start.9
  780.3 4.0 collective-permute-done.40
  (658 shorter events, 320.9 us)
Async XLA Ops:
  7.2 82.4 %all-gather.4.cloned.1.call-start = ((), (), s32[]{:S(2)}) async-start(), calls=%async_computation.12 | async-start | bytes 9732096 | tf_op jit(solution)/shard_map/all_gather | solution.py:439
  16.3 44.2 %all-to-all-start = ((bf16[32,72,512]{2,1,0:T(8,128)(2,1)}), bf16[32,72,512]{2,1,0:T(8,128)(2,1)}, u32[]{:S(2)}, u32[]{:S(2)}) async-start(bf16[32,72,512]{2,1,0:T(8,128)(2,1)} %bitcast.12), calls=%async_computation | async-start | bytes 4718592 | tf_op jit(solution)/shard_map/all_to_all | solution.py:119
  23.9 198.3 %all-gather.6.cloned.1.call-start = ((), (), s32[]{:S(2)}) async-start(), calls=%async_computation.13 | async-start | bytes 9191424 | tf_op jit(solution)/shard_map/all_gather | solution.py:553
  125.9 231.6 %all-gather.8.cloned.1.call-start = ((), (), s32[]{:S(2)}) async-start(), calls=%async_computation.14 | async-start | bytes 11796480 | tf_op jit(solution)/shard_map/all_gather | solution.py:496
  130.9 12.1 %collective-permute-start.2 = (bf16[192,512]{1,0:T(8,128)(2,1)S(1)}, bf16[192,512]{1,0:T(8,128)(2,1)S(1)}, u32[]{:S(2)}, u32[]{:S(2)}) collective-permute-start(bf16[192,512]{1,0:T(8,128)(2,1)S(1)} %get-tuple-element.257), channel_id=1, source_target_pairs={{0,2},{1,3},{2,0},{3,1},{4,6},{5,7},{6,4},{7,5},{8,10},{9,11},{10,... | collective-permute-start | bytes 589832 | tf_op jit(solution)/shard_map/ppermute | solution.py:78
  163.0 29.6 %all-to-all-start.1 = ((bf16[32,72,256]{2,1,0:T(8,128)(2,1)}), bf16[32,72,256]{2,1,0:T(8,128)(2,1)}, u32[]{:S(2)}, u32[]{:S(2)}) async-start(bf16[32,72,256]{2,1,0:T(8,128)(2,1)} %get-tuple-element.207), calls=%async_computation.1 | async-start | bytes 2359296 | tf_op jit(solution)/shard_map/all_to_all | solution.py:119
  192.7 23.0 %all-to-all-start.2 = ((bf16[32,72,256]{2,1,0:T(8,128)(2,1)}), bf16[32,72,256]{2,1,0:T(8,128)(2,1)}, u32[]{:S(2)}, u32[]{:S(2)}) async-start(bf16[32,72,256]{2,1,0:T(8,128)(2,1)} %get-tuple-element.91), calls=%async_computation.2 | async-start | bytes 2359296 | tf_op jit(solution)/shard_map/all_to_all | solution.py:119
  197.3 412.3 %reduce-scatter.3.cloned.1.call-start = ((), (), s32[]{:S(2)}) async-start(), calls=%async_computation.15 | async-start | bytes 9191424 | tf_op jit(solution)/shard_map/reduce_scatter | solution.py:596
  201.3 51.6 %collective-permute-start.7 = (bf16[2304,256]{1,0:T(8,128)(2,1)}, bf16[2304,256]{1,0:T(8,128)(2,1)}, u32[]{:S(2)}, u32[]{:S(2)}) collective-permute-start(bf16[2304,256]{1,0:T(8,128)(2,1)} %pad_maximum_fusion.6.refs_0_), channel_id=1, source_target_pairs={{0,1},{1,2},{2,3},{3,0},{4,5},{5,6},{6,7},{7,4},{8,9},{9,10},{10,1... | collective-permute-start | bytes 3538952 | tf_op jit(solution)/shard_map/ppermute | solution.py:78
  202.8 167.2 %collective-permute-start.6 = (bf16[2304,256]{1,0:T(8,128)(2,1)}, bf16[2304,256]{1,0:T(8,128)(2,1)}, u32[]{:S(2)}, u32[]{:S(2)}) collective-permute-start(bf16[2304,256]{1,0:T(8,128)(2,1)} %pad_maximum_fusion.6.refs_0_), channel_id=1, source_target_pairs={{0,3},{1,0},{2,1},{3,2},{4,7},{5,4},{6,5},{7,6},{8,11},{9,8},{10,9... | collective-permute-start | bytes 3538952 | tf_op jit(solution)/shard_map/ppermute | solution.py:78
  218.9 151.1 %collective-permute-start.11 = (bf16[2304,256]{1,0:T(8,128)(2,1)}, bf16[2304,256]{1,0:T(8,128)(2,1)}, u32[]{:S(2)}, u32[]{:S(2)}) collective-permute-start(bf16[2304,256]{1,0:T(8,128)(2,1)} %pad_maximum_fusion.7.refs_1_), channel_id=1, source_target_pairs={{0,1},{1,2},{2,3},{3,0},{4,5},{5,6},{6,7},{7,4},{8,9},{9,10},{10,1... | collective-permute-start | bytes 3538952 | tf_op jit(solution)/shard_map/ppermute | solution.py:78
  220.5 83.2 %collective-permute-start.8 = (bf16[2304,256]{1,0:T(8,128)(2,1)}, bf16[2304,256]{1,0:T(8,128)(2,1)}, u32[]{:S(2)}, u32[]{:S(2)}) collective-permute-start(bf16[2304,256]{1,0:T(8,128)(2,1)} %pad_maximum_fusion.7.refs_1_), channel_id=1, source_target_pairs={{0,3},{1,0},{2,1},{3,2},{4,7},{5,4},{6,5},{7,6},{8,11},{9,8},{10,9... | collective-permute-start | bytes 3538952 | tf_op jit(solution)/shard_map/ppermute | solution.py:78
  303.7 66.3 %collective-permute-start.10 = (bf16[2304,256]{1,0:T(8,128)(2,1)}, bf16[2304,256]{1,0:T(8,128)(2,1)}, u32[]{:S(2)}, u32[]{:S(2)}) collective-permute-start(bf16[2304,256]{1,0:T(8,128)(2,1)} %collective-permute-done.8.refs_3_), channel_id=1, source_target_pairs={{0,3},{1,0},{2,1},{3,2},{4,7},{5,4},{6,5},{7,6},{8,11},{9,8},{10,9... | collective-permute-start | bytes 3538952 | tf_op jit(solution)/shard_map/ppermute | solution.py:78
  307.4 62.6 %collective-permute-start.9 = (bf16[2304,256]{1,0:T(8,128)(2,1)}, bf16[2304,256]{1,0:T(8,128)(2,1)}, u32[]{:S(2)}, u32[]{:S(2)}) collective-permute-start(bf16[2304,256]{1,0:T(8,128)(2,1)} %collective-permute-done.7.refs_6_), channel_id=1, source_target_pairs={{0,1},{1,2},{2,3},{3,0},{4,5},{5,6},{6,7},{7,4},{8,9},{9,10},{10,1... | collective-permute-start | bytes 3538952 | tf_op jit(solution)/shard_map/ppermute | solution.py:78
  403.5 30.9 %collective-permute-start.12 = (bf16[2304,256]{1,0:T(8,128)(2,1)}, bf16[2304,256]{1,0:T(8,128)(2,1)}, u32[]{:S(2)}, u32[]{:S(2)}) collective-permute-start(bf16[2304,256]{1,0:T(8,128)(2,1)} %get-tuple-element.103), channel_id=1, source_target_pairs={{0,1},{1,2},{2,3},{3,0},{4,5},{5,6},{6,7},{7,4},{8,9},{9,10},{10,1... | collective-permute-start | bytes 3538952 | tf_op jit(solution)/shard_map/ppermute | solution.py:78
  404.7 29.7 %collective-permute-start.13 = (bf16[2304,256]{1,0:T(8,128)(2,1)}, bf16[2304,256]{1,0:T(8,128)(2,1)}, u32[]{:S(2)}, u32[]{:S(2)}) collective-permute-start(bf16[2304,256]{1,0:T(8,128)(2,1)} %get-tuple-element.104), channel_id=1, source_target_pairs={{0,3},{1,0},{2,1},{3,2},{4,7},{5,4},{6,5},{7,6},{8,11},{9,8},{10,9... | collective-permute-start | bytes 3538952 | tf_op jit(solution)/shard_map/ppermute | solution.py:78
  409.3 23.8 %all-to-all-start.4 = ((f32[32,1,72]{2,1,0:T(1,128)}), f32[32,1,72]{2,1,0:T(1,128)S(1)}, u32[]{:S(2)}, u32[]{:S(2)}) async-start(f32[32,1,72]{2,1,0:T(1,128)} %bitcast.37), calls=%async_computation.4 | async-start | bytes 32768 | tf_op jit(solution)/shard_map/all_to_all | solution.py:119
  434.4 29.2 %collective-permute-start.15 = (bf16[2304,256]{1,0:T(8,128)(2,1)}, bf16[2304,256]{1,0:T(8,128)(2,1)}, u32[]{:S(2)}, u32[]{:S(2)}) collective-permute-start(bf16[2304,256]{1,0:T(8,128)(2,1)} %copy-done.23), channel_id=1, source_target_pairs={{0,3},{1,0},{2,1},{3,2},{4,7},{5,4},{6,5},{7,6},{8,11},{9,8},{10,9... | collective-permute-start | bytes 3538952 | tf_op jit(solution)/shard_map/ppermute | solution.py:78
  439.1 30.8 %collective-permute-start.14 = (bf16[2304,256]{1,0:T(8,128)(2,1)}, bf16[2304,256]{1,0:T(8,128)(2,1)}, u32[]{:S(2)}, u32[]{:S(2)}) collective-permute-start(bf16[2304,256]{1,0:T(8,128)(2,1)} %add_convert_fusion.7), channel_id=1, source_target_pairs={{0,1},{1,2},{2,3},{3,0},{4,5},{5,6},{6,7},{7,4},{8,9},{9,10},{10,1... | collective-permute-start | bytes 3538952 | tf_op jit(solution)/shard_map/ppermute | solution.py:78
  440.9 108.1 %collective-permute-start.20 = (bf16[192,512]{1,0:T(8,128)(2,1)}, bf16[192,512]{1,0:T(8,128)(2,1)}, u32[]{:S(2)}, u32[]{:S(2)}) collective-permute-start(bf16[192,512]{1,0:T(8,128)(2,1)} %get-tuple-element.249), channel_id=1, source_target_pairs={{0,1},{1,2},{2,3},{3,0},{4,5},{5,6},{6,7},{7,4},{8,9},{9,10},{10,1... | collective-permute-start | bytes 589832 | tf_op jit(solution)/shard_map/ppermute | solution.py:78
  441.0 108.0 %collective-permute-start.22 = (bf16[192,512]{1,0:T(8,128)(2,1)}, bf16[192,512]{1,0:T(8,128)(2,1)}, u32[]{:S(2)}, u32[]{:S(2)}) collective-permute-start(bf16[192,512]{1,0:T(8,128)(2,1)} %get-tuple-element.250), channel_id=1, source_target_pairs={{0,2},{1,3},{2,0},{3,1},{4,6},{5,7},{6,4},{7,5},{8,10},{9,11},{10,... | collective-permute-start | bytes 589832 | tf_op jit(solution)/shard_map/ppermute | solution.py:78
  447.2 69.2 %collective-permute-start.28 = (f32[192,6]{0,1:T(8,128)}, f32[192,6]{0,1:T(8,128)}, u32[]{:S(2)}, u32[]{:S(2)}) collective-permute-start(f32[192,6]{0,1:T(8,128)} %stack.78), channel_id=1, source_target_pairs={{0,2},{1,3},{2,0},{3,1},{4,6},{5,7},{6,4},{7,5},{8,10},{9,11},{10,... | collective-permute-start | bytes 13832 | tf_op jit(solution)/shard_map/ppermute | solution.py:78
  469.9 32.3 %collective-permute-start.16 = (bf16[2304,256]{1,0:T(8,128)(2,1)}, bf16[2304,256]{1,0:T(8,128)(2,1)}, u32[]{:S(2)}, u32[]{:S(2)}) collective-permute-start(bf16[2304,256]{1,0:T(8,128)(2,1)} %get-tuple-element.126), channel_id=1, source_target_pairs={{0,1},{1,2},{2,3},{3,0},{4,5},{5,6},{6,7},{7,4},{8,9},{9,10},{10,1... | collective-permute-start | bytes 3538952 | tf_op jit(solution)/shard_map/ppermute | solution.py:78
  469.9 32.3 %collective-permute-start.17 = (bf16[2304,256]{1,0:T(8,128)(2,1)}, bf16[2304,256]{1,0:T(8,128)(2,1)}, u32[]{:S(2)}, u32[]{:S(2)}) collective-permute-start(bf16[2304,256]{1,0:T(8,128)(2,1)} %add_convert_fusion.5), channel_id=1, source_target_pairs={{0,3},{1,0},{2,1},{3,2},{4,7},{5,4},{6,5},{7,6},{8,11},{9,8},{10,9... | collective-permute-start | bytes 3538952 | tf_op jit(solution)/shard_map/ppermute | solution.py:78
  476.6 31.3 %all-to-all-start.5 = ((bf16[32,72,256]{2,1,0:T(8,128)(2,1)}), bf16[32,72,256]{2,1,0:T(8,128)(2,1)}, u32[]{:S(2)}, u32[]{:S(2)}) async-start(bf16[32,72,256]{2,1,0:T(8,128)(2,1)} %pad_maximum_fusion.8), calls=%async_computation.5 | async-start | bytes 2359296 | tf_op jit(solution)/shard_map/all_to_all | solution.py:119
  502.2 15.4 %collective-permute-start.27 = (f32[192,6]{0,1:T(8,128)}, f32[192,6]{0,1:T(8,128)}, u32[]{:S(2)}, u32[]{:S(2)}) collective-permute-start(f32[192,6]{0,1:T(8,128)} %stack.78), channel_id=1, source_target_pairs={{0,3},{1,0},{2,1},{3,2},{4,7},{5,4},{6,5},{7,6},{8,11},{9,8},{10,9... | collective-permute-start | bytes 13832 | tf_op jit(solution)/shard_map/ppermute | solution.py:78
  502.2 15.4 %collective-permute-start.26 = (f32[192,6]{0,1:T(8,128)}, f32[192,6]{0,1:T(8,128)}, u32[]{:S(2)}, u32[]{:S(2)}) collective-permute-start(f32[192,6]{0,1:T(8,128)} %stack.78), channel_id=1, source_target_pairs={{0,1},{1,2},{2,3},{3,0},{4,5},{5,6},{6,7},{7,4},{8,9},{9,10},{10,1... | collective-permute-start | bytes 13832 | tf_op jit(solution)/shard_map/ppermute | solution.py:78
  507.9 25.9 %all-to-all-start.6 = ((bf16[32,72,256]{2,1,0:T(8,128)(2,1)}), bf16[32,72,256]{2,1,0:T(8,128)(2,1)}, u32[]{:S(2)}, u32[]{:S(2)}) async-start(bf16[32,72,256]{2,1,0:T(8,128)(2,1)} %pad_maximum_fusion.9), calls=%async_computation.6 | async-start | bytes 2359296 | tf_op jit(solution)/shard_map/all_to_all | solution.py:119
  515.4 270.3 %reduce-scatter.5.cloned.1.call-start = ((), (), s32[]{:S(2)}) async-start(), calls=%async_computation.16 | async-start | bytes 9732096 | tf_op jit(solution)/shard_map/reduce_scatter | solution.py:793
  516.4 32.6 %collective-permute-start.21 = (bf16[192,512]{1,0:T(8,128)(2,1)}, bf16[192,512]{1,0:T(8,128)(2,1)S(1)}, u32[]{:S(2)}, u32[]{:S(2)}) collective-permute-start(bf16[192,512]{1,0:T(8,128)(2,1)} %get-tuple-element.251), channel_id=1, source_target_pairs={{0,3},{1,0},{2,1},{3,2},{4,7},{5,4},{6,5},{7,6},{8,11},{9,8},{10,9... | collective-permute-start | bytes 589832 | tf_op jit(solution)/shard_map/ppermute | solution.py:78
  518.4 29.4 %collective-permute-start.18 = (bf16[2304,256]{1,0:T(8,128)(2,1)}, bf16[2304,256]{1,0:T(8,128)(2,1)}, u32[]{:S(2)}, u32[]{:S(2)}) collective-permute-start(bf16[2304,256]{1,0:T(8,128)(2,1)} %copy-done.22), channel_id=1, source_target_pairs={{0,1},{1,2},{2,3},{3,0},{4,5},{5,6},{6,7},{7,4},{8,9},{9,10},{10,1... | collective-permute-start | bytes 3538952 | tf_op jit(solution)/shard_map/ppermute | solution.py:78
  519.3 29.7 %collective-permute-start.19 = (bf16[2304,256]{1,0:T(8,128)(2,1)}, bf16[2304,256]{1,0:T(8,128)(2,1)}, u32[]{:S(2)}, u32[]{:S(2)}) collective-permute-start(bf16[2304,256]{1,0:T(8,128)(2,1)} %copy-done.21), channel_id=1, source_target_pairs={{0,3},{1,0},{2,1},{3,2},{4,7},{5,4},{6,5},{7,6},{8,11},{9,8},{10,9... | collective-permute-start | bytes 3538952 | tf_op jit(solution)/shard_map/ppermute | solution.py:78
  547.8 222.3 %collective-permute-start.36 = (bf16[192,512]{1,0:T(8,128)(2,1)}, bf16[192,512]{1,0:T(8,128)(2,1)}, u32[]{:S(2)}, u32[]{:S(2)}) collective-permute-start(bf16[192,512]{1,0:T(8,128)(2,1)} %get-tuple-element.242), channel_id=1, source_target_pairs={{0,1},{1,2},{2,3},{3,0},{4,5},{5,6},{6,7},{7,4},{8,9},{9,10},{10,1... | collective-permute-start | bytes 589832 | tf_op jit(solution)/shard_map/ppermute | solution.py:78
  550.3 13.2 %collective-permute-start.25 = (bf16[192,512]{1,0:T(8,128)(2,1)S(1)}, bf16[192,512]{1,0:T(8,128)(2,1)S(1)}, u32[]{:S(2)}, u32[]{:S(2)}) collective-permute-start(bf16[192,512]{1,0:T(8,128)(2,1)S(1)} %add_convert_fusion.10), channel_id=1, source_target_pairs={{0,1},{1,2},{2,3},{3,0},{4,5},{5,6},{6,7},{7,4},{8,9},{9,10},{10,1... | collective-permute-start | bytes 589832 | tf_op jit(solution)/shard_map/ppermute | solution.py:78
  550.4 13.1 %collective-permute-start.24 = (bf16[192,512]{1,0:T(8,128)(2,1)S(1)}, bf16[192,512]{1,0:T(8,128)(2,1)S(1)}, u32[]{:S(2)}, u32[]{:S(2)}) collective-permute-start(bf16[192,512]{1,0:T(8,128)(2,1)S(1)} %add_convert_fusion.10), channel_id=1, source_target_pairs={{0,2},{1,3},{2,0},{3,1},{4,6},{5,7},{6,4},{7,5},{8,10},{9,11},{10,... | collective-permute-start | bytes 589832 | tf_op jit(solution)/shard_map/ppermute | solution.py:78
  567.0 28.1 %collective-permute-start.29 = (bf16[2304,256]{1,0:T(8,128)(2,1)S(1)}, bf16[2304,256]{1,0:T(8,128)(2,1)S(1)}, u32[]{:S(2)}, u32[]{:S(2)}) collective-permute-start(bf16[2304,256]{1,0:T(8,128)(2,1)S(1)} %add_convert_fusion.3), channel_id=1, source_target_pairs={{0,1},{1,2},{2,3},{3,0},{4,5},{5,6},{6,7},{7,4},{8,9},{9,10},{10,1... | collective-permute-start | bytes 3538952 | tf_op jit(solution)/shard_map/ppermute | solution.py:78
  567.1 28.0 %collective-permute-start.30 = (bf16[2304,256]{1,0:T(8,128)(2,1)S(1)}, bf16[2304,256]{1,0:T(8,128)(2,1)S(1)}, u32[]{:S(2)}, u32[]{:S(2)}) collective-permute-start(bf16[2304,256]{1,0:T(8,128)(2,1)S(1)} %add_convert_fusion.2), channel_id=1, source_target_pairs={{0,3},{1,0},{2,1},{3,2},{4,7},{5,4},{6,5},{7,6},{8,11},{9,8},{10,9... | collective-permute-start | bytes 3538952 | tf_op jit(solution)/shard_map/ppermute | solution.py:78
  635.1 51.8 %collective-permute-start.42 = (bf16[192,512]{1,0:T(8,128)(2,1)}, bf16[192,512]{1,0:T(8,128)(2,1)S(1)}, u32[]{:S(2)}, u32[]{:S(2)}) collective-permute-start(bf16[192,512]{1,0:T(8,128)(2,1)} %get-tuple-element.235), channel_id=1, source_target_pairs={{0,1},{1,2},{2,3},{3,0},{4,5},{5,6},{6,7},{7,4},{8,9},{9,10},{10,1... | collective-permute-start | bytes 589832 | tf_op jit(solution)/shard_map/ppermute | solution.py:78
  636.5 50.5 %collective-permute-start.44 = (bf16[192,512]{1,0:T(8,128)(2,1)}, bf16[192,512]{1,0:T(8,128)(2,1)}, u32[]{:S(2)}, u32[]{:S(2)}) collective-permute-start(bf16[192,512]{1,0:T(8,128)(2,1)} %get-tuple-element.236), channel_id=1, source_target_pairs={{0,2},{1,3},{2,0},{3,1},{4,6},{5,7},{6,4},{7,5},{8,10},{9,11},{10,... | collective-permute-start | bytes 589832 | tf_op jit(solution)/shard_map/ppermute | solution.py:78
  638.6 48.3 %collective-permute-start.43 = (bf16[192,512]{1,0:T(8,128)(2,1)S(1)}, bf16[192,512]{1,0:T(8,128)(2,1)}, u32[]{:S(2)}, u32[]{:S(2)}) collective-permute-start(bf16[192,512]{1,0:T(8,128)(2,1)S(1)} %get-tuple-element.237), channel_id=1, source_target_pairs={{0,3},{1,0},{2,1},{3,2},{4,7},{5,4},{6,5},{7,6},{8,11},{9,8},{10,9... | collective-permute-start | bytes 589832 | tf_op jit(solution)/shard_map/ppermute | solution.py:78
  640.6 68.7 %collective-permute-start.34 = (bf16[2304,256]{1,0:T(8,128)(2,1)}, bf16[2304,256]{1,0:T(8,128)(2,1)}, u32[]{:S(2)}, u32[]{:S(2)}) collective-permute-start(bf16[2304,256]{1,0:T(8,128)(2,1)} %get-tuple-element.146), channel_id=1, source_target_pairs={{0,3},{1,0},{2,1},{3,2},{4,7},{5,4},{6,5},{7,6},{8,11},{9,8},{10,9... | collective-permute-start | bytes 3538952 | tf_op jit(solution)/shard_map/ppermute | solution.py:78
  689.0 13.2 %collective-permute-start.47 = (bf16[192,512]{1,0:T(8,128)(2,1)S(1)}, bf16[192,512]{1,0:T(8,128)(2,1)S(1)}, u32[]{:S(2)}, u32[]{:S(2)}) collective-permute-start(bf16[192,512]{1,0:T(8,128)(2,1)S(1)} %add_convert_fusion.8), channel_id=1, source_target_pairs={{0,1},{1,2},{2,3},{3,0},{4,5},{5,6},{6,7},{7,4},{8,9},{9,10},{10,1... | collective-permute-start | bytes 589832 | tf_op jit(solution)/shard_map/ppermute | solution.py:78
  702.2 67.9 %collective-permute-start.38 = (bf16[192,512]{1,0:T(8,128)(2,1)}, bf16[192,512]{1,0:T(8,128)(2,1)}, u32[]{:S(2)}, u32[]{:S(2)}) collective-permute-start(bf16[192,512]{1,0:T(8,128)(2,1)} %get-tuple-element.243), channel_id=1, source_target_pairs={{0,2},{1,3},{2,0},{3,1},{4,6},{5,7},{6,4},{7,5},{8,10},{9,11},{10,... | collective-permute-start | bytes 589832 | tf_op jit(solution)/shard_map/ppermute | solution.py:78
  702.2 67.9 %collective-permute-start.37 = (bf16[192,512]{1,0:T(8,128)(2,1)}, bf16[192,512]{1,0:T(8,128)(2,1)}, u32[]{:S(2)}, u32[]{:S(2)}) collective-permute-start(bf16[192,512]{1,0:T(8,128)(2,1)} %get-tuple-element.244), channel_id=1, source_target_pairs={{0,3},{1,0},{2,1},{3,2},{4,7},{5,4},{6,5},{7,6},{8,11},{9,8},{10,9... | collective-permute-start | bytes 589832 | tf_op jit(solution)/shard_map/ppermute | solution.py:78
  703.2 29.1 %collective-permute-start.35 = (bf16[2304,256]{1,0:T(8,128)(2,1)S(1)}, bf16[2304,256]{1,0:T(8,128)(2,1)}, u32[]{:S(2)}, u32[]{:S(2)}) collective-permute-start(bf16[2304,256]{1,0:T(8,128)(2,1)S(1)} %copy-done.20), channel_id=1, source_target_pairs={{0,1},{1,2},{2,3},{3,0},{4,5},{5,6},{6,7},{7,4},{8,9},{9,10},{10,1... | collective-permute-start | bytes 3538952 | tf_op jit(solution)/shard_map/ppermute | solution.py:78
  712.5 27.8 %all-to-all-start.7 = ((bf16[32,72,256]{2,1,0:T(8,128)(2,1)}), bf16[32,72,256]{2,1,0:T(8,128)(2,1)}, u32[]{:S(2)}, u32[]{:S(2)}) async-start(bf16[32,72,256]{2,1,0:T(8,128)(2,1)} %pad_maximum_fusion.10), calls=%async_computation.8 | async-start | bytes 2359296 | tf_op jit(solution)/shard_map/all_to_all | solution.py:119
  740.3 23.3 %all-to-all-start.8 = ((bf16[32,72,256]{2,1,0:T(8,128)(2,1)}), bf16[32,72,256]{2,1,0:T(8,128)(2,1)}, u32[]{:S(2)}, u32[]{:S(2)}) async-start(bf16[32,72,256]{2,1,0:T(8,128)(2,1)} %pad_maximum_fusion.11), calls=%async_computation.9 | async-start | bytes 2359296 | tf_op jit(solution)/shard_map/all_to_all | solution.py:119
  763.5 15.2 %all-to-all-start.9 = ((f32[32,1,64]{2,1,0:T(1,128)}), f32[32,1,64]{2,1,0:T(1,128)S(1)}, u32[]{:S(2)}, u32[]{:S(2)}) async-start(f32[32,1,64]{2,1,0:T(1,128)} %all_to_all.53), calls=%async_computation.10 | async-start | bytes 32768 | tf_op jit(solution)/shard_map/all_to_all | solution.py:119
  (185 other events, 1896.4 us)
Sparse Core Ops, SparseCore 0:
  11.4 78.1 all-gather.3
  126.0 63.6 all-gather.5
  191.9 165.4 all-gather.7
  408.1 100.7 reduce-scatter.2
  632.7 104.4 reduce-scatter.4

commit v4 on v3

--- a/solution.py
+++ b/solution.py
@@ -549,8 +549,6 @@
     probs16 = probs.astype(bf16)
     attended = jnp.einsum("hts,shd->thd", probs16, values, preferred_element_type=f32)
     attended = attended.reshape(tok_count, head_count * DV).astype(bf16)
-    second_pack = jnp.concatenate([shgate_w, shup_w, shdown_w.T], 1)
-    second_full = lax.all_gather(after(second_pack, attended), "ep", axis=0, tiled=True)
     attn_sum = gather_quarters(sum_to_quarter(matmul_nt(attended, output_t)).astype(bf16))
     mid_resid = resid_in + attn_sum.astype(f32)
     mid_scale = rms_scale(mid_resid)
@@ -560,6 +558,8 @@
     sent = matmul(pick, quarter_of(normed2, 0)).astype(bf16).reshape(owner_count, width, -1)
     one = exchange(sent[:, :, :half])
     two = exchange(after(sent[:, :, half:], one))
+    second_pack = jnp.concatenate([shgate_w, shup_w, shdown_w.T], 1)
+    second_full = lax.all_gather(after(second_pack, dy_all, one), "ep", axis=0, tiled=True)
     own = (to_experts(one), to_experts(two))
     first = ring_gather_first(*own)
     dy_all = after(dy_all, two)
@@ -685,9 +685,6 @@
     out_far = after(tuple(out_parts[4:6]), drow_two)
     out_top = shift(out_far[0], 1)
     out_bottom = shift(out_far[1], 3)
-    routed_grad_q, out_top, out_bottom = lax.optimization_barrier(
-        (routed_grad_q, out_top, out_bottom)
-    )
 
     dgate_part = jnp.stack(
         [jnp.sum(jnp.where(matches[k], dgate_rows[:, None], 0.0), 0) for k in range(TOPK)], 1
@@ -702,11 +699,6 @@
     dmid_norm, midnorm_grad = rms_back(mid_resid, mid_scale, mid_weight, dnormed2)
     dmid = upstream + dmid_norm
     dmid16 = dmid.astype(bf16)
-    out_prev_one, out_next_two = after(
-        (plus(out_parts[2], out_top), plus(out_parts[7], out_bottom)), dmid16
-    )
-    out_prev_one = shift(out_prev_one, 1)
-    out_next_two = shift(out_next_two, 3)
     dattended = matmul(dmid16, output_t).astype(bf16).reshape(tok_count, head_count, DV)
     dprobs = jnp.einsum("thd,shd->hts", dattended, values, preferred_element_type=f32)
     dscores = (probs * (dprobs - jnp.sum(probs * dprobs, -1, keepdims=True))).astype(bf16)
@@ -727,22 +719,14 @@
     dlatent_part = matmul_nt(dkeyval, keyval_full)
     dkey_part = jnp.sum(dkey_all[..., DN:], 1)
     dlat_part = jnp.concatenate([dlatent_part, dkey_part], 1).astype(bf16)
-    dlat_part, out_prev_one, out_next_two = lax.optimization_barrier(
-        (dlat_part, out_prev_one, out_next_two)
-    )
     dlat_sum = sum_small(dlat_part)
-    dnormed_q = sum_to_quarter(matmul_nt(dquery, query_full))
-    dlat_sum, second_sum = lax.optimization_barrier((dlat_sum, second_sum))
+    dlat_sum, second_sum, out_top, out_bottom = lax.optimization_barrier(
+        (dlat_sum, second_sum, out_top, out_bottom)
+    )
     dlatent, latnorm_grad = rms_back(latent, lat_scale, lat_weight, dlat_sum[:, :KVR])
     dlatent_all = jnp.concatenate(
         [dlatent, rotate(dlat_sum[:, KVR:], cos_tab, -sine_tab)], -1
     ).astype(bf16)
-    dnormed = gather_quarters(dnormed_q.astype(bf16)).astype(f32) + matmul_nt(
-        dlatent_all, latent_full
-    )
-    dtokens, prenorm_grad = rms_back(resid_in, pre_scale, pre_weight, dnormed)
-    tokens_grad = (dmid + dtokens).astype(bf16)
-    prenorm_sum = jnp.sum(exchange(prenorm_grad.reshape(owner_count, shard)), 0)
     gain_grads = jnp.stack(
         [
             jnp.pad(
@@ -767,9 +751,33 @@
         dkeyval,
         gain_grads.astype(bf16),
     )
-    down_grad = grads_of_down(first_grad)
-    all_rows = jnp.concatenate(after(rows, first_grad), 1)
-    late_dboth = after(ex_dboth, first_grad)
+    out_late = after((*out_parts, out_top, out_bottom), first_grad)
+    out_prev_one = shift(plus(out_late[2], out_late[8]), 1)
+    out_next_one = shift(out_late[6], 3)
+    out_prev_two, out_next_two = after(
+        (out_late[3], plus(out_late[7], out_late[9])), out_prev_one, out_next_one
+    )
+    out_prev_two = shift(out_prev_two, 1)
+    out_next_two = shift(out_next_two, 3)
+    out_one = add_three(out_parts[0], out_prev_one, out_next_one)
+    out_two = add_three(out_parts[1], out_prev_two, out_next_two)
+    back_one = exchange(from_experts(out_one, owner_count))
+    out_two = after(out_two, back_one)
+    back_two = exchange(from_experts(out_two, owner_count))
+    routed_q = jnp.concatenate(
+        [matmul_tn(pick, b.reshape(slot_rows, -1)) for b in (back_one, back_two)], 1
+    )
+    late_dquery, late_dlat = after((dquery, dlatent_all), out_prev_one, out_next_one)
+    dnormed_q = sum_to_quarter(matmul_nt(late_dquery, query_full))
+    dnormed = gather_quarters(dnormed_q.astype(bf16)).astype(f32) + matmul_nt(
+        late_dlat, latent_full
+    )
+    dtokens, prenorm_grad = rms_back(resid_in, pre_scale, pre_weight, dnormed)
+    tokens_grad = (dmid + dtokens).astype(bf16)
+    prenorm_sum = jnp.sum(exchange(prenorm_grad.reshape(owner_count, shard)), 0)
+    down_grad = grads_of_down(back_one)
+    all_rows = jnp.concatenate(after(rows, back_one), 1)
+    late_dboth = after(ex_dboth, back_one)
     exgate_grad = jnp.stack(
         [grads_of(e, all_rows, late_dboth, slice(0, hid_cols)) for e in range(EXP_DEV)]
     )
@@ -781,13 +789,6 @@
     )
     exgate_grad = to_lane(exgate_grad, 1)
     exup_grad = to_lane(exup_grad, 1)
-    out_late = after((out_parts[6], out_parts[3]), first_grad)
-    out_next_one = shift(out_late[0], 3)
-    out_prev_two = shift(out_late[1], 1)
-    routed_q = bring_back(
-        add_three(out_parts[0], out_prev_one, out_next_one),
-        add_three(out_parts[1], out_prev_two, out_next_two),
-    )
     layer_q = (quarter_of(mid_resid, 0) + routed_q + shared_q).astype(bf16)
     layer_out = gather_quarters(layer_q)
     first_sum = lax.psum_scatter(first_grad, "ep", scatter_dimension=0, tiled=True).astype(f32)

time: 809 us -> 770 us (0.952)
  waiting for transfers between devices: 289 us -> 244 us
    ppermute x48, waiting for transfers between devices: 180 us -> 137 us  [shift(): lax.ppermute(value, 'tp', [(i, (i + step) % lanes) for i in range(lanes)])]
    all_gather x1, waiting for transfers between devices: 0.01 us -> 26.4 us  [per_device(): lax.all_gather(after(second_pack, dy_all, one), 'ep', axis=0, tiled=True)]
    all_gather x1, waiting for transfers between devices: 26.2 us -> 0.01 us  [per_device(): lax.all_gather(after(dy_sent, first_full), 'tp', axis=0, tiled=True)]
    unnamed x359 -> x329, local copies, waits for them, and re-layouts: 54.8 us -> 53.7 us
  transfers between devices with their start and end apart: 62 -> 62, of which waited for: 29 -> 29; matrix products, arithmetic and copies ran while one was open for 27% -> 31% of each run, Pallas kernels for 5% -> 8%
where the time goes in v4:
time: 770 us; the launch traced here: 761 us
  waiting for transfers between devices  244 us (32%)
  starting transfers between devices  128 us (17%)
  local copies, waits for them, and re-layouts  122 us (16%)
  other arithmetic  88.4 us (11%)
  matrix products  82.6 us (11%)
  Pallas kernels  66.8 us (9%)
  between operations  16.4 us (2%)
  blocking collectives  12.6 us (2%)
    ppermute x48, waiting for transfers between devices, shift(): lax.ppermute(value, 'tp', [(i, (i + step) % lanes) for i in range(lanes)])  137 us
    ppermute x48, starting transfers between devices, shift(): lax.ppermute(value, 'tp', [(i, (i + step) % lanes) for i in range(lanes)])  74.7 us
    all_to_all x9, waiting for transfers between devices, exchange(): return lax.all_to_all(value, 'ep', 0, 0, tiled=True)  55.5 us
    unnamed x329, local copies, waits for them, and re-layouts  53.7 us
    all_to_all x9, starting transfers between devices, exchange(): return lax.all_to_all(value, 'ep', 0, 0, tiled=True)  53.1 us
    pallas_call x3, Pallas kernels, row_call(): pl.pallas_call(body, grid=(total // tile,), in_specs=in_specs, out_specs=...  52 us
    dot_general x10, matrix products, matmul_tn(): lax.dot_general(left_mat, right_mat, (((0,), (0,)), ((), ())), preferred_...  29.4 us
    all_gather x1, waiting for transfers between devices, per_device(): lax.all_gather(after(second_pack, dy_all, one), 'ep', axis=0, tiled=True)  26.4 us
  transfers between devices with their start and end apart: 62, of which 29 were waited for; matrix products, arithmetic and copies ran while one was open for 31% of the time, Pallas kernels for 8%

profile of v4, /device:TPU:0, one launch (start us, length us, event | category | flops | bytes accessed | tf_op | source)
XLA Modules:
  0.0 761.3 jit_solution(10314024561376916825)
XLA Ops:
  12.1 4.1 convolution_convert_fusion.1
  16.2 7.8 %all-to-all-start = ((bf16[32,72,512]{2,1,0:T(8,128)(2,1)}), bf16[32,72,512]{2,1,0:T(8,128)(2,1)}, u32[]{:S(2)}, u32[]{:S(2)}) async-start(bf16[32,72,512]{2,1,0:T(8,128)(2,1)} %bitcast.151), calls=%async_computation | async-start | bytes 4718592 | tf_op jit(solution)/shard_map/all_to_all | solution.py:119
  24.1 4.6 constant_dynamic-slice_fusion.35
  64.4 25.2 %all-gather.4.cloned.1.call-done = bf16[2048,2304]{1,0:T(8,128)(2,1)} async-done(((bf16[64,2304]{1,0:T(8,128)(2,1)}), bf16[2048,2304]{1,0:T(8,128)(2,1)}) %all-gather.4.cloned.1.call-update) | async-done | bytes 9437200 | tf_op jit(solution)/shard_map/all_gather | solution.py:439
  99.7 3.9 fusion.62
  134.4 7.1 collective-permute-done
  141.6 9.6 %collective-permute-done.2 = bf16[192,512]{1,0:T(8,128)(2,1)S(1)} collective-permute-done((bf16[192,512]{1,0:T(8,128)(2,1)S(1)}, bf16[192,512]{1,0:T(8,128)(2,1)S(1)}, u32[]{:S(2)}, u32[]{:S(2)}) %collective-permute-start.2) | collective-permute-done | bytes 196640 | tf_op jit(solution)/shard_map/ppermute | solution.py:78
  156.9 8.0 %collective-permute-done.5 = bf16[192,512]{1,0:T(8,128)(2,1)S(1)} collective-permute-done((bf16[192,512]{1,0:T(8,128)(2,1)S(1)}, bf16[192,512]{1,0:T(8,128)(2,1)S(1)}, u32[]{:S(2)}, u32[]{:S(2)}) %collective-permute-start.5) | collective-permute-done | bytes 196640 | tf_op jit(solution)/shard_map/ppermute | solution.py:78
  164.9 7.2 collective-permute-done.4
  179.3 5.4 all-to-all-start.1
  185.6 17.4 %all-to-all-done.1 = bf16[32,72,256]{2,1,0:T(8,128)(2,1)} async-done(((bf16[32,72,256]{2,1,0:T(8,128)(2,1)}), bf16[32,72,256]{2,1,0:T(8,128)(2,1)}, u32[]{:S(2)}, u32[]{:S(2)}) %all-to-all-start.1) | async-done | bytes 1179680 | tf_op jit(solution)/shard_map/all_to_all | solution.py:119
  205.1 4.7 all-to-all-start.2
  216.5 14.0 %all-to-all-done.2 = bf16[32,72,256]{2,1,0:T(8,128)(2,1)} async-done(((bf16[32,72,256]{2,1,0:T(8,128)(2,1)}), bf16[32,72,256]{2,1,0:T(8,128)(2,1)}, u32[]{:S(2)}, u32[]{:S(2)}) %all-to-all-start.2) | async-done | bytes 1179680 | tf_op jit(solution)/shard_map/all_to_all | solution.py:119
  237.0 26.4 %all-gather.8.cloned.1.call-done = bf16[2048,2112]{1,0:T(8,128)(2,1)} async-done(((bf16[64,2112]{1,0:T(8,128)(2,1)}), bf16[2048,2112]{1,0:T(8,128)(2,1)}) %all-gather.8.cloned.1.call-update) | async-done | bytes 8650768 | tf_op jit(solution)/shard_map/all_gather | solution.py:562
  263.5 4.3 fusion.19
  270.8 7.0 shard_map.306
  278.6 4.0 fusion.67
  282.6 5.6 fusion.70
  293.3 12.6 %all_to_all.65 = f32[32,1,72]{2,1,0:T(1,128)S(1)} all-to-all(f32[32,1,72]{2,1,0:T(1,128)S(1)} %bitcast.175), channel_id=1, replica_groups=mesh['ep'=32,'tp'=4] {'ep'}, dimensions={0} | all-to-all | bytes 18432 | tf_op jit(solution)/shard_map/all_to_all | solution.py:119
  307.7 10.7 %shard_map.307.refs_9_ = f32[2304,384]{1,0:T(8,128)S(1)} custom-call(bf16[9216,512]{1,0:T(8,128)(2,1)} %all-gather.6.cloned.1.call-done.refs_0_.refs_1_.refs_2_.refs_3_, bf16[9216,512]{1,0:T(8,128)(2,1)} %all-gather.6.cloned.1.call-done.refs_0_.refs_1_.refs_2_.refs_3_, bf16[9216,512]{1,0:T(8,128)(2,1)} %all-gather.6.cloned.1.call-done.refs_0_.refs_1_.refs_2_.refs_3_, ...), custom_call_target="tpu_custom_call" | custom-call | flops 4026531840 | bytes 44433408 | tf_op jit(solution)/shard_map/pallas_call | solution.py:278
  320.7 29.3 %shard_map.308 = (bf16[2304,384]{1,0:T(8,128)(2,1)}, bf16[2304,768]{1,0:T(8,128)(2,1)}, f32[2304,1]{1,0:T(8,128)S(1)}, bf16[2304,256]{1,0:T(8,128)(2,1)S(1)}, bf...) custom-call(bf16[2304,256]{1,0:T(8,128)(2,1)} %pad_maximum_fusion.6., ...), custom_call_target="tpu_custom_call" | custom-call | flops 16106127360 | bytes 34031616 | tf_op jit(solution)/shard_map/pallas_call | solution.py:278
  362.2 5.6 all-to-all-start.4
  367.8 12.0 %shard_map.309 = (bf16[2304,256]{1,0:T(8,128)(2,1)S(1)}, bf16[2304,256]{1,0:T(8,128)(2,1)S(1)}, bf16[2304,256]{1,0:T(8,128)(2,1)S(1)}, bf16[2304,256]{1,0:T(8,12...) custom-call(bf16[2304,384]{1,0:T(8,128)(2,1)} %get-tuple-element.109, ...), custom_call_target="tpu_custom_call" | custom-call | flops 4026531840 | bytes 14352384 | tf_op jit(solution)/shard_map/pallas_call | solution.py:278
  398.2 19.7 %collective-permute-done.15 = bf16[2304,256]{1,0:T(8,128)(2,1)S(1)} collective-permute-done((bf16[2304,256]{1,0:T(8,128)(2,1)S(1)}, bf16[2304,256]{1,0:T(8,128)(2,1)S(1)}, u32[]{:S(2)}, u32[]{:S(2)}) %collective-permute-start.15) | collective-permute-done | bytes 1179680 | tf_op jit(solution)/shard_map/ppermute | solution.py:78
  426.4 7.3 all-to-all-start.5
  433.7 16.2 %collective-permute-done.16 = bf16[2304,256]{1,0:T(8,128)(2,1)} collective-permute-done((bf16[2304,256]{1,0:T(8,128)(2,1)S(1)}, bf16[2304,256]{1,0:T(8,128)(2,1)}, u32[]{:S(2)}, u32[]{:S(2)}) %collective-permute-start.16) | collective-permute-done | bytes 1179680 | tf_op jit(solution)/shard_map/ppermute | solution.py:78
  453.2 7.5 all-to-all-start.6
  483.3 4.1 collective-permute-start.22
  491.8 5.5 collective-permute-done.22
  511.5 15.9 %collective-permute-done.28 = bf16[192,576]{1,0:T(8,128)(2,1)S(1)} collective-permute-done((bf16[192,576]{1,0:T(8,128)(2,1)S(1)}, bf16[192,576]{1,0:T(8,128)(2,1)S(1)}, u32[]{:S(2)}, u32[]{:S(2)}) %collective-permute-start.28) | collective-permute-done | bytes 221216 | tf_op jit(solution)/shard_map/ppermute | solution.py:78
  527.3 5.1 collective-permute-done.29
  551.8 7.9 %shard_map.310 = bf16[2048,2304]{1,0:T(8,128)(2,1)} custom-call(bf16[192,2048]{1,0:T(8,128)(2,1)S(1)} %copy-done.8, bf16[192,2048]{1,0:T(8,128)(2,1)S(1)} %copy-done.2, bf16[192,2048]{1,0:T(8,128)(2,1)S(1)} %fusion.194.dmid, bf16[192,768]{1,0:T(8,128)(2,1)S(1)} %copy-done.22, bf16[192,640]{1,0:T(8,128)(2,1)S(1)} %copy-done.24, ...), custom_call_target="tpu_custom_call" | custom-call | flops 1811939328 | bytes 14155776 | tf_op jit(solution)/shard_map/pallas_call | solution.py:343
  573.3 19.9 %collective-permute-done.32 = bf16[2304,256]{1,0:T(8,128)(2,1)} collective-permute-done((bf16[2304,256]{1,0:T(8,128)(2,1)}, bf16[2304,256]{1,0:T(8,128)(2,1)}, u32[]{:S(2)}, u32[]{:S(2)}) %collective-permute-start.32) | collective-permute-done | bytes 1179680 | tf_op jit(solution)/shard_map/ppermute | solution.py:78
  598.1 5.2 collective-permute-start.44
  615.0 4.5 collective-permute-done.47
  622.7 4.7 fusion.95
  628.1 4.5 all-to-all-start.9
  633.7 6.4 all-to-all-done.9
  640.1 4.7 all-to-all-start.7
  652.3 4.4 fusion.91
  658.0 6.9 all-to-all-done.7
  686.3 3.8 fusion.53
  690.1 3.9 fusion.41
  694.0 3.9 fusion.50
  697.8 3.9 fusion.47
  704.9 5.7 all-to-all-start.8
  722.7 6.3 all-to-all-done.8
  741.0 3.8 collective-permute-done.40
  (624 shorter events, 326.8 us)
Async XLA Ops:
  7.2 82.5 %all-gather.4.cloned.1.call-start = ((), (), s32[]{:S(2)}) async-start(), calls=%async_computation.12 | async-start | bytes 9732096 | tf_op jit(solution)/shard_map/all_gather | solution.py:439
  16.2 43.8 %all-to-all-start = ((bf16[32,72,512]{2,1,0:T(8,128)(2,1)}), bf16[32,72,512]{2,1,0:T(8,128)(2,1)}, u32[]{:S(2)}, u32[]{:S(2)}) async-start(bf16[32,72,512]{2,1,0:T(8,128)(2,1)} %bitcast.151), calls=%async_computation | async-start | bytes 4718592 | tf_op jit(solution)/shard_map/all_to_all | solution.py:119
  24.0 179.0 %all-gather.6.cloned.1.call-start = ((), (), s32[]{:S(2)}) async-start(), calls=%async_computation.13 | async-start | bytes 11796480 | tf_op jit(solution)/shard_map/all_gather | solution.py:496
  128.6 13.0 %collective-permute-start = (bf16[192,512]{1,0:T(8,128)(2,1)S(1)}, bf16[192,512]{1,0:T(8,128)(2,1)S(1)}, u32[]{:S(2)}, u32[]{:S(2)}) collective-permute-start(bf16[192,512]{1,0:T(8,128)(2,1)S(1)} %get-tuple-element.262), channel_id=1, source_target_pairs={{0,1},{1,2},{2,3},{3,0},{4,5},{5,6},{6,7},{7,4},{8,9},{9,10},{10,1... | collective-permute-start | bytes 589832 | tf_op jit(solution)/shard_map/ppermute | solution.py:78
  130.2 21.0 %collective-permute-start.2 = (bf16[192,512]{1,0:T(8,128)(2,1)S(1)}, bf16[192,512]{1,0:T(8,128)(2,1)S(1)}, u32[]{:S(2)}, u32[]{:S(2)}) collective-permute-start(bf16[192,512]{1,0:T(8,128)(2,1)S(1)} %get-tuple-element.263), channel_id=1, source_target_pairs={{0,2},{1,3},{2,0},{3,1},{4,6},{5,7},{6,4},{7,5},{8,10},{9,11},{10,... | collective-permute-start | bytes 589832 | tf_op jit(solution)/shard_map/ppermute | solution.py:78
  133.1 18.1 %collective-permute-start.1 = (bf16[192,512]{1,0:T(8,128)(2,1)S(1)}, bf16[192,512]{1,0:T(8,128)(2,1)S(1)}, u32[]{:S(2)}, u32[]{:S(2)}) collective-permute-start(bf16[192,512]{1,0:T(8,128)(2,1)S(1)} %get-tuple-element.264), channel_id=1, source_target_pairs={{0,3},{1,0},{2,1},{3,2},{4,7},{5,4},{6,5},{7,6},{8,11},{9,8},{10,9... | collective-permute-start | bytes 589832 | tf_op jit(solution)/shard_map/ppermute | solution.py:78
  151.3 13.6 %collective-permute-start.5 = (bf16[192,512]{1,0:T(8,128)(2,1)S(1)}, bf16[192,512]{1,0:T(8,128)(2,1)S(1)}, u32[]{:S(2)}, u32[]{:S(2)}) collective-permute-start(bf16[192,512]{1,0:T(8,128)(2,1)S(1)} %add_convert_fusion.10), channel_id=1, source_target_pairs={{0,1},{1,2},{2,3},{3,0},{4,5},{5,6},{6,7},{7,4},{8,9},{9,10},{10,1... | collective-permute-start | bytes 589832 | tf_op jit(solution)/shard_map/ppermute | solution.py:78
  151.4 20.7 %collective-permute-start.4 = (bf16[192,512]{1,0:T(8,128)(2,1)S(1)}, bf16[192,512]{1,0:T(8,128)(2,1)}, u32[]{:S(2)}, u32[]{:S(2)}) collective-permute-start(bf16[192,512]{1,0:T(8,128)(2,1)S(1)} %add_convert_fusion.10), channel_id=1, source_target_pairs={{0,2},{1,3},{2,0},{3,1},{4,6},{5,7},{6,4},{7,5},{8,10},{9,11},{10,... | collective-permute-start | bytes 589832 | tf_op jit(solution)/shard_map/ppermute | solution.py:78
  154.2 19.1 %collective-permute-start.3 = (bf16[192,512]{1,0:T(8,128)(2,1)S(1)}, bf16[192,512]{1,0:T(8,128)(2,1)}, u32[]{:S(2)}, u32[]{:S(2)}) collective-permute-start(bf16[192,512]{1,0:T(8,128)(2,1)S(1)} %add_convert_fusion.10), channel_id=1, source_target_pairs={{0,3},{1,0},{2,1},{3,2},{4,7},{5,4},{6,5},{7,6},{8,11},{9,8},{10,9... | collective-permute-start | bytes 589832 | tf_op jit(solution)/shard_map/ppermute | solution.py:78
  179.3 23.8 %all-to-all-start.1 = ((bf16[32,72,256]{2,1,0:T(8,128)(2,1)}), bf16[32,72,256]{2,1,0:T(8,128)(2,1)}, u32[]{:S(2)}, u32[]{:S(2)}) async-start(bf16[32,72,256]{2,1,0:T(8,128)(2,1)} %get-tuple-element.213), calls=%async_computation.1 | async-start | bytes 2359296 | tf_op jit(solution)/shard_map/all_to_all | solution.py:119
  184.7 78.7 %all-gather.8.cloned.1.call-start = ((), (), s32[]{:S(2)}) async-start(), calls=%async_computation.14 | async-start | bytes 9191424 | tf_op jit(solution)/shard_map/all_gather | solution.py:562
  205.1 25.3 %all-to-all-start.2 = ((bf16[32,72,256]{2,1,0:T(8,128)(2,1)}), bf16[32,72,256]{2,1,0:T(8,128)(2,1)}, u32[]{:S(2)}, u32[]{:S(2)}) async-start(bf16[32,72,256]{2,1,0:T(8,128)(2,1)} %get-tuple-element.94), calls=%async_computation.2 | async-start | bytes 2359296 | tf_op jit(solution)/shard_map/all_to_all | solution.py:119
  209.8 322.8 %reduce-scatter.3.cloned.1.call-start = ((), (), s32[]{:S(2)}) async-start(), calls=%async_computation.15 | async-start | bytes 9191424 | tf_op jit(solution)/shard_map/reduce_scatter | solution.py:596
  213.3 74.9 %collective-permute-start.7 = (bf16[2304,256]{1,0:T(8,128)(2,1)}, bf16[2304,256]{1,0:T(8,128)(2,1)}, u32[]{:S(2)}, u32[]{:S(2)}) collective-permute-start(bf16[2304,256]{1,0:T(8,128)(2,1)} %pad_maximum_fusion.6.refs_0_), channel_id=1, source_target_pairs={{0,1},{1,2},{2,3},{3,0},{4,5},{5,6},{6,7},{7,4},{8,9},{9,10},{10,1... | collective-permute-start | bytes 3538952 | tf_op jit(solution)/shard_map/ppermute | solution.py:78
  214.7 105.6 %collective-permute-start.6 = (bf16[2304,256]{1,0:T(8,128)(2,1)}, bf16[2304,256]{1,0:T(8,128)(2,1)}, u32[]{:S(2)}, u32[]{:S(2)}) collective-permute-start(bf16[2304,256]{1,0:T(8,128)(2,1)} %pad_maximum_fusion.6.refs_0_), channel_id=1, source_target_pairs={{0,3},{1,0},{2,1},{3,2},{4,7},{5,4},{6,5},{7,6},{8,11},{9,8},{10,9... | collective-permute-start | bytes 3538952 | tf_op jit(solution)/shard_map/ppermute | solution.py:78
  233.8 86.6 %collective-permute-start.11 = (bf16[2304,256]{1,0:T(8,128)(2,1)}, bf16[2304,256]{1,0:T(8,128)(2,1)}, u32[]{:S(2)}, u32[]{:S(2)}) collective-permute-start(bf16[2304,256]{1,0:T(8,128)(2,1)} %pad_maximum_fusion.7.refs_1_), channel_id=1, source_target_pairs={{0,1},{1,2},{2,3},{3,0},{4,5},{5,6},{6,7},{7,4},{8,9},{9,10},{10,1... | collective-permute-start | bytes 3538952 | tf_op jit(solution)/shard_map/ppermute | solution.py:78
  235.3 52.9 %collective-permute-start.8 = (bf16[2304,256]{1,0:T(8,128)(2,1)}, bf16[2304,256]{1,0:T(8,128)(2,1)}, u32[]{:S(2)}, u32[]{:S(2)}) collective-permute-start(bf16[2304,256]{1,0:T(8,128)(2,1)} %pad_maximum_fusion.7.refs_1_), channel_id=1, source_target_pairs={{0,3},{1,0},{2,1},{3,2},{4,7},{5,4},{6,5},{7,6},{8,11},{9,8},{10,9... | collective-permute-start | bytes 3538952 | tf_op jit(solution)/shard_map/ppermute | solution.py:78
  288.2 32.2 %collective-permute-start.10 = (bf16[2304,256]{1,0:T(8,128)(2,1)}, bf16[2304,256]{1,0:T(8,128)(2,1)}, u32[]{:S(2)}, u32[]{:S(2)}) collective-permute-start(bf16[2304,256]{1,0:T(8,128)(2,1)} %collective-permute-done.8.refs_3_), channel_id=1, source_target_pairs={{0,3},{1,0},{2,1},{3,2},{4,7},{5,4},{6,5},{7,6},{8,11},{9,8},{10,9... | collective-permute-start | bytes 3538952 | tf_op jit(solution)/shard_map/ppermute | solution.py:78
  291.1 29.6 %collective-permute-start.9 = (bf16[2304,256]{1,0:T(8,128)(2,1)}, bf16[2304,256]{1,0:T(8,128)(2,1)}, u32[]{:S(2)}, u32[]{:S(2)}) collective-permute-start(bf16[2304,256]{1,0:T(8,128)(2,1)} %collective-permute-done.7.refs_6_), channel_id=1, source_target_pairs={{0,1},{1,2},{2,3},{3,0},{4,5},{5,6},{6,7},{7,4},{8,9},{9,10},{10,1... | collective-permute-start | bytes 3538952 | tf_op jit(solution)/shard_map/ppermute | solution.py:78
  353.0 36.8 %collective-permute-start.12 = (bf16[2304,256]{1,0:T(8,128)(2,1)}, bf16[2304,256]{1,0:T(8,128)(2,1)}, u32[]{:S(2)}, u32[]{:S(2)}) collective-permute-start(bf16[2304,256]{1,0:T(8,128)(2,1)} %get-tuple-element.106), channel_id=1, source_target_pairs={{0,1},{1,2},{2,3},{3,0},{4,5},{5,6},{6,7},{7,4},{8,9},{9,10},{10,1... | collective-permute-start | bytes 3538952 | tf_op jit(solution)/shard_map/ppermute | solution.py:78
  353.3 36.6 %collective-permute-start.13 = (bf16[2304,256]{1,0:T(8,128)(2,1)}, bf16[2304,256]{1,0:T(8,128)(2,1)}, u32[]{:S(2)}, u32[]{:S(2)}) collective-permute-start(bf16[2304,256]{1,0:T(8,128)(2,1)} %get-tuple-element.107), channel_id=1, source_target_pairs={{0,3},{1,0},{2,1},{3,2},{4,7},{5,4},{6,5},{7,6},{8,11},{9,8},{10,9... | collective-permute-start | bytes 3538952 | tf_op jit(solution)/shard_map/ppermute | solution.py:78
  362.2 23.8 %all-to-all-start.4 = ((f32[32,1,72]{2,1,0:T(1,128)}), f32[32,1,72]{2,1,0:T(1,128)}, u32[]{:S(2)}, u32[]{:S(2)}) async-start(f32[32,1,72]{2,1,0:T(1,128)} %bitcast.37), calls=%async_computation.4 | async-start | bytes 32768 | tf_op jit(solution)/shard_map/all_to_all | solution.py:119
  389.9 28.1 %collective-permute-start.15 = (bf16[2304,256]{1,0:T(8,128)(2,1)S(1)}, bf16[2304,256]{1,0:T(8,128)(2,1)S(1)}, u32[]{:S(2)}, u32[]{:S(2)}) collective-permute-start(bf16[2304,256]{1,0:T(8,128)(2,1)S(1)} %copy-done.34), channel_id=1, source_target_pairs={{0,3},{1,0},{2,1},{3,2},{4,7},{5,4},{6,5},{7,6},{8,11},{9,8},{10,9... | collective-permute-start | bytes 3538952 | tf_op jit(solution)/shard_map/ppermute | solution.py:78
  391.7 29.7 %collective-permute-start.14 = (bf16[2304,256]{1,0:T(8,128)(2,1)S(1)}, bf16[2304,256]{1,0:T(8,128)(2,1)S(1)}, u32[]{:S(2)}, u32[]{:S(2)}) collective-permute-start(bf16[2304,256]{1,0:T(8,128)(2,1)S(1)} %add_convert_fusion.7), channel_id=1, source_target_pairs={{0,1},{1,2},{2,3},{3,0},{4,5},{5,6},{6,7},{7,4},{8,9},{9,10},{10,1... | collective-permute-start | bytes 3538952 | tf_op jit(solution)/shard_map/ppermute | solution.py:78
  421.4 28.5 %collective-permute-start.16 = (bf16[2304,256]{1,0:T(8,128)(2,1)S(1)}, bf16[2304,256]{1,0:T(8,128)(2,1)}, u32[]{:S(2)}, u32[]{:S(2)}) collective-permute-start(bf16[2304,256]{1,0:T(8,128)(2,1)S(1)} %copy-done.32), channel_id=1, source_target_pairs={{0,1},{1,2},{2,3},{3,0},{4,5},{5,6},{6,7},{7,4},{8,9},{9,10},{10,1... | collective-permute-start | bytes 3538952 | tf_op jit(solution)/shard_map/ppermute | solution.py:78
  421.9 28.0 %collective-permute-start.17 = (bf16[2304,256]{1,0:T(8,128)(2,1)}, bf16[2304,256]{1,0:T(8,128)(2,1)}, u32[]{:S(2)}, u32[]{:S(2)}) collective-permute-start(bf16[2304,256]{1,0:T(8,128)(2,1)} %add_convert_fusion.5), channel_id=1, source_target_pairs={{0,3},{1,0},{2,1},{3,2},{4,7},{5,4},{6,5},{7,6},{8,11},{9,8},{10,9... | collective-permute-start | bytes 3538952 | tf_op jit(solution)/shard_map/ppermute | solution.py:78
  426.4 26.8 %all-to-all-start.5 = ((bf16[32,72,256]{2,1,0:T(8,128)(2,1)}), bf16[32,72,256]{2,1,0:T(8,128)(2,1)S(1)}, u32[]{:S(2)}, u32[]{:S(2)}) async-start(bf16[32,72,256]{2,1,0:T(8,128)(2,1)} %pad_maximum_fusion.8), calls=%async_computation.5 | async-start | bytes 2359296 | tf_op jit(solution)/shard_map/all_to_all | solution.py:119
  453.2 25.9 %all-to-all-start.6 = ((bf16[32,72,256]{2,1,0:T(8,128)(2,1)}), bf16[32,72,256]{2,1,0:T(8,128)(2,1)S(1)}, u32[]{:S(2)}, u32[]{:S(2)}) async-start(bf16[32,72,256]{2,1,0:T(8,128)(2,1)} %pad_maximum_fusion.9), calls=%async_computation.6 | async-start | bytes 2359296 | tf_op jit(solution)/shard_map/all_to_all | solution.py:119
  460.7 285.8 %reduce-scatter.5.cloned.1.call-start = ((), (), s32[]{:S(2)}) async-start(), calls=%async_computation.16 | async-start | bytes 9732096 | tf_op jit(solution)/shard_map/reduce_scatter | solution.py:794
  467.7 13.7 %collective-permute-start.18 = (bf16[192,512]{1,0:T(8,128)(2,1)}, bf16[192,512]{1,0:T(8,128)(2,1)S(1)}, u32[]{:S(2)}, u32[]{:S(2)}) collective-permute-start(bf16[192,512]{1,0:T(8,128)(2,1)} %get-tuple-element.255), channel_id=1, source_target_pairs={{0,1},{1,2},{2,3},{3,0},{4,5},{5,6},{6,7},{7,4},{8,9},{9,10},{10,1... | collective-permute-start | bytes 589832 | tf_op jit(solution)/shard_map/ppermute | solution.py:78
  469.8 11.7 %collective-permute-start.20 = (bf16[192,512]{1,0:T(8,128)(2,1)}, bf16[192,512]{1,0:T(8,128)(2,1)}, u32[]{:S(2)}, u32[]{:S(2)}) collective-permute-start(bf16[192,512]{1,0:T(8,128)(2,1)} %get-tuple-element.256), channel_id=1, source_target_pairs={{0,2},{1,3},{2,0},{3,1},{4,6},{5,7},{6,4},{7,5},{8,10},{9,11},{10,... | collective-permute-start | bytes 589832 | tf_op jit(solution)/shard_map/ppermute | solution.py:78
  483.3 14.0 %collective-permute-start.22 = (bf16[192,512]{1,0:T(8,128)(2,1)S(1)}, bf16[192,512]{1,0:T(8,128)(2,1)S(1)}, u32[]{:S(2)}, u32[]{:S(2)}) collective-permute-start(bf16[192,512]{1,0:T(8,128)(2,1)S(1)} %fusion.144), channel_id=1, source_target_pairs={{0,2},{1,3},{2,0},{3,1},{4,6},{5,7},{6,4},{7,5},{8,10},{9,11},{10,... | collective-permute-start | bytes 589832 | tf_op jit(solution)/shard_map/ppermute | solution.py:78
  488.4 44.1 %collective-permute-start.30 = (bf16[2304,256]{1,0:T(8,128)(2,1)}, bf16[2304,256]{1,0:T(8,128)(2,1)}, u32[]{:S(2)}, u32[]{:S(2)}) collective-permute-start(bf16[2304,256]{1,0:T(8,128)(2,1)} %get-tuple-element.140), channel_id=1, source_target_pairs={{0,1},{1,2},{2,3},{3,0},{4,5},{5,6},{6,7},{7,4},{8,9},{9,10},{10,1... | collective-permute-start | bytes 3538952 | tf_op jit(solution)/shard_map/ppermute | solution.py:78
  490.4 42.1 %collective-permute-start.31 = (bf16[2304,256]{1,0:T(8,128)(2,1)}, bf16[2304,256]{1,0:T(8,128)(2,1)}, u32[]{:S(2)}, u32[]{:S(2)}) collective-permute-start(bf16[2304,256]{1,0:T(8,128)(2,1)} %get-tuple-element.141), channel_id=1, source_target_pairs={{0,3},{1,0},{2,1},{3,2},{4,7},{5,4},{6,5},{7,6},{8,11},{9,8},{10,9... | collective-permute-start | bytes 3538952 | tf_op jit(solution)/shard_map/ppermute | solution.py:78
  507.2 20.2 %collective-permute-start.28 = (bf16[192,576]{1,0:T(8,128)(2,1)S(1)}, bf16[192,576]{1,0:T(8,128)(2,1)S(1)}, u32[]{:S(2)}, u32[]{:S(2)}) collective-permute-start(bf16[192,576]{1,0:T(8,128)(2,1)S(1)} %pad_maximum_fusion.23), channel_id=1, source_target_pairs={{0,3},{1,0},{2,1},{3,2},{4,7},{5,4},{6,5},{7,6},{8,11},{9,8},{10,9... | collective-permute-start | bytes 663560 | tf_op jit(solution)/shard_map/ppermute | solution.py:78
  508.8 18.6 %collective-permute-start.27 = (bf16[192,576]{1,0:T(8,128)(2,1)S(1)}, bf16[192,576]{1,0:T(8,128)(2,1)S(1)}, u32[]{:S(2)}, u32[]{:S(2)}) collective-permute-start(bf16[192,576]{1,0:T(8,128)(2,1)S(1)} %pad_maximum_fusion.23), channel_id=1, source_target_pairs={{0,1},{1,2},{2,3},{3,0},{4,5},{5,6},{6,7},{7,4},{8,9},{9,10},{10,1... | collective-permute-start | bytes 663560 | tf_op jit(solution)/shard_map/ppermute | solution.py:78
  509.3 23.2 %collective-permute-start.29 = (bf16[192,576]{1,0:T(8,128)(2,1)S(1)}, bf16[192,576]{1,0:T(8,128)(2,1)S(1)}, u32[]{:S(2)}, u32[]{:S(2)}) collective-permute-start(bf16[192,576]{1,0:T(8,128)(2,1)S(1)} %pad_maximum_fusion.23), channel_id=1, source_target_pairs={{0,2},{1,3},{2,0},{3,1},{4,6},{5,7},{6,4},{7,5},{8,10},{9,11},{10,... | collective-permute-start | bytes 663560 | tf_op jit(solution)/shard_map/ppermute | solution.py:78
  562.7 30.4 %collective-permute-start.32 = (bf16[2304,256]{1,0:T(8,128)(2,1)}, bf16[2304,256]{1,0:T(8,128)(2,1)}, u32[]{:S(2)}, u32[]{:S(2)}) collective-permute-start(bf16[2304,256]{1,0:T(8,128)(2,1)} %add_convert_fusion.3), channel_id=1, source_target_pairs={{0,1},{1,2},{2,3},{3,0},{4,5},{5,6},{6,7},{7,4},{8,9},{9,10},{10,1... | collective-permute-start | bytes 3538952 | tf_op jit(solution)/shard_map/ppermute | solution.py:78
  563.0 31.8 %collective-permute-start.33 = (bf16[2304,256]{1,0:T(8,128)(2,1)S(1)}, bf16[2304,256]{1,0:T(8,128)(2,1)}, u32[]{:S(2)}, u32[]{:S(2)}) collective-permute-start(bf16[2304,256]{1,0:T(8,128)(2,1)S(1)} %copy-done.30), channel_id=1, source_target_pairs={{0,3},{1,0},{2,1},{3,2},{4,7},{5,4},{6,5},{7,6},{8,11},{9,8},{10,9... | collective-permute-start | bytes 3538952 | tf_op jit(solution)/shard_map/ppermute | solution.py:78
  567.4 163.3 %collective-permute-start.36 = (bf16[192,512]{1,0:T(8,128)(2,1)}, bf16[192,512]{1,0:T(8,128)(2,1)}, u32[]{:S(2)}, u32[]{:S(2)}) collective-permute-start(bf16[192,512]{1,0:T(8,128)(2,1)} %get-tuple-element.248), channel_id=1, source_target_pairs={{0,1},{1,2},{2,3},{3,0},{4,5},{5,6},{6,7},{7,4},{8,9},{9,10},{10,1... | collective-permute-start | bytes 589832 | tf_op jit(solution)/shard_map/ppermute | solution.py:78
  567.4 163.3 %collective-permute-start.38 = (bf16[192,512]{1,0:T(8,128)(2,1)}, bf16[192,512]{1,0:T(8,128)(2,1)}, u32[]{:S(2)}, u32[]{:S(2)}) collective-permute-start(bf16[192,512]{1,0:T(8,128)(2,1)} %get-tuple-element.249), channel_id=1, source_target_pairs={{0,2},{1,3},{2,0},{3,1},{4,6},{5,7},{6,4},{7,5},{8,10},{9,11},{10,... | collective-permute-start | bytes 589832 | tf_op jit(solution)/shard_map/ppermute | solution.py:78
  598.1 12.1 %collective-permute-start.44 = (bf16[192,512]{1,0:T(8,128)(2,1)S(1)}, bf16[192,512]{1,0:T(8,128)(2,1)S(1)}, u32[]{:S(2)}, u32[]{:S(2)}) collective-permute-start(bf16[192,512]{1,0:T(8,128)(2,1)S(1)} %get-tuple-element.242), channel_id=1, source_target_pairs={{0,2},{1,3},{2,0},{3,1},{4,6},{5,7},{6,4},{7,5},{8,10},{9,11},{10,... | collective-permute-start | bytes 589832 | tf_op jit(solution)/shard_map/ppermute | solution.py:78
  619.5 111.2 %collective-permute-start.37 = (bf16[192,512]{1,0:T(8,128)(2,1)}, bf16[192,512]{1,0:T(8,128)(2,1)}, u32[]{:S(2)}, u32[]{:S(2)}) collective-permute-start(bf16[192,512]{1,0:T(8,128)(2,1)} %get-tuple-element.250), channel_id=1, source_target_pairs={{0,3},{1,0},{2,1},{3,2},{4,7},{5,4},{6,5},{7,6},{8,11},{9,8},{10,9... | collective-permute-start | bytes 589832 | tf_op jit(solution)/shard_map/ppermute | solution.py:78
  628.1 12.0 %all-to-all-start.9 = ((f32[32,1,64]{2,1,0:T(1,128)}), f32[32,1,64]{2,1,0:T(1,128)}, u32[]{:S(2)}, u32[]{:S(2)}) async-start(f32[32,1,64]{2,1,0:T(1,128)} %all_to_all.53), calls=%async_computation.10 | async-start | bytes 32768 | tf_op jit(solution)/shard_map/all_to_all | solution.py:119
  640.1 24.7 %all-to-all-start.7 = ((bf16[32,72,256]{2,1,0:T(8,128)(2,1)}), bf16[32,72,256]{2,1,0:T(8,128)(2,1)}, u32[]{:S(2)}, u32[]{:S(2)}) async-start(bf16[32,72,256]{2,1,0:T(8,128)(2,1)} %pad_maximum_fusion.10), calls=%async_computation.8 | async-start | bytes 2359296 | tf_op jit(solution)/shard_map/all_to_all | solution.py:119
  648.2 53.5 %collective-permute-start.34 = (bf16[2304,256]{1,0:T(8,128)(2,1)S(1)}, bf16[2304,256]{1,0:T(8,128)(2,1)}, u32[]{:S(2)}, u32[]{:S(2)}) collective-permute-start(bf16[2304,256]{1,0:T(8,128)(2,1)S(1)} %copy-done.28), channel_id=1, source_target_pairs={{0,1},{1,2},{2,3},{3,0},{4,5},{5,6},{6,7},{7,4},{8,9},{9,10},{10,1... | collective-permute-start | bytes 3538952 | tf_op jit(solution)/shard_map/ppermute | solution.py:78
  649.2 52.5 %collective-permute-start.35 = (bf16[2304,256]{1,0:T(8,128)(2,1)}, bf16[2304,256]{1,0:T(8,128)(2,1)}, u32[]{:S(2)}, u32[]{:S(2)}) collective-permute-start(bf16[2304,256]{1,0:T(8,128)(2,1)} %add_convert_fusion.1), channel_id=1, source_target_pairs={{0,3},{1,0},{2,1},{3,2},{4,7},{5,4},{6,5},{7,6},{8,11},{9,8},{10,9... | collective-permute-start | bytes 3538952 | tf_op jit(solution)/shard_map/ppermute | solution.py:78
  704.9 24.2 %all-to-all-start.8 = ((bf16[32,72,256]{2,1,0:T(8,128)(2,1)}), bf16[32,72,256]{2,1,0:T(8,128)(2,1)S(1)}, u32[]{:S(2)}, u32[]{:S(2)}) async-start(bf16[32,72,256]{2,1,0:T(8,128)(2,1)} %pad_maximum_fusion.11), calls=%async_computation.9 | async-start | bytes 2359296 | tf_op jit(solution)/shard_map/all_to_all | solution.py:119
  (169 other events, 1306.4 us)
Sparse Core Ops, SparseCore 0:
  11.4 78.1 all-gather.3
  91.9 108.5 all-gather.5
  203.2 60.1 all-gather.7
  320.4 91.8 reduce-scatter.2
  569.9 100.0 reduce-scatter.4

commit v5 on v4

--- a/solution.py
+++ b/solution.py
@@ -194,8 +194,8 @@
 
 
 def hidden_back_kernel(tiles, spill, *refs):
-    pieces, weight, out = refs[:-2], refs[-2], refs[-1]
-    rows = jnp.concatenate([p[...] for p in pieces], 1)
+    value, weight, out = refs
+    rows = value[...]
 
     def run(owner, mine):
         if owner is None:
@@ -248,18 +248,18 @@
     per_owner(tiles, rows.shape[0], spill, back)
 
 
-def out_kernel(tiles, spill, value, weight, *outs):
+def out_kernel(tiles, spill, value, weight, out):
     def run(owner, mine):
         rows = value[...]
         none = jnp.zeros_like(rows)
-        for j, out in enumerate(outs):
-            at = slice(j * out.shape[1], (j + 1) * out.shape[1])
+        for j in range(out.shape[0]):
+            at = slice(j * out.shape[2], (j + 1) * out.shape[2])
             if owner is None:
                 total = matmul(jnp.where(mine, rows, none), weight[0, :, at])
                 total = total + matmul(jnp.where(mine, none, rows), weight[1, :, at])
             else:
                 total = matmul(rows, weight[owner, :, at])
-            out[...] = total.astype(bf16)
+            out[j] = total.astype(bf16)
 
     per_owner(tiles, value.shape[0], spill, run)
 
@@ -451,9 +451,10 @@
         pick = pick | matches[k]
     pick = pick.astype(bf16)
 
+    token_iota = lax.broadcasted_iota(jnp.int32, (slot_rows, tok_count), 1)
+    table = jnp.sum(jnp.where(pick > 0, token_iota + 1, 0), 1).astype(jnp.int32) - 1
+    table = exchange(table.reshape(owner_count, width))
     half = D // 8
-    dy_sent = matmul(pick, quarter_of(cotangent, 0)).astype(bf16)
-    dy_sent = to_experts(exchange(dy_sent.reshape(owner_count, width, -1)))
     lanes = lax.axis_size("tp")
     lane = lax.axis_index("tp")
     quarter = D // lanes
@@ -483,17 +484,16 @@
         2,
     )
     down_plain = jnp.pad(exdown_w, ((0, 0), (0, fill), (0, 0)))
-    down_w = jnp.pad(from_lane(exdown_w, 2), ((0, 0), (0, fill), (0, 0)))
     edge = owner_count * MAIN
     extra = slot_rows - 2 * edge
     span = edge + extra
     tile = 256 if edge % 256 == 0 else 128
     tiles = (edge // tile, extra // tile)
     big = 2 * (slot_rows + extra) * D * hid_wide
-    first_full, dy_sent, gateup_w, down_w, down_plain = lax.optimization_barrier(
-        (first_full, dy_sent, gateup_w, down_w, down_plain)
-    )
-    dy_all = lax.all_gather(after(dy_sent, first_full), "tp", axis=0, tiled=True)
+    first_full, table, gateup_w, down_plain = lax.optimization_barrier(
+        (first_full, table, gateup_w, down_plain)
+    )
+    dy_all = lax.all_gather(after(cotangent, first_full), "ep", axis=0, tiled=True)
     edges = [0]
     for cols in (q_cols, lat_cols, experts, kv_cols, out_cols, 128):
         edges.append(edges[-1] + cols)
@@ -562,17 +562,22 @@
     second_full = lax.all_gather(after(second_pack, dy_all, one), "ep", axis=0, tiled=True)
     own = (to_experts(one), to_experts(two))
     first = ring_gather_first(*own)
-    dy_all = after(dy_all, two)
+    pick_in = (
+        table[:, :, None] == lax.broadcasted_iota(jnp.int32, (owner_count, width, tok_count), 2)
+    ).astype(bf16)
+    dy_rows = jnp.einsum(
+        "ist,itd->isd",
+        pick_in,
+        after(dy_all, two).reshape(owner_count, tok_count, D),
+        preferred_element_type=f32,
+    )
+    dy_rows = to_experts(dy_rows.astype(bf16))
     (ex_dh,) = row_call(
         functools.partial(hidden_back_kernel, tiles, spill),
         tile,
         slot_rows,
-        (*[dy_all] * lanes, down_plain),
-        [
-            pl.BlockSpec((tile, quarter), lambda i, q=q: (q * (slot_rows // tile) + i, 0))
-            for q in range(lanes)
-        ]
-        + [whole_spec(down_plain.shape)],
+        (dy_rows, down_plain),
+        [tile_spec(tile, D), whole_spec(down_plain.shape)],
         [(hid_wide, f32)],
         big,
     )
@@ -595,14 +600,6 @@
     second_grad = second_grads(normed2, cotangent, sh_dboth, sh_hidden)
     second_sum = lax.psum_scatter(second_grad, "ep", scatter_dimension=0, tiled=True)
 
-    going, shared_part, sh_dnormed_part, second_grad = lax.optimization_barrier(
-        (first[:2], shared_part, sh_dnormed_part, second_grad)
-    )
-    first = (*going, *first[2:])
-    shared_q = sum_to_quarter(shared_part)
-    sh_dnormed_q = sum_to_quarter(sh_dnormed_part)
-    rows = ring_gather_parts(*own, first, ring_gather_second(first))
-
     logits = matmul(normed2, router_full)
     onehot = (
         expert_ids[:, :, None] == jnp.arange(experts, dtype=jnp.int32)[None, None, :]
@@ -617,6 +614,13 @@
     gate_rows = jnp.sum(gate_rows, 1).reshape(owner_count, width)
     gate_rows = to_experts(exchange(after(gate_rows, two)))[:, None]
 
+    going, ex_dh, gate_rows = lax.optimization_barrier((first[:2], ex_dh, gate_rows))
+    rows = ring_gather_parts(*own, (*going, *first[2:]), ring_gather_second(going))
+    ex_dh, shared_part, sh_dnormed_part, second_grad = lax.optimization_barrier(
+        (ex_dh, shared_part, sh_dnormed_part, second_grad)
+    )
+    shared_q = sum_to_quarter(shared_part)
+    sh_dnormed_q = sum_to_quarter(sh_dnormed_part)
     ex_hidden, ex_dboth, dgate_rows, *drow = row_call(
         functools.partial(hidden_kernel, tiles, spill),
         tile,
@@ -643,8 +647,7 @@
         return matmul_tn(expert_rows(left, e), kept)
 
     def grads_of_down(late):
-        wide_dy = after(dy_all, late).reshape(lanes, slot_rows, quarter)
-        wide_dy = jnp.concatenate([wide_dy[q] for q in range(lanes)], 1)
+        wide_dy = after(dy_rows, late)
         hidden = after(ex_hidden[:, :hid_cols], late)
         parts = []
         for e in range(EXP_DEV):
@@ -657,20 +660,24 @@
         back_two = exchange(from_experts(two, owner_count)).reshape(slot_rows, -1)
         return jnp.concatenate([matmul_tn(pick, back_one), matmul_tn(pick, back_two)], 1)
 
-    out_parts = row_call(
+    out_rows = pl.pallas_call(
         functools.partial(out_kernel, tiles, spill),
-        tile,
-        slot_rows,
-        (ex_hidden, down_w),
-        [tile_spec(tile, hid_wide), whole_spec(down_w.shape)],
-        [(half, bf16)] * 8,
-        big,
-    )
+        grid=(slot_rows // tile,),
+        in_specs=[tile_spec(tile, hid_wide), whole_spec(down_plain.shape)],
+        out_specs=pl.BlockSpec((lanes, tile, quarter), lambda i: (0, i, 0)),
+        out_shape=jax.ShapeDtypeStruct((lanes, slot_rows, quarter), bf16),
+        cost_estimate=pl.CostEstimate(
+            flops=big, bytes_accessed=3 * slot_rows * D, transcendentals=0
+        ),
+        compiler_params=pltpu.CompilerParams(
+            dimension_semantics=("arbitrary",), vmem_limit_bytes=VMEM_BYTES
+        ),
+    )(ex_hidden, down_plain).reshape(lanes * slot_rows, quarter)
     top = shift(drow[4], 1)
     bottom = shift(drow[5], 3)
     dgate_rows = exchange(from_experts(dgate_rows[:, 0], owner_count)).reshape(-1)
-    top, bottom, dgate_rows, out_parts = lax.optimization_barrier(
-        (top, bottom, dgate_rows, out_parts)
+    top, bottom, dgate_rows, out_rows = lax.optimization_barrier(
+        (top, bottom, dgate_rows, out_rows)
     )
     from_prev_one = shift(plus(drow[2], top), 1)
     from_next_one = shift(after(drow[6], bottom), 3)
@@ -682,9 +689,8 @@
     drow_one = add_three(drow[0], from_prev_one, from_next_one)
     drow_two = add_three(drow[1], from_prev_two, from_next_two)
     routed_grad_q = bring_back(drow_one, drow_two)
-    out_far = after(tuple(out_parts[4:6]), drow_two)
-    out_top = shift(out_far[0], 1)
-    out_bottom = shift(out_far[1], 3)
+    out_rows = after(out_rows, drow_one, second_sum)
+    out_sum = lax.psum_scatter(out_rows, "tp", scatter_dimension=0, tiled=True)
 
     dgate_part = jnp.stack(
         [jnp.sum(jnp.where(matches[k], dgate_rows[:, None], 0.0), 0) for k in range(TOPK)], 1
@@ -720,9 +726,6 @@
     dkey_part = jnp.sum(dkey_all[..., DN:], 1)
     dlat_part = jnp.concatenate([dlatent_part, dkey_part], 1).astype(bf16)
     dlat_sum = sum_small(dlat_part)
-    dlat_sum, second_sum, out_top, out_bottom = lax.optimization_barrier(
-        (dlat_sum, second_sum, out_top, out_bottom)
-    )
     dlatent, latnorm_grad = rms_back(latent, lat_scale, lat_weight, dlat_sum[:, :KVR])
     dlatent_all = jnp.concatenate(
         [dlatent, rotate(dlat_sum[:, KVR:], cos_tab, -sine_tab)], -1
@@ -749,25 +752,12 @@
         attended,
         latent_n,
         dkeyval,
-        gain_grads.astype(bf16),
-    )
-    out_late = after((*out_parts, out_top, out_bottom), first_grad)
-    out_prev_one = shift(plus(out_late[2], out_late[8]), 1)
-    out_next_one = shift(out_late[6], 3)
-    out_prev_two, out_next_two = after(
-        (out_late[3], plus(out_late[7], out_late[9])), out_prev_one, out_next_one
-    )
-    out_prev_two = shift(out_prev_two, 1)
-    out_next_two = shift(out_next_two, 3)
-    out_one = add_three(out_parts[0], out_prev_one, out_next_one)
-    out_two = add_three(out_parts[1], out_prev_two, out_next_two)
-    back_one = exchange(from_experts(out_one, owner_count))
-    out_two = after(out_two, back_one)
-    back_two = exchange(from_experts(out_two, owner_count))
-    routed_q = jnp.concatenate(
-        [matmul_tn(pick, b.reshape(slot_rows, -1)) for b in (back_one, back_two)], 1
-    )
-    late_dquery, late_dlat = after((dquery, dlatent_all), out_prev_one, out_next_one)
+        after(gain_grads.astype(bf16), out_sum),
+    )
+    late = shift(first_grad[:16, :128], 1)
+    back = exchange(from_experts(after(out_sum, late), owner_count)).reshape(slot_rows, -1)
+    routed_q = matmul_tn(pick, back)
+    late_dquery, late_dlat = after((dquery, dlatent_all), late)
     dnormed_q = sum_to_quarter(matmul_nt(late_dquery, query_full))
     dnormed = gather_quarters(dnormed_q.astype(bf16)).astype(f32) + matmul_nt(
         late_dlat, latent_full
@@ -775,9 +765,9 @@
     dtokens, prenorm_grad = rms_back(resid_in, pre_scale, pre_weight, dnormed)
     tokens_grad = (dmid + dtokens).astype(bf16)
     prenorm_sum = jnp.sum(exchange(prenorm_grad.reshape(owner_count, shard)), 0)
-    down_grad = grads_of_down(back_one)
-    all_rows = jnp.concatenate(after(rows, back_one), 1)
-    late_dboth = after(ex_dboth, back_one)
+    down_grad = grads_of_down(late)
+    all_rows = jnp.concatenate(after(rows, late), 1)
+    late_dboth = after(ex_dboth, late)
     exgate_grad = jnp.stack(
         [grads_of(e, all_rows, late_dboth, slice(0, hid_cols)) for e in range(EXP_DEV)]
     )

time: 770 us -> 735 us (0.955)
  other arithmetic: 88.4 us -> 66.4 us
  blocking collectives: 12.6 us -> 0 us
  matrix products: 82.6 us -> 93.4 us
  local copies, waits for them, and re-layouts: 122 us -> 113 us
  waiting for transfers between devices: 244 us -> 252 us
    dot_general x0 -> x1, matrix products: none -> 15.6 us  [per_device(): jnp.einsum('ist,itd->isd', pick_in, after(dy_all, two).reshape(owner_coun...]
    all_to_all x1 -> x0, blocking collectives: 12.6 us -> none  [exchange(): return lax.all_to_all(value, 'ep', 0, 0, tiled=True)]
    all_to_all x9, waiting for transfers between devices: 55.5 us -> 43.1 us  [exchange(): return lax.all_to_all(value, 'ep', 0, 0, tiled=True)]
    pallas_call x3 -> x2, Pallas kernels: 52 us -> 40.4 us  [row_call(): pl.pallas_call(body, grid=(total // tile,), in_specs=in_specs, out_specs=...]
    ppermute x48 -> x43, waiting for transfers between devices: 137 us -> 148 us  [shift(): lax.ppermute(value, 'tp', [(i, (i + step) % lanes) for i in range(lanes)])]
    pallas_call x0 -> x1, Pallas kernels: none -> 9.29 us  [per_device(): pl.pallas_call(functools.partial(out_kernel, tiles, spill), grid=(slot_ro...]
    all_gather x1, waiting for transfers between devices: 26.4 us -> 35 us  [per_device(): lax.all_gather(after(second_pack, dy_all, one), 'ep', axis=0, tiled=True)]
    ppermute x48 -> x43, starting transfers between devices: 74.7 us -> 68.3 us  [shift(): lax.ppermute(value, 'tp', [(i, (i + step) % lanes) for i in range(lanes)])]
  transfers between devices with their start and end apart: 62 -> 58, of which waited for: 29 -> 32; matrix products, arithmetic and copies ran while one was open for 31% -> 31% of each run, Pallas kernels for 8% -> 7%
where the time goes in v5:
time: 735 us; the launch traced here: 729 us
  waiting for transfers between devices  252 us (34%)
  starting transfers between devices  123 us (17%)
  local copies, waits for them, and re-layouts  113 us (15%)
  matrix products  93.4 us (13%)
  other arithmetic  66.4 us (9%)
  Pallas kernels  64.3 us (9%)
  between operations  16.7 us (2%)
    ppermute x43, waiting for transfers between devices, shift(): lax.ppermute(value, 'tp', [(i, (i + step) % lanes) for i in range(lanes)])  148 us
    ppermute x43, starting transfers between devices, shift(): lax.ppermute(value, 'tp', [(i, (i + step) % lanes) for i in range(lanes)])  68.3 us
    all_to_all x9, starting transfers between devices, exchange(): return lax.all_to_all(value, 'ep', 0, 0, tiled=True)  54.6 us
    unnamed x309, local copies, waits for them, and re-layouts  51.3 us
    all_to_all x9, waiting for transfers between devices, exchange(): return lax.all_to_all(value, 'ep', 0, 0, tiled=True)  43.1 us
    pallas_call x2, Pallas kernels, row_call(): pl.pallas_call(body, grid=(total // tile,), in_specs=in_specs, out_specs=...  40.4 us
    all_gather x1, waiting for transfers between devices, per_device(): lax.all_gather(after(second_pack, dy_all, one), 'ep', axis=0, tiled=True)  35 us
    dot_general x9, matrix products, matmul_tn(): lax.dot_general(left_mat, right_mat, (((0,), (0,)), ((), ())), preferred_...  30 us
  transfers between devices with their start and end apart: 58, of which 32 were waited for; matrix products, arithmetic and copies ran while one was open for 31% of the time, Pallas kernels for 7%

profile of v5, /device:TPU:0, one launch (start us, length us, event | category | flops | bytes accessed | tf_op | source)
XLA Modules:
  0.0 729.0 jit_solution(2789290896319374160)
XLA Ops:
  15.1 7.4 %all-to-all-start = ((s32[32,1,72]{2,1,0:T(1,128)}), s32[32,1,72]{2,1,0:T(1,128)S(1)}, u32[]{:S(2)}, u32[]{:S(2)}) async-start(s32[32,1,72]{2,1,0:T(1,128)} %sub.102), calls=%async_computation | async-start | bytes 32768 | tf_op jit(solution)/shard_map/all_to_all | solution.py:119
  22.8 4.8 constant_dynamic-slice_fusion.31
  45.2 24.1 %all-gather.4.cloned.1.call-done = bf16[2048,2304]{1,0:T(8,128)(2,1)} async-done(((bf16[64,2304]{1,0:T(8,128)(2,1)}), bf16[2048,2304]{1,0:T(8,128)(2,1)}) %all-gather.4.cloned.1.call-update) | async-done | bytes 9437200 | tf_op jit(solution)/shard_map/all_gather | solution.py:439
  79.4 3.8 fusion.55
  117.2 5.1 collective-permute-done.2
  130.0 5.5 collective-permute-done.4
  141.4 5.1 all-to-all-start.1
  147.4 26.1 %all-to-all-done.1 = bf16[32,72,256]{2,1,0:T(8,128)(2,1)} async-done(((bf16[32,72,256]{2,1,0:T(8,128)(2,1)}), bf16[32,72,256]{2,1,0:T(8,128)(2,1)}, u32[]{:S(2)}, u32[]{:S(2)}) %all-to-all-start.1) | async-done | bytes 1179680 | tf_op jit(solution)/shard_map/all_to_all | solution.py:119
  175.0 6.2 all-to-all-start.2
  185.9 15.5 %all-to-all-done.2 = bf16[32,72,256]{2,1,0:T(8,128)(2,1)} async-done(((bf16[32,72,256]{2,1,0:T(8,128)(2,1)}), bf16[32,72,256]{2,1,0:T(8,128)(2,1)}, u32[]{:S(2)}, u32[]{:S(2)}) %all-to-all-start.2) | async-done | bytes 1179680 | tf_op jit(solution)/shard_map/all_to_all | solution.py:119
  201.5 35.0 %all-gather.8.cloned.1.call-done = bf16[2048,2112]{1,0:T(8,128)(2,1)} async-done(((bf16[64,2112]{1,0:T(8,128)(2,1)}), bf16[2048,2112]{1,0:T(8,128)(2,1)}) %all-gather.8.cloned.1.call-update) | async-done | bytes 8650768 | tf_op jit(solution)/shard_map/all_gather | solution.py:562
  236.5 4.3 fusion.15
  243.8 6.8 shard_map.307
  258.0 5.5 all-to-all-start.3
  271.2 15.6 %convolution_convert_fusion = bf16[32,72,2048]{2,1,0:T(8,128)(2,1)} fusion(bf16[32,192,2048]{2,1,0:T(8,128)(2,1)} %bitcast.144, s32[32,72]{1,0:T(8,128)S(1)} %bitcast.168), kind=kOutput, calls=%fused_computation.31 | convolution fusion | flops 1817100288 | bytes 34612224 | tf_op jit(solution)/shard_map/ist,itd->isd/dot_general | solution.py:568
  288.1 4.3 fusion.191
  292.4 4.3 pad_maximum_fusion.refs_0_
  296.6 11.0 %shard_map.306.refs_9_ = f32[2304,384]{1,0:T(8,128)S(1)} custom-call(bf16[2304,2048]{1,0:T(8,128)(2,1)} %pad_maximum_fusion.refs_0_, bf16[2,384,2048]{2,1,0:T(8,128)(2,1)S(1)} %pad.41.refs_1_.weight), custom_call_target="tpu_custom_call" | custom-call | flops 4026531840 | bytes 16121856 | tf_op jit(solution)/shard_map/pallas_call | solution.py:278
  314.1 4.2 fusion.60
  318.2 5.7 fusion.63
  323.9 13.6 %collective-permute-done.10.refs_5_ = bf16[2304,256]{1,0:T(8,128)(2,1)} collective-permute-done((bf16[2304,256]{1,0:T(8,128)(2,1)}, bf16[2304,256]{1,0:T(8,128)(2,1)}, u32[]{:S(2)}, u32[]{:S(2)}) %collective-permute-start.10) | collective-permute-done | bytes 1179680 | tf_op jit(solution)/shard_map/ppermute | solution.py:78
  337.5 3.4 collective-permute-done.9.refs_4_
  340.9 29.3 %shard_map.308 = (bf16[2304,384]{1,0:T(8,128)(2,1)}, bf16[2304,768]{1,0:T(8,128)(2,1)}, f32[2304,1]{1,0:T(8,128)S(1)}, bf16[2304,256]{1,0:T(8,128)(2,1)S(1)}, bf...) custom-call(bf16[2304,256]{1,0:T(8,128)(2,1)} %pad_maximum_fusion.6., ...), custom_call_target="tpu_custom_call" | custom-call | flops 16106127360 | bytes 34031616 | tf_op jit(solution)/shard_map/pallas_call | solution.py:278
  375.5 3.5 collective-permute-start.13
  381.2 5.4 all-to-all-start.4
  388.2 9.3 %shard_map.309 = bf16[4,2304,512]{2,1,0:T(8,128)(2,1)} custom-call(bf16[2304,384]{1,0:T(8,128)(2,1)S(1)} %copy-done.28, bf16[2,384,2048]{2,1,0:T(8,128)(2,1)S(1)} %pad.41.refs_1_.weight), custom_call_target="tpu_custom_call" | custom-call | flops 4026531840 | bytes 14155776 | tf_op jit(solution)/shard_map/pallas_call | solution.py:663
  399.3 3.5 collective-permute-done.12
  408.1 20.3 %collective-permute-done.15 = bf16[2304,256]{1,0:T(8,128)(2,1)S(1)} collective-permute-done((bf16[2304,256]{1,0:T(8,128)(2,1)}, bf16[2304,256]{1,0:T(8,128)(2,1)S(1)}, u32[]{:S(2)}, u32[]{:S(2)}) %collective-permute-start.15) | collective-permute-done | bytes 1179680 | tf_op jit(solution)/shard_map/ppermute | solution.py:78
  428.5 5.2 collective-permute-done.14
  438.2 3.2 collective-permute-start.17
  443.8 5.6 all-to-all-start.5
  449.4 38.3 %collective-permute-done.16 = bf16[2304,256]{1,0:T(8,128)(2,1)} collective-permute-done((bf16[2304,256]{1,0:T(8,128)(2,1)S(1)}, bf16[2304,256]{1,0:T(8,128)(2,1)}, u32[]{:S(2)}, u32[]{:S(2)}) %collective-permute-start.16) | collective-permute-done | bytes 1179680 | tf_op jit(solution)/shard_map/ppermute | solution.py:78
  492.8 4.6 all-to-all-start.6
  500.0 3.4 collective-permute-start.25
  518.3 8.9 %collective-permute-done.20 = bf16[192,512]{1,0:T(8,128)(2,1)} collective-permute-done((bf16[192,512]{1,0:T(8,128)(2,1)}, bf16[192,512]{1,0:T(8,128)(2,1)}, u32[]{:S(2)}, u32[]{:S(2)}) %collective-permute-start.20) | collective-permute-done | bytes 196640 | tf_op jit(solution)/shard_map/ppermute | solution.py:78
  534.3 8.7 %collective-permute-done.23 = bf16[192,512]{1,0:T(8,128)(2,1)S(1)} collective-permute-done((bf16[192,512]{1,0:T(8,128)(2,1)S(1)}, bf16[192,512]{1,0:T(8,128)(2,1)S(1)}, u32[]{:S(2)}, u32[]{:S(2)}) %collective-permute-start.23) | collective-permute-done | bytes 196640 | tf_op jit(solution)/shard_map/ppermute | solution.py:78
  543.0 5.5 collective-permute-done.22
  589.7 7.9 %shard_map.310 = bf16[2048,2304]{1,0:T(8,128)(2,1)} custom-call(bf16[192,2048]{1,0:T(8,128)(2,1)S(1)} %copy-done.8, bf16[192,2048]{1,0:T(8,128)(2,1)S(1)} %copy-done.4, bf16[192,2048]{1,0:T(8,128)(2,1)S(1)} %fusion.184.dmid, bf16[192,768]{1,0:T(8,128)(2,1)S(1)} %copy-done.20, bf16[192,640]{1,0:T(8,128)(2,1)S(1)} %copy-done.22, ...), custom_call_target="tpu_custom_call" | custom-call | flops 1811939328 | bytes 14155776 | tf_op jit(solution)/shard_map/pallas_call | solution.py:343
  610.6 7.5 %all-to-all-start.7 = ((bf16[32,72,512]{2,1,0:T(8,128)(2,1)}), bf16[32,72,512]{2,1,0:T(8,128)(2,1)}, u32[]{:S(2)}, u32[]{:S(2)}) async-start(bf16[32,72,512]{2,1,0:T(8,128)(2,1)} %pad_maximum_fusion.5), calls=%async_computation.9 | async-start | bytes 4718592 | tf_op jit(solution)/shard_map/all_to_all | solution.py:119
  618.1 3.2 fusion.57
  640.7 4.9 fusion.40
  654.6 4.8 fusion.31
  659.5 5.1 fusion.37
  675.3 4.0 collective-permute-done.42
  681.9 3.2 fusion.88
  688.5 7.4 %all-to-all-start.8 = ((f32[32,1,64]{2,1,0:T(1,128)}), f32[32,1,64]{2,1,0:T(1,128)S(1)}, u32[]{:S(2)}, u32[]{:S(2)}) async-start(f32[32,1,64]{2,1,0:T(1,128)} %all_to_all.53), calls=%async_computation.10 | async-start | bytes 32768 | tf_op jit(solution)/shard_map/all_to_all | solution.py:119
  696.0 3.5 add_convert_fusion.5
  708.3 3.8 collective-permute-done.36
  (589 shorter events, 285.2 us)
Async XLA Ops:
  7.2 62.0 %all-gather.4.cloned.1.call-start = ((), (), s32[]{:S(2)}) async-start(), calls=%async_computation.12 | async-start | bytes 9732096 | tf_op jit(solution)/shard_map/all_gather | solution.py:439
  15.1 30.0 %all-to-all-start = ((s32[32,1,72]{2,1,0:T(1,128)}), s32[32,1,72]{2,1,0:T(1,128)S(1)}, u32[]{:S(2)}, u32[]{:S(2)}) async-start(s32[32,1,72]{2,1,0:T(1,128)} %sub.102), calls=%async_computation | async-start | bytes 32768 | tf_op jit(solution)/shard_map/all_to_all | solution.py:119
  22.5 152.4 %all-gather.6.cloned.1.call-start = ((), (), s32[]{:S(2)}) async-start(), calls=%async_computation.13 | async-start | bytes 25952256 | tf_op jit(solution)/shard_map/all_gather | solution.py:496
  110.1 12.2 %collective-permute-start.2 = (bf16[192,512]{1,0:T(8,128)(2,1)S(1)}, bf16[192,512]{1,0:T(8,128)(2,1)S(1)}, u32[]{:S(2)}, u32[]{:S(2)}) collective-permute-start(bf16[192,512]{1,0:T(8,128)(2,1)S(1)} %get-tuple-element.203), channel_id=1, source_target_pairs={{0,2},{1,3},{2,0},{3,1},{4,6},{5,7},{6,4},{7,5},{8,10},{9,11},{10,... | collective-permute-start | bytes 589832 | tf_op jit(solution)/shard_map/ppermute | solution.py:78
  123.9 11.6 %collective-permute-start.4 = (bf16[192,512]{1,0:T(8,128)(2,1)S(1)}, bf16[192,512]{1,0:T(8,128)(2,1)}, u32[]{:S(2)}, u32[]{:S(2)}) collective-permute-start(bf16[192,512]{1,0:T(8,128)(2,1)S(1)} %add_convert_fusion.7), channel_id=1, source_target_pairs={{0,2},{1,3},{2,0},{3,1},{4,6},{5,7},{6,4},{7,5},{8,10},{9,11},{10,... | collective-permute-start | bytes 589832 | tf_op jit(solution)/shard_map/ppermute | solution.py:78
  141.4 32.1 %all-to-all-start.1 = ((bf16[32,72,256]{2,1,0:T(8,128)(2,1)}), bf16[32,72,256]{2,1,0:T(8,128)(2,1)}, u32[]{:S(2)}, u32[]{:S(2)}) async-start(bf16[32,72,256]{2,1,0:T(8,128)(2,1)} %get-tuple-element.159), calls=%async_computation.1 | async-start | bytes 2359296 | tf_op jit(solution)/shard_map/all_to_all | solution.py:119
  146.5 90.0 %all-gather.8.cloned.1.call-start = ((), (), s32[]{:S(2)}) async-start(), calls=%async_computation.14 | async-start | bytes 9191424 | tf_op jit(solution)/shard_map/all_gather | solution.py:562
  175.0 26.4 %all-to-all-start.2 = ((bf16[32,72,256]{2,1,0:T(8,128)(2,1)}), bf16[32,72,256]{2,1,0:T(8,128)(2,1)}, u32[]{:S(2)}, u32[]{:S(2)}) async-start(bf16[32,72,256]{2,1,0:T(8,128)(2,1)} %get-tuple-element.69), calls=%async_computation.2 | async-start | bytes 2359296 | tf_op jit(solution)/shard_map/all_to_all | solution.py:119
  181.2 253.0 %reduce-scatter.4.cloned.1.call-start = ((), (), s32[]{:S(2)}) async-start(), calls=%async_computation.15 | async-start | bytes 9191424 | tf_op jit(solution)/shard_map/reduce_scatter | solution.py:601
  254.7 54.7 %collective-permute-start.7 = (bf16[2304,256]{1,0:T(8,128)(2,1)}, bf16[2304,256]{1,0:T(8,128)(2,1)}, u32[]{:S(2)}, u32[]{:S(2)}) collective-permute-start(bf16[2304,256]{1,0:T(8,128)(2,1)} %pad_maximum_fusion.6.refs_0_), channel_id=1, source_target_pairs={{0,1},{1,2},{2,3},{3,0},{4,5},{5,6},{6,7},{7,4},{8,9},{9,10},{10,1... | collective-permute-start | bytes 3538952 | tf_op jit(solution)/shard_map/ppermute | solution.py:78
  256.3 67.6 %collective-permute-start.6 = (bf16[2304,256]{1,0:T(8,128)(2,1)}, bf16[2304,256]{1,0:T(8,128)(2,1)}, u32[]{:S(2)}, u32[]{:S(2)}) collective-permute-start(bf16[2304,256]{1,0:T(8,128)(2,1)} %pad_maximum_fusion.6.refs_0_), channel_id=1, source_target_pairs={{0,3},{1,0},{2,1},{3,2},{4,7},{5,4},{6,5},{7,6},{8,11},{9,8},{10,9... | collective-permute-start | bytes 3538952 | tf_op jit(solution)/shard_map/ppermute | solution.py:78
  258.0 12.8 %all-to-all-start.3 = ((f32[32,1,72]{2,1,0:T(1,128)}), f32[32,1,72]{2,1,0:T(1,128)S(1)}, u32[]{:S(2)}, u32[]{:S(2)}) async-start(f32[32,1,72]{2,1,0:T(1,128)} %bitcast.34), calls=%async_computation.3 | async-start | bytes 32768 | tf_op jit(solution)/shard_map/all_to_all | solution.py:119
  266.9 57.0 %collective-permute-start.11 = (bf16[2304,256]{1,0:T(8,128)(2,1)}, bf16[2304,256]{1,0:T(8,128)(2,1)}, u32[]{:S(2)}, u32[]{:S(2)}) collective-permute-start(bf16[2304,256]{1,0:T(8,128)(2,1)} %pad_maximum_fusion.7.refs_1_), channel_id=1, source_target_pairs={{0,1},{1,2},{2,3},{3,0},{4,5},{5,6},{6,7},{7,4},{8,9},{9,10},{10,1... | collective-permute-start | bytes 3538952 | tf_op jit(solution)/shard_map/ppermute | solution.py:78
  267.2 42.5 %collective-permute-start.8 = (bf16[2304,256]{1,0:T(8,128)(2,1)}, bf16[2304,256]{1,0:T(8,128)(2,1)}, u32[]{:S(2)}, u32[]{:S(2)}) collective-permute-start(bf16[2304,256]{1,0:T(8,128)(2,1)} %pad_maximum_fusion.7.refs_1_), channel_id=1, source_target_pairs={{0,3},{1,0},{2,1},{3,2},{4,7},{5,4},{6,5},{7,6},{8,11},{9,8},{10,9... | collective-permute-start | bytes 3538952 | tf_op jit(solution)/shard_map/ppermute | solution.py:78
  309.7 27.8 %collective-permute-start.10 = (bf16[2304,256]{1,0:T(8,128)(2,1)}, bf16[2304,256]{1,0:T(8,128)(2,1)}, u32[]{:S(2)}, u32[]{:S(2)}) collective-permute-start(bf16[2304,256]{1,0:T(8,128)(2,1)} %collective-permute-done.8.refs_3_), channel_id=1, source_target_pairs={{0,3},{1,0},{2,1},{3,2},{4,7},{5,4},{6,5},{7,6},{8,11},{9,8},{10,9... | collective-permute-start | bytes 3538952 | tf_op jit(solution)/shard_map/ppermute | solution.py:78
  312.6 28.3 %collective-permute-start.9 = (bf16[2304,256]{1,0:T(8,128)(2,1)}, bf16[2304,256]{1,0:T(8,128)(2,1)}, u32[]{:S(2)}, u32[]{:S(2)}) collective-permute-start(bf16[2304,256]{1,0:T(8,128)(2,1)} %collective-permute-done.7.refs_6_), channel_id=1, source_target_pairs={{0,1},{1,2},{2,3},{3,0},{4,5},{5,6},{6,7},{7,4},{8,9},{9,10},{10,1... | collective-permute-start | bytes 3538952 | tf_op jit(solution)/shard_map/ppermute | solution.py:78
  375.5 27.3 %collective-permute-start.12 = (bf16[2304,256]{1,0:T(8,128)(2,1)}, bf16[2304,256]{1,0:T(8,128)(2,1)}, u32[]{:S(2)}, u32[]{:S(2)}) collective-permute-start(bf16[2304,256]{1,0:T(8,128)(2,1)} %get-tuple-element.84), channel_id=1, source_target_pairs={{0,1},{1,2},{2,3},{3,0},{4,5},{5,6},{6,7},{7,4},{8,9},{9,10},{10,1... | collective-permute-start | bytes 3538952 | tf_op jit(solution)/shard_map/ppermute | solution.py:78
  375.5 27.3 %collective-permute-start.13 = (bf16[2304,256]{1,0:T(8,128)(2,1)}, bf16[2304,256]{1,0:T(8,128)(2,1)}, u32[]{:S(2)}, u32[]{:S(2)}) collective-permute-start(bf16[2304,256]{1,0:T(8,128)(2,1)} %get-tuple-element.85), channel_id=1, source_target_pairs={{0,3},{1,0},{2,1},{3,2},{4,7},{5,4},{6,5},{7,6},{8,11},{9,8},{10,9... | collective-permute-start | bytes 3538952 | tf_op jit(solution)/shard_map/ppermute | solution.py:78
  381.2 16.2 %all-to-all-start.4 = ((f32[32,1,72]{2,1,0:T(1,128)}), f32[32,1,72]{2,1,0:T(1,128)S(1)}, u32[]{:S(2)}, u32[]{:S(2)}) async-start(f32[32,1,72]{2,1,0:T(1,128)} %bitcast.38), calls=%async_computation.4 | async-start | bytes 32768 | tf_op jit(solution)/shard_map/all_to_all | solution.py:119
  386.6 197.4 %reduce-scatter.6.cloned.1.call-start = ((), (), s32[]{:S(2)}) async-start(), calls=%async_computation.16 | async-start | bytes 11796480 | tf_op jit(solution)/shard_map/reduce_scatter | solution.py:693
  402.8 25.6 %collective-permute-start.15 = (bf16[2304,256]{1,0:T(8,128)(2,1)}, bf16[2304,256]{1,0:T(8,128)(2,1)S(1)}, u32[]{:S(2)}, u32[]{:S(2)}) collective-permute-start(bf16[2304,256]{1,0:T(8,128)(2,1)} %copy-done.27), channel_id=1, source_target_pairs={{0,3},{1,0},{2,1},{3,2},{4,7},{5,4},{6,5},{7,6},{8,11},{9,8},{10,9... | collective-permute-start | bytes 3538952 | tf_op jit(solution)/shard_map/ppermute | solution.py:78
  408.0 25.6 %collective-permute-start.14 = (bf16[2304,256]{1,0:T(8,128)(2,1)S(1)}, bf16[2304,256]{1,0:T(8,128)(2,1)S(1)}, u32[]{:S(2)}, u32[]{:S(2)}) collective-permute-start(bf16[2304,256]{1,0:T(8,128)(2,1)S(1)} %add_convert_fusion.3), channel_id=1, source_target_pairs={{0,1},{1,2},{2,3},{3,0},{4,5},{5,6},{6,7},{7,4},{8,9},{9,10},{10,1... | collective-permute-start | bytes 3538952 | tf_op jit(solution)/shard_map/ppermute | solution.py:78
  438.2 49.6 %collective-permute-start.16 = (bf16[2304,256]{1,0:T(8,128)(2,1)S(1)}, bf16[2304,256]{1,0:T(8,128)(2,1)}, u32[]{:S(2)}, u32[]{:S(2)}) collective-permute-start(bf16[2304,256]{1,0:T(8,128)(2,1)S(1)} %copy-done.26), channel_id=1, source_target_pairs={{0,1},{1,2},{2,3},{3,0},{4,5},{5,6},{6,7},{7,4},{8,9},{9,10},{10,1... | collective-permute-start | bytes 3538952 | tf_op jit(solution)/shard_map/ppermute | solution.py:78
  438.2 51.3 %collective-permute-start.17 = (bf16[2304,256]{1,0:T(8,128)(2,1)}, bf16[2304,256]{1,0:T(8,128)(2,1)}, u32[]{:S(2)}, u32[]{:S(2)}) collective-permute-start(bf16[2304,256]{1,0:T(8,128)(2,1)} %add_convert_fusion.1), channel_id=1, source_target_pairs={{0,3},{1,0},{2,1},{3,2},{4,7},{5,4},{6,5},{7,6},{8,11},{9,8},{10,9... | collective-permute-start | bytes 3538952 | tf_op jit(solution)/shard_map/ppermute | solution.py:78
  443.8 49.0 %all-to-all-start.5 = ((bf16[32,72,256]{2,1,0:T(8,128)(2,1)}), bf16[32,72,256]{2,1,0:T(8,128)(2,1)S(1)}, u32[]{:S(2)}, u32[]{:S(2)}) async-start(bf16[32,72,256]{2,1,0:T(8,128)(2,1)} %pad_maximum_fusion.8), calls=%async_computation.7 | async-start | bytes 2359296 | tf_op jit(solution)/shard_map/all_to_all | solution.py:119
  492.8 23.0 %all-to-all-start.6 = ((bf16[32,72,256]{2,1,0:T(8,128)(2,1)}), bf16[32,72,256]{2,1,0:T(8,128)(2,1)S(1)}, u32[]{:S(2)}, u32[]{:S(2)}) async-start(bf16[32,72,256]{2,1,0:T(8,128)(2,1)} %pad_maximum_fusion.9), calls=%async_computation.8 | async-start | bytes 2359296 | tf_op jit(solution)/shard_map/all_to_all | solution.py:119
  497.5 216.3 %reduce-scatter.8.cloned.1.call-start = ((), (), s32[]{:S(2)}) async-start(), calls=%async_computation.17 | async-start | bytes 9732096 | tf_op jit(solution)/shard_map/reduce_scatter | solution.py:784
  500.0 10.2 %collective-permute-start.25 = (f32[192,6]{0,1:T(8,128)}, f32[192,6]{0,1:T(8,128)S(1)}, u32[]{:S(2)}, u32[]{:S(2)}) collective-permute-start(f32[192,6]{0,1:T(8,128)} %stack.78), channel_id=1, source_target_pairs={{0,3},{1,0},{2,1},{3,2},{4,7},{5,4},{6,5},{7,6},{8,11},{9,8},{10,9... | collective-permute-start | bytes 13832 | tf_op jit(solution)/shard_map/ppermute | solution.py:78
  505.1 13.2 %collective-permute-start.18 = (bf16[192,512]{1,0:T(8,128)(2,1)}, bf16[192,512]{1,0:T(8,128)(2,1)S(1)}, u32[]{:S(2)}, u32[]{:S(2)}) collective-permute-start(bf16[192,512]{1,0:T(8,128)(2,1)} %get-tuple-element.192), channel_id=1, source_target_pairs={{0,1},{1,2},{2,3},{3,0},{4,5},{5,6},{6,7},{7,4},{8,9},{9,10},{10,1... | collective-permute-start | bytes 589832 | tf_op jit(solution)/shard_map/ppermute | solution.py:78
  507.1 20.1 %collective-permute-start.20 = (bf16[192,512]{1,0:T(8,128)(2,1)}, bf16[192,512]{1,0:T(8,128)(2,1)}, u32[]{:S(2)}, u32[]{:S(2)}) collective-permute-start(bf16[192,512]{1,0:T(8,128)(2,1)} %get-tuple-element.193), channel_id=1, source_target_pairs={{0,2},{1,3},{2,0},{3,1},{4,6},{5,7},{6,4},{7,5},{8,10},{9,11},{10,... | collective-permute-start | bytes 589832 | tf_op jit(solution)/shard_map/ppermute | solution.py:78
  508.9 18.4 %collective-permute-start.19 = (bf16[192,512]{1,0:T(8,128)(2,1)S(1)}, bf16[192,512]{1,0:T(8,128)(2,1)}, u32[]{:S(2)}, u32[]{:S(2)}) collective-permute-start(bf16[192,512]{1,0:T(8,128)(2,1)S(1)} %get-tuple-element.194), channel_id=1, source_target_pairs={{0,3},{1,0},{2,1},{3,2},{4,7},{5,4},{6,5},{7,6},{8,11},{9,8},{10,9... | collective-permute-start | bytes 589832 | tf_op jit(solution)/shard_map/ppermute | solution.py:78
  528.5 14.5 %collective-permute-start.23 = (bf16[192,512]{1,0:T(8,128)(2,1)S(1)}, bf16[192,512]{1,0:T(8,128)(2,1)S(1)}, u32[]{:S(2)}, u32[]{:S(2)}) collective-permute-start(bf16[192,512]{1,0:T(8,128)(2,1)S(1)} %fusion.138), channel_id=1, source_target_pairs={{0,1},{1,2},{2,3},{3,0},{4,5},{5,6},{6,7},{7,4},{8,9},{9,10},{10,1... | collective-permute-start | bytes 589832 | tf_op jit(solution)/shard_map/ppermute | solution.py:78
  528.6 19.9 %collective-permute-start.22 = (bf16[192,512]{1,0:T(8,128)(2,1)S(1)}, bf16[192,512]{1,0:T(8,128)(2,1)S(1)}, u32[]{:S(2)}, u32[]{:S(2)}) collective-permute-start(bf16[192,512]{1,0:T(8,128)(2,1)S(1)} %fusion.138), channel_id=1, source_target_pairs={{0,2},{1,3},{2,0},{3,1},{4,6},{5,7},{6,4},{7,5},{8,10},{9,11},{10,... | collective-permute-start | bytes 589832 | tf_op jit(solution)/shard_map/ppermute | solution.py:78
  530.7 19.7 %collective-permute-start.21 = (bf16[192,512]{1,0:T(8,128)(2,1)S(1)}, bf16[192,512]{1,0:T(8,128)(2,1)S(1)}, u32[]{:S(2)}, u32[]{:S(2)}) collective-permute-start(bf16[192,512]{1,0:T(8,128)(2,1)S(1)} %fusion.138), channel_id=1, source_target_pairs={{0,3},{1,0},{2,1},{3,2},{4,7},{5,4},{6,5},{7,6},{8,11},{9,8},{10,9... | collective-permute-start | bytes 589832 | tf_op jit(solution)/shard_map/ppermute | solution.py:78
  562.2 10.4 %collective-permute-start.29 = (bf16[192,576]{1,0:T(8,128)(2,1)S(1)}, bf16[192,576]{1,0:T(8,128)(2,1)S(1)}, u32[]{:S(2)}, u32[]{:S(2)}) collective-permute-start(bf16[192,576]{1,0:T(8,128)(2,1)S(1)} %pad_maximum_fusion.21), channel_id=1, source_target_pairs={{0,2},{1,3},{2,0},{3,1},{4,6},{5,7},{6,4},{7,5},{8,10},{9,11},{10,... | collective-permute-start | bytes 663560 | tf_op jit(solution)/shard_map/ppermute | solution.py:78
  599.5 96.4 %collective-permute-start.31 = (bf16[192,512]{1,0:T(8,128)(2,1)}, bf16[192,512]{1,0:T(8,128)(2,1)}, u32[]{:S(2)}, u32[]{:S(2)}) collective-permute-start(bf16[192,512]{1,0:T(8,128)(2,1)} %get-tuple-element.195), channel_id=1, source_target_pairs={{0,1},{1,2},{2,3},{3,0},{4,5},{5,6},{6,7},{7,4},{8,9},{9,10},{10,1... | collective-permute-start | bytes 589832 | tf_op jit(solution)/shard_map/ppermute | solution.py:78
  599.5 96.4 %collective-permute-start.33 = (bf16[192,512]{1,0:T(8,128)(2,1)S(1)}, bf16[192,512]{1,0:T(8,128)(2,1)}, u32[]{:S(2)}, u32[]{:S(2)}) collective-permute-start(bf16[192,512]{1,0:T(8,128)(2,1)S(1)} %get-tuple-element.196), channel_id=1, source_target_pairs={{0,2},{1,3},{2,0},{3,1},{4,6},{5,7},{6,4},{7,5},{8,10},{9,11},{10,... | collective-permute-start | bytes 589832 | tf_op jit(solution)/shard_map/ppermute | solution.py:78
  610.6 77.9 %all-to-all-start.7 = ((bf16[32,72,512]{2,1,0:T(8,128)(2,1)}), bf16[32,72,512]{2,1,0:T(8,128)(2,1)}, u32[]{:S(2)}, u32[]{:S(2)}) async-start(bf16[32,72,512]{2,1,0:T(8,128)(2,1)} %pad_maximum_fusion.5), calls=%async_computation.9 | async-start | bytes 4718592 | tf_op jit(solution)/shard_map/all_to_all | solution.py:119
  621.4 45.9 %collective-permute-start.37 = (bf16[192,512]{1,0:T(8,128)(2,1)S(1)}, bf16[192,512]{1,0:T(8,128)(2,1)S(1)}, u32[]{:S(2)}, u32[]{:S(2)}) collective-permute-start(bf16[192,512]{1,0:T(8,128)(2,1)S(1)} %get-tuple-element.181), channel_id=1, source_target_pairs={{0,1},{1,2},{2,3},{3,0},{4,5},{5,6},{6,7},{7,4},{8,9},{9,10},{10,1... | collective-permute-start | bytes 589832 | tf_op jit(solution)/shard_map/ppermute | solution.py:78
  621.5 45.9 %collective-permute-start.39 = (bf16[192,512]{1,0:T(8,128)(2,1)S(1)}, bf16[192,512]{1,0:T(8,128)(2,1)S(1)}, u32[]{:S(2)}, u32[]{:S(2)}) collective-permute-start(bf16[192,512]{1,0:T(8,128)(2,1)S(1)} %get-tuple-element.182), channel_id=1, source_target_pairs={{0,2},{1,3},{2,0},{3,1},{4,6},{5,7},{6,4},{7,5},{8,10},{9,11},{10,... | collective-permute-start | bytes 589832 | tf_op jit(solution)/shard_map/ppermute | solution.py:78
  623.0 44.3 %collective-permute-start.38 = (bf16[192,512]{1,0:T(8,128)(2,1)S(1)}, bf16[192,512]{1,0:T(8,128)(2,1)S(1)}, u32[]{:S(2)}, u32[]{:S(2)}) collective-permute-start(bf16[192,512]{1,0:T(8,128)(2,1)S(1)} %get-tuple-element.183), channel_id=1, source_target_pairs={{0,3},{1,0},{2,1},{3,2},{4,7},{5,4},{6,5},{7,6},{8,11},{9,8},{10,9... | collective-permute-start | bytes 589832 | tf_op jit(solution)/shard_map/ppermute | solution.py:78
  667.5 11.9 %collective-permute-start.42 = (bf16[192,512]{1,0:T(8,128)(2,1)S(1)}, bf16[192,512]{1,0:T(8,128)(2,1)S(1)}, u32[]{:S(2)}, u32[]{:S(2)}) collective-permute-start(bf16[192,512]{1,0:T(8,128)(2,1)S(1)} %add_convert_fusion.4), channel_id=1, source_target_pairs={{0,1},{1,2},{2,3},{3,0},{4,5},{5,6},{6,7},{7,4},{8,9},{9,10},{10,1... | collective-permute-start | bytes 589832 | tf_op jit(solution)/shard_map/ppermute | solution.py:78
  668.4 10.9 %collective-permute-start.41 = (bf16[192,512]{1,0:T(8,128)(2,1)S(1)}, bf16[192,512]{1,0:T(8,128)(2,1)S(1)}, u32[]{:S(2)}, u32[]{:S(2)}) collective-permute-start(bf16[192,512]{1,0:T(8,128)(2,1)S(1)} %add_convert_fusion.4), channel_id=1, source_target_pairs={{0,2},{1,3},{2,0},{3,1},{4,6},{5,7},{6,4},{7,5},{8,10},{9,11},{10,... | collective-permute-start | bytes 589832 | tf_op jit(solution)/shard_map/ppermute | solution.py:78
  670.6 11.1 %collective-permute-start.40 = (bf16[192,512]{1,0:T(8,128)(2,1)S(1)}, bf16[192,512]{1,0:T(8,128)(2,1)S(1)}, u32[]{:S(2)}, u32[]{:S(2)}) collective-permute-start(bf16[192,512]{1,0:T(8,128)(2,1)S(1)} %add_convert_fusion.4), channel_id=1, source_target_pairs={{0,3},{1,0},{2,1},{3,2},{4,7},{5,4},{6,5},{7,6},{8,11},{9,8},{10,9... | collective-permute-start | bytes 589832 | tf_op jit(solution)/shard_map/ppermute | solution.py:78
  679.4 16.5 %collective-permute-start.32 = (bf16[192,512]{1,0:T(8,128)(2,1)S(1)}, bf16[192,512]{1,0:T(8,128)(2,1)}, u32[]{:S(2)}, u32[]{:S(2)}) collective-permute-start(bf16[192,512]{1,0:T(8,128)(2,1)S(1)} %get-tuple-element.197), channel_id=1, source_target_pairs={{0,3},{1,0},{2,1},{3,2},{4,7},{5,4},{6,5},{7,6},{8,11},{9,8},{10,9... | collective-permute-start | bytes 589832 | tf_op jit(solution)/shard_map/ppermute | solution.py:78
  688.5 19.2 %all-to-all-start.8 = ((f32[32,1,64]{2,1,0:T(1,128)}), f32[32,1,64]{2,1,0:T(1,128)S(1)}, u32[]{:S(2)}, u32[]{:S(2)}) async-start(f32[32,1,64]{2,1,0:T(1,128)} %all_to_all.53), calls=%async_computation.10 | async-start | bytes 32768 | tf_op jit(solution)/shard_map/all_to_all | solution.py:119
  699.4 12.6 %collective-permute-start.36 = (bf16[192,512]{1,0:T(8,128)(2,1)S(1)}, bf16[192,512]{1,0:T(8,128)(2,1)S(1)}, u32[]{:S(2)}, u32[]{:S(2)}) collective-permute-start(bf16[192,512]{1,0:T(8,128)(2,1)S(1)} %add_convert_fusion.5), channel_id=1, source_target_pairs={{0,1},{1,2},{2,3},{3,0},{4,5},{5,6},{6,7},{7,4},{8,9},{9,10},{10,1... | collective-permute-start | bytes 589832 | tf_op jit(solution)/shard_map/ppermute | solution.py:78
  699.9 12.1 %collective-permute-start.35 = (bf16[192,512]{1,0:T(8,128)(2,1)S(1)}, bf16[192,512]{1,0:T(8,128)(2,1)S(1)}, u32[]{:S(2)}, u32[]{:S(2)}) collective-permute-start(bf16[192,512]{1,0:T(8,128)(2,1)S(1)} %add_convert_fusion.5), channel_id=1, source_target_pairs={{0,2},{1,3},{2,0},{3,1},{4,6},{5,7},{6,4},{7,5},{8,10},{9,11},{10,... | collective-permute-start | bytes 589832 | tf_op jit(solution)/shard_map/ppermute | solution.py:78
  (155 other events, 1123.3 us)
Sparse Core Ops, SparseCore 0:
  11.4 57.7 all-gather.3
  71.5 103.4 all-gather.5
  177.8 58.6 all-gather.7
  251.5 93.7 reduce-scatter.3
  434.4 122.8 reduce-scatter.5
  597.8 95.3 reduce-scatter.7

commit v6 on v5

--- a/solution.py
+++ b/solution.py
@@ -208,8 +208,9 @@
 
 def hidden_kernel(tiles, spill, *refs):
     pieces, (weight, dh_ref, gate_ref, hid, dboth, dgate), refs = refs[:8], refs[8:14], refs[14:]
-    drow, acc = refs[:8], refs[8]
+    drow, rows_out, acc = refs[:8], refs[8], refs[9]
     rows = jnp.concatenate([p[...] for p in pieces], 1)
+    rows_out[...] = rows
 
     def run(owner, mine):
         if owner is None:
@@ -381,6 +382,74 @@
             dimension_semantics=("arbitrary",), vmem_limit_bytes=VMEM_BYTES
         ),
     )(normed2, cotangent, dboth, hidden)
+
+
+def weight_grad_kernel(edge, spill, lane, rows, dy, dboth, hid, gate_out, up_out, down_out, dm, hm):
+    span = dm.shape[1]
+
+    @pl.when((pl.program_id(0) == 0) & (pl.program_id(1) == 0))
+    def _():
+        row = lax.broadcasted_iota(jnp.int32, (span, 1), 0)
+        first = (row < edge) | (lax.rem(jnp.maximum(row - edge, 0), EXP_DEV * spill) < spill)
+        second = (row >= span - edge) | (lax.rem(row, EXP_DEV * spill) >= spill)
+        for e, (at, keep) in enumerate(((0, first), (edge, second))):
+            part = dboth[at : at + span, :]
+            dm[e] = jnp.where(keep, part, jnp.zeros_like(part))
+            part = hid[at : at + span, :]
+            hm[e] = jnp.where(keep, part, jnp.zeros_like(part))
+
+    owner = pl.program_id(1)
+    at = pl.ds(pl.multiple_of(owner * edge, edge), span)
+    cols = gate_out.shape[2]
+    wide = hid.shape[1]
+    both = matmul_tn(rows[at, :], dm[owner])
+    gate_out[0] = both[:, :cols]
+    up_out[0] = both[:, wide : wide + cols]
+    down_out[0] = matmul_tn(hm[owner], dy[at, :])[:cols]
+
+
+def weight_grads(edge, spill, hid_cols, lane, rows, dy, dboth, hid):
+    total = rows.shape[0]
+    span = total - edge
+    block = D // 8
+    assert (span - edge) % (EXP_DEV * spill) == 0
+    up_shape = jax.ShapeDtypeStruct((EXP_DEV, D, hid_cols), f32)
+    up_spec = pl.BlockSpec(
+        (1, block, hid_cols), lambda j, e, lane: (e, lax.rem(lane[0] * 2 + j, 8), 0)
+    )
+    col_spec = pl.BlockSpec((total, block), lambda j, e, lane: (0, j))
+    grid_spec = pltpu.PrefetchScalarGridSpec(
+        num_scalar_prefetch=1,
+        grid=(8, EXP_DEV),
+        in_specs=[
+            col_spec,
+            col_spec,
+            pl.BlockSpec(dboth.shape, lambda j, e, lane: (0, 0)),
+            pl.BlockSpec(hid.shape, lambda j, e, lane: (0, 0)),
+        ],
+        out_specs=[
+            up_spec,
+            up_spec,
+            pl.BlockSpec((1, hid_cols, block), lambda j, e, lane: (e, 0, j)),
+        ],
+        scratch_shapes=[
+            pltpu.VMEM((EXP_DEV, span, dboth.shape[1]), bf16),
+            pltpu.VMEM((EXP_DEV, span, hid.shape[1]), bf16),
+        ],
+    )
+    return pl.pallas_call(
+        functools.partial(weight_grad_kernel, edge, spill),
+        grid_spec=grid_spec,
+        out_shape=[up_shape, up_shape, jax.ShapeDtypeStruct((EXP_DEV, hid_cols, D), f32)],
+        cost_estimate=pl.CostEstimate(
+            flops=4 * EXP_DEV * span * D * (dboth.shape[1] + hid.shape[1]) // 2,
+            bytes_accessed=4 * total * D + 12 * EXP_DEV * hid_cols * D,
+            transcendentals=0,
+        ),
+        compiler_params=pltpu.CompilerParams(
+            dimension_semantics=("arbitrary", "arbitrary"), vmem_limit_bytes=VMEM_BYTES
+        ),
+    )(lane.reshape(1), rows, dy, dboth, hid)
 
 
 def per_device(
@@ -468,13 +537,6 @@
             parts.append(lax.dynamic_slice_in_dim(value, at, quarter, axis))
         return jnp.concatenate(parts, axis)
 
-    def to_lane(value, axis):
-        parts = []
-        for step in range(lanes):
-            at = lax.rem(lanes - lane + step, lanes) * quarter
-            parts.append(lax.dynamic_slice_in_dim(value, at, quarter, axis))
-        return jnp.concatenate(parts, axis)
-
     fill = hid_wide - hid_cols
     gateup_w = jnp.concatenate(
         [
@@ -582,8 +644,24 @@
         big,
     )
 
+    logits = matmul(normed2, router_full)
+    onehot = (
+        expert_ids[:, :, None] == jnp.arange(experts, dtype=jnp.int32)[None, None, :]
+    ).astype(f32)
+    chosen = jnp.sum(onehot * logits[:, None, :], -1)
+    sel_vals = 1.0 / (1.0 + jnp.exp(-chosen))
+    sel_total = jnp.sum(sel_vals, -1, keepdims=True)
+    gate_vals = route_scale * sel_vals / sel_total
+    gate_rows = jnp.zeros((slot_rows, tok_count), f32)
+    for k in range(TOPK):
+        gate_rows = gate_rows + jnp.where(matches[k], gate_vals[:, k][None, :], 0.0)
+    gate_rows = jnp.sum(gate_rows, 1).reshape(owner_count, width)
+    gate_rows = to_experts(exchange(after(gate_rows, two)))[:, None]
+
+    going, ex_dh, gate_rows = lax.optimization_barrier((first[:2], ex_dh, gate_rows))
+    rows = ring_gather_parts(*own, (*going, *first[2:]), ring_gather_second(going))
     upstream = cotangent.astype(f32)
-    sh_in, sh_dy = after((normed2, cotangent), two)
+    sh_in, sh_dy = after((normed2, cotangent), going)
     gateup_full = second_full[:, : 2 * sh_cols]
     shdown_t = second_full[:, 2 * sh_cols :]
     sh_both = matmul(sh_in, gateup_full)
@@ -600,65 +678,22 @@
     second_grad = second_grads(normed2, cotangent, sh_dboth, sh_hidden)
     second_sum = lax.psum_scatter(second_grad, "ep", scatter_dimension=0, tiled=True)
 
-    logits = matmul(normed2, router_full)
-    onehot = (
-        expert_ids[:, :, None] == jnp.arange(experts, dtype=jnp.int32)[None, None, :]
-    ).astype(f32)
-    chosen = jnp.sum(onehot * logits[:, None, :], -1)
-    sel_vals = 1.0 / (1.0 + jnp.exp(-chosen))
-    sel_total = jnp.sum(sel_vals, -1, keepdims=True)
-    gate_vals = route_scale * sel_vals / sel_total
-    gate_rows = jnp.zeros((slot_rows, tok_count), f32)
-    for k in range(TOPK):
-        gate_rows = gate_rows + jnp.where(matches[k], gate_vals[:, k][None, :], 0.0)
-    gate_rows = jnp.sum(gate_rows, 1).reshape(owner_count, width)
-    gate_rows = to_experts(exchange(after(gate_rows, two)))[:, None]
-
-    going, ex_dh, gate_rows = lax.optimization_barrier((first[:2], ex_dh, gate_rows))
-    rows = ring_gather_parts(*own, (*going, *first[2:]), ring_gather_second(going))
     ex_dh, shared_part, sh_dnormed_part, second_grad = lax.optimization_barrier(
         (ex_dh, shared_part, sh_dnormed_part, second_grad)
     )
     shared_q = sum_to_quarter(shared_part)
     sh_dnormed_q = sum_to_quarter(sh_dnormed_part)
-    ex_hidden, ex_dboth, dgate_rows, *drow = row_call(
+    ex_hidden, ex_dboth, dgate_rows, *drow, all_rows = row_call(
         functools.partial(hidden_kernel, tiles, spill),
         tile,
         slot_rows,
         (*rows, gateup_w, ex_dh, gate_rows),
         [tile_spec(tile, half)] * 8
         + [whole_spec(gateup_w.shape), tile_spec(tile, hid_wide), tile_spec(tile, 1)],
-        [(hid_wide, bf16), (2 * hid_wide, bf16), (1, f32)] + [(half, bf16)] * 8,
+        [(hid_wide, bf16), (2 * hid_wide, bf16), (1, f32)] + [(half, bf16)] * 8 + [(D, bf16)],
         4 * big,
         [pltpu.VMEM((tile, 2 * hid_wide), f32)],
     )
-
-    extra_iota = lax.broadcasted_iota(jnp.int32, (span, 1), 0)
-    owned = (
-        (extra_iota < edge) | ((extra_iota - edge) % (EXP_DEV * spill) < spill),
-        (extra_iota >= extra) | (extra_iota % (EXP_DEV * spill) >= spill),
-    )
-
-    def expert_rows(value, e):
-        return value[:span] if e == 0 else value[edge:]
-
-    def grads_of(e, left, right, cols):
-        kept = jnp.where(owned[e], expert_rows(right, e)[:, cols], jnp.zeros((), bf16))
-        return matmul_tn(expert_rows(left, e), kept)
-
-    def grads_of_down(late):
-        wide_dy = after(dy_rows, late)
-        hidden = after(ex_hidden[:, :hid_cols], late)
-        parts = []
-        for e in range(EXP_DEV):
-            kept = jnp.where(owned[e], expert_rows(hidden, e), jnp.zeros((), bf16))
-            parts.append(matmul_tn(kept, expert_rows(wide_dy, e)))
-        return jnp.stack(parts)
-
-    def bring_back(one, two):
-        back_one = exchange(from_experts(one, owner_count)).reshape(slot_rows, -1)
-        back_two = exchange(from_experts(two, owner_count)).reshape(slot_rows, -1)
-        return jnp.concatenate([matmul_tn(pick, back_one), matmul_tn(pick, back_two)], 1)
 
     out_rows = pl.pallas_call(
         functools.partial(out_kernel, tiles, spill),
@@ -688,8 +723,12 @@
     from_next_two = shift(prev_two, 3)
     drow_one = add_three(drow[0], from_prev_one, from_next_one)
     drow_two = add_three(drow[1], from_prev_two, from_next_two)
-    routed_grad_q = bring_back(drow_one, drow_two)
-    out_rows = after(out_rows, drow_one, second_sum)
+    back_one = exchange(from_experts(drow_one, owner_count))
+    back_two = exchange(from_experts(drow_two, owner_count))
+    routed_grad_q = jnp.concatenate(
+        [matmul_tn(pick, b.reshape(slot_rows, -1)) for b in (back_one, back_two)], 1
+    )
+    out_rows = after(out_rows, drow_two, second_sum, back_one)
     out_sum = lax.psum_scatter(out_rows, "tp", scatter_dimension=0, tiled=True)
 
     dgate_part = jnp.stack(
@@ -765,20 +804,9 @@
     dtokens, prenorm_grad = rms_back(resid_in, pre_scale, pre_weight, dnormed)
     tokens_grad = (dmid + dtokens).astype(bf16)
     prenorm_sum = jnp.sum(exchange(prenorm_grad.reshape(owner_count, shard)), 0)
-    down_grad = grads_of_down(late)
-    all_rows = jnp.concatenate(after(rows, late), 1)
-    late_dboth = after(ex_dboth, late)
-    exgate_grad = jnp.stack(
-        [grads_of(e, all_rows, late_dboth, slice(0, hid_cols)) for e in range(EXP_DEV)]
-    )
-    exup_grad = jnp.stack(
-        [
-            grads_of(e, all_rows, late_dboth, slice(hid_wide, hid_wide + hid_cols))
-            for e in range(EXP_DEV)
-        ]
-    )
-    exgate_grad = to_lane(exgate_grad, 1)
-    exup_grad = to_lane(exup_grad, 1)
+    exgate_grad, exup_grad, exdown_grad = weight_grads(
+        edge, spill, hid_cols, lane, *after((all_rows, dy_rows, ex_dboth, ex_hidden), late)
+    )
     layer_q = (quarter_of(mid_resid, 0) + routed_q + shared_q).astype(bf16)
     layer_out = gather_quarters(layer_q)
     first_sum = lax.psum_scatter(first_grad, "ep", scatter_dimension=0, tiled=True).astype(f32)
@@ -802,7 +830,7 @@
         second_sum[:, 2 * sh_cols :].T,
         exgate_grad,
         exup_grad,
-        down_grad,
+        exdown_grad,
     )
 
 

time: 735 us -> 715 us (0.973)
  Pallas kernels: 64.3 us -> 93.4 us
  matrix products: 93.4 us -> 72.1 us
  waiting for transfers between devices: 252 us -> 232 us
  other arithmetic: 66.4 us -> 54.6 us
    all_gather x1, waiting for transfers between devices: 35 us -> 0.01 us  [per_device(): lax.all_gather(after(second_pack, dy_all, one), 'ep', axis=0, tiled=True)]
    pallas_call x0 -> x1, Pallas kernels: none -> 28.4 us  [weight_grads(): pl.pallas_call(functools.partial(weight_grad_kernel, edge, spill), grid_s...]
    dot_general x9 -> x3, matrix products: 30 us -> 7.62 us  [matmul_tn(): lax.dot_general(left_mat, right_mat, (((0,), (0,)), ((), ())), preferred_...]
    reduce_scatter x1, waiting for transfers between devices: 0.01 us -> 12.3 us  [per_device(): out_sum = lax.psum_scatter(out_rows, 'tp', scatter_dimension=0, tiled=True)]
    unnamed x309 -> x256, local copies, waits for them, and re-layouts: 51.3 us -> 51.2 us
  transfers between devices with their start and end apart: 58 -> 58, of which waited for: 32 -> 33; matrix products, arithmetic and copies ran while one was open for 31% -> 28% of each run, Pallas kernels for 7% -> 11%
where the time goes in v6:
time: 715 us; the launch traced here: 708 us
  waiting for transfers between devices  232 us (32%)
  starting transfers between devices  128 us (18%)
  local copies, waits for them, and re-layouts  112 us (16%)
  Pallas kernels  93.4 us (13%)
  matrix products  72.1 us (10%)
  other arithmetic  54.6 us (8%)
  between operations  16.4 us (2%)
    ppermute x43, waiting for transfers between devices, shift(): lax.ppermute(value, 'tp', [(i, (i + step) % lanes) for i in range(lanes)])  155 us
    ppermute x43, starting transfers between devices, shift(): lax.ppermute(value, 'tp', [(i, (i + step) % lanes) for i in range(lanes)])  69 us
    all_to_all x9, starting transfers between devices, exchange(): return lax.all_to_all(value, 'ep', 0, 0, tiled=True)  58.4 us
    unnamed x256, local copies, waits for them, and re-layouts  51.2 us
    all_to_all x9, waiting for transfers between devices, exchange(): return lax.all_to_all(value, 'ep', 0, 0, tiled=True)  44.5 us
    pallas_call x2, Pallas kernels, row_call(): pl.pallas_call(body, grid=(total // tile,), in_specs=in_specs, out_specs=...  41.1 us
    pallas_call x1, Pallas kernels, weight_grads(): pl.pallas_call(functools.partial(weight_grad_kernel, edge, spill), grid_s...  28.4 us
    dot_general x7, matrix products, matmul_nt(): lax.dot_general(left_mat, right_mat, (((1,), (1,)), ((), ())), preferred_...  22.7 us
  transfers between devices with their start and end apart: 58, of which 33 were waited for; matrix products, arithmetic and copies ran while one was open for 28% of the time, Pallas kernels for 11%

profile of v6, /device:TPU:0, one launch (start us, length us, event | category | flops | bytes accessed | tf_op | source)
XLA Modules:
  0.0 708.5 jit_solution(7894732590917328766)
XLA Ops:
  15.1 7.4 %all-to-all-start = ((s32[32,1,72]{2,1,0:T(1,128)}), s32[32,1,72]{2,1,0:T(1,128)S(1)}, u32[]{:S(2)}, u32[]{:S(2)}) async-start(s32[32,1,72]{2,1,0:T(1,128)} %sub.87), calls=%async_computation | async-start | bytes 32768 | tf_op jit(solution)/shard_map/all_to_all | solution.py:119
  22.8 4.7 constant_dynamic-slice_fusion.30
  48.7 20.5 %all-gather.4.cloned.1.call-done = bf16[2048,2304]{1,0:T(8,128)(2,1)} async-done(((bf16[64,2304]{1,0:T(8,128)(2,1)}), bf16[2048,2304]{1,0:T(8,128)(2,1)}) %all-gather.4.cloned.1.call-update) | async-done | bytes 9437200 | tf_op jit(solution)/shard_map/all_gather | solution.py:508
  81.0 3.7 fusion.25
  119.1 5.3 collective-permute-done.2
  132.2 5.5 collective-permute-done.4
  143.6 5.4 all-to-all-start.1
  150.0 23.5 %all-to-all-done.1 = bf16[32,72,256]{2,1,0:T(8,128)(2,1)} async-done(((bf16[32,72,256]{2,1,0:T(8,128)(2,1)}), bf16[32,72,256]{2,1,0:T(8,128)(2,1)}, u32[]{:S(2)}, u32[]{:S(2)}) %all-to-all-start.1) | async-done | bytes 1179680 | tf_op jit(solution)/shard_map/all_to_all | solution.py:119
  175.7 7.5 %all-to-all-start.2 = ((bf16[32,72,256]{2,1,0:T(8,128)(2,1)}), bf16[32,72,256]{2,1,0:T(8,128)(2,1)}, u32[]{:S(2)}, u32[]{:S(2)}) async-start(bf16[32,72,256]{2,1,0:T(8,128)(2,1)} %get-tuple-element.66), calls=%async_computation.2 | async-start | bytes 2359296 | tf_op jit(solution)/shard_map/all_to_all | solution.py:119
  190.7 12.6 %all-to-all-done.2 = bf16[32,72,256]{2,1,0:T(8,128)(2,1)} async-done(((bf16[32,72,256]{2,1,0:T(8,128)(2,1)}), bf16[32,72,256]{2,1,0:T(8,128)(2,1)}, u32[]{:S(2)}, u32[]{:S(2)}) %all-to-all-start.2) | async-done | bytes 1179680 | tf_op jit(solution)/shard_map/all_to_all | solution.py:119
  203.3 5.9 all-to-all-start.3
  217.0 14.7 %convolution_convert_fusion = bf16[32,72,2048]{2,1,0:T(8,128)(2,1)} fusion(bf16[32,192,2048]{2,1,0:T(8,128)(2,1)} %bitcast.128, s32[32,72]{1,0:T(8,128)S(1)} %bitcast.151), kind=kOutput, calls=%fused_computation.12 | convolution fusion | flops 1817100288 | bytes 34612224 | tf_op jit(solution)/shard_map/ist,itd->isd/dot_general | solution.py:630
  233.1 4.2 fusion.114
  237.3 4.2 pad_maximum_fusion.refs_0_.dy
  241.5 10.7 %shard_map.306.refs_9_ = f32[2304,384]{1,0:T(8,128)S(1)} custom-call(bf16[2304,2048]{1,0:T(8,128)(2,1)} %pad_maximum_fusion.refs_0_.dy, bf16[2,384,2048]{2,1,0:T(8,128)(2,1)S(1)} %pad.41.refs_1_.weight), custom_call_target="tpu_custom_call" | custom-call | flops 4026531840 | bytes 16121856 | tf_op jit(solution)/shard_map/pallas_call | solution.py:279
  254.1 4.3 fusion.11
  261.5 6.8 shard_map.307
  277.0 4.2 fusion.30
  281.2 5.9 fusion.33
  287.1 11.7 %collective-permute-done.6.refs_2_ = bf16[2304,256]{1,0:T(8,128)(2,1)} collective-permute-done((bf16[2304,256]{1,0:T(8,128)(2,1)}, bf16[2304,256]{1,0:T(8,128)(2,1)}, u32[]{:S(2)}, u32[]{:S(2)}) %collective-permute-start.6) | collective-permute-done | bytes 1179680 | tf_op jit(solution)/shard_map/ppermute | solution.py:78
  298.9 3.7 collective-permute-done.11.refs_7_
  302.6 20.3 %collective-permute-done.10.refs_5_ = bf16[2304,256]{1,0:T(8,128)(2,1)} collective-permute-done((bf16[2304,256]{1,0:T(8,128)(2,1)}, bf16[2304,256]{1,0:T(8,128)(2,1)}, u32[]{:S(2)}, u32[]{:S(2)}) %collective-permute-start.10) | collective-permute-done | bytes 1179680 | tf_op jit(solution)/shard_map/ppermute | solution.py:78
  326.4 30.3 %shard_map.308 = (bf16[2304,384]{1,0:T(8,128)(2,1)}, bf16[2304,768]{1,0:T(8,128)(2,1)}, f32[2304,1]{1,0:T(8,128)}, bf16[2304,256]{1,0:T(8,128)(2,1)S(1)}, bf16[2...) custom-call(bf16[2304,256]{1,0:T(8,128)(2,1)} %pad_maximum_fusion.3., ...), custom_call_target="tpu_custom_call" | custom-call | flops 16106127360 | bytes 43468800 | tf_op jit(solution)/shard_map/pallas_call | solution.py:279
  368.6 5.4 all-to-all-start.4
  375.5 9.2 %shard_map.309 = bf16[4,2304,512]{2,1,0:T(8,128)(2,1)} custom-call(bf16[2304,384]{1,0:T(8,128)(2,1)S(1)} %copy-done.29, bf16[2,384,2048]{2,1,0:T(8,128)(2,1)S(1)} %pad.41.refs_1_.weight), custom_call_target="tpu_custom_call" | custom-call | flops 4026531840 | bytes 14155776 | tf_op jit(solution)/shard_map/pallas_call | solution.py:698
  386.0 3.9 collective-permute-done.12
  397.7 18.2 %collective-permute-done.15 = bf16[2304,256]{1,0:T(8,128)(2,1)S(1)} collective-permute-done((bf16[2304,256]{1,0:T(8,128)(2,1)}, bf16[2304,256]{1,0:T(8,128)(2,1)S(1)}, u32[]{:S(2)}, u32[]{:S(2)}) %collective-permute-start.15) | collective-permute-done | bytes 1179680 | tf_op jit(solution)/shard_map/ppermute | solution.py:78
  415.9 5.2 collective-permute-done.14
  426.3 6.8 all-to-all-start.5
  433.1 13.4 %collective-permute-done.16 = bf16[2304,256]{1,0:T(8,128)(2,1)} collective-permute-done((bf16[2304,256]{1,0:T(8,128)(2,1)S(1)}, bf16[2304,256]{1,0:T(8,128)(2,1)}, u32[]{:S(2)}, u32[]{:S(2)}) %collective-permute-start.16) | collective-permute-done | bytes 1179680 | tf_op jit(solution)/shard_map/ppermute | solution.py:78
  453.4 5.3 all-to-all-start.6
  472.1 4.9 all-to-all-done.6
  478.6 7.9 %collective-permute-done.20 = bf16[192,512]{1,0:T(8,128)(2,1)S(1)} collective-permute-done((bf16[192,512]{1,0:T(8,128)(2,1)S(1)}, bf16[192,512]{1,0:T(8,128)(2,1)S(1)}, u32[]{:S(2)}, u32[]{:S(2)}) %collective-permute-start.20) | collective-permute-done | bytes 196640 | tf_op jit(solution)/shard_map/ppermute | solution.py:78
  493.0 8.1 %collective-permute-done.23 = bf16[192,512]{1,0:T(8,128)(2,1)S(1)} collective-permute-done((bf16[192,512]{1,0:T(8,128)(2,1)S(1)}, bf16[192,512]{1,0:T(8,128)(2,1)S(1)}, u32[]{:S(2)}, u32[]{:S(2)}) %collective-permute-start.23) | collective-permute-done | bytes 196640 | tf_op jit(solution)/shard_map/ppermute | solution.py:78
  501.1 5.7 collective-permute-done.22
  523.2 9.6 %collective-permute-done.28 = bf16[192,576]{1,0:T(8,128)(2,1)S(1)} collective-permute-done((bf16[192,576]{1,0:T(8,128)(2,1)S(1)}, bf16[192,576]{1,0:T(8,128)(2,1)S(1)}, u32[]{:S(2)}, u32[]{:S(2)}) %collective-permute-start.28) | collective-permute-done | bytes 221216 | tf_op jit(solution)/shard_map/ppermute | solution.py:78
  534.1 10.1 %collective-permute-done.29 = bf16[192,576]{1,0:T(8,128)(2,1)S(1)} collective-permute-done((bf16[192,576]{1,0:T(8,128)(2,1)S(1)}, bf16[192,576]{1,0:T(8,128)(2,1)S(1)}, u32[]{:S(2)}, u32[]{:S(2)}) %collective-permute-start.29) | collective-permute-done | bytes 221216 | tf_op jit(solution)/shard_map/ppermute | solution.py:78
  555.0 12.3 %reduce-scatter.6.cloned.1.call-done = bf16[2304,512]{1,0:T(8,128)(2,1)} async-done(((bf16[9216,512]{1,0:T(8,128)(2,1)}), bf16[2304,512]{1,0:T(8,128)(2,1)}) %reduce-scatter.6.cloned.1.call-update) | async-done | bytes 2359312 | tf_op jit(solution)/shard_map/reduce_scatter | solution.py:732
  573.0 7.9 %shard_map.310 = bf16[2048,2304]{1,0:T(8,128)(2,1)} custom-call(bf16[192,2048]{1,0:T(8,128)(2,1)S(1)} %copy-done.8, bf16[192,2048]{1,0:T(8,128)(2,1)S(1)} %copy-done.4, bf16[192,2048]{1,0:T(8,128)(2,1)S(1)} %copy-done.10, bf16[192,768]{1,0:T(8,128)(2,1)S(1)} %copy-done.21, bf16[192,640]{1,0:T(8,128)(2,1)S(1)} %copy-done.23, bf16[192,640]{1,0:T(8,128)(2,1)S(1)} %copy-done.24, ...), custom_call_target="tpu_custom_call" | custom-call | flops 1811939328 | bytes 14155776 | tf_op jit(solution)/shard_map/pallas_call | solution.py:344
  590.9 7.4 %all-to-all-start.7 = ((bf16[32,72,512]{2,1,0:T(8,128)(2,1)}), bf16[32,72,512]{2,1,0:T(8,128)(2,1)}, u32[]{:S(2)}, u32[]{:S(2)}) async-start(bf16[32,72,512]{2,1,0:T(8,128)(2,1)} %pad_maximum_fusion.2), calls=%async_computation.9 | async-start | bytes 4718592 | tf_op jit(solution)/shard_map/all_to_all | solution.py:119
  605.9 8.2 %collective-permute-done.37 = bf16[192,512]{1,0:T(8,128)(2,1)S(1)} collective-permute-done((bf16[192,512]{1,0:T(8,128)(2,1)S(1)}, bf16[192,512]{1,0:T(8,128)(2,1)S(1)}, u32[]{:S(2)}, u32[]{:S(2)}) %collective-permute-start.37) | collective-permute-done | bytes 196640 | tf_op jit(solution)/shard_map/ppermute | solution.py:78
  615.2 3.8 collective-permute-start.41
  629.4 3.5 fusion.58
  636.3 7.3 %all-to-all-start.8 = ((f32[32,1,64]{2,1,0:T(1,128)}), f32[32,1,64]{2,1,0:T(1,128)S(1)}, u32[]{:S(2)}, u32[]{:S(2)}) async-start(f32[32,1,64]{2,1,0:T(1,128)} %all_to_all.53), calls=%async_computation.10 | async-start | bytes 32768 | tf_op jit(solution)/shard_map/all_to_all | solution.py:119
  643.7 3.5 add_convert_fusion.5
  650.4 28.4 %shard_map.311 = (f32[2,2048,352]{2,1,0:T(8,128)}, f32[2,2048,352]{2,1,0:T(8,128)}, f32[2,352,2048]{2,1,0:T(8,128)}) custom-call(s32[1]{0:T(128)} %bitcast.66.lane, bf16[2304,2048]{1,0:T(8,128)(2,1)} %get-tuple-element.107.rows, bf16[2304,2048]{1,0:T(8,128)(2,1)} %pad_maximum_fusion.refs_0_.dy, bf16[2304,768]{1,0:T(8,128)(2,1)S(1)} %copy-done.31, ...), custom_call_target="tpu_custom_call" | custom-call | flops 12079595520 | bytes 36175872 | tf_op jit(solution)/shard_map/pallas_call | solution.py:440
  678.9 6.4 copy.210
  685.3 6.4 copy.211
  (523 shorter events, 260.1 us)
Async XLA Ops:
  7.2 62.0 %all-gather.4.cloned.1.call-start = ((), (), s32[]{:S(2)}) async-start(), calls=%async_computation.12 | async-start | bytes 9732096 | tf_op jit(solution)/shard_map/all_gather | solution.py:508
  15.1 33.7 %all-to-all-start = ((s32[32,1,72]{2,1,0:T(1,128)}), s32[32,1,72]{2,1,0:T(1,128)S(1)}, u32[]{:S(2)}, u32[]{:S(2)}) async-start(s32[32,1,72]{2,1,0:T(1,128)} %sub.87), calls=%async_computation | async-start | bytes 32768 | tf_op jit(solution)/shard_map/all_to_all | solution.py:119
  22.5 151.1 %all-gather.6.cloned.1.call-start = ((), (), s32[]{:S(2)}) async-start(), calls=%async_computation.13 | async-start | bytes 25952256 | tf_op jit(solution)/shard_map/all_gather | solution.py:558
  112.2 12.2 %collective-permute-start.2 = (bf16[192,512]{1,0:T(8,128)(2,1)S(1)}, bf16[192,512]{1,0:T(8,128)(2,1)S(1)}, u32[]{:S(2)}, u32[]{:S(2)}) collective-permute-start(bf16[192,512]{1,0:T(8,128)(2,1)S(1)} %get-tuple-element.269), channel_id=1, source_target_pairs={{0,2},{1,3},{2,0},{3,1},{4,6},{5,7},{6,4},{7,5},{8,10},{9,11},{10,... | collective-permute-start | bytes 589832 | tf_op jit(solution)/shard_map/ppermute | solution.py:78
  126.1 11.6 %collective-permute-start.4 = (bf16[192,512]{1,0:T(8,128)(2,1)S(1)}, bf16[192,512]{1,0:T(8,128)(2,1)}, u32[]{:S(2)}, u32[]{:S(2)}) collective-permute-start(bf16[192,512]{1,0:T(8,128)(2,1)S(1)} %add_convert_fusion.7), channel_id=1, source_target_pairs={{0,2},{1,3},{2,0},{3,1},{4,6},{5,7},{6,4},{7,5},{8,10},{9,11},{10,... | collective-permute-start | bytes 589832 | tf_op jit(solution)/shard_map/ppermute | solution.py:78
  143.6 29.9 %all-to-all-start.1 = ((bf16[32,72,256]{2,1,0:T(8,128)(2,1)}), bf16[32,72,256]{2,1,0:T(8,128)(2,1)}, u32[]{:S(2)}, u32[]{:S(2)}) async-start(bf16[32,72,256]{2,1,0:T(8,128)(2,1)} %get-tuple-element.225), calls=%async_computation.1 | async-start | bytes 2359296 | tf_op jit(solution)/shard_map/all_to_all | solution.py:119
  149.0 105.0 %all-gather.8.cloned.1.call-start = ((), (), s32[]{:S(2)}) async-start(), calls=%async_computation.14 | async-start | bytes 9191424 | tf_op jit(solution)/shard_map/all_gather | solution.py:624
  175.7 27.6 %all-to-all-start.2 = ((bf16[32,72,256]{2,1,0:T(8,128)(2,1)}), bf16[32,72,256]{2,1,0:T(8,128)(2,1)}, u32[]{:S(2)}, u32[]{:S(2)}) async-start(bf16[32,72,256]{2,1,0:T(8,128)(2,1)} %get-tuple-element.66), calls=%async_computation.2 | async-start | bytes 2359296 | tf_op jit(solution)/shard_map/all_to_all | solution.py:119
  189.2 64.9 %collective-permute-start.7 = (bf16[2304,256]{1,0:T(8,128)(2,1)}, bf16[2304,256]{1,0:T(8,128)(2,1)}, u32[]{:S(2)}, u32[]{:S(2)}) collective-permute-start(bf16[2304,256]{1,0:T(8,128)(2,1)} %pad_maximum_fusion.3.refs_0_), channel_id=1, source_target_pairs={{0,1},{1,2},{2,3},{3,0},{4,5},{5,6},{6,7},{7,4},{8,9},{9,10},{10,1... | collective-permute-start | bytes 3538952 | tf_op jit(solution)/shard_map/ppermute | solution.py:78
  203.3 13.2 %all-to-all-start.3 = ((f32[32,1,72]{2,1,0:T(1,128)}), f32[32,1,72]{2,1,0:T(1,128)S(1)}, u32[]{:S(2)}, u32[]{:S(2)}) async-start(f32[32,1,72]{2,1,0:T(1,128)} %bitcast.34), calls=%async_computation.3 | async-start | bytes 32768 | tf_op jit(solution)/shard_map/all_to_all | solution.py:119
  209.3 242.2 %reduce-scatter.4.cloned.1.call-start = ((), (), s32[]{:S(2)}) async-start(), calls=%async_computation.15 | async-start | bytes 9191424 | tf_op jit(solution)/shard_map/reduce_scatter | solution.py:679
  212.6 41.5 %collective-permute-start.8 = (bf16[2304,256]{1,0:T(8,128)(2,1)}, bf16[2304,256]{1,0:T(8,128)(2,1)}, u32[]{:S(2)}, u32[]{:S(2)}) collective-permute-start(bf16[2304,256]{1,0:T(8,128)(2,1)} %pad_maximum_fusion.4.refs_1_), channel_id=1, source_target_pairs={{0,3},{1,0},{2,1},{3,2},{4,7},{5,4},{6,5},{7,6},{8,11},{9,8},{10,9... | collective-permute-start | bytes 3538952 | tf_op jit(solution)/shard_map/ppermute | solution.py:78
  269.1 29.7 %collective-permute-start.6 = (bf16[2304,256]{1,0:T(8,128)(2,1)}, bf16[2304,256]{1,0:T(8,128)(2,1)}, u32[]{:S(2)}, u32[]{:S(2)}) collective-permute-start(bf16[2304,256]{1,0:T(8,128)(2,1)} %pad_maximum_fusion.3.refs_0_), channel_id=1, source_target_pairs={{0,3},{1,0},{2,1},{3,2},{4,7},{5,4},{6,5},{7,6},{8,11},{9,8},{10,9... | collective-permute-start | bytes 3538952 | tf_op jit(solution)/shard_map/ppermute | solution.py:78
  272.2 30.4 %collective-permute-start.11 = (bf16[2304,256]{1,0:T(8,128)(2,1)}, bf16[2304,256]{1,0:T(8,128)(2,1)}, u32[]{:S(2)}, u32[]{:S(2)}) collective-permute-start(bf16[2304,256]{1,0:T(8,128)(2,1)} %pad_maximum_fusion.4.refs_1_), channel_id=1, source_target_pairs={{0,1},{1,2},{2,3},{3,0},{4,5},{5,6},{6,7},{7,4},{8,9},{9,10},{10,1... | collective-permute-start | bytes 3538952 | tf_op jit(solution)/shard_map/ppermute | solution.py:78
  272.2 50.8 %collective-permute-start.10 = (bf16[2304,256]{1,0:T(8,128)(2,1)}, bf16[2304,256]{1,0:T(8,128)(2,1)}, u32[]{:S(2)}, u32[]{:S(2)}) collective-permute-start(bf16[2304,256]{1,0:T(8,128)(2,1)} %collective-permute-done.8.refs_3_), channel_id=1, source_target_pairs={{0,3},{1,0},{2,1},{3,2},{4,7},{5,4},{6,5},{7,6},{8,11},{9,8},{10,9... | collective-permute-start | bytes 3538952 | tf_op jit(solution)/shard_map/ppermute | solution.py:78
  275.4 50.9 %collective-permute-start.9 = (bf16[2304,256]{1,0:T(8,128)(2,1)}, bf16[2304,256]{1,0:T(8,128)(2,1)}, u32[]{:S(2)}, u32[]{:S(2)}) collective-permute-start(bf16[2304,256]{1,0:T(8,128)(2,1)} %collective-permute-done.7.refs_6_), channel_id=1, source_target_pairs={{0,1},{1,2},{2,3},{3,0},{4,5},{5,6},{6,7},{7,4},{8,9},{9,10},{10,1... | collective-permute-start | bytes 3538952 | tf_op jit(solution)/shard_map/ppermute | solution.py:78
  361.8 28.0 %collective-permute-start.12 = (bf16[2304,256]{1,0:T(8,128)(2,1)}, bf16[2304,256]{1,0:T(8,128)(2,1)}, u32[]{:S(2)}, u32[]{:S(2)}) collective-permute-start(bf16[2304,256]{1,0:T(8,128)(2,1)} %get-tuple-element.81), channel_id=1, source_target_pairs={{0,1},{1,2},{2,3},{3,0},{4,5},{5,6},{6,7},{7,4},{8,9},{9,10},{10,1... | collective-permute-start | bytes 3538952 | tf_op jit(solution)/shard_map/ppermute | solution.py:78
  361.9 28.0 %collective-permute-start.13 = (bf16[2304,256]{1,0:T(8,128)(2,1)}, bf16[2304,256]{1,0:T(8,128)(2,1)}, u32[]{:S(2)}, u32[]{:S(2)}) collective-permute-start(bf16[2304,256]{1,0:T(8,128)(2,1)} %get-tuple-element.82), channel_id=1, source_target_pairs={{0,3},{1,0},{2,1},{3,2},{4,7},{5,4},{6,5},{7,6},{8,11},{9,8},{10,9... | collective-permute-start | bytes 3538952 | tf_op jit(solution)/shard_map/ppermute | solution.py:78
  368.6 16.1 %all-to-all-start.4 = ((f32[32,1,72]{2,1,0:T(1,128)}), f32[32,1,72]{2,1,0:T(1,128)S(1)}, u32[]{:S(2)}, u32[]{:S(2)}) async-start(f32[32,1,72]{2,1,0:T(1,128)} %bitcast.38), calls=%async_computation.4 | async-start | bytes 32768 | tf_op jit(solution)/shard_map/all_to_all | solution.py:119
  389.9 26.1 %collective-permute-start.15 = (bf16[2304,256]{1,0:T(8,128)(2,1)}, bf16[2304,256]{1,0:T(8,128)(2,1)S(1)}, u32[]{:S(2)}, u32[]{:S(2)}) collective-permute-start(bf16[2304,256]{1,0:T(8,128)(2,1)} %copy-done.28), channel_id=1, source_target_pairs={{0,3},{1,0},{2,1},{3,2},{4,7},{5,4},{6,5},{7,6},{8,11},{9,8},{10,9... | collective-permute-start | bytes 3538952 | tf_op jit(solution)/shard_map/ppermute | solution.py:78
  394.8 26.3 %collective-permute-start.14 = (bf16[2304,256]{1,0:T(8,128)(2,1)S(1)}, bf16[2304,256]{1,0:T(8,128)(2,1)S(1)}, u32[]{:S(2)}, u32[]{:S(2)}) collective-permute-start(bf16[2304,256]{1,0:T(8,128)(2,1)S(1)} %add_convert_fusion.2), channel_id=1, source_target_pairs={{0,1},{1,2},{2,3},{3,0},{4,5},{5,6},{6,7},{7,4},{8,9},{9,10},{10,1... | collective-permute-start | bytes 3538952 | tf_op jit(solution)/shard_map/ppermute | solution.py:78
  421.1 25.4 %collective-permute-start.16 = (bf16[2304,256]{1,0:T(8,128)(2,1)S(1)}, bf16[2304,256]{1,0:T(8,128)(2,1)}, u32[]{:S(2)}, u32[]{:S(2)}) collective-permute-start(bf16[2304,256]{1,0:T(8,128)(2,1)S(1)} %copy-done.27), channel_id=1, source_target_pairs={{0,1},{1,2},{2,3},{3,0},{4,5},{5,6},{6,7},{7,4},{8,9},{9,10},{10,1... | collective-permute-start | bytes 3538952 | tf_op jit(solution)/shard_map/ppermute | solution.py:78
  421.1 25.4 %collective-permute-start.17 = (bf16[2304,256]{1,0:T(8,128)(2,1)}, bf16[2304,256]{1,0:T(8,128)(2,1)}, u32[]{:S(2)}, u32[]{:S(2)}) collective-permute-start(bf16[2304,256]{1,0:T(8,128)(2,1)} %add_convert_fusion.3), channel_id=1, source_target_pairs={{0,3},{1,0},{2,1},{3,2},{4,7},{5,4},{6,5},{7,6},{8,11},{9,8},{10,9... | collective-permute-start | bytes 3538952 | tf_op jit(solution)/shard_map/ppermute | solution.py:78
  426.3 25.1 %all-to-all-start.5 = ((bf16[32,72,256]{2,1,0:T(8,128)(2,1)}), bf16[32,72,256]{2,1,0:T(8,128)(2,1)}, u32[]{:S(2)}, u32[]{:S(2)}) async-start(bf16[32,72,256]{2,1,0:T(8,128)(2,1)} %pad_maximum_fusion.5), calls=%async_computation.6 | async-start | bytes 2359296 | tf_op jit(solution)/shard_map/all_to_all | solution.py:119
  433.1 134.2 %reduce-scatter.6.cloned.1.call-start = ((), (), s32[]{:S(2)}) async-start(), calls=%async_computation.16 | async-start | bytes 11796480 | tf_op jit(solution)/shard_map/reduce_scatter | solution.py:732
  453.4 23.6 %all-to-all-start.6 = ((bf16[32,72,256]{2,1,0:T(8,128)(2,1)}), bf16[32,72,256]{2,1,0:T(8,128)(2,1)S(1)}, u32[]{:S(2)}, u32[]{:S(2)}) async-start(bf16[32,72,256]{2,1,0:T(8,128)(2,1)} %pad_maximum_fusion.6), calls=%async_computation.8 | async-start | bytes 2359296 | tf_op jit(solution)/shard_map/all_to_all | solution.py:119
  458.7 234.7 %reduce-scatter.8.cloned.1.call-start = ((), (), s32[]{:S(2)}) async-start(), calls=%async_computation.17 | async-start | bytes 9732096 | tf_op jit(solution)/shard_map/reduce_scatter | solution.py:812
  464.6 14.0 %collective-permute-start.18 = (bf16[192,512]{1,0:T(8,128)(2,1)S(1)}, bf16[192,512]{1,0:T(8,128)(2,1)S(1)}, u32[]{:S(2)}, u32[]{:S(2)}) collective-permute-start(bf16[192,512]{1,0:T(8,128)(2,1)S(1)} %get-tuple-element.258), channel_id=1, source_target_pairs={{0,1},{1,2},{2,3},{3,0},{4,5},{5,6},{6,7},{7,4},{8,9},{9,10},{10,1... | collective-permute-start | bytes 589832 | tf_op jit(solution)/shard_map/ppermute | solution.py:78
  466.7 19.8 %collective-permute-start.20 = (bf16[192,512]{1,0:T(8,128)(2,1)S(1)}, bf16[192,512]{1,0:T(8,128)(2,1)S(1)}, u32[]{:S(2)}, u32[]{:S(2)}) collective-permute-start(bf16[192,512]{1,0:T(8,128)(2,1)S(1)} %get-tuple-element.259), channel_id=1, source_target_pairs={{0,2},{1,3},{2,0},{3,1},{4,6},{5,7},{6,4},{7,5},{8,10},{9,11},{10,... | collective-permute-start | bytes 589832 | tf_op jit(solution)/shard_map/ppermute | solution.py:78
  468.6 18.0 %collective-permute-start.19 = (bf16[192,512]{1,0:T(8,128)(2,1)S(1)}, bf16[192,512]{1,0:T(8,128)(2,1)S(1)}, u32[]{:S(2)}, u32[]{:S(2)}) collective-permute-start(bf16[192,512]{1,0:T(8,128)(2,1)S(1)} %get-tuple-element.260), channel_id=1, source_target_pairs={{0,3},{1,0},{2,1},{3,2},{4,7},{5,4},{6,5},{7,6},{8,11},{9,8},{10,9... | collective-permute-start | bytes 589832 | tf_op jit(solution)/shard_map/ppermute | solution.py:78
  486.7 14.4 %collective-permute-start.23 = (bf16[192,512]{1,0:T(8,128)(2,1)S(1)}, bf16[192,512]{1,0:T(8,128)(2,1)S(1)}, u32[]{:S(2)}, u32[]{:S(2)}) collective-permute-start(bf16[192,512]{1,0:T(8,128)(2,1)S(1)} %fusion.76), channel_id=1, source_target_pairs={{0,1},{1,2},{2,3},{3,0},{4,5},{5,6},{6,7},{7,4},{8,9},{9,10},{10,1... | collective-permute-start | bytes 589832 | tf_op jit(solution)/shard_map/ppermute | solution.py:78
  486.8 20.1 %collective-permute-start.22 = (bf16[192,512]{1,0:T(8,128)(2,1)S(1)}, bf16[192,512]{1,0:T(8,128)(2,1)S(1)}, u32[]{:S(2)}, u32[]{:S(2)}) collective-permute-start(bf16[192,512]{1,0:T(8,128)(2,1)S(1)} %fusion.76), channel_id=1, source_target_pairs={{0,2},{1,3},{2,0},{3,1},{4,6},{5,7},{6,4},{7,5},{8,10},{9,11},{10,... | collective-permute-start | bytes 589832 | tf_op jit(solution)/shard_map/ppermute | solution.py:78
  489.0 19.6 %collective-permute-start.21 = (bf16[192,512]{1,0:T(8,128)(2,1)S(1)}, bf16[192,512]{1,0:T(8,128)(2,1)S(1)}, u32[]{:S(2)}, u32[]{:S(2)}) collective-permute-start(bf16[192,512]{1,0:T(8,128)(2,1)S(1)} %fusion.76), channel_id=1, source_target_pairs={{0,3},{1,0},{2,1},{3,2},{4,7},{5,4},{6,5},{7,6},{8,11},{9,8},{10,9... | collective-permute-start | bytes 589832 | tf_op jit(solution)/shard_map/ppermute | solution.py:78
  518.7 14.1 %collective-permute-start.28 = (bf16[192,576]{1,0:T(8,128)(2,1)S(1)}, bf16[192,576]{1,0:T(8,128)(2,1)S(1)}, u32[]{:S(2)}, u32[]{:S(2)}) collective-permute-start(bf16[192,576]{1,0:T(8,128)(2,1)S(1)} %pad_maximum_fusion.18), channel_id=1, source_target_pairs={{0,3},{1,0},{2,1},{3,2},{4,7},{5,4},{6,5},{7,6},{8,11},{9,8},{10,9... | collective-permute-start | bytes 663560 | tf_op jit(solution)/shard_map/ppermute | solution.py:78
  519.0 15.1 %collective-permute-start.27 = (bf16[192,576]{1,0:T(8,128)(2,1)S(1)}, bf16[192,576]{1,0:T(8,128)(2,1)S(1)}, u32[]{:S(2)}, u32[]{:S(2)}) collective-permute-start(bf16[192,576]{1,0:T(8,128)(2,1)S(1)} %pad_maximum_fusion.18), channel_id=1, source_target_pairs={{0,1},{1,2},{2,3},{3,0},{4,5},{5,6},{6,7},{7,4},{8,9},{9,10},{10,1... | collective-permute-start | bytes 663560 | tf_op jit(solution)/shard_map/ppermute | solution.py:78
  520.8 23.3 %collective-permute-start.29 = (bf16[192,576]{1,0:T(8,128)(2,1)S(1)}, bf16[192,576]{1,0:T(8,128)(2,1)S(1)}, u32[]{:S(2)}, u32[]{:S(2)}) collective-permute-start(bf16[192,576]{1,0:T(8,128)(2,1)S(1)} %pad_maximum_fusion.18), channel_id=1, source_target_pairs={{0,2},{1,3},{2,0},{3,1},{4,6},{5,7},{6,4},{7,5},{8,10},{9,11},{10,... | collective-permute-start | bytes 663560 | tf_op jit(solution)/shard_map/ppermute | solution.py:78
  582.8 60.7 %collective-permute-start.31 = (bf16[192,512]{1,0:T(8,128)(2,1)}, bf16[192,512]{1,0:T(8,128)(2,1)}, u32[]{:S(2)}, u32[]{:S(2)}) collective-permute-start(bf16[192,512]{1,0:T(8,128)(2,1)} %get-tuple-element.261), channel_id=1, source_target_pairs={{0,1},{1,2},{2,3},{3,0},{4,5},{5,6},{6,7},{7,4},{8,9},{9,10},{10,1... | collective-permute-start | bytes 589832 | tf_op jit(solution)/shard_map/ppermute | solution.py:78
  584.0 59.6 %collective-permute-start.33 = (bf16[192,512]{1,0:T(8,128)(2,1)}, bf16[192,512]{1,0:T(8,128)(2,1)}, u32[]{:S(2)}, u32[]{:S(2)}) collective-permute-start(bf16[192,512]{1,0:T(8,128)(2,1)} %get-tuple-element.262), channel_id=1, source_target_pairs={{0,2},{1,3},{2,0},{3,1},{4,6},{5,7},{6,4},{7,5},{8,10},{9,11},{10,... | collective-permute-start | bytes 589832 | tf_op jit(solution)/shard_map/ppermute | solution.py:78
  590.9 45.4 %all-to-all-start.7 = ((bf16[32,72,512]{2,1,0:T(8,128)(2,1)}), bf16[32,72,512]{2,1,0:T(8,128)(2,1)}, u32[]{:S(2)}, u32[]{:S(2)}) async-start(bf16[32,72,512]{2,1,0:T(8,128)(2,1)} %pad_maximum_fusion.2), calls=%async_computation.9 | async-start | bytes 4718592 | tf_op jit(solution)/shard_map/all_to_all | solution.py:119
  601.6 12.5 %collective-permute-start.37 = (bf16[192,512]{1,0:T(8,128)(2,1)S(1)}, bf16[192,512]{1,0:T(8,128)(2,1)S(1)}, u32[]{:S(2)}, u32[]{:S(2)}) collective-permute-start(bf16[192,512]{1,0:T(8,128)(2,1)S(1)} %get-tuple-element.247), channel_id=1, source_target_pairs={{0,1},{1,2},{2,3},{3,0},{4,5},{5,6},{6,7},{7,4},{8,9},{9,10},{10,1... | collective-permute-start | bytes 589832 | tf_op jit(solution)/shard_map/ppermute | solution.py:78
  601.7 12.4 %collective-permute-start.39 = (bf16[192,512]{1,0:T(8,128)(2,1)S(1)}, bf16[192,512]{1,0:T(8,128)(2,1)S(1)}, u32[]{:S(2)}, u32[]{:S(2)}) collective-permute-start(bf16[192,512]{1,0:T(8,128)(2,1)S(1)} %get-tuple-element.248), channel_id=1, source_target_pairs={{0,2},{1,3},{2,0},{3,1},{4,6},{5,7},{6,4},{7,5},{8,10},{9,11},{10,... | collective-permute-start | bytes 589832 | tf_op jit(solution)/shard_map/ppermute | solution.py:78
  603.2 11.5 %collective-permute-start.38 = (bf16[192,512]{1,0:T(8,128)(2,1)S(1)}, bf16[192,512]{1,0:T(8,128)(2,1)S(1)}, u32[]{:S(2)}, u32[]{:S(2)}) collective-permute-start(bf16[192,512]{1,0:T(8,128)(2,1)S(1)} %get-tuple-element.249), channel_id=1, source_target_pairs={{0,3},{1,0},{2,1},{3,2},{4,7},{5,4},{6,5},{7,6},{8,11},{9,8},{10,9... | collective-permute-start | bytes 589832 | tf_op jit(solution)/shard_map/ppermute | solution.py:78
  615.2 12.8 %collective-permute-start.41 = (bf16[192,512]{1,0:T(8,128)(2,1)S(1)}, bf16[192,512]{1,0:T(8,128)(2,1)S(1)}, u32[]{:S(2)}, u32[]{:S(2)}) collective-permute-start(bf16[192,512]{1,0:T(8,128)(2,1)S(1)} %add_convert_fusion.4), channel_id=1, source_target_pairs={{0,2},{1,3},{2,0},{3,1},{4,6},{5,7},{6,4},{7,5},{8,10},{9,11},{10,... | collective-permute-start | bytes 589832 | tf_op jit(solution)/shard_map/ppermute | solution.py:78
  622.6 20.9 %collective-permute-start.32 = (bf16[192,512]{1,0:T(8,128)(2,1)}, bf16[192,512]{1,0:T(8,128)(2,1)S(1)}, u32[]{:S(2)}, u32[]{:S(2)}) collective-permute-start(bf16[192,512]{1,0:T(8,128)(2,1)} %get-tuple-element.263), channel_id=1, source_target_pairs={{0,3},{1,0},{2,1},{3,2},{4,7},{5,4},{6,5},{7,6},{8,11},{9,8},{10,9... | collective-permute-start | bytes 589832 | tf_op jit(solution)/shard_map/ppermute | solution.py:78
  636.3 55.4 %all-to-all-start.8 = ((f32[32,1,64]{2,1,0:T(1,128)}), f32[32,1,64]{2,1,0:T(1,128)S(1)}, u32[]{:S(2)}, u32[]{:S(2)}) async-start(f32[32,1,64]{2,1,0:T(1,128)} %all_to_all.53), calls=%async_computation.10 | async-start | bytes 32768 | tf_op jit(solution)/shard_map/all_to_all | solution.py:119
  647.1 45.0 %collective-permute-start.36 = (bf16[192,512]{1,0:T(8,128)(2,1)S(1)}, bf16[192,512]{1,0:T(8,128)(2,1)S(1)}, u32[]{:S(2)}, u32[]{:S(2)}) collective-permute-start(bf16[192,512]{1,0:T(8,128)(2,1)S(1)} %add_convert_fusion.5), channel_id=1, source_target_pairs={{0,1},{1,2},{2,3},{3,0},{4,5},{5,6},{6,7},{7,4},{8,9},{9,10},{10,1... | collective-permute-start | bytes 589832 | tf_op jit(solution)/shard_map/ppermute | solution.py:78
  647.2 45.0 %collective-permute-start.35 = (bf16[192,512]{1,0:T(8,128)(2,1)S(1)}, bf16[192,512]{1,0:T(8,128)(2,1)S(1)}, u32[]{:S(2)}, u32[]{:S(2)}) collective-permute-start(bf16[192,512]{1,0:T(8,128)(2,1)S(1)} %add_convert_fusion.5), channel_id=1, source_target_pairs={{0,2},{1,3},{2,0},{3,1},{4,6},{5,7},{6,4},{7,5},{8,10},{9,11},{10,... | collective-permute-start | bytes 589832 | tf_op jit(solution)/shard_map/ppermute | solution.py:78
  649.5 42.7 %collective-permute-start.34 = (bf16[192,512]{1,0:T(8,128)(2,1)S(1)}, bf16[192,512]{1,0:T(8,128)(2,1)S(1)}, u32[]{:S(2)}, u32[]{:S(2)}) collective-permute-start(bf16[192,512]{1,0:T(8,128)(2,1)S(1)} %add_convert_fusion.5), channel_id=1, source_target_pairs={{0,3},{1,0},{2,1},{3,2},{4,7},{5,4},{6,5},{7,6},{8,11},{9,8},{10,9... | collective-permute-start | bytes 589832 | tf_op jit(solution)/shard_map/ppermute | solution.py:78
  (131 other events, 1205.4 us)
Sparse Core Ops, SparseCore 0:
  11.4 57.7 all-gather.3
  71.5 102.0 all-gather.5
  176.4 61.1 all-gather.7
  269.2 93.2 reduce-scatter.3
  451.6 115.5 reduce-scatter.5
  581.0 95.0 reduce-scatter.7

commit v7 on v6

--- a/solution.py
+++ b/solution.py
@@ -171,6 +171,7 @@
 
 
 VMEM_BYTES = 44 * 1024 * 1024
+SMALL_COST = pl.CostEstimate(flops=1, bytes_accessed=1, transcendentals=0)
 
 
 def first_owner_rows(tiles, tile, spill):
@@ -283,7 +284,7 @@
         out_specs=[tile_spec(tile, w) for w, _ in outs],
         out_shape=out_shape,
         scratch_shapes=list(scratch),
-        cost_estimate=pl.CostEstimate(flops=flops, bytes_accessed=moved, transcendentals=0),
+        cost_estimate=SMALL_COST,
         compiler_params=pltpu.CompilerParams(
             dimension_semantics=("arbitrary",), vmem_limit_bytes=VMEM_BYTES
         ),
@@ -350,9 +351,7 @@
         out_specs=tile_spec(block, width),
         out_shape=jax.ShapeDtypeStruct((D, width), bf16),
         scratch_shapes=[pltpu.VMEM((KVR, dkeyval.shape[1]), bf16)],
-        cost_estimate=pl.CostEstimate(
-            flops=2 * D * width * normed.shape[0], bytes_accessed=3 * D * width, transcendentals=0
-        ),
+        cost_estimate=SMALL_COST,
         compiler_params=pltpu.CompilerParams(
             dimension_semantics=("arbitrary",), vmem_limit_bytes=VMEM_BYTES
         ),
@@ -375,81 +374,90 @@
         in_specs=[cols, cols, whole_spec(dboth.shape), whole_spec(hidden.shape)],
         out_specs=tile_spec(block, width),
         out_shape=jax.ShapeDtypeStruct((D, width), bf16),
-        cost_estimate=pl.CostEstimate(
-            flops=2 * D * width * normed2.shape[0], bytes_accessed=3 * D * width, transcendentals=0
-        ),
+        cost_estimate=SMALL_COST,
         compiler_params=pltpu.CompilerParams(
             dimension_semantics=("arbitrary",), vmem_limit_bytes=VMEM_BYTES
         ),
     )(normed2, cotangent, dboth, hidden)
 
 
-def weight_grad_kernel(edge, spill, lane, rows, dy, dboth, hid, gate_out, up_out, down_out, dm, hm):
-    span = dm.shape[1]
-
-    @pl.when((pl.program_id(0) == 0) & (pl.program_id(1) == 0))
+def weight_grad_kernel(edge, spill, lane, left, right, *refs):
+    outs, kept = refs[:-1], refs[-1]
+    span = kept.shape[2]
+    owner = pl.program_id(1)
+
+    @pl.when((pl.program_id(0) == 0) & (owner == 0))
     def _():
         row = lax.broadcasted_iota(jnp.int32, (span, 1), 0)
         first = (row < edge) | (lax.rem(jnp.maximum(row - edge, 0), EXP_DEV * spill) < spill)
         second = (row >= span - edge) | (lax.rem(row, EXP_DEV * spill) >= spill)
         for e, (at, keep) in enumerate(((0, first), (edge, second))):
-            part = dboth[at : at + span, :]
-            dm[e] = jnp.where(keep, part, jnp.zeros_like(part))
-            part = hid[at : at + span, :]
-            hm[e] = jnp.where(keep, part, jnp.zeros_like(part))
-
-    owner = pl.program_id(1)
+            part = left[at : at + span, :].astype(f32)
+            kept[e] = jnp.where(keep, part, 0.0).T.astype(bf16)
+
     at = pl.ds(pl.multiple_of(owner * edge, edge), span)
-    cols = gate_out.shape[2]
-    wide = hid.shape[1]
-    both = matmul_tn(rows[at, :], dm[owner])
-    gate_out[0] = both[:, :cols]
-    up_out[0] = both[:, wide : wide + cols]
-    down_out[0] = matmul_tn(hm[owner], dy[at, :])[:cols]
-
-
-def weight_grads(edge, spill, hid_cols, lane, rows, dy, dboth, hid):
-    total = rows.shape[0]
+    total = matmul(kept[owner], right[at, :])
+    wide = total.shape[0] // len(outs)
+    for k, out in enumerate(outs):
+        out[0] = total[k * wide : k * wide + out.shape[1]]
+
+
+def weight_grads(edge, spill, hid_cols, count, lane, left, right):
+    total, wide = left.shape
     span = total - edge
     block = D // 8
-    assert (span - edge) % (EXP_DEV * spill) == 0
-    up_shape = jax.ShapeDtypeStruct((EXP_DEV, D, hid_cols), f32)
-    up_spec = pl.BlockSpec(
-        (1, block, hid_cols), lambda j, e, lane: (e, lax.rem(lane[0] * 2 + j, 8), 0)
-    )
-    col_spec = pl.BlockSpec((total, block), lambda j, e, lane: (0, j))
     grid_spec = pltpu.PrefetchScalarGridSpec(
         num_scalar_prefetch=1,
         grid=(8, EXP_DEV),
         in_specs=[
-            col_spec,
-            col_spec,
-            pl.BlockSpec(dboth.shape, lambda j, e, lane: (0, 0)),
-            pl.BlockSpec(hid.shape, lambda j, e, lane: (0, 0)),
+            pl.BlockSpec(left.shape, lambda j, e, lane: (0, 0)),
+            pl.BlockSpec((total, block), lambda j, e, lane: (0, j)),
         ],
         out_specs=[
-            up_spec,
-            up_spec,
-            pl.BlockSpec((1, hid_cols, block), lambda j, e, lane: (e, 0, j)),
-        ],
-        scratch_shapes=[
-            pltpu.VMEM((EXP_DEV, span, dboth.shape[1]), bf16),
-            pltpu.VMEM((EXP_DEV, span, hid.shape[1]), bf16),
-        ],
+            pl.BlockSpec(
+                (1, hid_cols, block), lambda j, e, lane: (e, 0, lax.rem(lane[0] * 2 + j, 8))
+            )
+        ]
+        * count,
+        scratch_shapes=[pltpu.VMEM((EXP_DEV, wide, span), bf16)],
     )
     return pl.pallas_call(
         functools.partial(weight_grad_kernel, edge, spill),
         grid_spec=grid_spec,
-        out_shape=[up_shape, up_shape, jax.ShapeDtypeStruct((EXP_DEV, hid_cols, D), f32)],
-        cost_estimate=pl.CostEstimate(
-            flops=4 * EXP_DEV * span * D * (dboth.shape[1] + hid.shape[1]) // 2,
-            bytes_accessed=4 * total * D + 12 * EXP_DEV * hid_cols * D,
-            transcendentals=0,
-        ),
+        out_shape=[jax.ShapeDtypeStruct((EXP_DEV, hid_cols, D), f32)] * count,
+        cost_estimate=SMALL_COST,
         compiler_params=pltpu.CompilerParams(
             dimension_semantics=("arbitrary", "arbitrary"), vmem_limit_bytes=VMEM_BYTES
         ),
-    )(lane.reshape(1), rows, dy, dboth, hid)
+    )(lane.reshape(1), left, right)
+
+
+def shared_kernel(normed2, cotangent, weights, dboth, hidden, part, dnormed):
+    wide = hidden.shape[1]
+    gate_w, up_w, down_w = (weights.at[:, k * wide : (k + 1) * wide] for k in range(3))
+    pre = matmul(normed2[...], gate_w[...])
+    up = matmul(normed2[...], up_w[...])
+    sig = 1.0 / (1.0 + jnp.exp(-pre))
+    act = pre * sig
+    hidden[...] = (act * up).astype(bf16)
+    dh = matmul(cotangent[...], down_w[...])
+    dboth[:, :wide] = (dh * up * (sig * (1.0 + pre * (1.0 - sig)))).astype(bf16)
+    dboth[:, wide:] = (dh * act).astype(bf16)
+    part[...] = matmul_nt(hidden[...], down_w[...]).astype(bf16)
+    dnormed[...] = (
+        matmul_nt(dboth[:, :wide], gate_w[...]) + matmul_nt(dboth[:, wide:], up_w[...])
+    ).astype(bf16)
+
+
+def shared_experts(normed2, cotangent, weights):
+    rows = normed2.shape[0]
+    wide = weights.shape[1] // 3
+    return pl.pallas_call(
+        shared_kernel,
+        out_shape=[jax.ShapeDtypeStruct((rows, w), bf16) for w in (2 * wide, wide, D, D)],
+        cost_estimate=SMALL_COST,
+        compiler_params=pltpu.CompilerParams(vmem_limit_bytes=VMEM_BYTES),
+    )(normed2, cotangent, weights)
 
 
 def per_device(
@@ -620,7 +628,14 @@
     sent = matmul(pick, quarter_of(normed2, 0)).astype(bf16).reshape(owner_count, width, -1)
     one = exchange(sent[:, :, :half])
     two = exchange(after(sent[:, :, half:], one))
-    second_pack = jnp.concatenate([shgate_w, shup_w, shdown_w.T], 1)
+    sh_wide = -(-sh_cols // 128) * 128
+    second_pack = jnp.concatenate(
+        [
+            jnp.pad(w, ((0, 0), (0, sh_wide - sh_cols)))
+            for w in (shgate_w, shup_w, shdown_w.T)
+        ],
+        1,
+    )
     second_full = lax.all_gather(after(second_pack, dy_all, one), "ep", axis=0, tiled=True)
     own = (to_experts(one), to_experts(two))
     first = ring_gather_first(*own)
@@ -634,16 +649,6 @@
         preferred_element_type=f32,
     )
     dy_rows = to_experts(dy_rows.astype(bf16))
-    (ex_dh,) = row_call(
-        functools.partial(hidden_back_kernel, tiles, spill),
-        tile,
-        slot_rows,
-        (dy_rows, down_plain),
-        [tile_spec(tile, D), whole_spec(down_plain.shape)],
-        [(hid_wide, f32)],
-        big,
-    )
-
     logits = matmul(normed2, router_full)
     onehot = (
         expert_ids[:, :, None] == jnp.arange(experts, dtype=jnp.int32)[None, None, :]
@@ -658,23 +663,21 @@
     gate_rows = jnp.sum(gate_rows, 1).reshape(owner_count, width)
     gate_rows = to_experts(exchange(after(gate_rows, two)))[:, None]
 
-    going, ex_dh, gate_rows = lax.optimization_barrier((first[:2], ex_dh, gate_rows))
-    rows = ring_gather_parts(*own, (*going, *first[2:]), ring_gather_second(going))
+    going, dy_rows, gate_rows = lax.optimization_barrier((first, dy_rows, gate_rows))
+    rows = ring_gather_parts(*own, going, ring_gather_second(going))
+    (ex_dh,) = row_call(
+        functools.partial(hidden_back_kernel, tiles, spill),
+        tile,
+        slot_rows,
+        (dy_rows, down_plain),
+        [tile_spec(tile, D), whole_spec(down_plain.shape)],
+        [(hid_wide, f32)],
+        big,
+    )
     upstream = cotangent.astype(f32)
-    sh_in, sh_dy = after((normed2, cotangent), going)
-    gateup_full = second_full[:, : 2 * sh_cols]
-    shdown_t = second_full[:, 2 * sh_cols :]
-    sh_both = matmul(sh_in, gateup_full)
-    sh_gate = sh_both[:, :sh_cols]
-    sh_up = sh_both[:, sh_cols:]
-    sh_sig = 1.0 / (1.0 + jnp.exp(-sh_gate))
-    sh_hidden = (sh_gate * sh_sig * sh_up).astype(bf16)
-    shared_part = matmul_nt(sh_hidden, shdown_t).astype(bf16)
-    sh_dhidden = matmul(sh_dy, shdown_t)
-    sh_dgate = (sh_dhidden * sh_up * sh_sig * (1.0 + sh_gate * (1.0 - sh_sig))).astype(bf16)
-    sh_dup = (sh_dhidden * sh_gate * sh_sig).astype(bf16)
-    sh_dboth = jnp.concatenate([sh_dgate, sh_dup], 1)
-    sh_dnormed_part = matmul_nt(sh_dboth, gateup_full).astype(bf16)
+    sh_dboth, sh_hidden, shared_part, sh_dnormed_part = shared_experts(
+        *after((normed2, cotangent), going), second_full
+    )
     second_grad = second_grads(normed2, cotangent, sh_dboth, sh_hidden)
     second_sum = lax.psum_scatter(second_grad, "ep", scatter_dimension=0, tiled=True)
 
@@ -701,9 +704,7 @@
         in_specs=[tile_spec(tile, hid_wide), whole_spec(down_plain.shape)],
         out_specs=pl.BlockSpec((lanes, tile, quarter), lambda i: (0, i, 0)),
         out_shape=jax.ShapeDtypeStruct((lanes, slot_rows, quarter), bf16),
-        cost_estimate=pl.CostEstimate(
-            flops=big, bytes_accessed=3 * slot_rows * D, transcendentals=0
-        ),
+        cost_estimate=SMALL_COST,
         compiler_params=pltpu.CompilerParams(
             dimension_semantics=("arbitrary",), vmem_limit_bytes=VMEM_BYTES
         ),
@@ -716,8 +717,17 @@
     )
     from_prev_one = shift(plus(drow[2], top), 1)
     from_next_one = shift(after(drow[6], bottom), 3)
-    next_two, prev_two = after(
-        (drow[3], plus(drow[7], bottom)), from_prev_one, from_next_one
+    exgate_grad, exup_grad = weight_grads(
+        edge, spill, hid_cols, 2, lane, *after((ex_dboth, all_rows), top, bottom)
+    )
+    (next_two, prev_two), exgate_grad, exup_grad, _, _ = lax.optimization_barrier(
+        (
+            (drow[3], plus(drow[7], bottom)),
+            exgate_grad,
+            exup_grad,
+            from_prev_one,
+            from_next_one,
+        )
     )
     from_prev_two = shift(next_two, 1)
     from_next_two = shift(prev_two, 3)
@@ -804,8 +814,8 @@
     dtokens, prenorm_grad = rms_back(resid_in, pre_scale, pre_weight, dnormed)
     tokens_grad = (dmid + dtokens).astype(bf16)
     prenorm_sum = jnp.sum(exchange(prenorm_grad.reshape(owner_count, shard)), 0)
-    exgate_grad, exup_grad, exdown_grad = weight_grads(
-        edge, spill, hid_cols, lane, *after((all_rows, dy_rows, ex_dboth, ex_hidden), late)
+    (exdown_grad,) = weight_grads(
+        edge, spill, hid_cols, 1, jnp.zeros_like(lane), *after((ex_hidden, dy_rows), late)
     )
     layer_q = (quarter_of(mid_resid, 0) + routed_q + shared_q).astype(bf16)
     layer_out = gather_quarters(layer_q)
@@ -826,10 +836,10 @@
         first_sum[:, edges[5] + 1],
         first_sum[:, edges[2] : edges[3]],
         second_sum[:, :sh_cols],
-        second_sum[:, sh_cols : 2 * sh_cols],
-        second_sum[:, 2 * sh_cols :].T,
-        exgate_grad,
-        exup_grad,
+        second_sum[:, sh_wide : sh_wide + sh_cols],
+        second_sum[:, 2 * sh_wide : 2 * sh_wide + sh_cols].T,
+        exgate_grad.swapaxes(1, 2),
+        exup_grad.swapaxes(1, 2),
         exdown_grad,
     )
 

time: 715 us -> 676 us (0.945)
  waiting for transfers between devices: 232 us -> 199 us
  matrix products: 72.1 us -> 54.1 us
  Pallas kernels: 93.4 us -> 111 us
    ppermute x43, waiting for transfers between devices: 155 us -> 109 us  [shift(): lax.ppermute(value, 'tp', [(i, (i + step) % lanes) for i in range(lanes)])]
    dot_general x7 -> x5, matrix products: 22.7 us -> 11.3 us  [matmul_nt(): lax.dot_general(left_mat, right_mat, (((1,), (1,)), ((), ())), preferred_...]
    unnamed x256 -> x262, local copies, waits for them, and re-layouts: 51.2 us -> 40.2 us
    pallas_call x0 -> x1, Pallas kernels: none -> 8.72 us  [shared_experts(): pl.pallas_call(shared_kernel, out_shape=[jax.ShapeDtypeStruct((rows, w),...]
    pallas_call x1 -> x2, Pallas kernels: 28.4 us -> 36.7 us  [weight_grads(): pl.pallas_call(functools.partial(weight_grad_kernel, edge, spill), grid_s...]
    reduce_scatter x1, waiting for transfers between devices: 0.01 us -> 8.2 us  [per_device(): lax.psum_scatter(first_grad, 'ep', scatter_dimension=0, tiled=True)]
    dot_general x8 -> x6, matrix products: 21.2 us -> 13.9 us  [matmul(): return jnp.dot(left_mat, right_mat, preferred_element_type=f32)]
  transfers between devices with their start and end apart: 58 -> 58, of which waited for: 33 -> 32; matrix products, arithmetic and copies ran while one was open for 28% -> 27% of each run, Pallas kernels for 11% -> 13%
where the time goes in v7:
time: 676 us; the launch traced here: 669 us
  waiting for transfers between devices  199 us (29%)
  starting transfers between devices  123 us (18%)
  Pallas kernels  111 us (16%)
  local copies, waits for them, and re-layouts  108 us (16%)
  other arithmetic  57.8 us (9%)
  matrix products  54.1 us (8%)
  between operations  16.2 us (2%)
    ppermute x43, waiting for transfers between devices, shift(): lax.ppermute(value, 'tp', [(i, (i + step) % lanes) for i in range(lanes)])  109 us
    ppermute x43, starting transfers between devices, shift(): lax.ppermute(value, 'tp', [(i, (i + step) % lanes) for i in range(lanes)])  65.7 us
    all_to_all x9, starting transfers between devices, exchange(): return lax.all_to_all(value, 'ep', 0, 0, tiled=True)  56.7 us
    all_to_all x9, waiting for transfers between devices, exchange(): return lax.all_to_all(value, 'ep', 0, 0, tiled=True)  46.4 us
    pallas_call x2, Pallas kernels, row_call(): pl.pallas_call(body, grid=(total // tile,), in_specs=in_specs, out_specs=...  41.6 us
    unnamed x262, local copies, waits for them, and re-layouts  40.2 us
    pallas_call x2, Pallas kernels, weight_grads(): pl.pallas_call(functools.partial(weight_grad_kernel, edge, spill), grid_s...  36.7 us
    all_gather x1, waiting for transfers between devices, per_device(): first_full = lax.all_gather(first_pack, 'ep', axis=0, tiled=True)  24 us
  transfers between devices with their start and end apart: 58, of which 32 were waited for; matrix products, arithmetic and copies ran while one was open for 27% of the time, Pallas kernels for 13%

profile of v7, /device:TPU:0, one launch (start us, length us, event | category | flops | bytes accessed | tf_op | source)
XLA Modules:
  0.0 669.1 jit_solution(18397473711191875625)
XLA Ops:
  15.2 7.4 %all-to-all-start = ((s32[32,1,72]{2,1,0:T(1,128)}), s32[32,1,72]{2,1,0:T(1,128)S(1)}, u32[]{:S(2)}, u32[]{:S(2)}) async-start(s32[32,1,72]{2,1,0:T(1,128)} %sub.84), calls=%async_computation | async-start | bytes 32768 | tf_op jit(solution)/shard_map/all_to_all | solution.py:119
  22.8 4.8 constant_dynamic-slice_fusion.30
  41.7 3.2 pad_maximum_fusion.1.refs_8_
  45.2 24.0 %all-gather.4.cloned.1.call-done = bf16[2048,2304]{1,0:T(8,128)(2,1)} async-done(((bf16[64,2304]{1,0:T(8,128)(2,1)}), bf16[2048,2304]{1,0:T(8,128)(2,1)}) %all-gather.4.cloned.1.call-update) | async-done | bytes 9437200 | tf_op jit(solution)/shard_map/all_gather | solution.py:516
  79.3 3.8 fusion.17
  116.7 5.2 collective-permute-done.2
  129.5 5.5 collective-permute-done.4
  140.9 5.2 all-to-all-start.1
  147.9 25.6 %all-to-all-done.1 = bf16[32,72,256]{2,1,0:T(8,128)(2,1)} async-done(((bf16[32,72,256]{2,1,0:T(8,128)(2,1)}), bf16[32,72,256]{2,1,0:T(8,128)(2,1)}, u32[]{:S(2)}, u32[]{:S(2)}) %all-to-all-start.1) | async-done | bytes 1179680 | tf_op jit(solution)/shard_map/all_to_all | solution.py:119
  178.3 6.1 all-to-all-start.2
  194.1 11.1 %all-to-all-done.2 = bf16[32,72,256]{2,1,0:T(8,128)(2,1)} async-done(((bf16[32,72,256]{2,1,0:T(8,128)(2,1)}), bf16[32,72,256]{2,1,0:T(8,128)(2,1)}, u32[]{:S(2)}, u32[]{:S(2)}) %all-to-all-start.2) | async-done | bytes 1179680 | tf_op jit(solution)/shard_map/all_to_all | solution.py:119
  205.2 6.0 all-to-all-start.3
  223.6 15.4 %convolution_convert_fusion = bf16[32,72,2048]{2,1,0:T(8,128)(2,1)} fusion(bf16[32,192,2048]{2,1,0:T(8,128)(2,1)} %bitcast.127, s32[32,72]{1,0:T(8,128)} %bitcast.149), kind=kOutput, calls=%fused_computation.12 | convolution fusion | flops 1817100288 | bytes 34612224 | tf_op jit(solution)/shard_map/ist,itd->isd/dot_general | solution.py:645
  238.9 4.0 fusion.106
  244.3 4.3 pad_maximum_fusion.refs_0_.right
  251.0 8.7 %shard_map.307 = (bf16[192,1536]{1,0:T(8,128)(2,1)S(1)}, bf16[192,768]{1,0:T(8,128)(2,1)S(1)}, bf16[192,2048]{1,0:T(8,128)(2,1)S(1)}, bf16[192,2048]{1,0:T(8,128)(2,1)S(1)}) custom-call(bf16[192,2048]{1,0:T(8,128)(2,1)S(1)} %copy-done.3, bf16[192,2048]{1,0:T(8,128)(2,1)S(1)} %copy-done, bf16[2048,2304]{1,0:T(8,128)(2,1)} %all-gather.8.cloned.1.call-done.weights), custom_call_target="tpu_custom_call" | custom-call | flops 1 | bytes 1 | tf_op jit(solution)/shard_map/pallas_call | solution.py:455
  261.5 6.9 %shard_map.308 = bf16[2048,2304]{1,0:T(8,128)(2,1)} custom-call(bf16[192,2048]{1,0:T(8,128)(2,1)S(1)} %copy-done.4, bf16[192,2048]{1,0:T(8,128)(2,1)S(1)} %copy-done, bf16[192,1536]{1,0:T(8,128)(2,1)S(1)} %get-tuple-element.90.dboth, bf16[192,768]{1,0:T(8,128)(2,1)S(1)} %get-tuple-element.91.hidden), custom_call_target="tpu_custom_call" | custom-call | flops 1 | bytes 1 | tf_op jit(solution)/shard_map/pallas_call | solution.py:371
  271.6 11.0 %shard_map.306.refs_9_ = f32[2304,384]{1,0:T(8,128)S(1)} custom-call(bf16[2304,2048]{1,0:T(8,128)(2,1)} %pad_maximum_fusion.refs_0_.right, bf16[2,384,2048]{2,1,0:T(8,128)(2,1)S(1)} %pad.51.refs_1_.weight), custom_call_target="tpu_custom_call" | custom-call | flops 1 | bytes 1 | tf_op jit(solution)/shard_map/pallas_call | solution.py:280
  285.9 11.0 %collective-permute-done.11.refs_5_ = bf16[2304,256]{1,0:T(8,128)(2,1)} collective-permute-done((bf16[2304,256]{1,0:T(8,128)(2,1)}, bf16[2304,256]{1,0:T(8,128)(2,1)}, u32[]{:S(2)}, u32[]{:S(2)}) %collective-permute-start.11) | collective-permute-done | bytes 1179680 | tf_op jit(solution)/shard_map/ppermute | solution.py:78
  296.8 3.6 collective-permute-done.10.refs_4_
  300.4 30.6 %shard_map.309 = (bf16[2304,384]{1,0:T(8,128)(2,1)}, bf16[2304,768]{1,0:T(8,128)(2,1)}, f32[2304,1]{1,0:T(8,128)S(1)}, bf16[2304,256]{1,0:T(8,128)(2,1)S(1)}, bf...) custom-call(bf16[2304,256]{1,0:T(8,128)(2,1)} %pad_maximum_fusion.3., ...), custom_call_target="tpu_custom_call" | custom-call | flops 1 | bytes 1 | tf_op jit(solution)/shard_map/pallas_call | solution.py:280
  336.2 3.2 collective-permute-start.13
  346.8 5.7 all-to-all-start.4
  354.0 9.3 %shard_map.310 = bf16[4,2304,512]{2,1,0:T(8,128)(2,1)} custom-call(bf16[2304,384]{1,0:T(8,128)(2,1)S(1)} %copy-done.7, bf16[2,384,2048]{2,1,0:T(8,128)(2,1)S(1)} %pad.51.refs_1_.weight), custom_call_target="tpu_custom_call" | custom-call | flops 1 | bytes 1 | tf_op jit(solution)/shard_map/pallas_call | solution.py:701
  369.7 19.4 %shard_map.311 = (f32[2,352,2048]{2,1,0:T(8,128)}, f32[2,352,2048]{2,1,0:T(8,128)}) custom-call(s32[1]{0:T(128)} %bitcast.40.lane, bf16[2304,768]{1,0:T(8,128)(2,1)S(1)} %copy-done.9, bf16[2304,2048]{1,0:T(8,128)(2,1)} %get-tuple-element.107.right), custom_call_target="tpu_custom_call" | custom-call | flops 1 | bytes 1 | tf_op jit(solution)/shard_map/pallas_call | solution.py:424
  393.0 3.4 collective-permute-done.14
  401.3 7.5 %all-to-all-start.5 = ((bf16[32,72,256]{2,1,0:T(8,128)(2,1)}), bf16[32,72,256]{2,1,0:T(8,128)(2,1)}, u32[]{:S(2)}, u32[]{:S(2)}) async-start(bf16[32,72,256]{2,1,0:T(8,128)(2,1)} %pad_maximum_fusion.5), calls=%async_computation.6 | async-start | bytes 2359296 | tf_op jit(solution)/shard_map/all_to_all | solution.py:119
  408.9 13.6 %collective-permute-done.16 = bf16[2304,256]{1,0:T(8,128)(2,1)} collective-permute-done((bf16[2304,256]{1,0:T(8,128)(2,1)S(1)}, bf16[2304,256]{1,0:T(8,128)(2,1)}, u32[]{:S(2)}, u32[]{:S(2)}) %collective-permute-start.16) | collective-permute-done | bytes 1179680 | tf_op jit(solution)/shard_map/ppermute | solution.py:78
  429.2 7.5 %all-to-all-start.6 = ((bf16[32,72,256]{2,1,0:T(8,128)(2,1)}), bf16[32,72,256]{2,1,0:T(8,128)(2,1)S(1)}, u32[]{:S(2)}, u32[]{:S(2)}) async-start(bf16[32,72,256]{2,1,0:T(8,128)(2,1)} %pad_maximum_fusion.6), calls=%async_computation.8 | async-start | bytes 2359296 | tf_op jit(solution)/shard_map/all_to_all | solution.py:119
  447.4 3.3 fusion.103
  450.7 4.4 all-to-all-done.6
  456.7 7.8 %collective-permute-done.20 = bf16[192,512]{1,0:T(8,128)(2,1)S(1)} collective-permute-done((bf16[192,512]{1,0:T(8,128)(2,1)S(1)}, bf16[192,512]{1,0:T(8,128)(2,1)S(1)}, u32[]{:S(2)}, u32[]{:S(2)}) %collective-permute-start.20) | collective-permute-done | bytes 196640 | tf_op jit(solution)/shard_map/ppermute | solution.py:78
  472.0 8.1 %collective-permute-done.23 = bf16[192,512]{1,0:T(8,128)(2,1)S(1)} collective-permute-done((bf16[192,512]{1,0:T(8,128)(2,1)S(1)}, bf16[192,512]{1,0:T(8,128)(2,1)S(1)}, u32[]{:S(2)}, u32[]{:S(2)}) %collective-permute-start.23) | collective-permute-done | bytes 196640 | tf_op jit(solution)/shard_map/ppermute | solution.py:78
  480.1 5.7 collective-permute-done.22
  502.6 8.7 %collective-permute-done.28 = bf16[192,576]{1,0:T(8,128)(2,1)S(1)} collective-permute-done((bf16[192,576]{1,0:T(8,128)(2,1)S(1)}, bf16[192,576]{1,0:T(8,128)(2,1)S(1)}, u32[]{:S(2)}, u32[]{:S(2)}) %collective-permute-start.28) | collective-permute-done | bytes 221216 | tf_op jit(solution)/shard_map/ppermute | solution.py:78
  512.7 10.2 %collective-permute-done.29 = bf16[192,576]{1,0:T(8,128)(2,1)S(1)} collective-permute-done((bf16[192,576]{1,0:T(8,128)(2,1)S(1)}, bf16[192,576]{1,0:T(8,128)(2,1)S(1)}, u32[]{:S(2)}, u32[]{:S(2)}) %collective-permute-start.29) | collective-permute-done | bytes 221216 | tf_op jit(solution)/shard_map/ppermute | solution.py:78
  534.4 10.7 %reduce-scatter.6.cloned.1.call-done = bf16[2304,512]{1,0:T(8,128)(2,1)} async-done(((bf16[9216,512]{1,0:T(8,128)(2,1)}), bf16[2304,512]{1,0:T(8,128)(2,1)}) %reduce-scatter.6.cloned.1.call-update) | async-done | bytes 2359312 | tf_op jit(solution)/shard_map/reduce_scatter | solution.py:742
  550.8 7.9 %shard_map.312 = bf16[2048,2304]{1,0:T(8,128)(2,1)} custom-call(bf16[192,2048]{1,0:T(8,128)(2,1)S(1)} %copy-done.12, bf16[192,2048]{1,0:T(8,128)(2,1)S(1)} %copy-done.5, bf16[192,2048]{1,0:T(8,128)(2,1)S(1)} %fusion.99.dmid, bf16[192,768]{1,0:T(8,128)(2,1)S(1)} %copy-done.22, bf16[192,640]{1,0:T(8,128)(2,1)S(1)} %copy-done.24, ...), custom_call_target="tpu_custom_call" | custom-call | flops 1 | bytes 1 | tf_op jit(solution)/shard_map/pallas_call | solution.py:345
  559.6 4.7 collective-permute-done.30
  573.1 7.3 %all-to-all-start.7 = ((bf16[32,72,512]{2,1,0:T(8,128)(2,1)}), bf16[32,72,512]{2,1,0:T(8,128)(2,1)}, u32[]{:S(2)}, u32[]{:S(2)}) async-start(bf16[32,72,512]{2,1,0:T(8,128)(2,1)} %pad_maximum_fusion.2), calls=%async_computation.9 | async-start | bytes 4718592 | tf_op jit(solution)/shard_map/all_to_all | solution.py:119
  591.3 7.3 %collective-permute-done.42 = bf16[192,512]{1,0:T(8,128)(2,1)S(1)} collective-permute-done((bf16[192,512]{1,0:T(8,128)(2,1)S(1)}, bf16[192,512]{1,0:T(8,128)(2,1)S(1)}, u32[]{:S(2)}, u32[]{:S(2)}) %collective-permute-start.42) | collective-permute-done | bytes 196640 | tf_op jit(solution)/shard_map/ppermute | solution.py:78
  599.2 3.2 collective-permute-done.41
  602.8 3.2 fusion.44
  608.9 3.4 all-to-all-done.7
  612.3 3.9 all-to-all-start.8
  616.2 3.4 add_convert_fusion.5
  626.8 17.3 %shard_map.313 = f32[2,352,2048]{2,1,0:T(8,128)} custom-call(s32[1]{0:T(128)} %constant.114.clone.1.lane, bf16[2304,384]{1,0:T(8,128)(2,1)S(1)} %copy-done.8, bf16[2304,2048]{1,0:T(8,128)(2,1)} %pad_maximum_fusion.refs_0_.right), custom_call_target="tpu_custom_call" | custom-call | flops 1 | bytes 1 | tf_op jit(solution)/shard_map/pallas_call | solution.py:424
  645.8 8.2 %reduce-scatter.8.cloned.1.call-done = bf16[64,2304]{1,0:T(8,128)(2,1)} async-done(((bf16[2048,2304]{1,0:T(8,128)(2,1)}), bf16[64,2304]{1,0:T(8,128)(2,1)}) %reduce-scatter.8.cloned.1.call-update) | async-done | bytes 294928 | tf_op jit(solution)/shard_map/reduce_scatter | solution.py:822
  (526 shorter events, 251.3 us)
Async XLA Ops:
  7.2 62.1 %all-gather.4.cloned.1.call-start = ((), (), s32[]{:S(2)}) async-start(), calls=%async_computation.12 | async-start | bytes 9732096 | tf_op jit(solution)/shard_map/all_gather | solution.py:516
  15.2 30.1 %all-to-all-start = ((s32[32,1,72]{2,1,0:T(1,128)}), s32[32,1,72]{2,1,0:T(1,128)S(1)}, u32[]{:S(2)}, u32[]{:S(2)}) async-start(s32[32,1,72]{2,1,0:T(1,128)} %sub.84), calls=%async_computation | async-start | bytes 32768 | tf_op jit(solution)/shard_map/all_to_all | solution.py:119
  22.6 152.4 %all-gather.6.cloned.1.call-start = ((), (), s32[]{:S(2)}) async-start(), calls=%async_computation.13 | async-start | bytes 25952256 | tf_op jit(solution)/shard_map/all_gather | solution.py:566
  109.7 12.1 %collective-permute-start.2 = (bf16[192,512]{1,0:T(8,128)(2,1)S(1)}, bf16[192,512]{1,0:T(8,128)(2,1)S(1)}, u32[]{:S(2)}, u32[]{:S(2)}) collective-permute-start(bf16[192,512]{1,0:T(8,128)(2,1)S(1)} %get-tuple-element.200), channel_id=1, source_target_pairs={{0,2},{1,3},{2,0},{3,1},{4,6},{5,7},{6,4},{7,5},{8,10},{9,11},{10,... | collective-permute-start | bytes 589832 | tf_op jit(solution)/shard_map/ppermute | solution.py:78
  140.9 32.6 %all-to-all-start.1 = ((bf16[32,72,256]{2,1,0:T(8,128)(2,1)}), bf16[32,72,256]{2,1,0:T(8,128)(2,1)}, u32[]{:S(2)}, u32[]{:S(2)}) async-start(bf16[32,72,256]{2,1,0:T(8,128)(2,1)} %get-tuple-element.159), calls=%async_computation.1 | async-start | bytes 2359296 | tf_op jit(solution)/shard_map/all_to_all | solution.py:119
  146.1 102.6 %all-gather.8.cloned.1.call-start = ((), (), s32[]{:S(2)}) async-start(), calls=%async_computation.14 | async-start | bytes 9732096 | tf_op jit(solution)/shard_map/all_gather | solution.py:639
  178.3 26.9 %all-to-all-start.2 = ((bf16[32,72,256]{2,1,0:T(8,128)(2,1)}), bf16[32,72,256]{2,1,0:T(8,128)(2,1)}, u32[]{:S(2)}, u32[]{:S(2)}) async-start(bf16[32,72,256]{2,1,0:T(8,128)(2,1)} %get-tuple-element.73), calls=%async_computation.2 | async-start | bytes 2359296 | tf_op jit(solution)/shard_map/all_to_all | solution.py:119
  191.2 57.4 %collective-permute-start.9 = (bf16[2304,256]{1,0:T(8,128)(2,1)}, bf16[2304,256]{1,0:T(8,128)(2,1)}, u32[]{:S(2)}, u32[]{:S(2)}) collective-permute-start(bf16[2304,256]{1,0:T(8,128)(2,1)} %pad_maximum_fusion.3.refs_0_), channel_id=1, source_target_pairs={{0,3},{1,0},{2,1},{3,2},{4,7},{5,4},{6,5},{7,6},{8,11},{9,8},{10,9... | collective-permute-start | bytes 3538952 | tf_op jit(solution)/shard_map/ppermute | solution.py:78
  194.1 54.5 %collective-permute-start.6 = (bf16[2304,256]{1,0:T(8,128)(2,1)}, bf16[2304,256]{1,0:T(8,128)(2,1)}, u32[]{:S(2)}, u32[]{:S(2)}) collective-permute-start(bf16[2304,256]{1,0:T(8,128)(2,1)} %pad_maximum_fusion.3.refs_0_), channel_id=1, source_target_pairs={{0,1},{1,2},{2,3},{3,0},{4,5},{5,6},{6,7},{7,4},{8,9},{9,10},{10,1... | collective-permute-start | bytes 3538952 | tf_op jit(solution)/shard_map/ppermute | solution.py:78
  205.2 13.3 %all-to-all-start.3 = ((f32[32,1,72]{2,1,0:T(1,128)}), f32[32,1,72]{2,1,0:T(1,128)S(1)}, u32[]{:S(2)}, u32[]{:S(2)}) async-start(f32[32,1,72]{2,1,0:T(1,128)} %bitcast.154), calls=%async_computation.3 | async-start | bytes 32768 | tf_op jit(solution)/shard_map/all_to_all | solution.py:119
  211.3 216.0 %reduce-scatter.4.cloned.1.call-start = ((), (), s32[]{:S(2)}) async-start(), calls=%async_computation.15 | async-start | bytes 9732096 | tf_op jit(solution)/shard_map/reduce_scatter | solution.py:682
  214.6 34.1 %collective-permute-start.8 = (bf16[2304,256]{1,0:T(8,128)(2,1)}, bf16[2304,256]{1,0:T(8,128)(2,1)}, u32[]{:S(2)}, u32[]{:S(2)}) collective-permute-start(bf16[2304,256]{1,0:T(8,128)(2,1)} %pad_maximum_fusion.4.refs_1_), channel_id=1, source_target_pairs={{0,1},{1,2},{2,3},{3,0},{4,5},{5,6},{6,7},{7,4},{8,9},{9,10},{10,1... | collective-permute-start | bytes 3538952 | tf_op jit(solution)/shard_map/ppermute | solution.py:78
  216.2 32.6 %collective-permute-start.7 = (bf16[2304,256]{1,0:T(8,128)(2,1)}, bf16[2304,256]{1,0:T(8,128)(2,1)}, u32[]{:S(2)}, u32[]{:S(2)}) collective-permute-start(bf16[2304,256]{1,0:T(8,128)(2,1)} %pad_maximum_fusion.4.refs_1_), channel_id=1, source_target_pairs={{0,3},{1,0},{2,1},{3,2},{4,7},{5,4},{6,5},{7,6},{8,11},{9,8},{10,9... | collective-permute-start | bytes 3538952 | tf_op jit(solution)/shard_map/ppermute | solution.py:78
  268.5 28.4 %collective-permute-start.11 = (bf16[2304,256]{1,0:T(8,128)(2,1)}, bf16[2304,256]{1,0:T(8,128)(2,1)}, u32[]{:S(2)}, u32[]{:S(2)}) collective-permute-start(bf16[2304,256]{1,0:T(8,128)(2,1)} %collective-permute-done.7.refs_3_), channel_id=1, source_target_pairs={{0,3},{1,0},{2,1},{3,2},{4,7},{5,4},{6,5},{7,6},{8,11},{9,8},{10,9... | collective-permute-start | bytes 3538952 | tf_op jit(solution)/shard_map/ppermute | solution.py:78
  271.4 29.0 %collective-permute-start.10 = (bf16[2304,256]{1,0:T(8,128)(2,1)}, bf16[2304,256]{1,0:T(8,128)(2,1)}, u32[]{:S(2)}, u32[]{:S(2)}) collective-permute-start(bf16[2304,256]{1,0:T(8,128)(2,1)} %collective-permute-done.6.refs_6_), channel_id=1, source_target_pairs={{0,1},{1,2},{2,3},{3,0},{4,5},{5,6},{6,7},{7,4},{8,9},{9,10},{10,1... | collective-permute-start | bytes 3538952 | tf_op jit(solution)/shard_map/ppermute | solution.py:78
  336.2 28.4 %collective-permute-start.12 = (bf16[2304,256]{1,0:T(8,128)(2,1)}, bf16[2304,256]{1,0:T(8,128)(2,1)}, u32[]{:S(2)}, u32[]{:S(2)}) collective-permute-start(bf16[2304,256]{1,0:T(8,128)(2,1)} %get-tuple-element.94), channel_id=1, source_target_pairs={{0,1},{1,2},{2,3},{3,0},{4,5},{5,6},{6,7},{7,4},{8,9},{9,10},{10,1... | collective-permute-start | bytes 3538952 | tf_op jit(solution)/shard_map/ppermute | solution.py:78
  336.2 28.4 %collective-permute-start.13 = (bf16[2304,256]{1,0:T(8,128)(2,1)}, bf16[2304,256]{1,0:T(8,128)(2,1)}, u32[]{:S(2)}, u32[]{:S(2)}) collective-permute-start(bf16[2304,256]{1,0:T(8,128)(2,1)} %get-tuple-element.95), channel_id=1, source_target_pairs={{0,3},{1,0},{2,1},{3,2},{4,7},{5,4},{6,5},{7,6},{8,11},{9,8},{10,9... | collective-permute-start | bytes 3538952 | tf_op jit(solution)/shard_map/ppermute | solution.py:78
  346.8 16.4 %all-to-all-start.4 = ((f32[32,1,72]{2,1,0:T(1,128)}), f32[32,1,72]{2,1,0:T(1,128)S(1)}, u32[]{:S(2)}, u32[]{:S(2)}) async-start(f32[32,1,72]{2,1,0:T(1,128)} %bitcast.157), calls=%async_computation.4 | async-start | bytes 32768 | tf_op jit(solution)/shard_map/all_to_all | solution.py:119
  364.6 28.4 %collective-permute-start.15 = (bf16[2304,256]{1,0:T(8,128)(2,1)}, bf16[2304,256]{1,0:T(8,128)(2,1)S(1)}, u32[]{:S(2)}, u32[]{:S(2)}) collective-permute-start(bf16[2304,256]{1,0:T(8,128)(2,1)} %copy-done.33), channel_id=1, source_target_pairs={{0,3},{1,0},{2,1},{3,2},{4,7},{5,4},{6,5},{7,6},{8,11},{9,8},{10,9... | collective-permute-start | bytes 3538952 | tf_op jit(solution)/shard_map/ppermute | solution.py:78
  369.1 27.3 %collective-permute-start.14 = (bf16[2304,256]{1,0:T(8,128)(2,1)S(1)}, bf16[2304,256]{1,0:T(8,128)(2,1)S(1)}, u32[]{:S(2)}, u32[]{:S(2)}) collective-permute-start(bf16[2304,256]{1,0:T(8,128)(2,1)S(1)} %add_convert_fusion.2), channel_id=1, source_target_pairs={{0,1},{1,2},{2,3},{3,0},{4,5},{5,6},{6,7},{7,4},{8,9},{9,10},{10,1... | collective-permute-start | bytes 3538952 | tf_op jit(solution)/shard_map/ppermute | solution.py:78
  396.4 26.2 %collective-permute-start.16 = (bf16[2304,256]{1,0:T(8,128)(2,1)S(1)}, bf16[2304,256]{1,0:T(8,128)(2,1)}, u32[]{:S(2)}, u32[]{:S(2)}) collective-permute-start(bf16[2304,256]{1,0:T(8,128)(2,1)S(1)} %copy-done.32), channel_id=1, source_target_pairs={{0,1},{1,2},{2,3},{3,0},{4,5},{5,6},{6,7},{7,4},{8,9},{9,10},{10,1... | collective-permute-start | bytes 3538952 | tf_op jit(solution)/shard_map/ppermute | solution.py:78
  396.9 26.6 %collective-permute-start.17 = (bf16[2304,256]{1,0:T(8,128)(2,1)}, bf16[2304,256]{1,0:T(8,128)(2,1)}, u32[]{:S(2)}, u32[]{:S(2)}) collective-permute-start(bf16[2304,256]{1,0:T(8,128)(2,1)} %add_convert_fusion.3), channel_id=1, source_target_pairs={{0,3},{1,0},{2,1},{3,2},{4,7},{5,4},{6,5},{7,6},{8,11},{9,8},{10,9... | collective-permute-start | bytes 3538952 | tf_op jit(solution)/shard_map/ppermute | solution.py:78
  401.3 25.9 %all-to-all-start.5 = ((bf16[32,72,256]{2,1,0:T(8,128)(2,1)}), bf16[32,72,256]{2,1,0:T(8,128)(2,1)}, u32[]{:S(2)}, u32[]{:S(2)}) async-start(bf16[32,72,256]{2,1,0:T(8,128)(2,1)} %pad_maximum_fusion.5), calls=%async_computation.6 | async-start | bytes 2359296 | tf_op jit(solution)/shard_map/all_to_all | solution.py:119
  408.9 136.2 %reduce-scatter.6.cloned.1.call-start = ((), (), s32[]{:S(2)}) async-start(), calls=%async_computation.16 | async-start | bytes 11796480 | tf_op jit(solution)/shard_map/reduce_scatter | solution.py:742
  429.2 25.9 %all-to-all-start.6 = ((bf16[32,72,256]{2,1,0:T(8,128)(2,1)}), bf16[32,72,256]{2,1,0:T(8,128)(2,1)S(1)}, u32[]{:S(2)}, u32[]{:S(2)}) async-start(bf16[32,72,256]{2,1,0:T(8,128)(2,1)} %pad_maximum_fusion.6), calls=%async_computation.8 | async-start | bytes 2359296 | tf_op jit(solution)/shard_map/all_to_all | solution.py:119
  436.7 217.3 %reduce-scatter.8.cloned.1.call-start = ((), (), s32[]{:S(2)}) async-start(), calls=%async_computation.17 | async-start | bytes 9732096 | tf_op jit(solution)/shard_map/reduce_scatter | solution.py:822
  442.5 14.1 %collective-permute-start.18 = (bf16[192,512]{1,0:T(8,128)(2,1)S(1)}, bf16[192,512]{1,0:T(8,128)(2,1)S(1)}, u32[]{:S(2)}, u32[]{:S(2)}) collective-permute-start(bf16[192,512]{1,0:T(8,128)(2,1)S(1)} %get-tuple-element.189), channel_id=1, source_target_pairs={{0,1},{1,2},{2,3},{3,0},{4,5},{5,6},{6,7},{7,4},{8,9},{9,10},{10,1... | collective-permute-start | bytes 589832 | tf_op jit(solution)/shard_map/ppermute | solution.py:78
  444.6 19.8 %collective-permute-start.20 = (bf16[192,512]{1,0:T(8,128)(2,1)S(1)}, bf16[192,512]{1,0:T(8,128)(2,1)S(1)}, u32[]{:S(2)}, u32[]{:S(2)}) collective-permute-start(bf16[192,512]{1,0:T(8,128)(2,1)S(1)} %get-tuple-element.190), channel_id=1, source_target_pairs={{0,2},{1,3},{2,0},{3,1},{4,6},{5,7},{6,4},{7,5},{8,10},{9,11},{10,... | collective-permute-start | bytes 589832 | tf_op jit(solution)/shard_map/ppermute | solution.py:78
  446.5 18.1 %collective-permute-start.19 = (bf16[192,512]{1,0:T(8,128)(2,1)S(1)}, bf16[192,512]{1,0:T(8,128)(2,1)}, u32[]{:S(2)}, u32[]{:S(2)}) collective-permute-start(bf16[192,512]{1,0:T(8,128)(2,1)S(1)} %get-tuple-element.191), channel_id=1, source_target_pairs={{0,3},{1,0},{2,1},{3,2},{4,7},{5,4},{6,5},{7,6},{8,11},{9,8},{10,9... | collective-permute-start | bytes 589832 | tf_op jit(solution)/shard_map/ppermute | solution.py:78
  465.7 14.4 %collective-permute-start.23 = (bf16[192,512]{1,0:T(8,128)(2,1)S(1)}, bf16[192,512]{1,0:T(8,128)(2,1)S(1)}, u32[]{:S(2)}, u32[]{:S(2)}) collective-permute-start(bf16[192,512]{1,0:T(8,128)(2,1)S(1)} %fusion.66), channel_id=1, source_target_pairs={{0,1},{1,2},{2,3},{3,0},{4,5},{5,6},{6,7},{7,4},{8,9},{9,10},{10,1... | collective-permute-start | bytes 589832 | tf_op jit(solution)/shard_map/ppermute | solution.py:78
  465.8 20.0 %collective-permute-start.22 = (bf16[192,512]{1,0:T(8,128)(2,1)S(1)}, bf16[192,512]{1,0:T(8,128)(2,1)S(1)}, u32[]{:S(2)}, u32[]{:S(2)}) collective-permute-start(bf16[192,512]{1,0:T(8,128)(2,1)S(1)} %fusion.66), channel_id=1, source_target_pairs={{0,2},{1,3},{2,0},{3,1},{4,6},{5,7},{6,4},{7,5},{8,10},{9,11},{10,... | collective-permute-start | bytes 589832 | tf_op jit(solution)/shard_map/ppermute | solution.py:78
  468.0 19.6 %collective-permute-start.21 = (bf16[192,512]{1,0:T(8,128)(2,1)S(1)}, bf16[192,512]{1,0:T(8,128)(2,1)S(1)}, u32[]{:S(2)}, u32[]{:S(2)}) collective-permute-start(bf16[192,512]{1,0:T(8,128)(2,1)S(1)} %fusion.66), channel_id=1, source_target_pairs={{0,3},{1,0},{2,1},{3,2},{4,7},{5,4},{6,5},{7,6},{8,11},{9,8},{10,9... | collective-permute-start | bytes 589832 | tf_op jit(solution)/shard_map/ppermute | solution.py:78
  497.2 14.1 %collective-permute-start.28 = (bf16[192,576]{1,0:T(8,128)(2,1)S(1)}, bf16[192,576]{1,0:T(8,128)(2,1)S(1)}, u32[]{:S(2)}, u32[]{:S(2)}) collective-permute-start(bf16[192,576]{1,0:T(8,128)(2,1)S(1)} %pad_maximum_fusion.17), channel_id=1, source_target_pairs={{0,3},{1,0},{2,1},{3,2},{4,7},{5,4},{6,5},{7,6},{8,11},{9,8},{10,9... | collective-permute-start | bytes 663560 | tf_op jit(solution)/shard_map/ppermute | solution.py:78
  497.6 15.1 %collective-permute-start.27 = (bf16[192,576]{1,0:T(8,128)(2,1)S(1)}, bf16[192,576]{1,0:T(8,128)(2,1)S(1)}, u32[]{:S(2)}, u32[]{:S(2)}) collective-permute-start(bf16[192,576]{1,0:T(8,128)(2,1)S(1)} %pad_maximum_fusion.17), channel_id=1, source_target_pairs={{0,1},{1,2},{2,3},{3,0},{4,5},{5,6},{6,7},{7,4},{8,9},{9,10},{10,1... | collective-permute-start | bytes 663560 | tf_op jit(solution)/shard_map/ppermute | solution.py:78
  499.3 23.6 %collective-permute-start.29 = (bf16[192,576]{1,0:T(8,128)(2,1)S(1)}, bf16[192,576]{1,0:T(8,128)(2,1)S(1)}, u32[]{:S(2)}, u32[]{:S(2)}) collective-permute-start(bf16[192,576]{1,0:T(8,128)(2,1)S(1)} %pad_maximum_fusion.17), channel_id=1, source_target_pairs={{0,2},{1,3},{2,0},{3,1},{4,6},{5,7},{6,4},{7,5},{8,10},{9,11},{10,... | collective-permute-start | bytes 663560 | tf_op jit(solution)/shard_map/ppermute | solution.py:78
  568.1 17.2 %collective-permute-start.37 = (bf16[192,512]{1,0:T(8,128)(2,1)}, bf16[192,512]{1,0:T(8,128)(2,1)S(1)}, u32[]{:S(2)}, u32[]{:S(2)}) collective-permute-start(bf16[192,512]{1,0:T(8,128)(2,1)} %get-tuple-element.178), channel_id=1, source_target_pairs={{0,1},{1,2},{2,3},{3,0},{4,5},{5,6},{6,7},{7,4},{8,9},{9,10},{10,1... | collective-permute-start | bytes 589832 | tf_op jit(solution)/shard_map/ppermute | solution.py:78
  568.1 17.2 %collective-permute-start.39 = (bf16[192,512]{1,0:T(8,128)(2,1)}, bf16[192,512]{1,0:T(8,128)(2,1)}, u32[]{:S(2)}, u32[]{:S(2)}) collective-permute-start(bf16[192,512]{1,0:T(8,128)(2,1)} %get-tuple-element.179), channel_id=1, source_target_pairs={{0,2},{1,3},{2,0},{3,1},{4,6},{5,7},{6,4},{7,5},{8,10},{9,11},{10,... | collective-permute-start | bytes 589832 | tf_op jit(solution)/shard_map/ppermute | solution.py:78
  569.3 16.0 %collective-permute-start.38 = (bf16[192,512]{1,0:T(8,128)(2,1)S(1)}, bf16[192,512]{1,0:T(8,128)(2,1)}, u32[]{:S(2)}, u32[]{:S(2)}) collective-permute-start(bf16[192,512]{1,0:T(8,128)(2,1)S(1)} %get-tuple-element.180), channel_id=1, source_target_pairs={{0,3},{1,0},{2,1},{3,2},{4,7},{5,4},{6,5},{7,6},{8,11},{9,8},{10,9... | collective-permute-start | bytes 589832 | tf_op jit(solution)/shard_map/ppermute | solution.py:78
  573.1 39.1 %all-to-all-start.7 = ((bf16[32,72,512]{2,1,0:T(8,128)(2,1)}), bf16[32,72,512]{2,1,0:T(8,128)(2,1)}, u32[]{:S(2)}, u32[]{:S(2)}) async-start(bf16[32,72,512]{2,1,0:T(8,128)(2,1)} %pad_maximum_fusion.2), calls=%async_computation.9 | async-start | bytes 4718592 | tf_op jit(solution)/shard_map/all_to_all | solution.py:119
  581.2 35.0 %collective-permute-start.31 = (bf16[192,512]{1,0:T(8,128)(2,1)}, bf16[192,512]{1,0:T(8,128)(2,1)}, u32[]{:S(2)}, u32[]{:S(2)}) collective-permute-start(bf16[192,512]{1,0:T(8,128)(2,1)} %get-tuple-element.192), channel_id=1, source_target_pairs={{0,1},{1,2},{2,3},{3,0},{4,5},{5,6},{6,7},{7,4},{8,9},{9,10},{10,1... | collective-permute-start | bytes 589832 | tf_op jit(solution)/shard_map/ppermute | solution.py:78
  582.2 34.0 %collective-permute-start.33 = (bf16[192,512]{1,0:T(8,128)(2,1)S(1)}, bf16[192,512]{1,0:T(8,128)(2,1)}, u32[]{:S(2)}, u32[]{:S(2)}) collective-permute-start(bf16[192,512]{1,0:T(8,128)(2,1)S(1)} %get-tuple-element.193), channel_id=1, source_target_pairs={{0,2},{1,3},{2,0},{3,1},{4,6},{5,7},{6,4},{7,5},{8,10},{9,11},{10,... | collective-permute-start | bytes 589832 | tf_op jit(solution)/shard_map/ppermute | solution.py:78
  586.4 12.2 %collective-permute-start.42 = (bf16[192,512]{1,0:T(8,128)(2,1)S(1)}, bf16[192,512]{1,0:T(8,128)(2,1)S(1)}, u32[]{:S(2)}, u32[]{:S(2)}) collective-permute-start(bf16[192,512]{1,0:T(8,128)(2,1)S(1)} %add_convert_fusion.4), channel_id=1, source_target_pairs={{0,1},{1,2},{2,3},{3,0},{4,5},{5,6},{6,7},{7,4},{8,9},{9,10},{10,1... | collective-permute-start | bytes 589832 | tf_op jit(solution)/shard_map/ppermute | solution.py:78
  587.6 14.9 %collective-permute-start.41 = (bf16[192,512]{1,0:T(8,128)(2,1)S(1)}, bf16[192,512]{1,0:T(8,128)(2,1)S(1)}, u32[]{:S(2)}, u32[]{:S(2)}) collective-permute-start(bf16[192,512]{1,0:T(8,128)(2,1)S(1)} %add_convert_fusion.4), channel_id=1, source_target_pairs={{0,2},{1,3},{2,0},{3,1},{4,6},{5,7},{6,4},{7,5},{8,10},{9,11},{10,... | collective-permute-start | bytes 589832 | tf_op jit(solution)/shard_map/ppermute | solution.py:78
  598.6 17.6 %collective-permute-start.32 = (bf16[192,512]{1,0:T(8,128)(2,1)S(1)}, bf16[192,512]{1,0:T(8,128)(2,1)}, u32[]{:S(2)}, u32[]{:S(2)}) collective-permute-start(bf16[192,512]{1,0:T(8,128)(2,1)S(1)} %get-tuple-element.194), channel_id=1, source_target_pairs={{0,3},{1,0},{2,1},{3,2},{4,7},{5,4},{6,5},{7,6},{8,11},{9,8},{10,9... | collective-permute-start | bytes 589832 | tf_op jit(solution)/shard_map/ppermute | solution.py:78
  612.3 31.8 %all-to-all-start.8 = ((f32[32,1,64]{2,1,0:T(1,128)}), f32[32,1,64]{2,1,0:T(1,128)S(1)}, u32[]{:S(2)}, u32[]{:S(2)}) async-start(f32[32,1,64]{2,1,0:T(1,128)} %all_to_all.53), calls=%async_computation.10 | async-start | bytes 32768 | tf_op jit(solution)/shard_map/all_to_all | solution.py:119
  619.6 25.0 %collective-permute-start.36 = (bf16[192,512]{1,0:T(8,128)(2,1)S(1)}, bf16[192,512]{1,0:T(8,128)(2,1)S(1)}, u32[]{:S(2)}, u32[]{:S(2)}) collective-permute-start(bf16[192,512]{1,0:T(8,128)(2,1)S(1)} %add_convert_fusion.5), channel_id=1, source_target_pairs={{0,1},{1,2},{2,3},{3,0},{4,5},{5,6},{6,7},{7,4},{8,9},{9,10},{10,1... | collective-permute-start | bytes 589832 | tf_op jit(solution)/shard_map/ppermute | solution.py:78
  620.5 24.2 %collective-permute-start.35 = (bf16[192,512]{1,0:T(8,128)(2,1)S(1)}, bf16[192,512]{1,0:T(8,128)(2,1)S(1)}, u32[]{:S(2)}, u32[]{:S(2)}) collective-permute-start(bf16[192,512]{1,0:T(8,128)(2,1)S(1)} %add_convert_fusion.5), channel_id=1, source_target_pairs={{0,2},{1,3},{2,0},{3,1},{4,6},{5,7},{6,4},{7,5},{8,10},{9,11},{10,... | collective-permute-start | bytes 589832 | tf_op jit(solution)/shard_map/ppermute | solution.py:78
  623.4 21.2 %collective-permute-start.34 = (bf16[192,512]{1,0:T(8,128)(2,1)S(1)}, bf16[192,512]{1,0:T(8,128)(2,1)S(1)}, u32[]{:S(2)}, u32[]{:S(2)}) collective-permute-start(bf16[192,512]{1,0:T(8,128)(2,1)S(1)} %add_convert_fusion.5), channel_id=1, source_target_pairs={{0,3},{1,0},{2,1},{3,2},{4,7},{5,4},{6,5},{7,6},{8,11},{9,8},{10,9... | collective-permute-start | bytes 589832 | tf_op jit(solution)/shard_map/ppermute | solution.py:78
  (135 other events, 1775.0 us)
Sparse Core Ops, SparseCore 0:
  11.4 57.8 all-gather.3
  71.5 103.4 all-gather.5
  177.2 61.7 all-gather.7
  268.6 95.2 reduce-scatter.3
  427.4 117.6 reduce-scatter.5
  558.8 95.1 reduce-scatter.7

commit v8 on v7

--- a/solution.py
+++ b/solution.py
@@ -254,14 +254,15 @@
     def run(owner, mine):
         rows = value[...]
         none = jnp.zeros_like(rows)
-        for j in range(out.shape[0]):
-            at = slice(j * out.shape[2], (j + 1) * out.shape[2])
+        cols = out.shape[1] // 4
+        for j in range(4):
+            at = slice(j * cols, (j + 1) * cols)
             if owner is None:
                 total = matmul(jnp.where(mine, rows, none), weight[0, :, at])
                 total = total + matmul(jnp.where(mine, none, rows), weight[1, :, at])
             else:
                 total = matmul(rows, weight[owner, :, at])
-            out[j] = total.astype(bf16)
+            out[:, at] = total.astype(bf16)
 
     per_owner(tiles, value.shape[0], spill, run)
 
@@ -432,7 +433,7 @@
     )(lane.reshape(1), left, right)
 
 
-def shared_kernel(normed2, cotangent, weights, dboth, hidden, part, dnormed):
+def shared_kernel(normed2, cotangent, weights, _, dboth, hidden, part, dnormed):
     wide = hidden.shape[1]
     gate_w, up_w, down_w = (weights.at[:, k * wide : (k + 1) * wide] for k in range(3))
     pre = matmul(normed2[...], gate_w[...])
@@ -449,7 +450,7 @@
     ).astype(bf16)
 
 
-def shared_experts(normed2, cotangent, weights):
+def shared_experts(normed2, cotangent, weights, signal):
     rows = normed2.shape[0]
     wide = weights.shape[1] // 3
     return pl.pallas_call(
@@ -457,7 +458,7 @@
         out_shape=[jax.ShapeDtypeStruct((rows, w), bf16) for w in (2 * wide, wide, D, D)],
         cost_estimate=SMALL_COST,
         compiler_params=pltpu.CompilerParams(vmem_limit_bytes=VMEM_BYTES),
-    )(normed2, cotangent, weights)
+    )(normed2, cotangent, weights, signal)
 
 
 def per_device(
@@ -676,7 +677,7 @@
     )
     upstream = cotangent.astype(f32)
     sh_dboth, sh_hidden, shared_part, sh_dnormed_part = shared_experts(
-        *after((normed2, cotangent), going), second_full
+        normed2, cotangent, second_full, going[0][:16, :128]
     )
     second_grad = second_grads(normed2, cotangent, sh_dboth, sh_hidden)
     second_sum = lax.psum_scatter(second_grad, "ep", scatter_dimension=0, tiled=True)
@@ -684,8 +685,6 @@
     ex_dh, shared_part, sh_dnormed_part, second_grad = lax.optimization_barrier(
         (ex_dh, shared_part, sh_dnormed_part, second_grad)
     )
-    shared_q = sum_to_quarter(shared_part)
-    sh_dnormed_q = sum_to_quarter(sh_dnormed_part)
     ex_hidden, ex_dboth, dgate_rows, *drow, all_rows = row_call(
         functools.partial(hidden_kernel, tiles, spill),
         tile,
@@ -698,17 +697,15 @@
         [pltpu.VMEM((tile, 2 * hid_wide), f32)],
     )
 
-    out_rows = pl.pallas_call(
+    (out_rows,) = row_call(
         functools.partial(out_kernel, tiles, spill),
-        grid=(slot_rows // tile,),
-        in_specs=[tile_spec(tile, hid_wide), whole_spec(down_plain.shape)],
-        out_specs=pl.BlockSpec((lanes, tile, quarter), lambda i: (0, i, 0)),
-        out_shape=jax.ShapeDtypeStruct((lanes, slot_rows, quarter), bf16),
-        cost_estimate=SMALL_COST,
-        compiler_params=pltpu.CompilerParams(
-            dimension_semantics=("arbitrary",), vmem_limit_bytes=VMEM_BYTES
-        ),
-    )(ex_hidden, down_plain).reshape(lanes * slot_rows, quarter)
+        tile,
+        slot_rows,
+        (ex_hidden, down_plain),
+        [tile_spec(tile, hid_wide), whole_spec(down_plain.shape)],
+        [(D, bf16)],
+        big,
+    )
     top = shift(drow[4], 1)
     bottom = shift(drow[5], 3)
     dgate_rows = exchange(from_experts(dgate_rows[:, 0], owner_count)).reshape(-1)
@@ -717,14 +714,14 @@
     )
     from_prev_one = shift(plus(drow[2], top), 1)
     from_next_one = shift(after(drow[6], bottom), 3)
-    exgate_grad, exup_grad = weight_grads(
-        edge, spill, hid_cols, 2, lane, *after((ex_dboth, all_rows), top, bottom)
-    )
-    (next_two, prev_two), exgate_grad, exup_grad, _, _ = lax.optimization_barrier(
+    out_dense = jnp.einsum(
+        "ist,isd->itd", pick_in, from_experts(out_rows, owner_count), preferred_element_type=f32
+    )
+    out_dense = out_dense.astype(bf16).reshape(owner_count * tok_count, D)
+    (next_two, prev_two), out_dense, _, _ = lax.optimization_barrier(
         (
             (drow[3], plus(drow[7], bottom)),
-            exgate_grad,
-            exup_grad,
+            out_dense,
             from_prev_one,
             from_next_one,
         )
@@ -738,12 +735,15 @@
     routed_grad_q = jnp.concatenate(
         [matmul_tn(pick, b.reshape(slot_rows, -1)) for b in (back_one, back_two)], 1
     )
-    out_rows = after(out_rows, drow_two, second_sum, back_one)
-    out_sum = lax.psum_scatter(out_rows, "tp", scatter_dimension=0, tiled=True)
+    out_sum = lax.psum_scatter(
+        after(out_dense, second_sum), "ep", scatter_dimension=0, tiled=True
+    )
 
     dgate_part = jnp.stack(
         [jnp.sum(jnp.where(matches[k], dgate_rows[:, None], 0.0), 0) for k in range(TOPK)], 1
     )
+    dgate_part, sh_dnormed_part = after((dgate_part, sh_dnormed_part), drow_two)
+    sh_dnormed_q = sum_to_quarter(sh_dnormed_part)
     dgate_all = sum_small(dgate_part)
     weighted = jnp.sum(dgate_all * gate_vals, -1, keepdims=True) / route_scale
     dsel_vals = route_scale / sel_total * (dgate_all - weighted)
@@ -804,8 +804,8 @@
         after(gain_grads.astype(bf16), out_sum),
     )
     late = shift(first_grad[:16, :128], 1)
-    back = exchange(from_experts(after(out_sum, late), owner_count)).reshape(slot_rows, -1)
-    routed_q = matmul_tn(pick, back)
+    out_part = after(out_sum, late).astype(f32) + shared_part.astype(f32)
+    out_q = sum_to_quarter(out_part)
     late_dquery, late_dlat = after((dquery, dlatent_all), late)
     dnormed_q = sum_to_quarter(matmul_nt(late_dquery, query_full))
     dnormed = gather_quarters(dnormed_q.astype(bf16)).astype(f32) + matmul_nt(
@@ -814,10 +814,13 @@
     dtokens, prenorm_grad = rms_back(resid_in, pre_scale, pre_weight, dnormed)
     tokens_grad = (dmid + dtokens).astype(bf16)
     prenorm_sum = jnp.sum(exchange(prenorm_grad.reshape(owner_count, shard)), 0)
+    exgate_grad, exup_grad = weight_grads(
+        edge, spill, hid_cols, 2, lane, *after((ex_dboth, all_rows), late)
+    )
     (exdown_grad,) = weight_grads(
         edge, spill, hid_cols, 1, jnp.zeros_like(lane), *after((ex_hidden, dy_rows), late)
     )
-    layer_q = (quarter_of(mid_resid, 0) + routed_q + shared_q).astype(bf16)
+    layer_q = (quarter_of(mid_resid, 0) + out_q).astype(bf16)
     layer_out = gather_quarters(layer_q)
     first_sum = lax.psum_scatter(first_grad, "ep", scatter_dimension=0, tiled=True).astype(f32)
     second_sum = second_sum.astype(f32)

time: 676 us -> 671 us (level)
  waiting for transfers between devices: 199 us -> 176 us
  local copies, waits for them, and re-layouts: 108 us -> 118 us
  matrix products: 54.1 us -> 64.1 us
    ppermute x43, waiting for transfers between devices: 109 us -> 82.9 us  [shift(): lax.ppermute(value, 'tp', [(i, (i + step) % lanes) for i in range(lanes)])]
    reduce_scatter x1, waiting for transfers between devices: 10.7 us -> 23.7 us  [per_device(): lax.psum_scatter(after(out_dense, second_sum), 'ep', scatter_dimension=0,...]
    dot_general x0 -> x1, matrix products: none -> 12.9 us  [per_device(): jnp.einsum('ist,isd->itd', pick_in, from_experts(out_rows, owner_count),...]
    pallas_call x1 -> x0, Pallas kernels: 9.26 us -> none  [per_device(): pl.pallas_call(functools.partial(out_kernel, tiles, spill), grid=(slot_ro...]
    pallas_call x2 -> x3, Pallas kernels: 41.6 us -> 50.8 us  [row_call(): pl.pallas_call(body, grid=(total // tile,), in_specs=in_specs, out_specs=...]
    all_to_all x9 -> x8, waiting for transfers between devices: 46.4 us -> 39.1 us  [exchange(): return lax.all_to_all(value, 'ep', 0, 0, tiled=True)]
    all_to_all x9 -> x8, starting transfers between devices: 56.7 us -> 49.4 us  [exchange(): return lax.all_to_all(value, 'ep', 0, 0, tiled=True)]
    unnamed x262 -> x260, local copies, waits for them, and re-layouts: 40.2 us -> 40.3 us
  transfers between devices with their start and end apart: 58 -> 57, of which waited for: 32 -> 30; matrix products, arithmetic and copies ran while one was open for 27% -> 31% of each run, Pallas kernels for 13% -> 13%
where the time goes in v8:
time: 671 us; the launch traced here: 664 us
  waiting for transfers between devices  176 us (26%)
  local copies, waits for them, and re-layouts  118 us (18%)
  starting transfers between devices  117 us (17%)
  Pallas kernels  111 us (17%)
  matrix products  64.1 us (10%)
  other arithmetic  61.5 us (9%)
  between operations  16.2 us (2%)
    ppermute x43, waiting for transfers between devices, shift(): lax.ppermute(value, 'tp', [(i, (i + step) % lanes) for i in range(lanes)])  82.9 us
    ppermute x43, starting transfers between devices, shift(): lax.ppermute(value, 'tp', [(i, (i + step) % lanes) for i in range(lanes)])  67.5 us
    pallas_call x3, Pallas kernels, row_call(): pl.pallas_call(body, grid=(total // tile,), in_specs=in_specs, out_specs=...  50.8 us
    all_to_all x8, starting transfers between devices, exchange(): return lax.all_to_all(value, 'ep', 0, 0, tiled=True)  49.4 us
    unnamed x260, local copies, waits for them, and re-layouts  40.3 us
    all_to_all x8, waiting for transfers between devices, exchange(): return lax.all_to_all(value, 'ep', 0, 0, tiled=True)  39.1 us
    pallas_call x2, Pallas kernels, weight_grads(): pl.pallas_call(functools.partial(weight_grad_kernel, edge, spill), grid_s...  36.8 us
    all_gather x1, waiting for transfers between devices, per_device(): first_full = lax.all_gather(first_pack, 'ep', axis=0, tiled=True)  24 us
  transfers between devices with their start and end apart: 57, of which 30 were waited for; matrix products, arithmetic and copies ran while one was open for 31% of the time, Pallas kernels for 13%

profile of v8, /device:TPU:0, one launch (start us, length us, event | category | flops | bytes accessed | tf_op | source)
XLA Modules:
  0.0 664.0 jit_solution(17952256079029627324)
XLA Ops:
  15.2 7.4 %all-to-all-start = ((s32[32,1,72]{2,1,0:T(1,128)}), s32[32,1,72]{2,1,0:T(1,128)S(1)}, u32[]{:S(2)}, u32[]{:S(2)}) async-start(s32[32,1,72]{2,1,0:T(1,128)} %sub.84), calls=%async_computation | async-start | bytes 32768 | tf_op jit(solution)/shard_map/all_to_all | solution.py:119
  22.8 4.8 constant_dynamic-slice_fusion.30
  41.7 3.2 pad_maximum_fusion.1.refs_8_
  45.3 24.0 %all-gather.4.cloned.1.call-done = bf16[2048,2304]{1,0:T(8,128)(2,1)} async-done(((bf16[64,2304]{1,0:T(8,128)(2,1)}), bf16[2048,2304]{1,0:T(8,128)(2,1)}) %all-gather.4.cloned.1.call-update) | async-done | bytes 9437200 | tf_op jit(solution)/shard_map/all_gather | solution.py:517
  79.4 3.8 fusion.22
  89.6 3.0 fusion.28
  116.8 5.1 collective-permute-done.2
  129.7 5.5 collective-permute-done.4
  140.8 5.0 all-to-all-start.1
  147.7 25.8 %all-to-all-done.1 = bf16[32,72,256]{2,1,0:T(8,128)(2,1)} async-done(((bf16[32,72,256]{2,1,0:T(8,128)(2,1)}), bf16[32,72,256]{2,1,0:T(8,128)(2,1)}, u32[]{:S(2)}, u32[]{:S(2)}) %all-to-all-start.1) | async-done | bytes 1179680 | tf_op jit(solution)/shard_map/all_to_all | solution.py:119
  178.4 6.2 all-to-all-start.2
  184.6 3.3 add_reduce_fusion
  195.5 9.8 %all-to-all-done.2 = bf16[32,72,256]{2,1,0:T(8,128)(2,1)} async-done(((bf16[32,72,256]{2,1,0:T(8,128)(2,1)}), bf16[32,72,256]{2,1,0:T(8,128)(2,1)}, u32[]{:S(2)}, u32[]{:S(2)}) %all-to-all-start.2) | async-done | bytes 1179680 | tf_op jit(solution)/shard_map/all_to_all | solution.py:119
  205.3 6.2 all-to-all-start.3
  226.3 15.1 %convolution_convert_fusion.1 = bf16[32,72,2048]{2,1,0:T(8,128)(2,1)} fusion(bf16[32,192,2048]{2,1,0:T(8,128)(2,1)} %bitcast.125, s32[32,72]{1,0:T(8,128)} %bitcast.144), kind=kOutput, calls=%fused_computation.18 | convolution fusion | flops 1817100288 | bytes 34612224 | tf_op jit(solution)/shard_map/ist,itd->isd/dot_general | solution.py:646
  241.4 4.0 fusion.113
  246.8 4.3 pad_maximum_fusion.refs_0_.right
  254.1 8.7 %shard_map.307 = (bf16[192,1536]{1,0:T(8,128)(2,1)S(1)}, bf16[192,768]{1,0:T(8,128)(2,1)S(1)}, bf16[192,2048]{1,0:T(8,128)(2,1)S(1)}, bf16[192,2048]{1,0:T(8,128)(2,1)S(1)}) custom-call(bf16[192,2048]{1,0:T(8,128)(2,1)S(1)} %copy-done.3, bf16[192,2048]{1,0:T(8,128)(2,1)S(1)} %copy-done, bf16[2048,2304]{1,0:T(8,128)(2,1)} %all-gather.8.cloned.1.call-done.weights, ...), custom_call_target="tpu_custom_call" | custom-call | flops 1 | bytes 1 | tf_op jit(solution)/shard_map/pallas_call | solution.py:456
  264.6 6.9 %shard_map.308 = bf16[2048,2304]{1,0:T(8,128)(2,1)} custom-call(bf16[192,2048]{1,0:T(8,128)(2,1)S(1)} %copy-done.4, bf16[192,2048]{1,0:T(8,128)(2,1)S(1)} %copy-done, bf16[192,1536]{1,0:T(8,128)(2,1)S(1)} %get-tuple-element.87.dboth, bf16[192,768]{1,0:T(8,128)(2,1)S(1)} %get-tuple-element.88.hidden), custom_call_target="tpu_custom_call" | custom-call | flops 1 | bytes 1 | tf_op jit(solution)/shard_map/pallas_call | solution.py:372
  271.6 3.0 collective-permute-start.11
  274.8 11.0 %shard_map.306.refs_9_ = f32[2304,384]{1,0:T(8,128)S(1)} custom-call(bf16[2304,2048]{1,0:T(8,128)(2,1)} %pad_maximum_fusion.refs_0_.right, bf16[2,384,2048]{2,1,0:T(8,128)(2,1)S(1)} %pad.51.refs_1_.weight), custom_call_target="tpu_custom_call" | custom-call | flops 1 | bytes 1 | tf_op jit(solution)/shard_map/pallas_call | solution.py:281
  289.7 10.6 %collective-permute-done.11.refs_5_ = bf16[2304,256]{1,0:T(8,128)(2,1)} collective-permute-done((bf16[2304,256]{1,0:T(8,128)(2,1)}, bf16[2304,256]{1,0:T(8,128)(2,1)}, u32[]{:S(2)}, u32[]{:S(2)}) %collective-permute-start.11) | collective-permute-done | bytes 1179680 | tf_op jit(solution)/shard_map/ppermute | solution.py:78
  300.3 3.6 collective-permute-done.10.refs_4_
  303.8 30.6 %shard_map.309 = (bf16[2304,384]{1,0:T(8,128)(2,1)}, bf16[2304,768]{1,0:T(8,128)(2,1)}, f32[2304,1]{1,0:T(8,128)S(1)}, bf16[2304,256]{1,0:T(8,128)(2,1)S(1)}, bf...) custom-call(bf16[2304,256]{1,0:T(8,128)(2,1)} %pad_maximum_fusion.2., ...), custom_call_target="tpu_custom_call" | custom-call | flops 1 | bytes 1 | tf_op jit(solution)/shard_map/pallas_call | solution.py:281
  339.7 3.2 collective-permute-start.13
  350.2 5.6 all-to-all-start.4
  357.3 9.2 %shard_map.310 = bf16[2304,2048]{1,0:T(8,128)(2,1)} custom-call(bf16[2304,384]{1,0:T(8,128)(2,1)S(1)} %copy-done.7, bf16[2,384,2048]{2,1,0:T(8,128)(2,1)S(1)} %pad.51.refs_1_.weight), custom_call_target="tpu_custom_call" | custom-call | flops 1 | bytes 1 | tf_op jit(solution)/shard_map/pallas_call | solution.py:281
  374.3 5.3 fusion.112
  382.3 12.9 %convolution_convert_fusion = bf16[32,192,2048]{2,1,0:T(8,128)(2,1)} fusion(bf16[32,32,2048]{2,1,0:T(8,128)(2,1)} %bitcast.129, bf16[32,8,2048]{2,1,0:T(8,128)(2,1)S(1)} %slice_bitcast_fusion.1, bf16[32,32,2048]{2,1,0:T(8,128)(2,1)S(1)} %bitcast.128, s32[32,72]{1,0:T(8,128)S(1)} %bitcast.145), kind=kOutput, calls=%fused_computation.1 | convolution fusion | flops 1853276160 | bytes 34612224 | tf_op jit(solution)/shard_map/ist,isd->itd/dot_general | solution.py:717
  397.0 3.2 collective-permute-done.14
  408.9 7.5 %all-to-all-start.5 = ((bf16[32,72,256]{2,1,0:T(8,128)(2,1)}), bf16[32,72,256]{2,1,0:T(8,128)(2,1)}, u32[]{:S(2)}, u32[]{:S(2)}) async-start(bf16[32,72,256]{2,1,0:T(8,128)(2,1)} %pad_maximum_fusion.4), calls=%async_computation.7 | async-start | bytes 2359296 | tf_op jit(solution)/shard_map/all_to_all | solution.py:119
  416.5 12.3 %collective-permute-done.16 = bf16[2304,256]{1,0:T(8,128)(2,1)} collective-permute-done((bf16[2304,256]{1,0:T(8,128)(2,1)S(1)}, bf16[2304,256]{1,0:T(8,128)(2,1)}, u32[]{:S(2)}, u32[]{:S(2)}) %collective-permute-start.16) | collective-permute-done | bytes 1179680 | tf_op jit(solution)/shard_map/ppermute | solution.py:78
  434.8 7.1 %all-to-all-start.6 = ((bf16[32,72,256]{2,1,0:T(8,128)(2,1)}), bf16[32,72,256]{2,1,0:T(8,128)(2,1)S(1)}, u32[]{:S(2)}, u32[]{:S(2)}) async-start(bf16[32,72,256]{2,1,0:T(8,128)(2,1)} %pad_maximum_fusion.5), calls=%async_computation.8 | async-start | bytes 2359296 | tf_op jit(solution)/shard_map/all_to_all | solution.py:119
  472.6 5.4 collective-permute-done.22
  492.7 7.8 %collective-permute-done.28 = bf16[192,576]{1,0:T(8,128)(2,1)S(1)} collective-permute-done((bf16[192,576]{1,0:T(8,128)(2,1)S(1)}, bf16[192,576]{1,0:T(8,128)(2,1)S(1)}, u32[]{:S(2)}, u32[]{:S(2)}) %collective-permute-start.28) | collective-permute-done | bytes 221216 | tf_op jit(solution)/shard_map/ppermute | solution.py:78
  500.5 3.4 collective-permute-done.27
  516.6 23.7 %reduce-scatter.6.cloned.1.call-done = bf16[192,2048]{1,0:T(8,128)(2,1)} async-done(((bf16[6144,2048]{1,0:T(8,128)(2,1)}), bf16[192,2048]{1,0:T(8,128)(2,1)}) %reduce-scatter.6.cloned.1.call-update) | async-done | bytes 786448 | tf_op jit(solution)/shard_map/reduce_scatter | solution.py:738
  546.0 7.9 %shard_map.311 = bf16[2048,2304]{1,0:T(8,128)(2,1)} custom-call(bf16[192,2048]{1,0:T(8,128)(2,1)S(1)} %copy-done.12, bf16[192,2048]{1,0:T(8,128)(2,1)S(1)} %copy-done.5, bf16[192,2048]{1,0:T(8,128)(2,1)S(1)} %fusion.106.dmid, bf16[192,768]{1,0:T(8,128)(2,1)S(1)} %copy-done.22, bf16[192,640]{1,0:T(8,128)(2,1)S(1)} %copy-done.24, ...), custom_call_target="tpu_custom_call" | custom-call | flops 1 | bytes 1 | tf_op jit(solution)/shard_map/pallas_call | solution.py:346
  556.3 3.2 collective-permute-done.30
  559.5 3.1 fusion.24
  568.2 5.4 collective-permute-done.37
  584.9 3.7 collective-permute-done.41
  588.8 3.4 fusion.49
  596.7 3.2 collective-permute-start.35
  600.6 4.4 all-to-all-start.7
  605.8 17.4 %shard_map.313 = f32[2,352,2048]{2,1,0:T(8,128)} custom-call(s32[1]{0:T(128)} %constant.114.clone.1.lane, bf16[2304,384]{1,0:T(8,128)(2,1)S(1)} %copy-done.8, bf16[2304,2048]{1,0:T(8,128)(2,1)} %pad_maximum_fusion.refs_0_.right), custom_call_target="tpu_custom_call" | custom-call | flops 1 | bytes 1 | tf_op jit(solution)/shard_map/pallas_call | solution.py:425
  623.2 19.4 %shard_map.312 = (f32[2,352,2048]{2,1,0:T(8,128)}, f32[2,352,2048]{2,1,0:T(8,128)}) custom-call(s32[1]{0:T(128)} %bitcast.65.lane, bf16[2304,768]{1,0:T(8,128)(2,1)S(1)} %copy-done.9, bf16[2304,2048]{1,0:T(8,128)(2,1)} %get-tuple-element.121.right), custom_call_target="tpu_custom_call" | custom-call | flops 1 | bytes 1 | tf_op jit(solution)/shard_map/pallas_call | solution.py:425
  644.3 4.5 reduce-scatter.8.cloned.1.call-done
  (524 shorter events, 254.8 us)
Async XLA Ops:
  7.2 62.1 %all-gather.4.cloned.1.call-start = ((), (), s32[]{:S(2)}) async-start(), calls=%async_computation.11 | async-start | bytes 9732096 | tf_op jit(solution)/shard_map/all_gather | solution.py:517
  15.2 30.1 %all-to-all-start = ((s32[32,1,72]{2,1,0:T(1,128)}), s32[32,1,72]{2,1,0:T(1,128)S(1)}, u32[]{:S(2)}, u32[]{:S(2)}) async-start(s32[32,1,72]{2,1,0:T(1,128)} %sub.84), calls=%async_computation | async-start | bytes 32768 | tf_op jit(solution)/shard_map/all_to_all | solution.py:119
  22.6 152.4 %all-gather.6.cloned.1.call-start = ((), (), s32[]{:S(2)}) async-start(), calls=%async_computation.12 | async-start | bytes 25952256 | tf_op jit(solution)/shard_map/all_gather | solution.py:567
  109.8 12.1 %collective-permute-start.2 = (bf16[192,512]{1,0:T(8,128)(2,1)S(1)}, bf16[192,512]{1,0:T(8,128)(2,1)S(1)}, u32[]{:S(2)}, u32[]{:S(2)}) collective-permute-start(bf16[192,512]{1,0:T(8,128)(2,1)S(1)} %get-tuple-element.198), channel_id=1, source_target_pairs={{0,2},{1,3},{2,0},{3,1},{4,6},{5,7},{6,4},{7,5},{8,10},{9,11},{10,... | collective-permute-start | bytes 589832 | tf_op jit(solution)/shard_map/ppermute | solution.py:78
  112.7 9.2 %collective-permute-start.1 = (bf16[192,512]{1,0:T(8,128)(2,1)S(1)}, bf16[192,512]{1,0:T(8,128)(2,1)S(1)}, u32[]{:S(2)}, u32[]{:S(2)}) collective-permute-start(bf16[192,512]{1,0:T(8,128)(2,1)S(1)} %get-tuple-element.199), channel_id=1, source_target_pairs={{0,3},{1,0},{2,1},{3,2},{4,7},{5,4},{6,5},{7,6},{8,11},{9,8},{10,9... | collective-permute-start | bytes 589832 | tf_op jit(solution)/shard_map/ppermute | solution.py:78
  123.6 11.6 %collective-permute-start.4 = (bf16[192,512]{1,0:T(8,128)(2,1)S(1)}, bf16[192,512]{1,0:T(8,128)(2,1)}, u32[]{:S(2)}, u32[]{:S(2)}) collective-permute-start(bf16[192,512]{1,0:T(8,128)(2,1)S(1)} %add_convert_fusion.8), channel_id=1, source_target_pairs={{0,2},{1,3},{2,0},{3,1},{4,6},{5,7},{6,4},{7,5},{8,10},{9,11},{10,... | collective-permute-start | bytes 589832 | tf_op jit(solution)/shard_map/ppermute | solution.py:78
  125.9 9.2 %collective-permute-start.3 = (bf16[192,512]{1,0:T(8,128)(2,1)S(1)}, bf16[192,512]{1,0:T(8,128)(2,1)}, u32[]{:S(2)}, u32[]{:S(2)}) collective-permute-start(bf16[192,512]{1,0:T(8,128)(2,1)S(1)} %add_convert_fusion.8), channel_id=1, source_target_pairs={{0,3},{1,0},{2,1},{3,2},{4,7},{5,4},{6,5},{7,6},{8,11},{9,8},{10,9... | collective-permute-start | bytes 589832 | tf_op jit(solution)/shard_map/ppermute | solution.py:78
  140.8 32.7 %all-to-all-start.1 = ((bf16[32,72,256]{2,1,0:T(8,128)(2,1)}), bf16[32,72,256]{2,1,0:T(8,128)(2,1)}, u32[]{:S(2)}, u32[]{:S(2)}) async-start(bf16[32,72,256]{2,1,0:T(8,128)(2,1)} %get-tuple-element.157), calls=%async_computation.1 | async-start | bytes 2359296 | tf_op jit(solution)/shard_map/all_to_all | solution.py:119
  145.9 105.9 %all-gather.8.cloned.1.call-start = ((), (), s32[]{:S(2)}) async-start(), calls=%async_computation.13 | async-start | bytes 9732096 | tf_op jit(solution)/shard_map/all_gather | solution.py:640
  178.4 26.9 %all-to-all-start.2 = ((bf16[32,72,256]{2,1,0:T(8,128)(2,1)}), bf16[32,72,256]{2,1,0:T(8,128)(2,1)}, u32[]{:S(2)}, u32[]{:S(2)}) async-start(bf16[32,72,256]{2,1,0:T(8,128)(2,1)} %get-tuple-element.72), calls=%async_computation.2 | async-start | bytes 2359296 | tf_op jit(solution)/shard_map/all_to_all | solution.py:119
  192.6 58.5 %collective-permute-start.9 = (bf16[2304,256]{1,0:T(8,128)(2,1)}, bf16[2304,256]{1,0:T(8,128)(2,1)}, u32[]{:S(2)}, u32[]{:S(2)}) collective-permute-start(bf16[2304,256]{1,0:T(8,128)(2,1)} %pad_maximum_fusion.2.refs_0_), channel_id=1, source_target_pairs={{0,3},{1,0},{2,1},{3,2},{4,7},{5,4},{6,5},{7,6},{8,11},{9,8},{10,9... | collective-permute-start | bytes 3538952 | tf_op jit(solution)/shard_map/ppermute | solution.py:78
  195.5 55.6 %collective-permute-start.6 = (bf16[2304,256]{1,0:T(8,128)(2,1)}, bf16[2304,256]{1,0:T(8,128)(2,1)}, u32[]{:S(2)}, u32[]{:S(2)}) collective-permute-start(bf16[2304,256]{1,0:T(8,128)(2,1)} %pad_maximum_fusion.2.refs_0_), channel_id=1, source_target_pairs={{0,1},{1,2},{2,3},{3,0},{4,5},{5,6},{6,7},{7,4},{8,9},{9,10},{10,1... | collective-permute-start | bytes 3538952 | tf_op jit(solution)/shard_map/ppermute | solution.py:78
  205.3 13.3 %all-to-all-start.3 = ((f32[32,1,72]{2,1,0:T(1,128)}), f32[32,1,72]{2,1,0:T(1,128)}, u32[]{:S(2)}, u32[]{:S(2)}) async-start(f32[32,1,72]{2,1,0:T(1,128)} %bitcast.151), calls=%async_computation.3 | async-start | bytes 32768 | tf_op jit(solution)/shard_map/all_to_all | solution.py:119
  211.5 188.8 %reduce-scatter.4.cloned.1.call-start = ((), (), s32[]{:S(2)}) async-start(), calls=%async_computation.14 | async-start | bytes 9732096 | tf_op jit(solution)/shard_map/reduce_scatter | solution.py:683
  214.9 36.2 %collective-permute-start.8 = (bf16[2304,256]{1,0:T(8,128)(2,1)}, bf16[2304,256]{1,0:T(8,128)(2,1)}, u32[]{:S(2)}, u32[]{:S(2)}) collective-permute-start(bf16[2304,256]{1,0:T(8,128)(2,1)} %pad_maximum_fusion.3.refs_1_), channel_id=1, source_target_pairs={{0,1},{1,2},{2,3},{3,0},{4,5},{5,6},{6,7},{7,4},{8,9},{9,10},{10,1... | collective-permute-start | bytes 3538952 | tf_op jit(solution)/shard_map/ppermute | solution.py:78
  216.5 34.6 %collective-permute-start.7 = (bf16[2304,256]{1,0:T(8,128)(2,1)}, bf16[2304,256]{1,0:T(8,128)(2,1)}, u32[]{:S(2)}, u32[]{:S(2)}) collective-permute-start(bf16[2304,256]{1,0:T(8,128)(2,1)} %pad_maximum_fusion.3.refs_1_), channel_id=1, source_target_pairs={{0,3},{1,0},{2,1},{3,2},{4,7},{5,4},{6,5},{7,6},{8,11},{9,8},{10,9... | collective-permute-start | bytes 3538952 | tf_op jit(solution)/shard_map/ppermute | solution.py:78
  271.6 28.7 %collective-permute-start.11 = (bf16[2304,256]{1,0:T(8,128)(2,1)}, bf16[2304,256]{1,0:T(8,128)(2,1)}, u32[]{:S(2)}, u32[]{:S(2)}) collective-permute-start(bf16[2304,256]{1,0:T(8,128)(2,1)} %collective-permute-done.7.refs_3_), channel_id=1, source_target_pairs={{0,3},{1,0},{2,1},{3,2},{4,7},{5,4},{6,5},{7,6},{8,11},{9,8},{10,9... | collective-permute-start | bytes 3538952 | tf_op jit(solution)/shard_map/ppermute | solution.py:78
  274.6 29.2 %collective-permute-start.10 = (bf16[2304,256]{1,0:T(8,128)(2,1)}, bf16[2304,256]{1,0:T(8,128)(2,1)}, u32[]{:S(2)}, u32[]{:S(2)}) collective-permute-start(bf16[2304,256]{1,0:T(8,128)(2,1)} %collective-permute-done.6.refs_6_), channel_id=1, source_target_pairs={{0,1},{1,2},{2,3},{3,0},{4,5},{5,6},{6,7},{7,4},{8,9},{9,10},{10,1... | collective-permute-start | bytes 3538952 | tf_op jit(solution)/shard_map/ppermute | solution.py:78
  339.6 28.9 %collective-permute-start.12 = (bf16[2304,256]{1,0:T(8,128)(2,1)}, bf16[2304,256]{1,0:T(8,128)(2,1)}, u32[]{:S(2)}, u32[]{:S(2)}) collective-permute-start(bf16[2304,256]{1,0:T(8,128)(2,1)} %get-tuple-element.93), channel_id=1, source_target_pairs={{0,1},{1,2},{2,3},{3,0},{4,5},{5,6},{6,7},{7,4},{8,9},{9,10},{10,1... | collective-permute-start | bytes 3538952 | tf_op jit(solution)/shard_map/ppermute | solution.py:78
  339.7 28.9 %collective-permute-start.13 = (bf16[2304,256]{1,0:T(8,128)(2,1)}, bf16[2304,256]{1,0:T(8,128)(2,1)}, u32[]{:S(2)}, u32[]{:S(2)}) collective-permute-start(bf16[2304,256]{1,0:T(8,128)(2,1)} %get-tuple-element.94), channel_id=1, source_target_pairs={{0,3},{1,0},{2,1},{3,2},{4,7},{5,4},{6,5},{7,6},{8,11},{9,8},{10,9... | collective-permute-start | bytes 3538952 | tf_op jit(solution)/shard_map/ppermute | solution.py:78
  350.2 16.4 %all-to-all-start.4 = ((f32[32,1,72]{2,1,0:T(1,128)}), f32[32,1,72]{2,1,0:T(1,128)}, u32[]{:S(2)}, u32[]{:S(2)}) async-start(f32[32,1,72]{2,1,0:T(1,128)} %bitcast.154), calls=%async_computation.4 | async-start | bytes 32768 | tf_op jit(solution)/shard_map/all_to_all | solution.py:119
  355.8 184.5 %reduce-scatter.6.cloned.1.call-start = ((), (), s32[]{:S(2)}) async-start(), calls=%async_computation.15 | async-start | bytes 25952256 | tf_op jit(solution)/shard_map/reduce_scatter | solution.py:738
  368.6 28.5 %collective-permute-start.15 = (bf16[2304,256]{1,0:T(8,128)(2,1)}, bf16[2304,256]{1,0:T(8,128)(2,1)}, u32[]{:S(2)}, u32[]{:S(2)}) collective-permute-start(bf16[2304,256]{1,0:T(8,128)(2,1)} %copy-done.33), channel_id=1, source_target_pairs={{0,3},{1,0},{2,1},{3,2},{4,7},{5,4},{6,5},{7,6},{8,11},{9,8},{10,9... | collective-permute-start | bytes 3538952 | tf_op jit(solution)/shard_map/ppermute | solution.py:78
  372.7 27.5 %collective-permute-start.14 = (bf16[2304,256]{1,0:T(8,128)(2,1)S(1)}, bf16[2304,256]{1,0:T(8,128)(2,1)}, u32[]{:S(2)}, u32[]{:S(2)}) collective-permute-start(bf16[2304,256]{1,0:T(8,128)(2,1)S(1)} %add_convert_fusion.2), channel_id=1, source_target_pairs={{0,1},{1,2},{2,3},{3,0},{4,5},{5,6},{6,7},{7,4},{8,9},{9,10},{10,1... | collective-permute-start | bytes 3538952 | tf_op jit(solution)/shard_map/ppermute | solution.py:78
  402.5 26.3 %collective-permute-start.16 = (bf16[2304,256]{1,0:T(8,128)(2,1)S(1)}, bf16[2304,256]{1,0:T(8,128)(2,1)}, u32[]{:S(2)}, u32[]{:S(2)}) collective-permute-start(bf16[2304,256]{1,0:T(8,128)(2,1)S(1)} %copy-done.32), channel_id=1, source_target_pairs={{0,1},{1,2},{2,3},{3,0},{4,5},{5,6},{6,7},{7,4},{8,9},{9,10},{10,1... | collective-permute-start | bytes 3538952 | tf_op jit(solution)/shard_map/ppermute | solution.py:78
  403.0 26.8 %collective-permute-start.17 = (bf16[2304,256]{1,0:T(8,128)(2,1)}, bf16[2304,256]{1,0:T(8,128)(2,1)}, u32[]{:S(2)}, u32[]{:S(2)}) collective-permute-start(bf16[2304,256]{1,0:T(8,128)(2,1)} %add_convert_fusion.3), channel_id=1, source_target_pairs={{0,3},{1,0},{2,1},{3,2},{4,7},{5,4},{6,5},{7,6},{8,11},{9,8},{10,9... | collective-permute-start | bytes 3538952 | tf_op jit(solution)/shard_map/ppermute | solution.py:78
  408.9 25.9 %all-to-all-start.5 = ((bf16[32,72,256]{2,1,0:T(8,128)(2,1)}), bf16[32,72,256]{2,1,0:T(8,128)(2,1)}, u32[]{:S(2)}, u32[]{:S(2)}) async-start(bf16[32,72,256]{2,1,0:T(8,128)(2,1)} %pad_maximum_fusion.4), calls=%async_computation.7 | async-start | bytes 2359296 | tf_op jit(solution)/shard_map/all_to_all | solution.py:119
  434.8 25.4 %all-to-all-start.6 = ((bf16[32,72,256]{2,1,0:T(8,128)(2,1)}), bf16[32,72,256]{2,1,0:T(8,128)(2,1)S(1)}, u32[]{:S(2)}, u32[]{:S(2)}) async-start(bf16[32,72,256]{2,1,0:T(8,128)(2,1)} %pad_maximum_fusion.5), calls=%async_computation.8 | async-start | bytes 2359296 | tf_op jit(solution)/shard_map/all_to_all | solution.py:119
  441.9 206.9 %reduce-scatter.8.cloned.1.call-start = ((), (), s32[]{:S(2)}) async-start(), calls=%async_computation.16 | async-start | bytes 9732096 | tf_op jit(solution)/shard_map/reduce_scatter | solution.py:825
  451.2 11.4 %collective-permute-start.18 = (bf16[192,512]{1,0:T(8,128)(2,1)S(1)}, bf16[192,512]{1,0:T(8,128)(2,1)S(1)}, u32[]{:S(2)}, u32[]{:S(2)}) collective-permute-start(bf16[192,512]{1,0:T(8,128)(2,1)S(1)} %get-tuple-element.190), channel_id=1, source_target_pairs={{0,1},{1,2},{2,3},{3,0},{4,5},{5,6},{6,7},{7,4},{8,9},{9,10},{10,1... | collective-permute-start | bytes 589832 | tf_op jit(solution)/shard_map/ppermute | solution.py:78
  453.3 10.6 %collective-permute-start.20 = (bf16[192,512]{1,0:T(8,128)(2,1)S(1)}, bf16[192,512]{1,0:T(8,128)(2,1)S(1)}, u32[]{:S(2)}, u32[]{:S(2)}) collective-permute-start(bf16[192,512]{1,0:T(8,128)(2,1)S(1)} %get-tuple-element.191), channel_id=1, source_target_pairs={{0,2},{1,3},{2,0},{3,1},{4,6},{5,7},{6,4},{7,5},{8,10},{9,11},{10,... | collective-permute-start | bytes 589832 | tf_op jit(solution)/shard_map/ppermute | solution.py:78
  466.6 11.4 %collective-permute-start.22 = (bf16[192,512]{1,0:T(8,128)(2,1)S(1)}, bf16[192,512]{1,0:T(8,128)(2,1)S(1)}, u32[]{:S(2)}, u32[]{:S(2)}) collective-permute-start(bf16[192,512]{1,0:T(8,128)(2,1)S(1)} %fusion.72), channel_id=1, source_target_pairs={{0,2},{1,3},{2,0},{3,1},{4,6},{5,7},{6,4},{7,5},{8,10},{9,11},{10,... | collective-permute-start | bytes 589832 | tf_op jit(solution)/shard_map/ppermute | solution.py:78
  469.1 8.8 %collective-permute-start.21 = (bf16[192,512]{1,0:T(8,128)(2,1)S(1)}, bf16[192,512]{1,0:T(8,128)(2,1)S(1)}, u32[]{:S(2)}, u32[]{:S(2)}) collective-permute-start(bf16[192,512]{1,0:T(8,128)(2,1)S(1)} %fusion.72), channel_id=1, source_target_pairs={{0,3},{1,0},{2,1},{3,2},{4,7},{5,4},{6,5},{7,6},{8,11},{9,8},{10,9... | collective-permute-start | bytes 589832 | tf_op jit(solution)/shard_map/ppermute | solution.py:78
  488.1 12.4 %collective-permute-start.28 = (bf16[192,576]{1,0:T(8,128)(2,1)S(1)}, bf16[192,576]{1,0:T(8,128)(2,1)S(1)}, u32[]{:S(2)}, u32[]{:S(2)}) collective-permute-start(bf16[192,576]{1,0:T(8,128)(2,1)S(1)} %pad_maximum_fusion.16), channel_id=1, source_target_pairs={{0,3},{1,0},{2,1},{3,2},{4,7},{5,4},{6,5},{7,6},{8,11},{9,8},{10,9... | collective-permute-start | bytes 663560 | tf_op jit(solution)/shard_map/ppermute | solution.py:78
  489.8 14.1 %collective-permute-start.27 = (bf16[192,576]{1,0:T(8,128)(2,1)S(1)}, bf16[192,576]{1,0:T(8,128)(2,1)S(1)}, u32[]{:S(2)}, u32[]{:S(2)}) collective-permute-start(bf16[192,576]{1,0:T(8,128)(2,1)S(1)} %pad_maximum_fusion.16), channel_id=1, source_target_pairs={{0,1},{1,2},{2,3},{3,0},{4,5},{5,6},{6,7},{7,4},{8,9},{9,10},{10,1... | collective-permute-start | bytes 663560 | tf_op jit(solution)/shard_map/ppermute | solution.py:78
  490.2 13.7 %collective-permute-start.29 = (bf16[192,576]{1,0:T(8,128)(2,1)S(1)}, bf16[192,576]{1,0:T(8,128)(2,1)S(1)}, u32[]{:S(2)}, u32[]{:S(2)}) collective-permute-start(bf16[192,576]{1,0:T(8,128)(2,1)S(1)} %pad_maximum_fusion.16), channel_id=1, source_target_pairs={{0,2},{1,3},{2,0},{3,1},{4,6},{5,7},{6,4},{7,5},{8,10},{9,11},{10,... | collective-permute-start | bytes 663560 | tf_op jit(solution)/shard_map/ppermute | solution.py:78
  562.7 10.9 %collective-permute-start.37 = (bf16[192,512]{1,0:T(8,128)(2,1)S(1)}, bf16[192,512]{1,0:T(8,128)(2,1)S(1)}, u32[]{:S(2)}, u32[]{:S(2)}) collective-permute-start(bf16[192,512]{1,0:T(8,128)(2,1)S(1)} %get-tuple-element.176), channel_id=1, source_target_pairs={{0,1},{1,2},{2,3},{3,0},{4,5},{5,6},{6,7},{7,4},{8,9},{9,10},{10,1... | collective-permute-start | bytes 589832 | tf_op jit(solution)/shard_map/ppermute | solution.py:78
  563.3 10.3 %collective-permute-start.39 = (bf16[192,512]{1,0:T(8,128)(2,1)S(1)}, bf16[192,512]{1,0:T(8,128)(2,1)S(1)}, u32[]{:S(2)}, u32[]{:S(2)}) collective-permute-start(bf16[192,512]{1,0:T(8,128)(2,1)S(1)} %get-tuple-element.177), channel_id=1, source_target_pairs={{0,2},{1,3},{2,0},{3,1},{4,6},{5,7},{6,4},{7,5},{8,10},{9,11},{10,... | collective-permute-start | bytes 589832 | tf_op jit(solution)/shard_map/ppermute | solution.py:78
  574.3 9.5 %collective-permute-start.42 = (bf16[192,512]{1,0:T(8,128)(2,1)S(1)}, bf16[192,512]{1,0:T(8,128)(2,1)S(1)}, u32[]{:S(2)}, u32[]{:S(2)}) collective-permute-start(bf16[192,512]{1,0:T(8,128)(2,1)S(1)} %add_convert_fusion.5), channel_id=1, source_target_pairs={{0,1},{1,2},{2,3},{3,0},{4,5},{5,6},{6,7},{7,4},{8,9},{9,10},{10,1... | collective-permute-start | bytes 589832 | tf_op jit(solution)/shard_map/ppermute | solution.py:78
  575.8 12.8 %collective-permute-start.41 = (bf16[192,512]{1,0:T(8,128)(2,1)S(1)}, bf16[192,512]{1,0:T(8,128)(2,1)S(1)}, u32[]{:S(2)}, u32[]{:S(2)}) collective-permute-start(bf16[192,512]{1,0:T(8,128)(2,1)S(1)} %add_convert_fusion.5), channel_id=1, source_target_pairs={{0,2},{1,3},{2,0},{3,1},{4,6},{5,7},{6,4},{7,5},{8,10},{9,11},{10,... | collective-permute-start | bytes 589832 | tf_op jit(solution)/shard_map/ppermute | solution.py:78
  578.5 10.1 %collective-permute-start.40 = (bf16[192,512]{1,0:T(8,128)(2,1)S(1)}, bf16[192,512]{1,0:T(8,128)(2,1)S(1)}, u32[]{:S(2)}, u32[]{:S(2)}) collective-permute-start(bf16[192,512]{1,0:T(8,128)(2,1)S(1)} %add_convert_fusion.5), channel_id=1, source_target_pairs={{0,3},{1,0},{2,1},{3,2},{4,7},{5,4},{6,5},{7,6},{8,11},{9,8},{10,9... | collective-permute-start | bytes 589832 | tf_op jit(solution)/shard_map/ppermute | solution.py:78
  579.4 15.1 %collective-permute-start.31 = (bf16[192,512]{1,0:T(8,128)(2,1)S(1)}, bf16[192,512]{1,0:T(8,128)(2,1)S(1)}, u32[]{:S(2)}, u32[]{:S(2)}) collective-permute-start(bf16[192,512]{1,0:T(8,128)(2,1)S(1)} %get-tuple-element.183), channel_id=1, source_target_pairs={{0,1},{1,2},{2,3},{3,0},{4,5},{5,6},{6,7},{7,4},{8,9},{9,10},{10,1... | collective-permute-start | bytes 589832 | tf_op jit(solution)/shard_map/ppermute | solution.py:78
  581.0 13.8 %collective-permute-start.33 = (bf16[192,512]{1,0:T(8,128)(2,1)S(1)}, bf16[192,512]{1,0:T(8,128)(2,1)S(1)}, u32[]{:S(2)}, u32[]{:S(2)}) collective-permute-start(bf16[192,512]{1,0:T(8,128)(2,1)S(1)} %get-tuple-element.184), channel_id=1, source_target_pairs={{0,2},{1,3},{2,0},{3,1},{4,6},{5,7},{6,4},{7,5},{8,10},{9,11},{10,... | collective-permute-start | bytes 589832 | tf_op jit(solution)/shard_map/ppermute | solution.py:78
  583.8 10.9 %collective-permute-start.32 = (bf16[192,512]{1,0:T(8,128)(2,1)S(1)}, bf16[192,512]{1,0:T(8,128)(2,1)S(1)}, u32[]{:S(2)}, u32[]{:S(2)}) collective-permute-start(bf16[192,512]{1,0:T(8,128)(2,1)S(1)} %get-tuple-element.185), channel_id=1, source_target_pairs={{0,3},{1,0},{2,1},{3,2},{4,7},{5,4},{6,5},{7,6},{8,11},{9,8},{10,9... | collective-permute-start | bytes 589832 | tf_op jit(solution)/shard_map/ppermute | solution.py:78
  594.9 48.3 %collective-permute-start.36 = (bf16[192,512]{1,0:T(8,128)(2,1)S(1)}, bf16[192,512]{1,0:T(8,128)(2,1)S(1)}, u32[]{:S(2)}, u32[]{:S(2)}) collective-permute-start(bf16[192,512]{1,0:T(8,128)(2,1)S(1)} %add_convert_fusion.6), channel_id=1, source_target_pairs={{0,1},{1,2},{2,3},{3,0},{4,5},{5,6},{6,7},{7,4},{8,9},{9,10},{10,1... | collective-permute-start | bytes 589832 | tf_op jit(solution)/shard_map/ppermute | solution.py:78
  596.7 46.4 %collective-permute-start.35 = (bf16[192,512]{1,0:T(8,128)(2,1)S(1)}, bf16[192,512]{1,0:T(8,128)(2,1)S(1)}, u32[]{:S(2)}, u32[]{:S(2)}) collective-permute-start(bf16[192,512]{1,0:T(8,128)(2,1)S(1)} %add_convert_fusion.6), channel_id=1, source_target_pairs={{0,2},{1,3},{2,0},{3,1},{4,6},{5,7},{6,4},{7,5},{8,10},{9,11},{10,... | collective-permute-start | bytes 589832 | tf_op jit(solution)/shard_map/ppermute | solution.py:78
  599.9 43.2 %collective-permute-start.34 = (bf16[192,512]{1,0:T(8,128)(2,1)S(1)}, bf16[192,512]{1,0:T(8,128)(2,1)S(1)}, u32[]{:S(2)}, u32[]{:S(2)}) collective-permute-start(bf16[192,512]{1,0:T(8,128)(2,1)S(1)} %add_convert_fusion.6), channel_id=1, source_target_pairs={{0,3},{1,0},{2,1},{3,2},{4,7},{5,4},{6,5},{7,6},{8,11},{9,8},{10,9... | collective-permute-start | bytes 589832 | tf_op jit(solution)/shard_map/ppermute | solution.py:78
  600.6 42.0 %all-to-all-start.7 = ((f32[32,1,64]{2,1,0:T(1,128)}), f32[32,1,64]{2,1,0:T(1,128)S(1)}, u32[]{:S(2)}, u32[]{:S(2)}) async-start(f32[32,1,64]{2,1,0:T(1,128)} %all_to_all.49), calls=%async_computation.9 | async-start | bytes 32768 | tf_op jit(solution)/shard_map/all_to_all | solution.py:119
  (133 other events, 1478.8 us)
Sparse Core Ops, SparseCore 0:
  11.4 57.8 all-gather.3
  71.5 103.4 all-gather.5
  177.8 61.8 all-gather.7
  271.7 95.3 reduce-scatter.3
  400.4 139.8 reduce-scatter.5
  554.1 94.6 reduce-scatter.7

commit v9 on v8

--- a/solution.py
+++ b/solution.py
@@ -431,6 +431,54 @@
             dimension_semantics=("arbitrary", "arbitrary"), vmem_limit_bytes=VMEM_BYTES
         ),
     )(lane.reshape(1), left, right)
+
+
+def dense_kernel(blocks, spill, first, mixed, second, tab_first, tab_mixed, tab_second, out):
+    tokens = out.shape[0] // blocks
+    extra = EXP_DEV * spill * blocks
+    lane = lax.broadcasted_iota(jnp.int32, (1, tokens), 1)
+    owner = lax.broadcasted_iota(jnp.int32, (extra, 1), 0) // (EXP_DEV * spill)
+    for i in range(blocks):
+        at = slice(i * MAIN, (i + 1) * MAIN)
+        hits = jnp.concatenate(
+            [
+                tab_first[at, :] == lane,
+                (tab_mixed[...] == lane) & (owner == i),
+                tab_second[at, :] == lane,
+            ],
+            0,
+        )
+        rows = jnp.concatenate([first[at, :], mixed[...], second[at, :]], 0)
+        out[i * tokens : (i + 1) * tokens, :] = matmul_tn(
+            hits.astype(f32).astype(bf16), rows
+        ).astype(bf16)
+
+
+def dense_rows(spill, owners, tokens, rows, table):
+    blocks = 4
+    edge = owners * MAIN
+    extra = EXP_DEV * spill * blocks
+    assert edge % extra == 0 and (edge + owners * EXP_DEV * spill) % (MAIN * blocks) == 0
+    start = (edge + owners * EXP_DEV * spill) // (MAIN * blocks)
+
+    def specs(width):
+        return [
+            pl.BlockSpec((MAIN * blocks, width), lambda g: (g, 0)),
+            pl.BlockSpec((extra, width), lambda g: (edge // extra + g, 0)),
+            pl.BlockSpec((MAIN * blocks, width), lambda g: (start + g, 0)),
+        ]
+
+    return pl.pallas_call(
+        functools.partial(dense_kernel, blocks, spill),
+        grid=(owners // blocks,),
+        in_specs=specs(rows.shape[1]) + specs(1),
+        out_specs=pl.BlockSpec((blocks * tokens, rows.shape[1]), lambda g: (g, 0)),
+        out_shape=jax.ShapeDtypeStruct((owners * tokens, rows.shape[1]), bf16),
+        cost_estimate=SMALL_COST,
+        compiler_params=pltpu.CompilerParams(
+            dimension_semantics=("arbitrary",), vmem_limit_bytes=VMEM_BYTES
+        ),
+    )(rows, rows, rows, table, table, table)
 
 
 def shared_kernel(normed2, cotangent, weights, _, dboth, hidden, part, dnormed):
@@ -532,6 +580,7 @@
     token_iota = lax.broadcasted_iota(jnp.int32, (slot_rows, tok_count), 1)
     table = jnp.sum(jnp.where(pick > 0, token_iota + 1, 0), 1).astype(jnp.int32) - 1
     table = exchange(table.reshape(owner_count, width))
+    row_table = to_experts(table)[:, None]
     half = D // 8
     lanes = lax.axis_size("tp")
     lane = lax.axis_index("tp")
@@ -561,8 +610,8 @@
     tile = 256 if edge % 256 == 0 else 128
     tiles = (edge // tile, extra // tile)
     big = 2 * (slot_rows + extra) * D * hid_wide
-    first_full, table, gateup_w, down_plain = lax.optimization_barrier(
-        (first_full, table, gateup_w, down_plain)
+    first_full, table, row_table, gateup_w, down_plain = lax.optimization_barrier(
+        (first_full, table, row_table, gateup_w, down_plain)
     )
     dy_all = lax.all_gather(after(cotangent, first_full), "ep", axis=0, tiled=True)
     edges = [0]
@@ -708,20 +757,17 @@
     )
     top = shift(drow[4], 1)
     bottom = shift(drow[5], 3)
-    dgate_rows = exchange(from_experts(dgate_rows[:, 0], owner_count)).reshape(-1)
-    top, bottom, dgate_rows, out_rows = lax.optimization_barrier(
-        (top, bottom, dgate_rows, out_rows)
+    out_dense = dense_rows(spill, owner_count, tok_count, out_rows, row_table)
+    top, bottom, out_dense, dgate_rows = lax.optimization_barrier(
+        (top, bottom, out_dense, dgate_rows)
     )
     from_prev_one = shift(plus(drow[2], top), 1)
     from_next_one = shift(after(drow[6], bottom), 3)
-    out_dense = jnp.einsum(
-        "ist,isd->itd", pick_in, from_experts(out_rows, owner_count), preferred_element_type=f32
-    )
-    out_dense = out_dense.astype(bf16).reshape(owner_count * tok_count, D)
-    (next_two, prev_two), out_dense, _, _ = lax.optimization_barrier(
+    dgate_rows = exchange(from_experts(dgate_rows[:, 0], owner_count)).reshape(-1)
+    (next_two, prev_two), dgate_rows, _, _ = lax.optimization_barrier(
         (
             (drow[3], plus(drow[7], bottom)),
-            out_dense,
+            dgate_rows,
             from_prev_one,
             from_next_one,
         )

time: 671 us -> 649 us (0.967)
  Pallas kernels: 111 us -> 127 us
  local copies, waits for them, and re-layouts: 118 us -> 102 us
  matrix products: 64.1 us -> 50.4 us
    all_to_all x8, waiting for transfers between devices: 39.1 us -> 60.1 us  [exchange(): return lax.all_to_all(value, 'ep', 0, 0, tiled=True)]
    reduce_scatter x1, waiting for transfers between devices: 23.7 us -> 3.86 us  [per_device(): lax.psum_scatter(after(out_dense, second_sum), 'ep', scatter_dimension=0,...]
    pallas_call x0 -> x1, Pallas kernels: none -> 15.6 us  [dense_rows(): pl.pallas_call(functools.partial(dense_kernel, blocks, spill), grid=(owne...]
    dot_general x1 -> x0, matrix products: 12.9 us -> none  [per_device(): jnp.einsum('ist,isd->itd', pick_in, from_experts(out_rows, owner_count),...]
    unnamed x260 -> x282, local copies, waits for them, and re-layouts: 40.3 us -> 42.5 us
  transfers between devices with their start and end apart: 57 -> 57, of which waited for: 30 -> 31; matrix products, arithmetic and copies ran while one was open for 31% -> 26% of each run, Pallas kernels for 13% -> 16%
where the time goes in v9:
time: 649 us; the launch traced here: 642 us
  waiting for transfers between devices  176 us (27%)
  Pallas kernels  127 us (20%)
  starting transfers between devices  115 us (18%)
  local copies, waits for them, and re-layouts  102 us (16%)
  other arithmetic  56.4 us (9%)
  matrix products  50.4 us (8%)
  between operations  16.3 us (3%)
    ppermute x43, waiting for transfers between devices, shift(): lax.ppermute(value, 'tp', [(i, (i + step) % lanes) for i in range(lanes)])  84.2 us
    ppermute x43, starting transfers between devices, shift(): lax.ppermute(value, 'tp', [(i, (i + step) % lanes) for i in range(lanes)])  65.4 us
    all_to_all x8, waiting for transfers between devices, exchange(): return lax.all_to_all(value, 'ep', 0, 0, tiled=True)  60.1 us
    pallas_call x3, Pallas kernels, row_call(): pl.pallas_call(body, grid=(total // tile,), in_specs=in_specs, out_specs=...  50.7 us
    all_to_all x8, starting transfers between devices, exchange(): return lax.all_to_all(value, 'ep', 0, 0, tiled=True)  49.1 us
    unnamed x282, local copies, waits for them, and re-layouts  42.5 us
    pallas_call x2, Pallas kernels, weight_grads(): pl.pallas_call(functools.partial(weight_grad_kernel, edge, spill), grid_s...  36.8 us
    all_gather x1, waiting for transfers between devices, per_device(): first_full = lax.all_gather(first_pack, 'ep', axis=0, tiled=True)  23 us
  transfers between devices with their start and end apart: 57, of which 31 were waited for; matrix products, arithmetic and copies ran while one was open for 26% of the time, Pallas kernels for 16%

profile of v9, /device:TPU:0, one launch (start us, length us, event | category | flops | bytes accessed | tf_op | source)
XLA Modules:
  0.0 642.5 jit_solution(11117006066133697113)
XLA Ops:
  15.2 7.4 %all-to-all-start = ((s32[32,1,72]{2,1,0:T(1,128)}), s32[32,1,72]{2,1,0:T(1,128)S(1)}, u32[]{:S(2)}, u32[]{:S(2)}) async-start(s32[32,1,72]{2,1,0:T(1,128)} %sub.84), calls=%async_computation | async-start | bytes 32768 | tf_op jit(solution)/shard_map/all_to_all | solution.py:119
  22.8 4.8 constant_dynamic-slice_fusion.31
  41.7 3.2 pad_maximum_fusion.1.refs_8_
  46.2 23.0 %all-gather.4.cloned.1.call-done = bf16[2048,2304]{1,0:T(8,128)(2,1)} async-done(((bf16[64,2304]{1,0:T(8,128)(2,1)}), bf16[2048,2304]{1,0:T(8,128)(2,1)}) %all-gather.4.cloned.1.call-update) | async-done | bytes 9437200 | tf_op jit(solution)/shard_map/all_gather | solution.py:565
  80.4 3.8 fusion.17
  102.3 3.1 fusion.118
  107.6 3.1 convolution_convert_fusion.2
  119.3 5.4 collective-permute-done.2
  132.4 5.3 collective-permute-done.4
  143.7 5.2 all-to-all-start.1
  149.8 23.7 %all-to-all-done.1 = bf16[32,72,256]{2,1,0:T(8,128)(2,1)} async-done(((bf16[32,72,256]{2,1,0:T(8,128)(2,1)}), bf16[32,72,256]{2,1,0:T(8,128)(2,1)}, u32[]{:S(2)}, u32[]{:S(2)}) %all-to-all-start.1) | async-done | bytes 1179680 | tf_op jit(solution)/shard_map/all_to_all | solution.py:119
  175.7 7.5 %all-to-all-start.2 = ((bf16[32,72,256]{2,1,0:T(8,128)(2,1)}), bf16[32,72,256]{2,1,0:T(8,128)(2,1)}, u32[]{:S(2)}, u32[]{:S(2)}) async-start(bf16[32,72,256]{2,1,0:T(8,128)(2,1)} %get-tuple-element.73), calls=%async_computation.2 | async-start | bytes 2359296 | tf_op jit(solution)/shard_map/all_to_all | solution.py:119
  192.3 11.3 %all-to-all-done.2 = bf16[32,72,256]{2,1,0:T(8,128)(2,1)} async-done(((bf16[32,72,256]{2,1,0:T(8,128)(2,1)}), bf16[32,72,256]{2,1,0:T(8,128)(2,1)}, u32[]{:S(2)}, u32[]{:S(2)}) %all-to-all-start.2) | async-done | bytes 1179680 | tf_op jit(solution)/shard_map/all_to_all | solution.py:119
  203.5 5.9 all-to-all-start.3
  217.1 14.8 %convolution_convert_fusion = bf16[32,72,2048]{2,1,0:T(8,128)(2,1)} fusion(bf16[32,192,2048]{2,1,0:T(8,128)(2,1)} %bitcast.119, s32[32,72]{1,0:T(8,128)S(1)} %bitcast.139), kind=kOutput, calls=%fused_computation.12 | convolution fusion | flops 1817100288 | bytes 34612224 | tf_op jit(solution)/shard_map/ist,itd->isd/dot_general | solution.py:695
  231.9 4.2 fusion.105
  237.5 4.3 pad_maximum_fusion.refs_0_.right
  241.8 5.1 collective-permute-done.8.refs_7_
  249.8 8.7 %shard_map.307 = (bf16[192,1536]{1,0:T(8,128)(2,1)S(1)}, bf16[192,768]{1,0:T(8,128)(2,1)S(1)}, bf16[192,2048]{1,0:T(8,128)(2,1)S(1)}, bf16[192,2048]{1,0:T(8,128)(2,1)S(1)}) custom-call(bf16[192,2048]{1,0:T(8,128)(2,1)S(1)} %copy-done.3, bf16[192,2048]{1,0:T(8,128)(2,1)S(1)} %copy-done, bf16[2048,2304]{1,0:T(8,128)(2,1)} %all-gather.8.cloned.1.call-done.weights, ...), custom_call_target="tpu_custom_call" | custom-call | flops 1 | bytes 1 | tf_op jit(solution)/shard_map/pallas_call | solution.py:504
  260.4 6.9 %shard_map.308 = bf16[2048,2304]{1,0:T(8,128)(2,1)} custom-call(bf16[192,2048]{1,0:T(8,128)(2,1)S(1)} %copy-done.4, bf16[192,2048]{1,0:T(8,128)(2,1)S(1)} %copy-done, bf16[192,1536]{1,0:T(8,128)(2,1)S(1)} %get-tuple-element.88.dboth, bf16[192,768]{1,0:T(8,128)(2,1)S(1)} %get-tuple-element.89.hidden), custom_call_target="tpu_custom_call" | custom-call | flops 1 | bytes 1 | tf_op jit(solution)/shard_map/pallas_call | solution.py:372
  269.6 11.0 %shard_map.306.refs_9_ = f32[2304,384]{1,0:T(8,128)S(1)} custom-call(bf16[2304,2048]{1,0:T(8,128)(2,1)} %pad_maximum_fusion.refs_0_.right, bf16[2,384,2048]{2,1,0:T(8,128)(2,1)S(1)} %pad.51.refs_1_.weight), custom_call_target="tpu_custom_call" | custom-call | flops 1 | bytes 1 | tf_op jit(solution)/shard_map/pallas_call | solution.py:281
  283.9 10.8 %collective-permute-done.11.refs_5_ = bf16[2304,256]{1,0:T(8,128)(2,1)} collective-permute-done((bf16[2304,256]{1,0:T(8,128)(2,1)}, bf16[2304,256]{1,0:T(8,128)(2,1)}, u32[]{:S(2)}, u32[]{:S(2)}) %collective-permute-start.11) | collective-permute-done | bytes 1179680 | tf_op jit(solution)/shard_map/ppermute | solution.py:78
  296.4 30.6 %shard_map.309 = (bf16[2304,384]{1,0:T(8,128)(2,1)}, bf16[2304,768]{1,0:T(8,128)(2,1)}, f32[2304,1]{1,0:T(8,128)S(1)}, bf16[2304,256]{1,0:T(8,128)(2,1)S(1)}, bf...) custom-call(bf16[2304,256]{1,0:T(8,128)(2,1)} %pad_maximum_fusion.2., ...), custom_call_target="tpu_custom_call" | custom-call | flops 1 | bytes 1 | tf_op jit(solution)/shard_map/pallas_call | solution.py:281
  339.3 9.2 %shard_map.310.first.mixed.second = bf16[2304,2048]{1,0:T(8,128)(2,1)} custom-call(bf16[2304,384]{1,0:T(8,128)(2,1)S(1)} %copy-done.8, bf16[2,384,2048]{2,1,0:T(8,128)(2,1)S(1)} %pad.51.refs_1_.weight), custom_call_target="tpu_custom_call" | custom-call | flops 1 | bytes 1 | tf_op jit(solution)/shard_map/pallas_call | solution.py:281
  348.5 15.6 %shard_map.311 = bf16[6144,2048]{1,0:T(8,128)(2,1)} custom-call(bf16[2304,2048]{1,0:T(8,128)(2,1)} %shard_map.310.first.mixed.second, bf16[2304,2048]{1,0:T(8,128)(2,1)} %shard_map.310.first.mixed.second, bf16[2304,2048]{1,0:T(8,128)(2,1)} %shard_map.310.first.mixed.second, s32[2304,1]{1,0:T(8,128)S(1)} %copy-done.6, s32[2304,1]{1,0:T(8,128)S(1)} %copy-done.6, ...), custom_call_target="tpu_custom_call" | custom-call | flops 1 | bytes 1 | tf_op jit(solution)/shard_map/pallas_call | solution.py:471
  372.5 7.5 %all-to-all-start.5 = ((f32[32,1,72]{2,1,0:T(1,128)}), f32[32,1,72]{2,1,0:T(1,128)S(1)}, u32[]{:S(2)}, u32[]{:S(2)}) async-start(f32[32,1,72]{2,1,0:T(1,128)} %bitcast.42), calls=%async_computation.7 | async-start | bytes 32768 | tf_op jit(solution)/shard_map/all_to_all | solution.py:119
  380.0 3.4 add_convert_fusion.1
  383.4 3.9 all-to-all-done.5
  391.4 4.4 collective-permute-done.14
  402.7 7.1 %all-to-all-start.4 = ((bf16[32,72,256]{2,1,0:T(8,128)(2,1)}), bf16[32,72,256]{2,1,0:T(8,128)(2,1)S(1)}, u32[]{:S(2)}, u32[]{:S(2)}) async-start(bf16[32,72,256]{2,1,0:T(8,128)(2,1)} %pad_maximum_fusion.4), calls=%async_computation.6 | async-start | bytes 2359296 | tf_op jit(solution)/shard_map/all_to_all | solution.py:119
  409.8 12.1 %collective-permute-done.16 = bf16[2304,256]{1,0:T(8,128)(2,1)} collective-permute-done((bf16[2304,256]{1,0:T(8,128)(2,1)S(1)}, bf16[2304,256]{1,0:T(8,128)(2,1)}, u32[]{:S(2)}, u32[]{:S(2)}) %collective-permute-start.16) | collective-permute-done | bytes 1179680 | tf_op jit(solution)/shard_map/ppermute | solution.py:78
  428.2 3.9 all-to-all-start.6
  444.2 17.9 %all-to-all-done.6 = bf16[32,72,256]{2,1,0:T(8,128)(2,1)S(1)} async-done(((bf16[32,72,256]{2,1,0:T(8,128)(2,1)}), bf16[32,72,256]{2,1,0:T(8,128)(2,1)S(1)}, u32[]{:S(2)}, u32[]{:S(2)}) %all-to-all-start.6) | async-done | bytes 1179680 | tf_op jit(solution)/shard_map/all_to_all | solution.py:119
  464.7 4.4 collective-permute-start.22
  472.5 5.1 collective-permute-done.22
  492.0 8.1 %collective-permute-done.28 = bf16[192,576]{1,0:T(8,128)(2,1)S(1)} collective-permute-done((bf16[192,576]{1,0:T(8,128)(2,1)S(1)}, bf16[192,576]{1,0:T(8,128)(2,1)S(1)}, u32[]{:S(2)}, u32[]{:S(2)}) %collective-permute-start.28) | collective-permute-done | bytes 221216 | tf_op jit(solution)/shard_map/ppermute | solution.py:78
  500.1 3.4 collective-permute-done.27
  515.0 3.9 reduce-scatter.6.cloned.1.call-done
  524.6 7.9 %shard_map.312 = bf16[2048,2304]{1,0:T(8,128)(2,1)} custom-call(bf16[192,2048]{1,0:T(8,128)(2,1)S(1)} %copy-done.13, bf16[192,2048]{1,0:T(8,128)(2,1)S(1)} %copy-done.5, bf16[192,2048]{1,0:T(8,128)(2,1)S(1)} %fusion.99.dmid, bf16[192,768]{1,0:T(8,128)(2,1)S(1)} %copy-done.25, bf16[192,640]{1,0:T(8,128)(2,1)S(1)} %copy-done.27, ...), custom_call_target="tpu_custom_call" | custom-call | flops 1 | bytes 1 | tf_op jit(solution)/shard_map/pallas_call | solution.py:346
  534.8 3.2 collective-permute-done.30
  546.6 3.5 collective-permute-done.37
  563.2 3.7 collective-permute-done.41
  567.2 3.4 fusion.44
  575.2 3.1 collective-permute-start.35
  579.1 4.6 all-to-all-start.7
  584.3 17.4 %shard_map.314 = f32[2,352,2048]{2,1,0:T(8,128)} custom-call(s32[1]{0:T(128)} %constant.114.clone.1.lane, bf16[2304,384]{1,0:T(8,128)(2,1)S(1)} %copy-done.9, bf16[2304,2048]{1,0:T(8,128)(2,1)} %pad_maximum_fusion.refs_0_.right), custom_call_target="tpu_custom_call" | custom-call | flops 1 | bytes 1 | tf_op jit(solution)/shard_map/pallas_call | solution.py:425
  601.7 19.4 %shard_map.313 = (f32[2,352,2048]{2,1,0:T(8,128)}, f32[2,352,2048]{2,1,0:T(8,128)}) custom-call(s32[1]{0:T(128)} %bitcast.61.lane, bf16[2304,768]{1,0:T(8,128)(2,1)S(1)} %copy-done.10, bf16[2304,2048]{1,0:T(8,128)(2,1)} %get-tuple-element.123.right), custom_call_target="tpu_custom_call" | custom-call | flops 1 | bytes 1 | tf_op jit(solution)/shard_map/pallas_call | solution.py:425
  622.9 4.5 reduce-scatter.8.cloned.1.call-done
  (552 shorter events, 236.6 us)
Async XLA Ops:
  7.2 62.1 %all-gather.4.cloned.1.call-start = ((), (), s32[]{:S(2)}) async-start(), calls=%async_computation.11 | async-start | bytes 9732096 | tf_op jit(solution)/shard_map/all_gather | solution.py:565
  15.2 30.0 %all-to-all-start = ((s32[32,1,72]{2,1,0:T(1,128)}), s32[32,1,72]{2,1,0:T(1,128)S(1)}, u32[]{:S(2)}, u32[]{:S(2)}) async-start(s32[32,1,72]{2,1,0:T(1,128)} %sub.84), calls=%async_computation | async-start | bytes 32768 | tf_op jit(solution)/shard_map/all_to_all | solution.py:119
  22.6 151.0 %all-gather.6.cloned.1.call-start = ((), (), s32[]{:S(2)}) async-start(), calls=%async_computation.12 | async-start | bytes 25952256 | tf_op jit(solution)/shard_map/all_gather | solution.py:616
  112.6 12.1 %collective-permute-start.2 = (bf16[192,512]{1,0:T(8,128)(2,1)S(1)}, bf16[192,512]{1,0:T(8,128)(2,1)S(1)}, u32[]{:S(2)}, u32[]{:S(2)}) collective-permute-start(bf16[192,512]{1,0:T(8,128)(2,1)S(1)} %get-tuple-element.198), channel_id=1, source_target_pairs={{0,2},{1,3},{2,0},{3,1},{4,6},{5,7},{6,4},{7,5},{8,10},{9,11},{10,... | collective-permute-start | bytes 589832 | tf_op jit(solution)/shard_map/ppermute | solution.py:78
  115.4 9.3 %collective-permute-start.1 = (bf16[192,512]{1,0:T(8,128)(2,1)S(1)}, bf16[192,512]{1,0:T(8,128)(2,1)S(1)}, u32[]{:S(2)}, u32[]{:S(2)}) collective-permute-start(bf16[192,512]{1,0:T(8,128)(2,1)S(1)} %get-tuple-element.199), channel_id=1, source_target_pairs={{0,3},{1,0},{2,1},{3,2},{4,7},{5,4},{6,5},{7,6},{8,11},{9,8},{10,9... | collective-permute-start | bytes 589832 | tf_op jit(solution)/shard_map/ppermute | solution.py:78
  126.1 11.6 %collective-permute-start.4 = (bf16[192,512]{1,0:T(8,128)(2,1)S(1)}, bf16[192,512]{1,0:T(8,128)(2,1)}, u32[]{:S(2)}, u32[]{:S(2)}) collective-permute-start(bf16[192,512]{1,0:T(8,128)(2,1)S(1)} %add_convert_fusion.8), channel_id=1, source_target_pairs={{0,2},{1,3},{2,0},{3,1},{4,6},{5,7},{6,4},{7,5},{8,10},{9,11},{10,... | collective-permute-start | bytes 589832 | tf_op jit(solution)/shard_map/ppermute | solution.py:78
  128.5 9.2 %collective-permute-start.3 = (bf16[192,512]{1,0:T(8,128)(2,1)S(1)}, bf16[192,512]{1,0:T(8,128)(2,1)}, u32[]{:S(2)}, u32[]{:S(2)}) collective-permute-start(bf16[192,512]{1,0:T(8,128)(2,1)S(1)} %add_convert_fusion.8), channel_id=1, source_target_pairs={{0,3},{1,0},{2,1},{3,2},{4,7},{5,4},{6,5},{7,6},{8,11},{9,8},{10,9... | collective-permute-start | bytes 589832 | tf_op jit(solution)/shard_map/ppermute | solution.py:78
  143.7 29.8 %all-to-all-start.1 = ((bf16[32,72,256]{2,1,0:T(8,128)(2,1)}), bf16[32,72,256]{2,1,0:T(8,128)(2,1)}, u32[]{:S(2)}, u32[]{:S(2)}) async-start(bf16[32,72,256]{2,1,0:T(8,128)(2,1)} %get-tuple-element.157), calls=%async_computation.1 | async-start | bytes 2359296 | tf_op jit(solution)/shard_map/all_to_all | solution.py:119
  149.0 98.6 %all-gather.8.cloned.1.call-start = ((), (), s32[]{:S(2)}) async-start(), calls=%async_computation.13 | async-start | bytes 9732096 | tf_op jit(solution)/shard_map/all_gather | solution.py:689
  175.7 27.8 %all-to-all-start.2 = ((bf16[32,72,256]{2,1,0:T(8,128)(2,1)}), bf16[32,72,256]{2,1,0:T(8,128)(2,1)}, u32[]{:S(2)}, u32[]{:S(2)}) async-start(bf16[32,72,256]{2,1,0:T(8,128)(2,1)} %get-tuple-element.73), calls=%async_computation.2 | async-start | bytes 2359296 | tf_op jit(solution)/shard_map/all_to_all | solution.py:119
  189.3 52.5 %collective-permute-start.9 = (bf16[2304,256]{1,0:T(8,128)(2,1)}, bf16[2304,256]{1,0:T(8,128)(2,1)}, u32[]{:S(2)}, u32[]{:S(2)}) collective-permute-start(bf16[2304,256]{1,0:T(8,128)(2,1)} %pad_maximum_fusion.2.refs_0_), channel_id=1, source_target_pairs={{0,3},{1,0},{2,1},{3,2},{4,7},{5,4},{6,5},{7,6},{8,11},{9,8},{10,9... | collective-permute-start | bytes 3538952 | tf_op jit(solution)/shard_map/ppermute | solution.py:78
  192.3 49.5 %collective-permute-start.6 = (bf16[2304,256]{1,0:T(8,128)(2,1)}, bf16[2304,256]{1,0:T(8,128)(2,1)}, u32[]{:S(2)}, u32[]{:S(2)}) collective-permute-start(bf16[2304,256]{1,0:T(8,128)(2,1)} %pad_maximum_fusion.2.refs_0_), channel_id=1, source_target_pairs={{0,1},{1,2},{2,3},{3,0},{4,5},{5,6},{6,7},{7,4},{8,9},{9,10},{10,1... | collective-permute-start | bytes 3538952 | tf_op jit(solution)/shard_map/ppermute | solution.py:78
  203.5 13.2 %all-to-all-start.3 = ((f32[32,1,72]{2,1,0:T(1,128)}), f32[32,1,72]{2,1,0:T(1,128)S(1)}, u32[]{:S(2)}, u32[]{:S(2)}) async-start(f32[32,1,72]{2,1,0:T(1,128)} %bitcast.34), calls=%async_computation.3 | async-start | bytes 32768 | tf_op jit(solution)/shard_map/all_to_all | solution.py:119
  209.4 154.8 %reduce-scatter.4.cloned.1.call-start = ((), (), s32[]{:S(2)}) async-start(), calls=%async_computation.14 | async-start | bytes 9732096 | tf_op jit(solution)/shard_map/reduce_scatter | solution.py:732
  212.8 34.1 %collective-permute-start.8 = (bf16[2304,256]{1,0:T(8,128)(2,1)}, bf16[2304,256]{1,0:T(8,128)(2,1)}, u32[]{:S(2)}, u32[]{:S(2)}) collective-permute-start(bf16[2304,256]{1,0:T(8,128)(2,1)} %pad_maximum_fusion.3.refs_1_), channel_id=1, source_target_pairs={{0,1},{1,2},{2,3},{3,0},{4,5},{5,6},{6,7},{7,4},{8,9},{9,10},{10,1... | collective-permute-start | bytes 3538952 | tf_op jit(solution)/shard_map/ppermute | solution.py:78
  214.3 32.5 %collective-permute-start.7 = (bf16[2304,256]{1,0:T(8,128)(2,1)}, bf16[2304,256]{1,0:T(8,128)(2,1)}, u32[]{:S(2)}, u32[]{:S(2)}) collective-permute-start(bf16[2304,256]{1,0:T(8,128)(2,1)} %pad_maximum_fusion.3.refs_1_), channel_id=1, source_target_pairs={{0,3},{1,0},{2,1},{3,2},{4,7},{5,4},{6,5},{7,6},{8,11},{9,8},{10,9... | collective-permute-start | bytes 3538952 | tf_op jit(solution)/shard_map/ppermute | solution.py:78
  267.3 251.5 %reduce-scatter.6.cloned.1.call-start = ((), (), s32[]{:S(2)}) async-start(), calls=%async_computation.15 | async-start | bytes 25952256 | tf_op jit(solution)/shard_map/reduce_scatter | solution.py:784
  267.4 27.3 %collective-permute-start.11 = (bf16[2304,256]{1,0:T(8,128)(2,1)}, bf16[2304,256]{1,0:T(8,128)(2,1)}, u32[]{:S(2)}, u32[]{:S(2)}) collective-permute-start(bf16[2304,256]{1,0:T(8,128)(2,1)} %collective-permute-done.7.refs_3_), channel_id=1, source_target_pairs={{0,3},{1,0},{2,1},{3,2},{4,7},{5,4},{6,5},{7,6},{8,11},{9,8},{10,9... | collective-permute-start | bytes 3538952 | tf_op jit(solution)/shard_map/ppermute | solution.py:78
  267.7 28.7 %collective-permute-start.10 = (bf16[2304,256]{1,0:T(8,128)(2,1)}, bf16[2304,256]{1,0:T(8,128)(2,1)}, u32[]{:S(2)}, u32[]{:S(2)}) collective-permute-start(bf16[2304,256]{1,0:T(8,128)(2,1)} %collective-permute-done.6.refs_6_), channel_id=1, source_target_pairs={{0,1},{1,2},{2,3},{3,0},{4,5},{5,6},{6,7},{7,4},{8,9},{9,10},{10,1... | collective-permute-start | bytes 3538952 | tf_op jit(solution)/shard_map/ppermute | solution.py:78
  333.2 31.0 %collective-permute-start.12 = (bf16[2304,256]{1,0:T(8,128)(2,1)}, bf16[2304,256]{1,0:T(8,128)(2,1)}, u32[]{:S(2)}, u32[]{:S(2)}) collective-permute-start(bf16[2304,256]{1,0:T(8,128)(2,1)} %get-tuple-element.92), channel_id=1, source_target_pairs={{0,1},{1,2},{2,3},{3,0},{4,5},{5,6},{6,7},{7,4},{8,9},{9,10},{10,1... | collective-permute-start | bytes 3538952 | tf_op jit(solution)/shard_map/ppermute | solution.py:78
  333.4 30.7 %collective-permute-start.13 = (bf16[2304,256]{1,0:T(8,128)(2,1)}, bf16[2304,256]{1,0:T(8,128)(2,1)}, u32[]{:S(2)}, u32[]{:S(2)}) collective-permute-start(bf16[2304,256]{1,0:T(8,128)(2,1)} %get-tuple-element.93), channel_id=1, source_target_pairs={{0,3},{1,0},{2,1},{3,2},{4,7},{5,4},{6,5},{7,6},{8,11},{9,8},{10,9... | collective-permute-start | bytes 3538952 | tf_op jit(solution)/shard_map/ppermute | solution.py:78
  365.8 25.6 %collective-permute-start.15 = (bf16[2304,256]{1,0:T(8,128)(2,1)S(1)}, bf16[2304,256]{1,0:T(8,128)(2,1)}, u32[]{:S(2)}, u32[]{:S(2)}) collective-permute-start(bf16[2304,256]{1,0:T(8,128)(2,1)S(1)} %copy-done.37), channel_id=1, source_target_pairs={{0,3},{1,0},{2,1},{3,2},{4,7},{5,4},{6,5},{7,6},{8,11},{9,8},{10,9... | collective-permute-start | bytes 3538952 | tf_op jit(solution)/shard_map/ppermute | solution.py:78
  368.6 27.2 %collective-permute-start.14 = (bf16[2304,256]{1,0:T(8,128)(2,1)}, bf16[2304,256]{1,0:T(8,128)(2,1)}, u32[]{:S(2)}, u32[]{:S(2)}) collective-permute-start(bf16[2304,256]{1,0:T(8,128)(2,1)} %add_convert_fusion.3), channel_id=1, source_target_pairs={{0,1},{1,2},{2,3},{3,0},{4,5},{5,6},{6,7},{7,4},{8,9},{9,10},{10,1... | collective-permute-start | bytes 3538952 | tf_op jit(solution)/shard_map/ppermute | solution.py:78
  372.5 14.8 %all-to-all-start.5 = ((f32[32,1,72]{2,1,0:T(1,128)}), f32[32,1,72]{2,1,0:T(1,128)S(1)}, u32[]{:S(2)}, u32[]{:S(2)}) async-start(f32[32,1,72]{2,1,0:T(1,128)} %bitcast.42), calls=%async_computation.7 | async-start | bytes 32768 | tf_op jit(solution)/shard_map/all_to_all | solution.py:119
  395.8 26.1 %collective-permute-start.16 = (bf16[2304,256]{1,0:T(8,128)(2,1)S(1)}, bf16[2304,256]{1,0:T(8,128)(2,1)}, u32[]{:S(2)}, u32[]{:S(2)}) collective-permute-start(bf16[2304,256]{1,0:T(8,128)(2,1)S(1)} %copy-done.35), channel_id=1, source_target_pairs={{0,1},{1,2},{2,3},{3,0},{4,5},{5,6},{6,7},{7,4},{8,9},{9,10},{10,1... | collective-permute-start | bytes 3538952 | tf_op jit(solution)/shard_map/ppermute | solution.py:78
  396.5 25.4 %collective-permute-start.17 = (bf16[2304,256]{1,0:T(8,128)(2,1)}, bf16[2304,256]{1,0:T(8,128)(2,1)}, u32[]{:S(2)}, u32[]{:S(2)}) collective-permute-start(bf16[2304,256]{1,0:T(8,128)(2,1)} %add_convert_fusion.1), channel_id=1, source_target_pairs={{0,3},{1,0},{2,1},{3,2},{4,7},{5,4},{6,5},{7,6},{8,11},{9,8},{10,9... | collective-permute-start | bytes 3538952 | tf_op jit(solution)/shard_map/ppermute | solution.py:78
  402.7 25.4 %all-to-all-start.4 = ((bf16[32,72,256]{2,1,0:T(8,128)(2,1)}), bf16[32,72,256]{2,1,0:T(8,128)(2,1)S(1)}, u32[]{:S(2)}, u32[]{:S(2)}) async-start(bf16[32,72,256]{2,1,0:T(8,128)(2,1)} %pad_maximum_fusion.4), calls=%async_computation.6 | async-start | bytes 2359296 | tf_op jit(solution)/shard_map/all_to_all | solution.py:119
  428.2 34.0 %all-to-all-start.6 = ((bf16[32,72,256]{2,1,0:T(8,128)(2,1)}), bf16[32,72,256]{2,1,0:T(8,128)(2,1)S(1)}, u32[]{:S(2)}, u32[]{:S(2)}) async-start(bf16[32,72,256]{2,1,0:T(8,128)(2,1)} %pad_maximum_fusion.5), calls=%async_computation.8 | async-start | bytes 2359296 | tf_op jit(solution)/shard_map/all_to_all | solution.py:119
  432.1 195.2 %reduce-scatter.8.cloned.1.call-start = ((), (), s32[]{:S(2)}) async-start(), calls=%async_computation.16 | async-start | bytes 9732096 | tf_op jit(solution)/shard_map/reduce_scatter | solution.py:871
  439.3 25.1 %collective-permute-start.18 = (bf16[192,512]{1,0:T(8,128)(2,1)S(1)}, bf16[192,512]{1,0:T(8,128)(2,1)S(1)}, u32[]{:S(2)}, u32[]{:S(2)}) collective-permute-start(bf16[192,512]{1,0:T(8,128)(2,1)S(1)} %get-tuple-element.190), channel_id=1, source_target_pairs={{0,1},{1,2},{2,3},{3,0},{4,5},{5,6},{6,7},{7,4},{8,9},{9,10},{10,1... | collective-permute-start | bytes 589832 | tf_op jit(solution)/shard_map/ppermute | solution.py:78
  441.4 23.1 %collective-permute-start.20 = (bf16[192,512]{1,0:T(8,128)(2,1)S(1)}, bf16[192,512]{1,0:T(8,128)(2,1)S(1)}, u32[]{:S(2)}, u32[]{:S(2)}) collective-permute-start(bf16[192,512]{1,0:T(8,128)(2,1)S(1)} %get-tuple-element.191), channel_id=1, source_target_pairs={{0,2},{1,3},{2,0},{3,1},{4,6},{5,7},{6,4},{7,5},{8,10},{9,11},{10,... | collective-permute-start | bytes 589832 | tf_op jit(solution)/shard_map/ppermute | solution.py:78
  443.3 21.2 %collective-permute-start.19 = (bf16[192,512]{1,0:T(8,128)(2,1)S(1)}, bf16[192,512]{1,0:T(8,128)(2,1)S(1)}, u32[]{:S(2)}, u32[]{:S(2)}) collective-permute-start(bf16[192,512]{1,0:T(8,128)(2,1)S(1)} %get-tuple-element.192), channel_id=1, source_target_pairs={{0,3},{1,0},{2,1},{3,2},{4,7},{5,4},{6,5},{7,6},{8,11},{9,8},{10,9... | collective-permute-start | bytes 589832 | tf_op jit(solution)/shard_map/ppermute | solution.py:78
  464.7 12.9 %collective-permute-start.22 = (bf16[192,512]{1,0:T(8,128)(2,1)S(1)}, bf16[192,512]{1,0:T(8,128)(2,1)S(1)}, u32[]{:S(2)}, u32[]{:S(2)}) collective-permute-start(bf16[192,512]{1,0:T(8,128)(2,1)S(1)} %fusion.66), channel_id=1, source_target_pairs={{0,2},{1,3},{2,0},{3,1},{4,6},{5,7},{6,4},{7,5},{8,10},{9,11},{10,... | collective-permute-start | bytes 589832 | tf_op jit(solution)/shard_map/ppermute | solution.py:78
  487.2 12.9 %collective-permute-start.28 = (bf16[192,576]{1,0:T(8,128)(2,1)S(1)}, bf16[192,576]{1,0:T(8,128)(2,1)S(1)}, u32[]{:S(2)}, u32[]{:S(2)}) collective-permute-start(bf16[192,576]{1,0:T(8,128)(2,1)S(1)} %pad_maximum_fusion.16), channel_id=1, source_target_pairs={{0,3},{1,0},{2,1},{3,2},{4,7},{5,4},{6,5},{7,6},{8,11},{9,8},{10,9... | collective-permute-start | bytes 663560 | tf_op jit(solution)/shard_map/ppermute | solution.py:78
  489.4 14.1 %collective-permute-start.27 = (bf16[192,576]{1,0:T(8,128)(2,1)S(1)}, bf16[192,576]{1,0:T(8,128)(2,1)S(1)}, u32[]{:S(2)}, u32[]{:S(2)}) collective-permute-start(bf16[192,576]{1,0:T(8,128)(2,1)S(1)} %pad_maximum_fusion.16), channel_id=1, source_target_pairs={{0,1},{1,2},{2,3},{3,0},{4,5},{5,6},{6,7},{7,4},{8,9},{9,10},{10,1... | collective-permute-start | bytes 663560 | tf_op jit(solution)/shard_map/ppermute | solution.py:78
  489.4 14.1 %collective-permute-start.29 = (bf16[192,576]{1,0:T(8,128)(2,1)S(1)}, bf16[192,576]{1,0:T(8,128)(2,1)S(1)}, u32[]{:S(2)}, u32[]{:S(2)}) collective-permute-start(bf16[192,576]{1,0:T(8,128)(2,1)S(1)} %pad_maximum_fusion.16), channel_id=1, source_target_pairs={{0,2},{1,3},{2,0},{3,1},{4,6},{5,7},{6,4},{7,5},{8,10},{9,11},{10,... | collective-permute-start | bytes 663560 | tf_op jit(solution)/shard_map/ppermute | solution.py:78
  541.2 8.9 %collective-permute-start.37 = (bf16[192,512]{1,0:T(8,128)(2,1)S(1)}, bf16[192,512]{1,0:T(8,128)(2,1)S(1)}, u32[]{:S(2)}, u32[]{:S(2)}) collective-permute-start(bf16[192,512]{1,0:T(8,128)(2,1)S(1)} %get-tuple-element.176), channel_id=1, source_target_pairs={{0,1},{1,2},{2,3},{3,0},{4,5},{5,6},{6,7},{7,4},{8,9},{9,10},{10,1... | collective-permute-start | bytes 589832 | tf_op jit(solution)/shard_map/ppermute | solution.py:78
  541.6 10.4 %collective-permute-start.39 = (bf16[192,512]{1,0:T(8,128)(2,1)S(1)}, bf16[192,512]{1,0:T(8,128)(2,1)S(1)}, u32[]{:S(2)}, u32[]{:S(2)}) collective-permute-start(bf16[192,512]{1,0:T(8,128)(2,1)S(1)} %get-tuple-element.177), channel_id=1, source_target_pairs={{0,2},{1,3},{2,0},{3,1},{4,6},{5,7},{6,4},{7,5},{8,10},{9,11},{10,... | collective-permute-start | bytes 589832 | tf_op jit(solution)/shard_map/ppermute | solution.py:78
  552.7 9.6 %collective-permute-start.42 = (bf16[192,512]{1,0:T(8,128)(2,1)S(1)}, bf16[192,512]{1,0:T(8,128)(2,1)S(1)}, u32[]{:S(2)}, u32[]{:S(2)}) collective-permute-start(bf16[192,512]{1,0:T(8,128)(2,1)S(1)} %add_convert_fusion.5), channel_id=1, source_target_pairs={{0,1},{1,2},{2,3},{3,0},{4,5},{5,6},{6,7},{7,4},{8,9},{9,10},{10,1... | collective-permute-start | bytes 589832 | tf_op jit(solution)/shard_map/ppermute | solution.py:78
  554.0 12.9 %collective-permute-start.41 = (bf16[192,512]{1,0:T(8,128)(2,1)S(1)}, bf16[192,512]{1,0:T(8,128)(2,1)S(1)}, u32[]{:S(2)}, u32[]{:S(2)}) collective-permute-start(bf16[192,512]{1,0:T(8,128)(2,1)S(1)} %add_convert_fusion.5), channel_id=1, source_target_pairs={{0,2},{1,3},{2,0},{3,1},{4,6},{5,7},{6,4},{7,5},{8,10},{9,11},{10,... | collective-permute-start | bytes 589832 | tf_op jit(solution)/shard_map/ppermute | solution.py:78
  556.9 10.1 %collective-permute-start.40 = (bf16[192,512]{1,0:T(8,128)(2,1)S(1)}, bf16[192,512]{1,0:T(8,128)(2,1)S(1)}, u32[]{:S(2)}, u32[]{:S(2)}) collective-permute-start(bf16[192,512]{1,0:T(8,128)(2,1)S(1)} %add_convert_fusion.5), channel_id=1, source_target_pairs={{0,3},{1,0},{2,1},{3,2},{4,7},{5,4},{6,5},{7,6},{8,11},{9,8},{10,9... | collective-permute-start | bytes 589832 | tf_op jit(solution)/shard_map/ppermute | solution.py:78
  557.8 15.0 %collective-permute-start.31 = (bf16[192,512]{1,0:T(8,128)(2,1)S(1)}, bf16[192,512]{1,0:T(8,128)(2,1)S(1)}, u32[]{:S(2)}, u32[]{:S(2)}) collective-permute-start(bf16[192,512]{1,0:T(8,128)(2,1)S(1)} %get-tuple-element.183), channel_id=1, source_target_pairs={{0,1},{1,2},{2,3},{3,0},{4,5},{5,6},{6,7},{7,4},{8,9},{9,10},{10,1... | collective-permute-start | bytes 589832 | tf_op jit(solution)/shard_map/ppermute | solution.py:78
  559.5 13.6 %collective-permute-start.33 = (bf16[192,512]{1,0:T(8,128)(2,1)S(1)}, bf16[192,512]{1,0:T(8,128)(2,1)S(1)}, u32[]{:S(2)}, u32[]{:S(2)}) collective-permute-start(bf16[192,512]{1,0:T(8,128)(2,1)S(1)} %get-tuple-element.184), channel_id=1, source_target_pairs={{0,2},{1,3},{2,0},{3,1},{4,6},{5,7},{6,4},{7,5},{8,10},{9,11},{10,... | collective-permute-start | bytes 589832 | tf_op jit(solution)/shard_map/ppermute | solution.py:78
  562.3 10.8 %collective-permute-start.32 = (bf16[192,512]{1,0:T(8,128)(2,1)S(1)}, bf16[192,512]{1,0:T(8,128)(2,1)S(1)}, u32[]{:S(2)}, u32[]{:S(2)}) collective-permute-start(bf16[192,512]{1,0:T(8,128)(2,1)S(1)} %get-tuple-element.185), channel_id=1, source_target_pairs={{0,3},{1,0},{2,1},{3,2},{4,7},{5,4},{6,5},{7,6},{8,11},{9,8},{10,9... | collective-permute-start | bytes 589832 | tf_op jit(solution)/shard_map/ppermute | solution.py:78
  573.2 48.5 %collective-permute-start.36 = (bf16[192,512]{1,0:T(8,128)(2,1)S(1)}, bf16[192,512]{1,0:T(8,128)(2,1)S(1)}, u32[]{:S(2)}, u32[]{:S(2)}) collective-permute-start(bf16[192,512]{1,0:T(8,128)(2,1)S(1)} %add_convert_fusion.6), channel_id=1, source_target_pairs={{0,1},{1,2},{2,3},{3,0},{4,5},{5,6},{6,7},{7,4},{8,9},{9,10},{10,1... | collective-permute-start | bytes 589832 | tf_op jit(solution)/shard_map/ppermute | solution.py:78
  575.2 46.5 %collective-permute-start.35 = (bf16[192,512]{1,0:T(8,128)(2,1)S(1)}, bf16[192,512]{1,0:T(8,128)(2,1)S(1)}, u32[]{:S(2)}, u32[]{:S(2)}) collective-permute-start(bf16[192,512]{1,0:T(8,128)(2,1)S(1)} %add_convert_fusion.6), channel_id=1, source_target_pairs={{0,2},{1,3},{2,0},{3,1},{4,6},{5,7},{6,4},{7,5},{8,10},{9,11},{10,... | collective-permute-start | bytes 589832 | tf_op jit(solution)/shard_map/ppermute | solution.py:78
  578.4 43.3 %collective-permute-start.34 = (bf16[192,512]{1,0:T(8,128)(2,1)S(1)}, bf16[192,512]{1,0:T(8,128)(2,1)S(1)}, u32[]{:S(2)}, u32[]{:S(2)}) collective-permute-start(bf16[192,512]{1,0:T(8,128)(2,1)S(1)} %add_convert_fusion.6), channel_id=1, source_target_pairs={{0,3},{1,0},{2,1},{3,2},{4,7},{5,4},{6,5},{7,6},{8,11},{9,8},{10,9... | collective-permute-start | bytes 589832 | tf_op jit(solution)/shard_map/ppermute | solution.py:78
  579.1 42.1 %all-to-all-start.7 = ((f32[32,1,64]{2,1,0:T(1,128)}), f32[32,1,64]{2,1,0:T(1,128)S(1)}, u32[]{:S(2)}, u32[]{:S(2)}) async-start(f32[32,1,64]{2,1,0:T(1,128)} %all_to_all.49), calls=%async_computation.9 | async-start | bytes 32768 | tf_op jit(solution)/shard_map/all_to_all | solution.py:119
  (144 other events, 800.5 us)
Sparse Core Ops, SparseCore 0:
  11.4 57.8 all-gather.3
  71.5 102.0 all-gather.5
  176.4 62.1 all-gather.7
  267.5 94.1 reduce-scatter.3
  366.0 152.8 reduce-scatter.5
  532.6 94.6 reduce-scatter.7
